TPU v7x, 32 devices: a whole 2x2x4 slice. The times are simulated.
32 devices in a mesh: seq: 8 (over y, x, core), head: 4 (over z).
Axes of the slice: x: 2, y: 2, z: 4, core: 2. Of those that a mesh axis runs over, the one named last changes fastest.
Arguments:
- query: bfloat16 [6144, 4096], P('seq', 'head'), may hold values from -6 to 6
- key_in: bfloat16 [6144, 4096], P('seq', 'head'), may hold values from -6 to 6
- value: bfloat16 [6144, 4096], P('seq', 'head'), may hold values from -60 to 60
- out_grad: bfloat16 [6144, 4096], P('seq', 'head'), may hold values from -6 to 6
- gain: float32 [4096], P('head'), may hold values from 0.1 to 1.9
Outputs:
- query_grad: bfloat16 [6144, 4096], P('seq', 'head')
- key_grad: bfloat16 [6144, 4096], P('seq', 'head')
- value_grad: bfloat16 [6144, 4096], P('seq', 'head')
All inputs are finite; a program needn't handle non-finite values.
Results may differ from a plain program's by a relative error of at most 0.0058.
Values sent between devices are 32-bit elements; how exact they have to be, the bound alone decides.
No kernel may reach another device: no remote copies, remote signals or barrier semaphores. Data moves between devices by JAX's collectives and lax.ppermute only.
A program may use at most 128 MiB of HBM per device.

v0:
```python
import jax
import jax.numpy as jnp
from jax import lax
from jax.sharding import PartitionSpec as P

HEAD_DIM = 128


def entering(value, axis, join, neutral, backward):
    count, mine = (lax.axis_size(axis), lax.axis_index(axis))
    pieces = lax.all_gather(value, axis)
    if backward:
        pieces = pieces[::-1]
        mine = count - 1 - mine
    total = jnp.full_like(value, 0) + jnp.asarray(neutral, value.dtype)

    def hop(position, total):
        longer = join(total, pieces[position])
        return jnp.where(position < mine, longer, total)

    return lax.fori_loop(0, count - 1, hop, total)


def split_heads(x, heads, depth):
    return x.reshape(x.shape[0], heads, depth).transpose(1, 0, 2)


def join_heads(x):
    return x.transpose(1, 0, 2).reshape(x.shape[1], x.shape[0] * x.shape[2])


def lower_mask(rows):
    return jnp.arange(rows)[:, None] >= jnp.arange(rows)[None, :]


def add_states(earlier, later):
    return earlier + later


def shards(query, key_in, value, out_grad, gain):
    rows, width = query.shape
    depth = HEAD_DIM
    heads = width // depth
    mask = lower_mask(rows)
    qh = split_heads(query, heads, depth)
    kh = split_heads(key_in, heads, depth)
    vh = split_heads(value, heads, depth)
    kv_local = jnp.einsum("htd,hte->hde", kh, vh, preferred_element_type=jnp.float32)
    zero_state = jnp.zeros_like(kv_local)
    kv_sum = entering(kv_local, "seq", add_states, zero_state, False)
    kv_before = kv_sum.astype(jnp.bfloat16)

    def forward_head(args):
        qpart, kpart, vpart, state = args
        scores = jnp.dot(qpart, kpart.T, preferred_element_type=jnp.float32)
        scores = jnp.where(mask, scores, 0.0).astype(jnp.bfloat16)
        inner = jnp.dot(scores, vpart, preferred_element_type=jnp.float32)
        return (inner + jnp.dot(qpart, state, preferred_element_type=jnp.float32), scores)

    attn_heads, saved_scores = lax.map(forward_head, (qh, kh, vh, kv_before))
    attn = join_heads(attn_heads)
    full = width * lax.axis_size("head")
    scaled = gain[None, :] * out_grad.astype(jnp.float32)
    square_sum, cross_sum = lax.psum(
        (jnp.sum(attn * attn, axis=1), jnp.sum(scaled * attn, axis=1)), "head"
    )
    inv = lax.rsqrt(square_sum / full + 1e-06)
    cross_mean = cross_sum / full
    attn_grad = (inv[:, None] * scaled - attn * (inv * inv * inv * cross_mean)[:, None]).astype(
        jnp.bfloat16
    )
    gh = split_heads(attn_grad, heads, depth)
    dkv_local = jnp.einsum("htd,hte->hde", qh, gh, preferred_element_type=jnp.float32)
    dkv_sum = entering(dkv_local, "seq", add_states, zero_state, True)
    dkv_after = dkv_sum.astype(jnp.bfloat16)

    def backward_head(args):
        qpart, kpart, vpart, gpart, scores, state, gstate = args
        gscores = jnp.dot(gpart, vpart.T, preferred_element_type=jnp.float32)
        gscores = jnp.where(mask, gscores, 0.0).astype(jnp.bfloat16)
        qgrad = jnp.dot(gscores, kpart, preferred_element_type=jnp.float32)
        qgrad = qgrad + jnp.dot(gpart, state.T, preferred_element_type=jnp.float32)
        kgrad = jnp.dot(gscores.T, qpart, preferred_element_type=jnp.float32)
        kgrad = kgrad + jnp.dot(vpart, gstate.T, preferred_element_type=jnp.float32)
        vgrad = jnp.dot(scores.T, gpart, preferred_element_type=jnp.float32)
        vgrad = vgrad + jnp.dot(kpart, gstate, preferred_element_type=jnp.float32)
        return (qgrad.astype(jnp.bfloat16), kgrad.astype(jnp.bfloat16), vgrad.astype(jnp.bfloat16))

    qgrad, kgrad, vgrad = lax.map(
        backward_head, (qh, kh, vh, gh, saved_scores, kv_before, dkv_after)
    )
    return (join_heads(qgrad), join_heads(kgrad), join_heads(vgrad))


def solution(mesh):
    return jax.shard_map(
        shards,
        mesh=mesh,
        in_specs=(
            P("seq", "head"),
            P("seq", "head"),
            P("seq", "head"),
            P("seq", "head"),
            P("head"),
        ),
        out_specs=(P("seq", "head"), P("seq", "head"), P("seq", "head")),
        check_vma=False,
    )
```

profile of v0, /device:TPU:0, one launch (start us, length us, event | category | flops | bytes accessed | tf_op | source)
XLA Modules:
  0.0 281.1 jit_solution(1717723435991660030)
XLA Ops:
  7.2 2.6 copy.33
  11.5 2.8 fusion.67
  14.4 2.6 copy.37
  21.9 2.6 copy.40
  24.5 29.4 %all-gather.5.cloned.1.call-done = f32[64,128,128]{2,1,0:T(8,128)} async-done(((f32[8,128,128]{2,1,0:T(8,128)}), f32[64,128,128]{2,1,0:T(8,128)}) %all-gather.5.cloned.1.call-update) | async-done | bytes 4194320 | tf_op jit(solution)/shard_map/all_gather | solution.py:11
  53.9 8.7 %while.58 = (s32[]{:T(128)}, f32[8,128,128]{2,1,0:T(8,128)S(1)}, s32[]{:T(128)}, f32[8,8,128,128]{3,2,1,0:T(8,128)}, s32[]{:T(128)}, /*index=5*/s32[]{:T(128)}) while((s32[]{:T(128)}, f32[8,128,128]{2,1,0:T(8,128)S(1)}, s32[]{:T(128)}, f32[8,8,128,128]{3,2,1,0:T(8,128)}, s32[]{:T(128)}, /*index=5*/s32[]{:T(128)}) %tuple.124), condition=%wide.region_1.2_spmd.clone, body=%wide.region_0.1_spmd.clone.sunk | while | flops 393220 | bytes 1572957 | solution.py:21
  62.7 48.2 %while.56 = (s32[]{:T(128)}, f32[8,768,128]{1,2,0:T(8,128)}, bf16[8,768,768]{2,1,0:T(8,128)(2,1)}, bf16[8,768,128]{2,1,0:T(8,128)(2,1)}, bf16[8,768,128]{2,1,0:T...) while((s32[]{:T(128)}, f32[8,768,128]{1,2,0:T(8,128)}, ...), condition=%wide.region_3.4_spmd.clone, body=%wide.region_2.3_spmd.clone.sunk | while | flops 329023488 | bytes 7114325 | solution.py:60
  62.7 2.5 bitcast_dynamic-update-slice_fusion.2
  68.7 2.5 bitcast_dynamic-update-slice_fusion.2
  74.6 2.5 bitcast_dynamic-update-slice_fusion.2
  80.7 2.5 bitcast_dynamic-update-slice_fusion.2
  86.7 2.6 bitcast_dynamic-update-slice_fusion.2
  92.7 2.5 bitcast_dynamic-update-slice_fusion.2
  98.7 2.5 bitcast_dynamic-update-slice_fusion.2
  104.8 2.6 bitcast_dynamic-update-slice_fusion.2
  110.9 2.3 fusion.65
  113.7 2.3 fusion.62
  116.0 11.9 %all-reduce = (f32[768]{0:T(1024)S(1)}, f32[768]{0:T(1024)S(1)}) all-reduce(f32[768]{0:T(1024)S(1)} %fusion.62, f32[768]{0:T(1024)S(1)} %fusion.65), channel_id=1, replica_groups=mesh['seq'=8,'head'=4] {'head'}, use_global_device_ids=true, to_apply=%region_7.8 | all-reduce | flops 1536 | bytes 12288 | tf_op jit(solution)/shard_map/psum | solution.py:64
  127.9 2.5 fusion.64
  133.2 34.1 %all-gather.7.cloned.1.call-done = f32[64,128,128]{2,1,0:T(8,128)} async-done(((f32[8,128,128]{2,1,0:T(8,128)}), f32[64,128,128]{2,1,0:T(8,128)}) %all-gather.7.cloned.1.call-update) | async-done | bytes 4194320 | tf_op jit(solution)/shard_map/all_gather | solution.py:11
  167.3 4.8 %rev.3 = f32[8,8,128,128]{3,2,1,0:T(8,128)} reverse(f32[8,8,128,128]{3,2,1,0:T(8,128)} %bitcast.189), dimensions={0} | reverse | bytes 8388608 | tf_op jit(solution)/shard_map/rev | solution.py:13
  172.0 8.7 %while.59 = (s32[]{:T(128)}, f32[8,128,128]{2,1,0:T(8,128)S(1)}, s32[]{:T(128)}, f32[8,8,128,128]{3,2,1,0:T(8,128)}, s32[]{:T(128)}, /*index=5*/s32[]{:T(128)}) while((s32[]{:T(128)}, f32[8,128,128]{2,1,0:T(8,128)S(1)}, s32[]{:T(128)}, f32[8,8,128,128]{3,2,1,0:T(8,128)}, s32[]{:T(128)}, /*index=5*/s32[]{:T(128)}) %tuple.110), condition=%wide.region_9.10_spmd.clone, body=%wide.region_8.9_spmd.clone.sunk | while | flops 393220 | bytes 1572957 | solution.py:21
  180.8 87.9 %while.57 = (s32[]{:T(128)}, bf16[8,768,128]{2,1,0:T(8,128)(2,1)S(1)}, bf16[8,768,128]{2,1,0:T(8,128)(2,1)}, bf16[8,768,128]{2,1,0:T(8,128)(2,1)}, bf16[8,768,12...) while((s32[]{:T(128)}, ...), condition=%wide.region_11.12_spmd.clone, body=%wide.region_10.11_spmd.clone.sunk | while | flops 681836544 | bytes 9346677 | solution.py:89
  270.7 3.5 %copy_bitcast_fusion = (bf16[768,1024]{1,0:T(8,128)(2,1)}, bf16[768,1024]{1,0:T(8,128)(2,1)}) fusion(bf16[8,768,128]{2,1,0:T(8,128)(2,1)S(1)} %copy-done.4, bf16[8,768,128]{2,1,0:T(8,128)(2,1)} %get-tuple-element.274), kind=kLoop, calls=%fused_computation.80 | loop fusion | bytes 6291456 | tf_op jit(solution)/shard_map/reshape | solution.py:29
  (135 shorter events, 144.6 us)
Async XLA Ops:
  7.2 46.7 %all-gather.5.cloned.1.call-start = ((), (), s32[]{:S(2)}) async-start(), calls=%async_computation | async-start | bytes 4718592 | tf_op jit(solution)/shard_map/all_gather | solution.py:11
  14.3 153.0 %all-gather.7.cloned.1.call-start = ((), (), s32[]{:S(2)}) async-start(), calls=%async_computation.1 | async-start | bytes 4718592 | tf_op jit(solution)/shard_map/all_gather | solution.py:11
  20.2 1.7 copy-start.2
  110.9 2.8 %copy-start = (f32[8,768,128]{1,2,0:T(8,128)S(1)}, f32[8,768,128]{1,2,0:T(8,128)}, u32[]{:S(2)}) copy-start(f32[8,768,128]{1,2,0:T(8,128)} %get-tuple-element.269) | copy-start | bytes 9437188
  110.9 2.8 %copy-start.5 = (f32[1024]{0:T(1024)S(1)}, f32[1024]{0:T(1024)}, u32[]{:S(2)}) copy-start(f32[1024]{0:T(1024)} %param.17) | copy-start | bytes 12292
  127.9 3.7 %copy-start.3 = (bf16[768,1024]{0,1:T(8,128)(2,1)S(1)}, bf16[768,1024]{0,1:T(8,128)(2,1)}, u32[]{:S(2)}) copy-start(bf16[768,1024]{0,1:T(8,128)(2,1)} %copy-done.2) | copy-start | bytes 4718596
  130.4 1.2 copy-start.1
  268.7 2.0 copy-start.4
Sparse Core Ops, SparseCore 0:
  14.4 39.4 all-gather.4
  133.3 33.9 all-gather.6
where the time goes:
time: 284 us; the launch traced here: 281 us
  matrix products  131 us (46%)
  waiting for transfers between devices  63.5 us (22%)
  local copies, waits for them, and re-layouts  34.9 us (12%)
  other arithmetic  24.4 us (9%)
  between operations  14.2 us (5%)
  blocking collectives  11.9 us (4%)
    all_gather x2, waiting for transfers between devices, entering(): pieces = lax.all_gather(value, axis)  63.4 us
    dot_general x8, matrix products, forward_head(): scores = jnp.dot(qpart, kpart.T, preferred_element_type=jnp.float32)  20.3 us
    select_n x14, other arithmetic, hop(): return jnp.where(position < mine, longer, total)  17.2 us
    unnamed x19, local copies, waits for them, and re-layouts  16.7 us
    dot_general x8, matrix products, backward_head(): kgrad = kgrad + jnp.dot(vpart, gstate.T, preferred_element_type=jnp.float32)  14.6 us
    dot_general x8, matrix products, backward_head(): vgrad = vgrad + jnp.dot(kpart, gstate, preferred_element_type=jnp.float32)  14.4 us
    dot_general x8, matrix products, backward_head(): vgrad = jnp.dot(scores.T, gpart, preferred_element_type=jnp.float32)  14.3 us
    dot_general x8, matrix products, backward_head(): gscores = jnp.dot(gpart, vpart.T, preferred_element_type=jnp.float32)  12.1 us
  transfers between devices with their start and end apart: 2, of which 2 were waited for; matrix products, arithmetic and copies ran while one was open for 4% of the time, Pallas kernels for 0%

commit v1 on v0

v1 whole, which is shorter than its diff:
```python
import functools

import jax
import jax.numpy as jnp
from jax import lax
from jax.experimental import pallas as pl
from jax.experimental.pallas import tpu as pltpu
from jax.sharding import PartitionSpec as P

HEAD_DIM = 128
CHUNK = 256
VMEM_BYTES = 12 * 2**20
F32 = jnp.float32
BF16 = jnp.bfloat16
VMEM = pl.BlockSpec(memory_space=pltpu.VMEM)
HBM = pl.BlockSpec(memory_space=pltpu.HBM)
ANYWHERE = pl.BlockSpec(memory_space=pl.ANY)


def dot(a, b, contract_a=1, contract_b=0):
    dims = (((contract_a,), (contract_b,)), ((), ()))
    return lax.dot_general(a, b, dims, preferred_element_type=F32)


def chunks_of(rows):
    size = CHUNK if rows % CHUNK == 0 else rows
    return [slice(i, i + size) for i in range(0, rows, size)]


def shape(dims, dtype):
    return jax.ShapeDtypeStruct(dims, dtype)


def lanes_of(j):
    return slice(j * HEAD_DIM, (j + 1) * HEAD_DIM)


def lower(size):
    row = lax.broadcasted_iota(jnp.int32, (size, size), 0)
    return row >= lax.broadcasted_iota(jnp.int32, (size, size), 1)


def upper(size):
    row = lax.broadcasted_iota(jnp.int32, (size, size), 0)
    return row <= lax.broadcasted_iota(jnp.int32, (size, size), 1)


def run(kernel, flops, in_specs, out_specs, out_shape, args, scratch=(), aliases=None):
    nbytes = sum(a.size * a.dtype.itemsize for a in args)
    return pl.pallas_call(
        kernel,
        in_specs=in_specs,
        out_specs=out_specs,
        out_shape=out_shape,
        scratch_shapes=list(scratch),
        input_output_aliases=aliases or {},
        cost_estimate=pl.CostEstimate(flops=flops, bytes_accessed=nbytes, transcendentals=0),
        compiler_params=pltpu.CompilerParams(vmem_limit_bytes=VMEM_BYTES),
    )(*args)


def columns(same, width):
    odd = lax.rem(lax.axis_index("seq"), 2)
    half = odd if same else 1 - odd
    return pl.ds(pl.multiple_of(half * width, width), width)


def fetches(sources, targets, sems, same):
    rows, width = targets[0].shape
    lanes = columns(same, width)
    copies = []
    for part in chunks_of(rows):
        for source, target in zip(sources, targets):
            sem = sems.at[len(copies)]
            copies.append(pltpu.make_async_copy(source.at[part, lanes], target.at[part], sem))
    return copies


def sum_states(k_ref, v_ref, sum_ref, pre_ref, copies=None):
    heads = sum_ref.shape[0]
    totals = [None] * heads
    for i, part in enumerate(chunks_of(k_ref.shape[0])):
        if copies:
            for copy in copies[2 * i:2 * i + 2]:
                copy.wait()
        for j in range(heads):
            term = dot(k_ref[part, lanes_of(j)], v_ref[part, lanes_of(j)], 0, 0)
            if i:
                pre_ref[i, j] = totals[j].astype(BF16)
            else:
                pre_ref[i, j] = jnp.zeros_like(pre_ref[i, j])
            totals[j] = totals[j] + term if i else term
    for j in range(heads):
        sum_ref[j] = totals[j]


def first_kernel(k_hbm, v_hbm, k1, v1, k2, v2, sum_ref, pre_ref, sems1, sems2):
    now = fetches((k_hbm, v_hbm), (k1, v1), sems1, False)
    later = fetches((k_hbm, v_hbm), (k2, v2), sems2, True)
    for copy in now + later:
        copy.start()
    sum_states(k1, v1, sum_ref, pre_ref, now)
    for copy in later:
        copy.wait()


def second_kernel(k2, v2, q_hbm, og_hbm, q1, og1, q2, og2, sum_ref, pre_ref, sems1, sems2):
    copies = fetches((q_hbm, og_hbm), (q2, og2), sems2, True)
    copies += fetches((q_hbm, og_hbm), (q1, og1), sems1, False)
    for copy in copies:
        copy.start()
    sum_states(k2, v2, sum_ref, pre_ref)
    for copy in copies:
        copy.wait()


def inner_kernel(same, q_ref, k_ref, v_ref, og_ref, gain_ref, pre_ref, after_ref, *outs):
    inner_ref, scaled_ref, qturned_ref, turned_ref = outs
    rows, width = q_ref.shape
    gain = gain_ref[:, columns(same, width)]
    for j in range(width // HEAD_DIM):
        lanes = lanes_of(j)
        for i, part in enumerate(chunks_of(rows)):
            q, k = q_ref[part, lanes], k_ref[part, lanes]
            size = q.shape[0]
            scores = jnp.where(lower(size), dot(q, k, 1, 1), 0.0).astype(BF16)
            turned_ref[j, part] = jnp.where(upper(size), dot(k, q, 1, 1), 0.0).astype(BF16)
            inner = dot(scores, v_ref[part, lanes])
            inner_ref[part, lanes] = inner + dot(q, pre_ref[i, j]) if i else inner
            scaled_ref[part, lanes] = gain[:, lanes] * og_ref[part, lanes].astype(F32)
            qturned_ref[lanes, part] = q.T


def attn_kernel(last, q_ref, inner_ref, scaled_ref, state_ref, *refs):
    attn_ref = refs[-3] if not last else refs[-2]
    rows, width = q_ref.shape
    states = [state_ref[j].astype(BF16) for j in range(width // HEAD_DIM)]
    for part in chunks_of(rows):
        square, cross = (refs[0][part], refs[1][part]) if last else (None, None)
        for j, state in enumerate(states):
            lanes = lanes_of(j)
            attn = inner_ref[part, lanes] + dot(q_ref[part, lanes], state)
            attn_ref[part, lanes] = attn
            more, crossed = attn * attn, scaled_ref[part, lanes] * attn
            square = more if square is None else square + more
            cross = crossed if cross is None else cross + crossed
        if last:
            square = jnp.sum(square.T, axis=0, keepdims=True)
            cross = jnp.sum(cross.T, axis=0, keepdims=True)
            row = lax.broadcasted_iota(jnp.int32, (8, square.shape[1]), 0)
            refs[-1][:, part] = jnp.where(row == 0, square, jnp.where(row == 1, cross, 0.0))
        else:
            refs[-2][part] = square
            refs[-1][part] = cross


def factors_kernel(full, parts, refs):
    total = refs[0][...]
    for ref in refs[1:parts]:
        total = total + ref[...]
    inv = lax.rsqrt(total[0:1] / full + 1e-6)
    slope = inv * inv * inv * (total[1:2] / full)
    row = lax.broadcasted_iota(jnp.int32, total.shape, 0)
    both = jnp.where(row == 0, inv, slope).T
    wide = (both.shape[0], HEAD_DIM)
    return jnp.broadcast_to(both[:, 0:1], wide), jnp.broadcast_to(both[:, 1:2], wide)


def grad_kernel(full, parts, *refs):
    if parts:
        inv, slope = factors_kernel(full, parts, refs)
        refs[-2][...] = inv
        refs[-1][...] = slope
        inv_ref, slope_ref = refs[-2:]
        attn_ref, scaled_ref, qturned_ref, g_ref, sum_ref, post_ref = refs[parts:-2]
    else:
        inv_ref, slope_ref, attn_ref, scaled_ref, qturned_ref, g_ref, sum_ref, post_ref = refs
    heads = sum_ref.shape[0]
    totals = [None] * heads
    for i, part in reversed(list(enumerate(chunks_of(g_ref.shape[0])))):
        for j in range(heads):
            lanes = lanes_of(j)
            grad = inv_ref[part] * scaled_ref[part, lanes] - attn_ref[part, lanes] * slope_ref[part]
            grad = grad.astype(BF16)
            g_ref[part, lanes] = grad
            term = dot(qturned_ref[lanes, part], grad)
            if totals[j] is None:
                post_ref[i, j] = jnp.zeros_like(post_ref[i, j])
                totals[j] = term
            else:
                post_ref[i, j] = totals[j].astype(BF16)
                totals[j] = totals[j] + term
    for j in range(heads):
        sum_ref[j] = totals[j]


def local_kernel(same, q_ref, k_ref, v_ref, g_ref, turned_ref, state_ref, pre_ref, post_ref, *refs):
    qgrad_hbm, kpart_ref, vpart_ref, qgrad_ref, sems = refs[-5:]
    rows, width = q_ref.shape
    target = columns(same, width)
    parts = chunks_of(rows)
    copies = []
    for i, part in enumerate(parts):
        for j in range(width // HEAD_DIM):
            lanes = lanes_of(j)
            q, k, v, g = (ref[part, lanes] for ref in (q_ref, k_ref, v_ref, g_ref))
            size = q.shape[0]
            gscores = jnp.where(lower(size), dot(g, v, 1, 1), 0.0).astype(BF16)
            gturned = jnp.where(upper(size), dot(v, g, 1, 1), 0.0).astype(BF16)
            qgrad = dot(gscores, k) + dot(g, state_ref[j].astype(BF16), 1, 1)
            kgrad = dot(gturned, q)
            vgrad = dot(turned_ref[j, part], g)
            if i:
                qgrad = qgrad + dot(g, pre_ref[i, j], 1, 1)
            if i < len(parts) - 1:
                kgrad = kgrad + dot(v, post_ref[i, j], 1, 1)
                vgrad = vgrad + dot(k, post_ref[i, j])
            qgrad_ref[part, lanes] = qgrad.astype(BF16)
            kpart_ref[part, lanes] = kgrad
            vpart_ref[part, lanes] = vgrad
        copy = pltpu.make_async_copy(qgrad_ref.at[part], qgrad_hbm.at[part, target], sems.at[i])
        copy.start()
        copies.append(copy)
    for copy in copies:
        copy.wait()


def final_kernel(same, k_ref, v_ref, kpart_ref, vpart_ref, state_ref, *refs):
    kgrad_hbm, vgrad_hbm, kgrad_ref, vgrad_ref, sems = refs[-5:]
    rows, width = k_ref.shape
    target = columns(same, width)
    states = [state_ref[j].astype(BF16) for j in range(width // HEAD_DIM)]
    copies = []
    for part in chunks_of(rows):
        for j, state in enumerate(states):
            lanes = lanes_of(j)
            kgrad = kpart_ref[part, lanes] + dot(v_ref[part, lanes], state, 1, 1)
            vgrad = vpart_ref[part, lanes] + dot(k_ref[part, lanes], state)
            kgrad_ref[part, lanes] = kgrad.astype(BF16)
            vgrad_ref[part, lanes] = vgrad.astype(BF16)
        for source, out in ((kgrad_ref, kgrad_hbm), (vgrad_ref, vgrad_hbm)):
            sem = sems.at[len(copies)]
            copy = pltpu.make_async_copy(source.at[part], out.at[part, target], sem)
            copy.start()
            copies.append(copy)
    for copy in copies:
        copy.wait()


def scan_plan(count):
    bits = count.bit_length() - 1
    stages = []
    for stage in range(bits - 1):
        rising, falling = 1 + stage, bits - 1 - stage
        pairs = []
        for r in range(count):
            bit = falling if r & 1 else rising
            useless = stage == 0 if r & 1 else stage == bits - 2
            if not ((r >> bit) & 1 and useless):
                pairs.append((r, r ^ (1 << bit)))
        stages.append((rising, falling, pairs))
    return stages


def join_kernel(backward, done, final, *refs):
    count = lax.axis_size("seq")
    rank = lax.axis_index("seq")
    if backward:
        rank = count - 1 - rank
    odd = (rank & 1) == 1
    plan = scan_plan(count)
    keep_ref, extra_ref = refs[:2]
    came = refs[2:2 + done]
    total = keep_ref[...] + extra_ref[...]
    before = jnp.zeros_like(total)
    for (rising, falling, _), ref in zip(plan, came):
        high = (jnp.where(odd, rank >> falling, rank >> rising) & 1) == 1
        value = ref[...]
        before = before + jnp.where(odd | high, value, 0.0)
        total = total + jnp.where(odd, 0.0, value)
    if final:
        message_ref, state_ref = refs[-2:]
        message_ref[...] = before + jnp.where(odd, 0.0, keep_ref[...])
        state_ref[...] = before + jnp.where(odd, extra_ref[...], 0.0)
    else:
        rising, falling, _ = plan[done]
        high = (jnp.where(odd, rank >> falling, rank >> rising) & 1) == 1
        refs[-1][...] = jnp.where(odd, before + jnp.where(high, 0.0, total), total)


def join(backward, keep, extra, came, final, after=()):
    like = shape(keep.shape, F32)
    return run(
        functools.partial(join_kernel, backward, len(came), final), 4 * keep.size,
        [VMEM] * (2 + len(came)) + [ANYWHERE] * len(after),
        [VMEM, VMEM] if final else VMEM,
        [like, like] if final else like,
        (keep, extra, *came, *after),
    )


def scan_states(keep, extra, backward, beside):
    count = lax.axis_size("seq")
    plan = scan_plan(count)
    came, results = [], []
    message = join(backward, keep, extra, came, not plan)
    for stage, (_, _, pairs) in enumerate(plan):
        arrived = move(message, pairs, backward)
        mine = beside[stage::len(plan)] if stage < len(beside) else []
        made = [work(message) for work in mine]
        results += made
        came = came + [arrived]
        after = [leaf for item in made for leaf in item[-1:]]
        message = join(backward, keep, extra, came, stage == len(plan) - 1, after)
    message, state = message
    return state, nearby(message, backward), results


def move(value, pairs, backward):
    count = lax.axis_size("seq")
    if backward:
        pairs = [(count - 1 - a, count - 1 - b) for a, b in pairs]
    return lax.ppermute(value, "seq", pairs)


def nearby(value, backward):
    return move(value, [(r, r ^ 1) for r in range(lax.axis_size("seq"))], backward)


def add_kernel(left_ref, right_ref, out_ref):
    out_ref[...] = left_ref[...] + right_ref[...]


def head_sums(sums):
    peers = lax.axis_size("head")
    distance, parts = 1, [sums]
    while distance < peers:
        if len(parts) == 2:
            sums = run(add_kernel, sums.size, [VMEM, VMEM], VMEM, shape(sums.shape, F32), parts)
        pairs = [(r, (r + distance) % peers) for r in range(peers)]
        parts = [sums, lax.ppermute(sums, "head", pairs)]
        distance *= 2
    return parts


def shards(query, key_in, value, out_grad, gain):
    rows, width = query.shape
    half = width // 2
    heads = half // HEAD_DIM
    chunks = len(chunks_of(rows))
    full = width * lax.axis_size("head")
    gain = gain.reshape(1, width)
    pin = lambda x: pltpu.with_memory_space_constraint(x, pltpu.HBM)
    query, key_in, value, out_grad = (pin(x) for x in (query, key_in, value, out_grad))
    unit = 2 * rows * half * HEAD_DIM
    partial = functools.partial

    states = shape((heads, HEAD_DIM, HEAD_DIM), F32)
    inside = shape((chunks, heads, HEAD_DIM, HEAD_DIM), BF16)
    wide = shape((rows, half), F32)
    thin = shape((rows, half), BF16)
    lane_sums = shape((rows, HEAD_DIM), F32)
    whole = shape((rows, width), BF16)
    sems = pltpu.SemaphoreType.DMA((2 * chunks,))

    k1, v1, k2, v2, send, pre1 = run(
        first_kernel, unit, [HBM, HBM], [VMEM] * 6, [thin] * 4 + [states, inside],
        (key_in, value), [sems, sems],
    )
    extra = nearby(send, False)
    q1, og1, q2, og2, keep, pre2 = run(
        second_kernel, unit, [VMEM, VMEM, HBM, HBM], [VMEM] * 6, [thin] * 4 + [states, inside],
        (k2, v2, query, out_grad), [sems, sems],
    )

    def inner_of(same, q, k, v, og, pre):
        return lambda message: run(
            partial(inner_kernel, same), 6 * unit,
            [VMEM] * 6 + [ANYWHERE], [VMEM] * 4,
            [wide, wide, shape((half, rows), BF16), shape((heads, rows, rows // chunks), BF16)],
            (q, k, v, og, gain, pre, message),
        )

    state2, state1, made = scan_states(
        keep, extra, False,
        [inner_of(True, q2, k2, v2, og2, pre2), inner_of(False, q1, k1, v1, og1, pre1)],
    )
    (inner2, scaled2, qturned2, turned2), (inner1, scaled1, qturned1, turned1) = made

    attn2, square, cross = run(
        partial(attn_kernel, False), unit, [VMEM] * 4, [VMEM] * 3, [wide, lane_sums, lane_sums],
        (q2, inner2, scaled2, state2),
    )
    attn1, sums = run(
        partial(attn_kernel, True), unit, [VMEM] * 6, [VMEM] * 2, [wide, shape((8, rows), F32)],
        (q1, inner1, scaled1, state1, square, cross),
    )
    parts = head_sums(sums)

    g2, gsend, post2, inv, slope = run(
        partial(grad_kernel, full, len(parts)), unit,
        [VMEM] * (len(parts) + 3), [VMEM] * 5, [thin, states, inside, lane_sums, lane_sums],
        (*parts, attn2, scaled2, qturned2),
    )
    gextra = nearby(gsend, True)
    g1, gkeep, post1 = run(
        partial(grad_kernel, full, 0), unit, [VMEM] * 5, [VMEM] * 3, [thin, states, inside],
        (inv, slope, attn1, scaled1, qturned1),
    )

    qgrads = []

    def local_of(same, *args):
        def work(message):
            more = [message] + qgrads
            qgrad, kpart, vpart = run(
                partial(local_kernel, same), 9 * unit,
                [VMEM] * len(args) + [ANYWHERE] + [HBM] * len(qgrads), [HBM, VMEM, VMEM],
                [whole, wide, wide], (*args, *more),
                [pltpu.VMEM((rows, half), BF16), sems],
                {len(args) + 1: 0} if qgrads else None,
            )
            qgrads[:] = [qgrad]
            return kpart, vpart

        return work

    gstate1, gstate2, made = scan_states(
        gkeep, gextra, True,
        [
            local_of(False, q1, k1, v1, g1, turned1, state1, pre1, post1),
            local_of(True, q2, k2, v2, g2, turned2, state2, pre2, post2),
        ],
    )
    (kpart1, vpart1), (kpart2, vpart2) = made

    def final_of(same, *args, outs=()):
        scratch = [pltpu.VMEM((rows, half), BF16)] * 2 + [sems]
        aliases = {len(args) + i: i for i in range(len(outs))}
        return run(
            partial(final_kernel, same), 2 * unit, [VMEM] * len(args) + [HBM] * len(outs),
            [HBM, HBM], [whole, whole], (*args, *outs), scratch, aliases,
        )

    outs = final_of(False, k1, v1, kpart1, vpart1, gstate1)
    kgrad, vgrad = final_of(True, k2, v2, kpart2, vpart2, gstate2, outs=outs)
    return qgrads[0], kgrad, vgrad


def solution(mesh):
    spec = P("seq", "head")
    return jax.shard_map(
        shards,
        mesh=mesh,
        in_specs=(spec, spec, spec, spec, P("head")),
        out_specs=(spec, spec, spec),
        check_vma=False,
    )
```

time: 284 us -> 57.9 us (0.20)
  matrix products: 131 us -> 0 us
  waiting for transfers between devices: 63.5 us -> 18 us
  local copies, waits for them, and re-layouts: 34.9 us -> 0.01 us
  other arithmetic: 24.4 us -> 0 us
  Pallas kernels: 0 us -> 22.2 us
  starting transfers between devices: 0.08 us -> 16.4 us
  between operations: 14.2 us -> 0.97 us
  blocking collectives: 11.9 us -> 0 us
    dot_general x82 -> x0, matrix products: 131 us -> none  [the longest x8 20.3 us: forward_head(): scores = jnp.dot(qpart, kpart.T, preferred_element_type=jnp.float32)]
    all_gather x2 -> x0, waiting for transfers between devices: 63.4 us -> none  [entering(): pieces = lax.all_gather(value, axis)]
    pallas_call x0 -> x19, Pallas kernels: none -> 22.2 us  [run(): pl.pallas_call(kernel, in_specs=in_specs, out_specs=out_specs, out_shape=...]
    ppermute x0 -> x10, waiting for transfers between devices: none -> 18 us  [the longest x8 10 us: move(): return lax.ppermute(value, 'seq', pairs)]
    select_n x14 -> x0, other arithmetic: 17.2 us -> none  [hop(): return jnp.where(position < mine, longer, total)]
    unnamed x19 -> x2, local copies, waits for them, and re-layouts: 16.7 us -> 0.01 us
    ppermute x0 -> x10, starting transfers between devices: none -> 16.4 us  [the longest x8 14 us: move(): return lax.ppermute(value, 'seq', pairs)]
    psum x1 -> x0, blocking collectives: 11.9 us -> none  [shards(): lax.psum((jnp.sum(attn * attn, axis=1), jnp.sum(scaled * attn, axis=1)),...]
  transfers between devices with their start and end apart: 2 -> 10, of which waited for: 2 -> 8; matrix products, arithmetic and copies ran while one was open for 4% -> 0% of each run, Pallas kernels for 0% -> 29%
where the time goes in v1:
time: 57.9 us; the launch traced here: 57.6 us
  Pallas kernels  22.2 us (38%)
  waiting for transfers between devices  18 us (31%)
  starting transfers between devices  16.4 us (28%)
  between operations  0.97 us (2%)
    pallas_call x19, Pallas kernels, run(): pl.pallas_call(kernel, in_specs=in_specs, out_specs=out_specs, out_shape=...  22.2 us
    ppermute x8, starting transfers between devices, move(): return lax.ppermute(value, 'seq', pairs)  14 us
    ppermute x8, waiting for transfers between devices, move(): return lax.ppermute(value, 'seq', pairs)  10 us
    ppermute x2, waiting for transfers between devices, head_sums(): parts = [sums, lax.ppermute(sums, 'head', pairs)]  7.98 us
    ppermute x2, starting transfers between devices, head_sums(): parts = [sums, lax.ppermute(sums, 'head', pairs)]  2.42 us
  transfers between devices with their start and end apart: 10, of which 8 were waited for; matrix products, arithmetic and copies ran while one was open for 0% of the time, Pallas kernels for 29%

profile of v1, /device:TPU:0, one launch (start us, length us, event | category | flops | bytes accessed | tf_op | source)
XLA Modules:
  0.0 57.6 jit_solution(6471429359753141620)
XLA Ops:
  0.6 2.1 %shard_map.76 = (bf16[768,512]{1,0:T(8,128)(2,1)S(1)}, bf16[768,512]{1,0:T(8,128)(2,1)S(1)}, bf16[768,512]{1,0:T(8,128)(2,1)S(1)}, bf16[768,512]{1,0:T(8,128)(2,...) custom-call(bf16[768,1024]{1,0:T(8,128)(2,1)} %k_hbm.1, bf16[768,1024]{1,0:T(8,128)(2,1)} %v_hbm.1), custom_call_target="tpu_custom_call" | custom-call | flops 100663296 | bytes 3145728 | tf_op jit(solution)/shard_map/pallas_call | solution.py:50
  3.3 2.2 %shard_map.77 = (bf16[768,512]{1,0:T(8,128)(2,1)S(1)}, bf16[768,512]{1,0:T(8,128)(2,1)S(1)}, bf16[768,512]{1,0:T(8,128)(2,1)S(1)}, bf16[768,512]{1,0:T(8,128)(2,...) custom-call(bf16[768,512]{1,0:T(8,128)(2,1)S(1)} %get-tuple-element.50.k2.k_ref, ...), custom_call_target="tpu_custom_call" | custom-call | flops 100663296 | bytes 4718592 | tf_op jit(solution)/shard_map/pallas_call | solution.py:50
  5.6 4.4 %collective-permute-start.1 = (f32[4,128,128]{2,1,0:T(8,128)S(1)}, f32[4,128,128]{2,1,0:T(8,128)S(1)}, u32[]{:S(2)}, u32[]{:S(2)}) collective-permute-start(f32[4,128,128]{2,1,0:T(8,128)S(1)} %shard_map.78.after_ref), channel_id=1, source_target_pairs={{0,8},{4,20},{8,0},{12,28},{16,24},{24,16},{1,9},{5,21},{9,1},{13,... | collective-permute-start | bytes 786440 | tf_op jit(solution)/shard_map/ppermute | solution.py:323
  10.0 1.9 %shard_map.79 = (f32[768,512]{1,0:T(8,128)S(1)}, f32[768,512]{1,0:T(8,128)S(1)}, bf16[512,768]{1,0:T(8,128)(2,1)S(1)}, bf16[4,768,256]{2,1,0:T(8,128)(2,1)S(1)}) custom-call(bf16[768,512]{1,0:T(8,128)(2,1)S(1)} %get-tuple-element.52.q_ref, bf16[768,512]{1,0:T(8,128)(2,1)S(1)} %get-tuple-element.50.k2.k_ref, bf16[768,512]{1,0:T(8,128)(2,1)S(1)} %get-tuple-element.51.v2.v_ref, ...), custom_call_target="tpu_custom_call" | custom-call | flops 603979776 | bytes 3805184 | tf_op jit(solution)/shard_map/pallas_call | solution.py:50
  11.9 2.4 %collective-permute-done.1.refs_2_ = f32[4,128,128]{2,1,0:T(8,128)S(1)} collective-permute-done((f32[4,128,128]{2,1,0:T(8,128)S(1)}, f32[4,128,128]{2,1,0:T(8,128)S(1)}, u32[]{:S(2)}, u32[]{:S(2)}) %collective-permute-start.1) | collective-permute-done | bytes 262176 | tf_op jit(solution)/shard_map/ppermute | solution.py:323
  14.4 4.0 %collective-permute-start.2 = (f32[4,128,128]{2,1,0:T(8,128)S(1)}, f32[4,128,128]{2,1,0:T(8,128)S(1)}, u32[]{:S(2)}, u32[]{:S(2)}) collective-permute-start(f32[4,128,128]{2,1,0:T(8,128)S(1)} %shard_map.80.after_ref), channel_id=1, source_target_pairs={{0,16},{4,12},{8,24},{12,4},{20,28},{28,20},{1,17},{5,13},{9,25},{... | collective-permute-start | bytes 786440 | tf_op jit(solution)/shard_map/ppermute | solution.py:323
  18.4 1.9 %shard_map.81 = (f32[768,512]{1,0:T(8,128)S(1)}, f32[768,512]{1,0:T(8,128)S(1)}, bf16[512,768]{1,0:T(8,128)(2,1)S(1)}, bf16[4,768,256]{2,1,0:T(8,128)(2,1)S(1)}) custom-call(bf16[768,512]{1,0:T(8,128)(2,1)S(1)} %get-tuple-element.53.q_ref, bf16[768,512]{1,0:T(8,128)(2,1)S(1)} %get-tuple-element.54.k_ref, bf16[768,512]{1,0:T(8,128)(2,1)S(1)} %get-tuple-element.55.v_ref, ...), custom_call_target="tpu_custom_call" | custom-call | flops 603979776 | bytes 3805184 | tf_op jit(solution)/shard_map/pallas_call | solution.py:50
  20.3 2.0 %collective-permute-done.2.refs_3_ = f32[4,128,128]{2,1,0:T(8,128)S(1)} collective-permute-done((f32[4,128,128]{2,1,0:T(8,128)S(1)}, f32[4,128,128]{2,1,0:T(8,128)S(1)}, u32[]{:S(2)}, u32[]{:S(2)}) %collective-permute-start.2) | collective-permute-done | bytes 262176 | tf_op jit(solution)/shard_map/ppermute | solution.py:323
  22.9 1.1 %collective-permute-done.3.state_ref = f32[4,128,128]{2,1,0:T(8,128)S(1)} collective-permute-done((f32[4,128,128]{2,1,0:T(8,128)S(1)}, f32[4,128,128]{2,1,0:T(8,128)S(1)}, u32[]{:S(2)}, u32[]{:S(2)}) %collective-permute-start.3) | collective-permute-done | bytes 262176 | tf_op jit(solution)/shard_map/ppermute | solution.py:323
  23.9 0.7 %shard_map.84 = (f32[768,512]{1,0:T(8,128)S(1)}, f32[8,768]{1,0:T(8,128)S(1)}) custom-call(bf16[768,512]{1,0:T(8,128)(2,1)S(1)} %get-tuple-element.53.q_ref, f32[768,512]{1,0:T(8,128)S(1)} %get-tuple-element.63.inner_ref, f32[768,512]{1,0:T(8,128)S(1)} %get-tuple-element.64.scaled_ref.refs_3_, f32[4,128,128]{2,1,0:T(8,128)S(1)} %collective-permute-done.3.state_ref, ...), custom_call_target="tpu_custom_call" | custom-call | flops 100663296 | bytes 4980736 | tf_op jit(solution)/shard_map/pallas_call | solution.py:50
  24.7 1.6 %collective-permute-start.4 = (f32[8,768]{1,0:T(8,128)S(1)}, f32[8,768]{1,0:T(8,128)S(1)}, u32[]{:S(2)}, u32[]{:S(2)}) collective-permute-start(f32[8,768]{1,0:T(8,128)S(1)} %get-tuple-element.72.left_ref), channel_id=1, source_target_pairs={{0,1},{1,2},{2,3},{3,0},{4,5},{5,6},{6,7},{7,4},{8,9},{9,10},{10,1... | collective-permute-start | bytes 73736 | tf_op jit(solution)/shard_map/ppermute | solution.py:341
  26.3 4.0 %collective-permute-done.4.right_ref = f32[8,768]{1,0:T(8,128)S(1)} collective-permute-done((f32[8,768]{1,0:T(8,128)S(1)}, f32[8,768]{1,0:T(8,128)S(1)}, u32[]{:S(2)}, u32[]{:S(2)}) %collective-permute-start.4) | collective-permute-done | bytes 24608 | tf_op jit(solution)/shard_map/ppermute | solution.py:341
  30.3 0.8 %collective-permute-start.5 = (f32[8,768]{1,0:T(8,128)S(1)}, f32[8,768]{1,0:T(8,128)S(1)}, u32[]{:S(2)}, u32[]{:S(2)}) collective-permute-start(f32[8,768]{1,0:T(8,128)S(1)} %shard_map.85.refs_0_), channel_id=1, source_target_pairs={{0,2},{1,3},{2,0},{3,1},{4,6},{5,7},{6,4},{7,5},{8,10},{9,11},{10,... | collective-permute-start | bytes 73736 | tf_op jit(solution)/shard_map/ppermute | solution.py:341
  31.1 3.9 %collective-permute-done.5.refs_1_ = f32[8,768]{1,0:T(8,128)S(1)} collective-permute-done((f32[8,768]{1,0:T(8,128)S(1)}, f32[8,768]{1,0:T(8,128)S(1)}, u32[]{:S(2)}, u32[]{:S(2)}) %collective-permute-start.5) | collective-permute-done | bytes 24608 | tf_op jit(solution)/shard_map/ppermute | solution.py:341
  35.1 0.9 %shard_map.86 = (bf16[768,512]{1,0:T(8,128)(2,1)S(1)}, f32[4,128,128]{2,1,0:T(8,128)S(1)}, bf16[3,4,128,128]{3,2,1,0:T(8,128)(2,1)S(1)}, f32[768,128]{1,0:T(8,128)S(1)}, f32[768,128]{1,0:T(8,128)S(1)}) custom-call(f32[8,768]{1,0:T(8,128)S(1)} %shard_map.85.refs_0_, f32[8,768]{1,0:T(8,128)S(1)} %collective-permute-done.5.refs_1_, ...), custom_call_target="tpu_custom_call" | custom-call | flops 100663296 | bytes 3981312 | tf_op jit(solution)/shard_map/pallas_call | solution.py:50
  36.7 0.9 %collective-permute-done.6.refs_1_ = f32[4,128,128]{2,1,0:T(8,128)S(1)} collective-permute-done((f32[4,128,128]{2,1,0:T(8,128)S(1)}, f32[4,128,128]{2,1,0:T(8,128)S(1)}, u32[]{:S(2)}, u32[]{:S(2)}) %collective-permute-start.6) | collective-permute-done | bytes 262176 | tf_op jit(solution)/shard_map/ppermute | solution.py:323
  37.6 1.3 %collective-permute-start.7 = (f32[4,128,128]{2,1,0:T(8,128)S(1)}, f32[4,128,128]{2,1,0:T(8,128)S(1)}, u32[]{:S(2)}, u32[]{:S(2)}) collective-permute-start(f32[4,128,128]{2,1,0:T(8,128)S(1)} %shard_map.88.refs_0_), channel_id=1, source_target_pairs={{28,20},{24,8},{20,28},{16,0},{12,4},{4,12},{29,21},{25,9},{21,29}... | collective-permute-start | bytes 786440 | tf_op jit(solution)/shard_map/ppermute | solution.py:323
  38.9 4.0 %shard_map.89 = (bf16[768,1024]{1,0:T(8,128)(2,1)}, f32[768,512]{1,0:T(8,128)S(1)}, f32[768,512]{1,0:T(8,128)S(1)}) custom-call(bf16[768,512]{1,0:T(8,128)(2,1)S(1)} %get-tuple-element.53.q_ref, bf16[768,512]{1,0:T(8,128)(2,1)S(1)} %get-tuple-element.54.k_ref, bf16[768,512]{1,0:T(8,128)(2,1)S(1)} %get-tuple-element.55.v_ref, ...), custom_call_target="tpu_custom_call" | custom-call | flops 905969664 | bytes 6029312 | tf_op jit(solution)/shard_map/pallas_call | solution.py:50
  42.9 2.9 %collective-permute-done.7.refs_2_ = f32[4,128,128]{2,1,0:T(8,128)S(1)} collective-permute-done((f32[4,128,128]{2,1,0:T(8,128)S(1)}, f32[4,128,128]{2,1,0:T(8,128)S(1)}, u32[]{:S(2)}, u32[]{:S(2)}) %collective-permute-start.7) | collective-permute-done | bytes 262176 | tf_op jit(solution)/shard_map/ppermute | solution.py:323
  46.0 3.6 %collective-permute-start.8 = (f32[4,128,128]{2,1,0:T(8,128)S(1)}, f32[4,128,128]{2,1,0:T(8,128)S(1)}, u32[]{:S(2)}, u32[]{:S(2)}) collective-permute-start(f32[4,128,128]{2,1,0:T(8,128)S(1)} %shard_map.90.refs_0_), channel_id=1, source_target_pairs={{28,12},{24,16},{20,4},{16,24},{8,0},{0,8},{29,13},{25,17},{21,5},... | collective-permute-start | bytes 786440 | tf_op jit(solution)/shard_map/ppermute | solution.py:323
  49.6 4.0 %shard_map.91 = (bf16[768,1024]{1,0:T(8,128)(2,1)}, f32[768,512]{1,0:T(8,128)S(1)}, f32[768,512]{1,0:T(8,128)S(1)}) custom-call(bf16[768,512]{1,0:T(8,128)(2,1)S(1)} %get-tuple-element.52.q_ref, bf16[768,512]{1,0:T(8,128)(2,1)S(1)} %get-tuple-element.50.k2.k_ref, bf16[768,512]{1,0:T(8,128)(2,1)S(1)} %get-tuple-element.51.v2.v_ref, ...), custom_call_target="tpu_custom_call", output_to_operand_aliasing={{0}: (9, {})} | custom-call | flops 905969664 | bytes 7602176 | tf_op jit(solution)/shard_map/pallas_call | solution.py:50
  53.6 0.6 %collective-permute-done.8.refs_3_ = f32[4,128,128]{2,1,0:T(8,128)S(1)} collective-permute-done((f32[4,128,128]{2,1,0:T(8,128)S(1)}, f32[4,128,128]{2,1,0:T(8,128)S(1)}, u32[]{:S(2)}, u32[]{:S(2)}) %collective-permute-start.8) | collective-permute-done | bytes 262176 | tf_op jit(solution)/shard_map/ppermute | solution.py:323
  54.4 1.5 %shard_map.93 = (bf16[768,1024]{1,0:T(8,128)(2,1)}, bf16[768,1024]{1,0:T(8,128)(2,1)}) custom-call(bf16[768,512]{1,0:T(8,128)(2,1)S(1)} %get-tuple-element.54.k_ref, bf16[768,512]{1,0:T(8,128)(2,1)S(1)} %get-tuple-element.55.v_ref, f32[768,512]{1,0:T(8,128)S(1)} %get-tuple-element.91.kpart_ref, f32[768,512]{1,0:T(8,128)S(1)} %get-tuple-element.85.refs_3_.vpart_ref, ...), custom_call_target="tpu_custom_call" | custom-call | flops 201326592 | bytes 4980736 | tf_op jit(solution)/shard_map/pallas_call | solution.py:50
  55.9 1.5 %shard_map.94 = (bf16[768,1024]{1,0:T(8,128)(2,1)}, bf16[768,1024]{1,0:T(8,128)(2,1)}) custom-call(bf16[768,512]{1,0:T(8,128)(2,1)S(1)} %get-tuple-element.50.k2.k_ref, bf16[768,512]{1,0:T(8,128)(2,1)S(1)} %get-tuple-element.51.v2.v_ref, f32[768,512]{1,0:T(8,128)S(1)} %get-tuple-element.88.kpart_ref, ...), custom_call_target="tpu_custom_call", output_to_operand_aliasing={{0}: (5, {}), {1}: (6, {})} | custom-call | flops 201326592 | bytes 8126464 | tf_op jit(solution)/shard_map/pallas_call | solution.py:50
  (17 shorter events, 2.2 us)
Async XLA Ops:
  2.8 2.7 %collective-permute-start = (f32[4,128,128]{2,1,0:T(8,128)S(1)}, f32[4,128,128]{2,1,0:T(8,128)S(1)}, u32[]{:S(2)}, u32[]{:S(2)}) collective-permute-start(f32[4,128,128]{2,1,0:T(8,128)S(1)} %get-tuple-element.59), channel_id=1, source_target_pairs={{0,4},{4,0},{8,12},{12,8},{16,20},{20,16},{24,28},{28,24},{1,5},{5... | collective-permute-start | bytes 786440 | tf_op jit(solution)/shard_map/ppermute | solution.py:323
  3.3 6.7 %copy-start = (f32[1024]{0:T(1024)S(1)}, f32[1024]{0:T(1024)}, u32[]{:S(2)}) copy-start(f32[1024]{0:T(1024)} %param.9) | copy-start | bytes 12292
  5.6 8.8 %collective-permute-start.1 = (f32[4,128,128]{2,1,0:T(8,128)S(1)}, f32[4,128,128]{2,1,0:T(8,128)S(1)}, u32[]{:S(2)}, u32[]{:S(2)}) collective-permute-start(f32[4,128,128]{2,1,0:T(8,128)S(1)} %shard_map.78.after_ref), channel_id=1, source_target_pairs={{0,8},{4,20},{8,0},{12,28},{16,24},{24,16},{1,9},{5,21},{9,1},{13,... | collective-permute-start | bytes 786440 | tf_op jit(solution)/shard_map/ppermute | solution.py:323
  14.4 7.8 %collective-permute-start.2 = (f32[4,128,128]{2,1,0:T(8,128)S(1)}, f32[4,128,128]{2,1,0:T(8,128)S(1)}, u32[]{:S(2)}, u32[]{:S(2)}) collective-permute-start(f32[4,128,128]{2,1,0:T(8,128)S(1)} %shard_map.80.after_ref), channel_id=1, source_target_pairs={{0,16},{4,12},{8,24},{12,4},{20,28},{28,20},{1,17},{5,13},{9,25},{... | collective-permute-start | bytes 786440 | tf_op jit(solution)/shard_map/ppermute | solution.py:323
  22.3 1.6 %collective-permute-start.3 = (f32[4,128,128]{2,1,0:T(8,128)S(1)}, f32[4,128,128]{2,1,0:T(8,128)S(1)}, u32[]{:S(2)}, u32[]{:S(2)}) collective-permute-start(f32[4,128,128]{2,1,0:T(8,128)S(1)} %get-tuple-element.66), channel_id=1, source_target_pairs={{0,4},{4,0},{8,12},{12,8},{16,20},{20,16},{24,28},{28,24},{1,5},{5... | collective-permute-start | bytes 786440 | tf_op jit(solution)/shard_map/ppermute | solution.py:323
  24.7 5.7 %collective-permute-start.4 = (f32[8,768]{1,0:T(8,128)S(1)}, f32[8,768]{1,0:T(8,128)S(1)}, u32[]{:S(2)}, u32[]{:S(2)}) collective-permute-start(f32[8,768]{1,0:T(8,128)S(1)} %get-tuple-element.72.left_ref), channel_id=1, source_target_pairs={{0,1},{1,2},{2,3},{3,0},{4,5},{5,6},{6,7},{7,4},{8,9},{9,10},{10,1... | collective-permute-start | bytes 73736 | tf_op jit(solution)/shard_map/ppermute | solution.py:341
  30.3 4.7 %collective-permute-start.5 = (f32[8,768]{1,0:T(8,128)S(1)}, f32[8,768]{1,0:T(8,128)S(1)}, u32[]{:S(2)}, u32[]{:S(2)}) collective-permute-start(f32[8,768]{1,0:T(8,128)S(1)} %shard_map.85.refs_0_), channel_id=1, source_target_pairs={{0,2},{1,3},{2,0},{3,1},{4,6},{5,7},{6,4},{7,5},{8,10},{9,11},{10,... | collective-permute-start | bytes 73736 | tf_op jit(solution)/shard_map/ppermute | solution.py:341
  36.0 1.6 %collective-permute-start.6 = (f32[4,128,128]{2,1,0:T(8,128)S(1)}, f32[4,128,128]{2,1,0:T(8,128)S(1)}, u32[]{:S(2)}, u32[]{:S(2)}) collective-permute-start(f32[4,128,128]{2,1,0:T(8,128)S(1)} %get-tuple-element.82), channel_id=1, source_target_pairs={{28,24},{24,28},{20,16},{16,20},{12,8},{8,12},{4,0},{0,4},{29,25},... | collective-permute-start | bytes 786440 | tf_op jit(solution)/shard_map/ppermute | solution.py:323
  37.6 8.3 %collective-permute-start.7 = (f32[4,128,128]{2,1,0:T(8,128)S(1)}, f32[4,128,128]{2,1,0:T(8,128)S(1)}, u32[]{:S(2)}, u32[]{:S(2)}) collective-permute-start(f32[4,128,128]{2,1,0:T(8,128)S(1)} %shard_map.88.refs_0_), channel_id=1, source_target_pairs={{28,20},{24,8},{20,28},{16,0},{12,4},{4,12},{29,21},{25,9},{21,29}... | collective-permute-start | bytes 786440 | tf_op jit(solution)/shard_map/ppermute | solution.py:323
  46.0 8.3 %collective-permute-start.8 = (f32[4,128,128]{2,1,0:T(8,128)S(1)}, f32[4,128,128]{2,1,0:T(8,128)S(1)}, u32[]{:S(2)}, u32[]{:S(2)}) collective-permute-start(f32[4,128,128]{2,1,0:T(8,128)S(1)} %shard_map.90.refs_0_), channel_id=1, source_target_pairs={{28,12},{24,16},{20,4},{16,24},{8,0},{0,8},{29,13},{25,17},{21,5},... | collective-permute-start | bytes 786440 | tf_op jit(solution)/shard_map/ppermute | solution.py:323
  54.3 1.6 %collective-permute-start.9 = (f32[4,128,128]{2,1,0:T(8,128)S(1)}, f32[4,128,128]{2,1,0:T(8,128)S(1)}, u32[]{:S(2)}, u32[]{:S(2)}) collective-permute-start(f32[4,128,128]{2,1,0:T(8,128)S(1)} %get-tuple-element.90), channel_id=1, source_target_pairs={{28,24},{24,28},{20,16},{16,20},{12,8},{8,12},{4,0},{0,4},{29,25},... | collective-permute-start | bytes 786440 | tf_op jit(solution)/shard_map/ppermute | solution.py:323

commit v2 on v1

--- a/solution.py
+++ b/solution.py
@@ -104,23 +104,22 @@
         copy.wait()
 
 
-def second_kernel(k2, v2, q_hbm, og_hbm, q1, og1, q2, og2, sum_ref, pre_ref, sems1, sems2):
-    copies = fetches((q_hbm, og_hbm), (q2, og2), sems2, True)
-    copies += fetches((q_hbm, og_hbm), (q1, og1), sems1, False)
+def second_kernel(k2, v2, sum_ref, pre_ref):
+    sum_states(k2, v2, sum_ref, pre_ref)
+
+
+def inner_kernel(same, q_hbm, og_hbm, k_ref, v_ref, gain_ref, pre_ref, after_ref, *outs):
+    q_ref, inner_ref, scaled_ref, qturned_ref, turned_ref, og_ref, sems = outs
+    rows, width = q_ref.shape
+    copies = fetches((q_hbm, og_hbm), (q_ref, og_ref), sems, same)
     for copy in copies:
         copy.start()
-    sum_states(k2, v2, sum_ref, pre_ref)
-    for copy in copies:
-        copy.wait()
-
-
-def inner_kernel(same, q_ref, k_ref, v_ref, og_ref, gain_ref, pre_ref, after_ref, *outs):
-    inner_ref, scaled_ref, qturned_ref, turned_ref = outs
-    rows, width = q_ref.shape
     gain = gain_ref[:, columns(same, width)]
-    for j in range(width // HEAD_DIM):
-        lanes = lanes_of(j)
-        for i, part in enumerate(chunks_of(rows)):
+    for i, part in enumerate(chunks_of(rows)):
+        for copy in copies[2 * i:2 * i + 2]:
+            copy.wait()
+        for j in range(width // HEAD_DIM):
+            lanes = lanes_of(j)
             q, k = q_ref[part, lanes], k_ref[part, lanes]
             size = q.shape[0]
             scores = jnp.where(lower(size), dot(q, k, 1, 1), 0.0).astype(BF16)
@@ -148,16 +147,18 @@
             square = jnp.sum(square.T, axis=0, keepdims=True)
             cross = jnp.sum(cross.T, axis=0, keepdims=True)
             row = lax.broadcasted_iota(jnp.int32, (8, square.shape[1]), 0)
-            refs[-1][:, part] = jnp.where(row == 0, square, jnp.where(row == 1, cross, 0.0))
+            sums = jnp.where(row == 0, square, jnp.where(row == 1, cross, 0.0))
+            for peer in range(refs[-1].shape[0]):
+                refs[-1][peer, :, part] = sums
         else:
             refs[-2][part] = square
             refs[-1][part] = cross
 
 
 def factors_kernel(full, parts, refs):
-    total = refs[0][...]
-    for ref in refs[1:parts]:
-        total = total + ref[...]
+    total = refs[0][0]
+    for peer in range(1, parts):
+        total = total + refs[0][peer]
     inv = lax.rsqrt(total[0:1] / full + 1e-6)
     slope = inv * inv * inv * (total[1:2] / full)
     row = lax.broadcasted_iota(jnp.int32, total.shape, 0)
@@ -172,7 +173,7 @@
         refs[-2][...] = inv
         refs[-1][...] = slope
         inv_ref, slope_ref = refs[-2:]
-        attn_ref, scaled_ref, qturned_ref, g_ref, sum_ref, post_ref = refs[parts:-2]
+        attn_ref, scaled_ref, qturned_ref, g_ref, sum_ref, post_ref = refs[1:-2]
     else:
         inv_ref, slope_ref, attn_ref, scaled_ref, qturned_ref, g_ref, sum_ref, post_ref = refs
     heads = sum_ref.shape[0]
@@ -327,28 +328,13 @@
     return move(value, [(r, r ^ 1) for r in range(lax.axis_size("seq"))], backward)
 
 
-def add_kernel(left_ref, right_ref, out_ref):
-    out_ref[...] = left_ref[...] + right_ref[...]
-
-
-def head_sums(sums):
-    peers = lax.axis_size("head")
-    distance, parts = 1, [sums]
-    while distance < peers:
-        if len(parts) == 2:
-            sums = run(add_kernel, sums.size, [VMEM, VMEM], VMEM, shape(sums.shape, F32), parts)
-        pairs = [(r, (r + distance) % peers) for r in range(peers)]
-        parts = [sums, lax.ppermute(sums, "head", pairs)]
-        distance *= 2
-    return parts
-
-
 def shards(query, key_in, value, out_grad, gain):
     rows, width = query.shape
     half = width // 2
     heads = half // HEAD_DIM
     chunks = len(chunks_of(rows))
-    full = width * lax.axis_size("head")
+    peers = lax.axis_size("head")
+    full = width * peers
     gain = gain.reshape(1, width)
     pin = lambda x: pltpu.with_memory_space_constraint(x, pltpu.HBM)
     query, key_in, value, out_grad = (pin(x) for x in (query, key_in, value, out_grad))
@@ -368,39 +354,42 @@
         (key_in, value), [sems, sems],
     )
     extra = nearby(send, False)
-    q1, og1, q2, og2, keep, pre2 = run(
-        second_kernel, unit, [VMEM, VMEM, HBM, HBM], [VMEM] * 6, [thin] * 4 + [states, inside],
-        (k2, v2, query, out_grad), [sems, sems],
-    )
-
-    def inner_of(same, q, k, v, og, pre):
+    keep, pre2 = run(
+        second_kernel, unit, [VMEM, VMEM], [VMEM] * 2, [states, inside], (k2, v2),
+    )
+
+    def inner_of(same, k, v, pre):
         return lambda message: run(
             partial(inner_kernel, same), 6 * unit,
-            [VMEM] * 6 + [ANYWHERE], [VMEM] * 4,
-            [wide, wide, shape((half, rows), BF16), shape((heads, rows, rows // chunks), BF16)],
-            (q, k, v, og, gain, pre, message),
+            [HBM, HBM, VMEM, VMEM, VMEM, VMEM, ANYWHERE], [VMEM] * 5,
+            [
+                thin, wide, wide,
+                shape((half, rows), BF16), shape((heads, rows, rows // chunks), BF16),
+            ],
+            (query, out_grad, k, v, gain, pre, message),
+            [pltpu.VMEM((rows, half), BF16), sems],
         )
 
     state2, state1, made = scan_states(
         keep, extra, False,
-        [inner_of(True, q2, k2, v2, og2, pre2), inner_of(False, q1, k1, v1, og1, pre1)],
-    )
-    (inner2, scaled2, qturned2, turned2), (inner1, scaled1, qturned1, turned1) = made
+        [inner_of(True, k2, v2, pre2), inner_of(False, k1, v1, pre1)],
+    )
+    (q2, inner2, scaled2, qturned2, turned2), (q1, inner1, scaled1, qturned1, turned1) = made
 
     attn2, square, cross = run(
         partial(attn_kernel, False), unit, [VMEM] * 4, [VMEM] * 3, [wide, lane_sums, lane_sums],
         (q2, inner2, scaled2, state2),
     )
     attn1, sums = run(
-        partial(attn_kernel, True), unit, [VMEM] * 6, [VMEM] * 2, [wide, shape((8, rows), F32)],
+        partial(attn_kernel, True), unit, [VMEM] * 6, [VMEM] * 2, [wide, shape((peers, 8, rows), F32)],
         (q1, inner1, scaled1, state1, square, cross),
     )
-    parts = head_sums(sums)
+    sums = lax.all_to_all(sums, "head", 0, 0)
 
     g2, gsend, post2, inv, slope = run(
-        partial(grad_kernel, full, len(parts)), unit,
-        [VMEM] * (len(parts) + 3), [VMEM] * 5, [thin, states, inside, lane_sums, lane_sums],
-        (*parts, attn2, scaled2, qturned2),
+        partial(grad_kernel, full, peers), unit,
+        [VMEM] * 4, [VMEM] * 5, [thin, states, inside, lane_sums, lane_sums],
+        (sums, attn2, scaled2, qturned2),
     )
     gextra = nearby(gsend, True)
     g1, gkeep, post1 = run(

time: 57.9 us -> 57.2 us (0.988)
  blocking collectives: 0 us -> 10.5 us
  waiting for transfers between devices: 18 us -> 8.1 us
  starting transfers between devices: 16.4 us -> 14.3 us
  Pallas kernels: 22.2 us -> 22.9 us
    all_to_all x0 -> x1, blocking collectives: none -> 10.5 us  [shards(): sums = lax.all_to_all(sums, 'head', 0, 0)]
    ppermute x2 -> x0, waiting for transfers between devices: 7.98 us -> none  [head_sums(): parts = [sums, lax.ppermute(sums, 'head', pairs)]]
    ppermute x2 -> x0, starting transfers between devices: 2.42 us -> none  [head_sums(): parts = [sums, lax.ppermute(sums, 'head', pairs)]]
    ppermute x8, waiting for transfers between devices: 10 us -> 8.1 us  [move(): return lax.ppermute(value, 'seq', pairs)]
    pallas_call x19 -> x18, Pallas kernels: 22.2 us -> 22.9 us  [run(): pl.pallas_call(kernel, in_specs=in_specs, out_specs=out_specs, out_shape=...]
  transfers between devices with their start and end apart: 10 -> 8, of which waited for: 8 -> 7; matrix products, arithmetic and copies ran while one was open for 0% -> 0% of each run, Pallas kernels for 29% -> 31%
where the time goes in v2:
time: 57.2 us; the launch traced here: 56.8 us
  Pallas kernels  22.9 us (40%)
  starting transfers between devices  14.3 us (25%)
  blocking collectives  10.5 us (18%)
  waiting for transfers between devices  8.1 us (14%)
  between operations  0.96 us (2%)
    pallas_call x18, Pallas kernels, run(): pl.pallas_call(kernel, in_specs=in_specs, out_specs=out_specs, out_shape=...  22.9 us
    ppermute x8, starting transfers between devices, move(): return lax.ppermute(value, 'seq', pairs)  14.3 us
    all_to_all x1, blocking collectives, shards(): sums = lax.all_to_all(sums, 'head', 0, 0)  10.5 us
    ppermute x8, waiting for transfers between devices, move(): return lax.ppermute(value, 'seq', pairs)  8.1 us
  transfers between devices with their start and end apart: 8, of which 7 were waited for; matrix products, arithmetic and copies ran while one was open for 0% of the time, Pallas kernels for 31%

profile of v2, /device:TPU:0, one launch (start us, length us, event | category | flops | bytes accessed | tf_op | source)
XLA Modules:
  0.0 56.8 jit_solution(1372495095629809247)
XLA Ops:
  0.6 2.1 %shard_map.76 = (bf16[768,512]{1,0:T(8,128)(2,1)S(1)}, bf16[768,512]{1,0:T(8,128)(2,1)S(1)}, bf16[768,512]{1,0:T(8,128)(2,1)S(1)}, bf16[768,512]{1,0:T(8,128)(2,...) custom-call(bf16[768,1024]{1,0:T(8,128)(2,1)} %k_hbm.1, bf16[768,1024]{1,0:T(8,128)(2,1)} %v_hbm.1), custom_call_target="tpu_custom_call" | custom-call | flops 100663296 | bytes 3145728 | tf_op jit(solution)/shard_map/pallas_call | solution.py:50
  2.8 0.5 collective-permute-start
  3.7 0.7 %collective-permute-done.refs_1_ = f32[4,128,128]{2,1,0:T(8,128)S(1)} collective-permute-done((f32[4,128,128]{2,1,0:T(8,128)S(1)}, f32[4,128,128]{2,1,0:T(8,128)S(1)}, u32[]{:S(2)}, u32[]{:S(2)}) %collective-permute-start) | collective-permute-done | bytes 262176 | tf_op jit(solution)/shard_map/ppermute | solution.py:324
  4.5 4.8 %collective-permute-start.1 = (f32[4,128,128]{2,1,0:T(8,128)S(1)}, f32[4,128,128]{2,1,0:T(8,128)S(1)}, u32[]{:S(2)}, u32[]{:S(2)}) collective-permute-start(f32[4,128,128]{2,1,0:T(8,128)S(1)} %shard_map.78.after_ref), channel_id=1, source_target_pairs={{0,8},{4,20},{8,0},{12,28},{16,24},{24,16},{1,9},{5,21},{9,1},{13,... | collective-permute-start | bytes 786440 | tf_op jit(solution)/shard_map/ppermute | solution.py:324
  9.3 3.3 %shard_map.79 = (bf16[768,512]{1,0:T(8,128)(2,1)S(1)}, f32[768,512]{1,0:T(8,128)S(1)}, f32[768,512]{1,0:T(8,128)S(1)}, bf16[512,768]{1,0:T(8,128)(2,1)S(1)}, bf16[4,768,256]{2,1,0:T(8,128)(2,1)S(1)}) custom-call(bf16[768,1024]{1,0:T(8,128)(2,1)} %q_hbm.3, bf16[768,1024]{1,0:T(8,128)(2,1)} %og_hbm.3, bf16[768,512]{1,0:T(8,128)(2,1)S(1)} %get-tuple-element.48.k2.k_ref, ...), custom_call_target="tpu_custom_call" | custom-call | flops 603979776 | bytes 5378048 | tf_op jit(solution)/shard_map/pallas_call | solution.py:50
  12.7 1.0 %collective-permute-done.1.refs_2_ = f32[4,128,128]{2,1,0:T(8,128)S(1)} collective-permute-done((f32[4,128,128]{2,1,0:T(8,128)S(1)}, f32[4,128,128]{2,1,0:T(8,128)S(1)}, u32[]{:S(2)}, u32[]{:S(2)}) %collective-permute-start.1) | collective-permute-done | bytes 262176 | tf_op jit(solution)/shard_map/ppermute | solution.py:324
  13.7 4.0 %collective-permute-start.2 = (f32[4,128,128]{2,1,0:T(8,128)S(1)}, f32[4,128,128]{2,1,0:T(8,128)S(1)}, u32[]{:S(2)}, u32[]{:S(2)}) collective-permute-start(f32[4,128,128]{2,1,0:T(8,128)S(1)} %shard_map.80.after_ref), channel_id=1, source_target_pairs={{0,16},{4,12},{8,24},{12,4},{20,28},{28,20},{1,17},{5,13},{9,25},{... | collective-permute-start | bytes 786440 | tf_op jit(solution)/shard_map/ppermute | solution.py:324
  17.7 3.3 %shard_map.81 = (bf16[768,512]{1,0:T(8,128)(2,1)S(1)}, f32[768,512]{1,0:T(8,128)S(1)}, f32[768,512]{1,0:T(8,128)S(1)}, bf16[512,768]{1,0:T(8,128)(2,1)S(1)}, bf16[4,768,256]{2,1,0:T(8,128)(2,1)S(1)}) custom-call(bf16[768,1024]{1,0:T(8,128)(2,1)} %q_hbm.3, bf16[768,1024]{1,0:T(8,128)(2,1)} %og_hbm.3, bf16[768,512]{1,0:T(8,128)(2,1)S(1)} %get-tuple-element.54.k_ref, ...), custom_call_target="tpu_custom_call" | custom-call | flops 603979776 | bytes 5378048 | tf_op jit(solution)/shard_map/pallas_call | solution.py:50
  21.0 0.5 collective-permute-done.2.refs_3_
  21.7 0.4 shard_map.83
  22.2 1.1 %collective-permute-done.3.state_ref = f32[4,128,128]{2,1,0:T(8,128)S(1)} collective-permute-done((f32[4,128,128]{2,1,0:T(8,128)S(1)}, f32[4,128,128]{2,1,0:T(8,128)S(1)}, u32[]{:S(2)}, u32[]{:S(2)}) %collective-permute-start.3) | collective-permute-done | bytes 262176 | tf_op jit(solution)/shard_map/ppermute | solution.py:324
  23.3 0.6 %shard_map.84 = (f32[768,512]{1,0:T(8,128)S(1)}, f32[4,8,768]{2,1,0:T(8,128)S(1)}) custom-call(bf16[768,512]{1,0:T(8,128)(2,1)S(1)} %get-tuple-element.58.q_ref, f32[768,512]{1,0:T(8,128)S(1)} %get-tuple-element.59.inner_ref, f32[768,512]{1,0:T(8,128)S(1)} %get-tuple-element.60.scaled_ref.refs_3_, f32[4,128,128]{2,1,0:T(8,128)S(1)} %collective-permute-done.3.state_ref, ...), custom_call_target="tpu_custom_call" | custom-call | flops 100663296 | bytes 4980736 | tf_op jit(solution)/shard_map/pallas_call | solution.py:50
  23.9 10.5 %all_to_all.5.refs_0_ = f32[4,8,768]{2,1,0:T(8,128)S(1)} all-to-all(f32[4,8,768]{2,1,0:T(8,128)S(1)} %get-tuple-element.68), channel_id=1, replica_groups=mesh['seq'=8,'head'=4] {'head'}, dimensions={0} | all-to-all | bytes 196608 | tf_op jit(solution)/shard_map/all_to_all | solution.py:387
  34.4 0.9 %shard_map.85 = (bf16[768,512]{1,0:T(8,128)(2,1)S(1)}, f32[4,128,128]{2,1,0:T(8,128)S(1)}, bf16[3,4,128,128]{3,2,1,0:T(8,128)(2,1)S(1)}, f32[768,128]{1,0:T(8,128)S(1)}, f32[768,128]{1,0:T(8,128)S(1)}) custom-call(f32[4,8,768]{2,1,0:T(8,128)S(1)} %all_to_all.5.refs_0_, f32[768,512]{1,0:T(8,128)S(1)} %get-tuple-element.69.refs_1_, ...), custom_call_target="tpu_custom_call" | custom-call | flops 100663296 | bytes 4030464 | tf_op jit(solution)/shard_map/pallas_call | solution.py:50
  35.3 0.5 shard_map.86
  35.8 1.0 %collective-permute-done.4.refs_1_ = f32[4,128,128]{2,1,0:T(8,128)S(1)} collective-permute-done((f32[4,128,128]{2,1,0:T(8,128)S(1)}, f32[4,128,128]{2,1,0:T(8,128)S(1)}, u32[]{:S(2)}, u32[]{:S(2)}) %collective-permute-start.4) | collective-permute-done | bytes 262176 | tf_op jit(solution)/shard_map/ppermute | solution.py:324
  36.9 1.3 %collective-permute-start.5 = (f32[4,128,128]{2,1,0:T(8,128)S(1)}, f32[4,128,128]{2,1,0:T(8,128)S(1)}, u32[]{:S(2)}, u32[]{:S(2)}) collective-permute-start(f32[4,128,128]{2,1,0:T(8,128)S(1)} %shard_map.87.refs_0_), channel_id=1, source_target_pairs={{28,20},{24,8},{20,28},{16,0},{12,4},{4,12},{29,21},{25,9},{21,29}... | collective-permute-start | bytes 786440 | tf_op jit(solution)/shard_map/ppermute | solution.py:324
  38.2 4.0 %shard_map.88 = (bf16[768,1024]{1,0:T(8,128)(2,1)}, f32[768,512]{1,0:T(8,128)S(1)}, f32[768,512]{1,0:T(8,128)S(1)}) custom-call(bf16[768,512]{1,0:T(8,128)(2,1)S(1)} %get-tuple-element.58.q_ref, bf16[768,512]{1,0:T(8,128)(2,1)S(1)} %get-tuple-element.54.k_ref, bf16[768,512]{1,0:T(8,128)(2,1)S(1)} %get-tuple-element.55.v_ref, ...), custom_call_target="tpu_custom_call" | custom-call | flops 905969664 | bytes 6029312 | tf_op jit(solution)/shard_map/pallas_call | solution.py:50
  42.2 3.0 %collective-permute-done.5.refs_2_ = f32[4,128,128]{2,1,0:T(8,128)S(1)} collective-permute-done((f32[4,128,128]{2,1,0:T(8,128)S(1)}, f32[4,128,128]{2,1,0:T(8,128)S(1)}, u32[]{:S(2)}, u32[]{:S(2)}) %collective-permute-start.5) | collective-permute-done | bytes 262176 | tf_op jit(solution)/shard_map/ppermute | solution.py:324
  45.2 3.6 %collective-permute-start.6 = (f32[4,128,128]{2,1,0:T(8,128)S(1)}, f32[4,128,128]{2,1,0:T(8,128)S(1)}, u32[]{:S(2)}, u32[]{:S(2)}) collective-permute-start(f32[4,128,128]{2,1,0:T(8,128)S(1)} %shard_map.89.refs_0_), channel_id=1, source_target_pairs={{28,12},{24,16},{20,4},{16,24},{8,0},{0,8},{29,13},{25,17},{21,5},... | collective-permute-start | bytes 786440 | tf_op jit(solution)/shard_map/ppermute | solution.py:324
  48.8 4.0 %shard_map.90 = (bf16[768,1024]{1,0:T(8,128)(2,1)}, f32[768,512]{1,0:T(8,128)S(1)}, f32[768,512]{1,0:T(8,128)S(1)}) custom-call(bf16[768,512]{1,0:T(8,128)(2,1)S(1)} %get-tuple-element.53.q_ref, bf16[768,512]{1,0:T(8,128)(2,1)S(1)} %get-tuple-element.48.k2.k_ref, bf16[768,512]{1,0:T(8,128)(2,1)S(1)} %get-tuple-element.49.v2.v_ref, ...), custom_call_target="tpu_custom_call", output_to_operand_aliasing={{0}: (9, {})} | custom-call | flops 905969664 | bytes 7602176 | tf_op jit(solution)/shard_map/pallas_call | solution.py:50
  52.8 0.7 %collective-permute-done.6.refs_3_ = f32[4,128,128]{2,1,0:T(8,128)S(1)} collective-permute-done((f32[4,128,128]{2,1,0:T(8,128)S(1)}, f32[4,128,128]{2,1,0:T(8,128)S(1)}, u32[]{:S(2)}, u32[]{:S(2)}) %collective-permute-start.6) | collective-permute-done | bytes 262176 | tf_op jit(solution)/shard_map/ppermute | solution.py:324
  53.7 1.5 %shard_map.92 = (bf16[768,1024]{1,0:T(8,128)(2,1)}, bf16[768,1024]{1,0:T(8,128)(2,1)}) custom-call(bf16[768,512]{1,0:T(8,128)(2,1)S(1)} %get-tuple-element.54.k_ref, bf16[768,512]{1,0:T(8,128)(2,1)S(1)} %get-tuple-element.55.v_ref, f32[768,512]{1,0:T(8,128)S(1)} %get-tuple-element.87.kpart_ref, f32[768,512]{1,0:T(8,128)S(1)} %get-tuple-element.81.refs_3_.vpart_ref, ...), custom_call_target="tpu_custom_call" | custom-call | flops 201326592 | bytes 4980736 | tf_op jit(solution)/shard_map/pallas_call | solution.py:50
  55.2 1.5 %shard_map.93 = (bf16[768,1024]{1,0:T(8,128)(2,1)}, bf16[768,1024]{1,0:T(8,128)(2,1)}) custom-call(bf16[768,512]{1,0:T(8,128)(2,1)S(1)} %get-tuple-element.48.k2.k_ref, bf16[768,512]{1,0:T(8,128)(2,1)S(1)} %get-tuple-element.49.v2.v_ref, f32[768,512]{1,0:T(8,128)S(1)} %get-tuple-element.84.kpart_ref, ...), custom_call_target="tpu_custom_call", output_to_operand_aliasing={{0}: (5, {}), {1}: (6, {})} | custom-call | flops 201326592 | bytes 8126464 | tf_op jit(solution)/shard_map/pallas_call | solution.py:50
  (13 shorter events, 1.1 us)
Async XLA Ops:
  2.8 6.5 %copy-start = (f32[1024]{0:T(1024)S(1)}, f32[1024]{0:T(1024)}, u32[]{:S(2)}) copy-start(f32[1024]{0:T(1024)} %param.9) | copy-start | bytes 12292
  2.8 1.7 %collective-permute-start = (f32[4,128,128]{2,1,0:T(8,128)S(1)}, f32[4,128,128]{2,1,0:T(8,128)S(1)}, u32[]{:S(2)}, u32[]{:S(2)}) collective-permute-start(f32[4,128,128]{2,1,0:T(8,128)S(1)} %get-tuple-element.52), channel_id=1, source_target_pairs={{0,4},{4,0},{8,12},{12,8},{16,20},{20,16},{24,28},{28,24},{1,5},{5... | collective-permute-start | bytes 786440 | tf_op jit(solution)/shard_map/ppermute | solution.py:324
  4.5 9.1 %collective-permute-start.1 = (f32[4,128,128]{2,1,0:T(8,128)S(1)}, f32[4,128,128]{2,1,0:T(8,128)S(1)}, u32[]{:S(2)}, u32[]{:S(2)}) collective-permute-start(f32[4,128,128]{2,1,0:T(8,128)S(1)} %shard_map.78.after_ref), channel_id=1, source_target_pairs={{0,8},{4,20},{8,0},{12,28},{16,24},{24,16},{1,9},{5,21},{9,1},{13,... | collective-permute-start | bytes 786440 | tf_op jit(solution)/shard_map/ppermute | solution.py:324
  13.7 7.8 %collective-permute-start.2 = (f32[4,128,128]{2,1,0:T(8,128)S(1)}, f32[4,128,128]{2,1,0:T(8,128)S(1)}, u32[]{:S(2)}, u32[]{:S(2)}) collective-permute-start(f32[4,128,128]{2,1,0:T(8,128)S(1)} %shard_map.80.after_ref), channel_id=1, source_target_pairs={{0,16},{4,12},{8,24},{12,4},{20,28},{28,20},{1,17},{5,13},{9,25},{... | collective-permute-start | bytes 786440 | tf_op jit(solution)/shard_map/ppermute | solution.py:324
  21.6 1.6 %collective-permute-start.3 = (f32[4,128,128]{2,1,0:T(8,128)S(1)}, f32[4,128,128]{2,1,0:T(8,128)S(1)}, u32[]{:S(2)}, u32[]{:S(2)}) collective-permute-start(f32[4,128,128]{2,1,0:T(8,128)S(1)} %get-tuple-element.62), channel_id=1, source_target_pairs={{0,4},{4,0},{8,12},{12,8},{16,20},{20,16},{24,28},{28,24},{1,5},{5... | collective-permute-start | bytes 786440 | tf_op jit(solution)/shard_map/ppermute | solution.py:324
  35.3 1.6 %collective-permute-start.4 = (f32[4,128,128]{2,1,0:T(8,128)S(1)}, f32[4,128,128]{2,1,0:T(8,128)S(1)}, u32[]{:S(2)}, u32[]{:S(2)}) collective-permute-start(f32[4,128,128]{2,1,0:T(8,128)S(1)} %get-tuple-element.78), channel_id=1, source_target_pairs={{28,24},{24,28},{20,16},{16,20},{12,8},{8,12},{4,0},{0,4},{29,25},... | collective-permute-start | bytes 786440 | tf_op jit(solution)/shard_map/ppermute | solution.py:324
  36.9 8.3 %collective-permute-start.5 = (f32[4,128,128]{2,1,0:T(8,128)S(1)}, f32[4,128,128]{2,1,0:T(8,128)S(1)}, u32[]{:S(2)}, u32[]{:S(2)}) collective-permute-start(f32[4,128,128]{2,1,0:T(8,128)S(1)} %shard_map.87.refs_0_), channel_id=1, source_target_pairs={{28,20},{24,8},{20,28},{16,0},{12,4},{4,12},{29,21},{25,9},{21,29}... | collective-permute-start | bytes 786440 | tf_op jit(solution)/shard_map/ppermute | solution.py:324
  45.2 8.3 %collective-permute-start.6 = (f32[4,128,128]{2,1,0:T(8,128)S(1)}, f32[4,128,128]{2,1,0:T(8,128)S(1)}, u32[]{:S(2)}, u32[]{:S(2)}) collective-permute-start(f32[4,128,128]{2,1,0:T(8,128)S(1)} %shard_map.89.refs_0_), channel_id=1, source_target_pairs={{28,12},{24,16},{20,4},{16,24},{8,0},{0,8},{29,13},{25,17},{21,5},... | collective-permute-start | bytes 786440 | tf_op jit(solution)/shard_map/ppermute | solution.py:324
  53.6 1.6 %collective-permute-start.7 = (f32[4,128,128]{2,1,0:T(8,128)S(1)}, f32[4,128,128]{2,1,0:T(8,128)S(1)}, u32[]{:S(2)}, u32[]{:S(2)}) collective-permute-start(f32[4,128,128]{2,1,0:T(8,128)S(1)} %get-tuple-element.86), channel_id=1, source_target_pairs={{28,24},{24,28},{20,16},{16,20},{12,8},{8,12},{4,0},{0,4},{29,25},... | collective-permute-start | bytes 786440 | tf_op jit(solution)/shard_map/ppermute | solution.py:324

commit v3 on v2

--- a/solution.py
+++ b/solution.py
@@ -76,13 +76,15 @@
     return copies
 
 
-def sum_states(k_ref, v_ref, sum_ref, pre_ref, copies=None):
+def state_kernel(same, k_hbm, v_hbm, k_ref, v_ref, sum_ref, pre_ref, sems):
+    copies = fetches((k_hbm, v_hbm), (k_ref, v_ref), sems, same)
+    for copy in copies:
+        copy.start()
     heads = sum_ref.shape[0]
     totals = [None] * heads
     for i, part in enumerate(chunks_of(k_ref.shape[0])):
-        if copies:
-            for copy in copies[2 * i:2 * i + 2]:
-                copy.wait()
+        for copy in copies[2 * i:2 * i + 2]:
+            copy.wait()
         for j in range(heads):
             term = dot(k_ref[part, lanes_of(j)], v_ref[part, lanes_of(j)], 0, 0)
             if i:
@@ -92,20 +94,6 @@
             totals[j] = totals[j] + term if i else term
     for j in range(heads):
         sum_ref[j] = totals[j]
-
-
-def first_kernel(k_hbm, v_hbm, k1, v1, k2, v2, sum_ref, pre_ref, sems1, sems2):
-    now = fetches((k_hbm, v_hbm), (k1, v1), sems1, False)
-    later = fetches((k_hbm, v_hbm), (k2, v2), sems2, True)
-    for copy in now + later:
-        copy.start()
-    sum_states(k1, v1, sum_ref, pre_ref, now)
-    for copy in later:
-        copy.wait()
-
-
-def second_kernel(k2, v2, sum_ref, pre_ref):
-    sum_states(k2, v2, sum_ref, pre_ref)
 
 
 def inner_kernel(same, q_hbm, og_hbm, k_ref, v_ref, gain_ref, pre_ref, after_ref, *outs):
@@ -148,17 +136,16 @@
             cross = jnp.sum(cross.T, axis=0, keepdims=True)
             row = lax.broadcasted_iota(jnp.int32, (8, square.shape[1]), 0)
             sums = jnp.where(row == 0, square, jnp.where(row == 1, cross, 0.0))
-            for peer in range(refs[-1].shape[0]):
-                refs[-1][peer, :, part] = sums
+            refs[-1][:, part] = sums
         else:
             refs[-2][part] = square
             refs[-1][part] = cross
 
 
 def factors_kernel(full, parts, refs):
-    total = refs[0][0]
-    for peer in range(1, parts):
-        total = total + refs[0][peer]
+    total = refs[0][...]
+    for ref in refs[1:parts]:
+        total = total + ref[...]
     inv = lax.rsqrt(total[0:1] / full + 1e-6)
     slope = inv * inv * inv * (total[1:2] / full)
     row = lax.broadcasted_iota(jnp.int32, total.shape, 0)
@@ -173,7 +160,7 @@
         refs[-2][...] = inv
         refs[-1][...] = slope
         inv_ref, slope_ref = refs[-2:]
-        attn_ref, scaled_ref, qturned_ref, g_ref, sum_ref, post_ref = refs[1:-2]
+        attn_ref, scaled_ref, qturned_ref, g_ref, sum_ref, post_ref = refs[parts:-2]
     else:
         inv_ref, slope_ref, attn_ref, scaled_ref, qturned_ref, g_ref, sum_ref, post_ref = refs
     heads = sum_ref.shape[0]
@@ -226,24 +213,39 @@
         copy.wait()
 
 
-def final_kernel(same, k_ref, v_ref, kpart_ref, vpart_ref, state_ref, *refs):
-    kgrad_hbm, vgrad_hbm, kgrad_ref, vgrad_ref, sems = refs[-5:]
-    rows, width = k_ref.shape
-    target = columns(same, width)
-    states = [state_ref[j].astype(BF16) for j in range(width // HEAD_DIM)]
+def final_parts(k_ref, v_ref, kpart_ref, vpart_ref, state_ref, kgrad_ref, vgrad_ref, part):
+    for j in range(state_ref.shape[0]):
+        lanes = lanes_of(j)
+        state = state_ref[j].astype(BF16)
+        kgrad = kpart_ref[part, lanes] + dot(v_ref[part, lanes], state, 1, 1)
+        vgrad = vpart_ref[part, lanes] + dot(k_ref[part, lanes], state)
+        kgrad_ref[part, lanes] = kgrad.astype(BF16)
+        vgrad_ref[part, lanes] = vgrad.astype(BF16)
+
+
+def near_kernel(*refs):
+    for part in chunks_of(refs[0].shape[0]):
+        final_parts(*refs, part)
+
+
+def last_kernel(same, *refs):
+    kdone_ref, vdone_ref, kgrad_hbm, vgrad_hbm, kgrad_ref, vgrad_ref, sems = refs[5:]
+    rows, width = kgrad_ref.shape
     copies = []
+
+    def send(source, out, part, half):
+        sem = sems.at[len(copies)]
+        target = out.at[part, columns(half, width)]
+        copy = pltpu.make_async_copy(source.at[part], target, sem)
+        copy.start()
+        copies.append(copy)
+
+    send(kdone_ref, kgrad_hbm, slice(0, rows), not same)
+    send(vdone_ref, vgrad_hbm, slice(0, rows), not same)
     for part in chunks_of(rows):
-        for j, state in enumerate(states):
-            lanes = lanes_of(j)
-            kgrad = kpart_ref[part, lanes] + dot(v_ref[part, lanes], state, 1, 1)
-            vgrad = vpart_ref[part, lanes] + dot(k_ref[part, lanes], state)
-            kgrad_ref[part, lanes] = kgrad.astype(BF16)
-            vgrad_ref[part, lanes] = vgrad.astype(BF16)
-        for source, out in ((kgrad_ref, kgrad_hbm), (vgrad_ref, vgrad_hbm)):
-            sem = sems.at[len(copies)]
-            copy = pltpu.make_async_copy(source.at[part], out.at[part, target], sem)
-            copy.start()
-            copies.append(copy)
+        final_parts(*refs[:5], kgrad_ref, vgrad_ref, part)
+        send(kgrad_ref, kgrad_hbm, part, same)
+        send(vgrad_ref, vgrad_hbm, part, same)
     for copy in copies:
         copy.wait()
 
@@ -253,12 +255,7 @@
     stages = []
     for stage in range(bits - 1):
         rising, falling = 1 + stage, bits - 1 - stage
-        pairs = []
-        for r in range(count):
-            bit = falling if r & 1 else rising
-            useless = stage == 0 if r & 1 else stage == bits - 2
-            if not ((r >> bit) & 1 and useless):
-                pairs.append((r, r ^ (1 << bit)))
+        pairs = [(r, r ^ (1 << (falling if r & 1 else rising))) for r in range(count)]
         stages.append((rising, falling, pairs))
     return stages
 
@@ -349,14 +346,15 @@
     whole = shape((rows, width), BF16)
     sems = pltpu.SemaphoreType.DMA((2 * chunks,))
 
-    k1, v1, k2, v2, send, pre1 = run(
-        first_kernel, unit, [HBM, HBM], [VMEM] * 6, [thin] * 4 + [states, inside],
-        (key_in, value), [sems, sems],
-    )
+    def states_of(same):
+        return run(
+            partial(state_kernel, same), unit, [HBM, HBM], [VMEM] * 4, [thin, thin, states, inside],
+            (key_in, value), [sems],
+        )
+
+    k1, v1, send, pre1 = states_of(False)
     extra = nearby(send, False)
-    keep, pre2 = run(
-        second_kernel, unit, [VMEM, VMEM], [VMEM] * 2, [states, inside], (k2, v2),
-    )
+    k2, v2, keep, pre2 = states_of(True)
 
     def inner_of(same, k, v, pre):
         return lambda message: run(
@@ -381,15 +379,18 @@
         (q2, inner2, scaled2, state2),
     )
     attn1, sums = run(
-        partial(attn_kernel, True), unit, [VMEM] * 6, [VMEM] * 2, [wide, shape((peers, 8, rows), F32)],
+        partial(attn_kernel, True), unit, [VMEM] * 6, [VMEM] * 2, [wide, shape((8, rows), F32)],
         (q1, inner1, scaled1, state1, square, cross),
     )
-    sums = lax.all_to_all(sums, "head", 0, 0)
+    parts = [sums] + [
+        lax.ppermute(sums, "head", [(r, (r + shift) % peers) for r in range(peers)])
+        for shift in range(1, peers)
+    ]
 
     g2, gsend, post2, inv, slope = run(
         partial(grad_kernel, full, peers), unit,
-        [VMEM] * 4, [VMEM] * 5, [thin, states, inside, lane_sums, lane_sums],
-        (sums, attn2, scaled2, qturned2),
+        [VMEM] * (peers + 3), [VMEM] * 5, [thin, states, inside, lane_sums, lane_sums],
+        (*parts, attn2, scaled2, qturned2),
     )
     gextra = nearby(gsend, True)
     g1, gkeep, post1 = run(
@@ -423,16 +424,15 @@
     )
     (kpart1, vpart1), (kpart2, vpart2) = made
 
-    def final_of(same, *args, outs=()):
-        scratch = [pltpu.VMEM((rows, half), BF16)] * 2 + [sems]
-        aliases = {len(args) + i: i for i in range(len(outs))}
-        return run(
-            partial(final_kernel, same), 2 * unit, [VMEM] * len(args) + [HBM] * len(outs),
-            [HBM, HBM], [whole, whole], (*args, *outs), scratch, aliases,
-        )
-
-    outs = final_of(False, k1, v1, kpart1, vpart1, gstate1)
-    kgrad, vgrad = final_of(True, k2, v2, kpart2, vpart2, gstate2, outs=outs)
+    done = run(
+        near_kernel, 2 * unit, [VMEM] * 5, [VMEM] * 2, [thin, thin],
+        (k1, v1, kpart1, vpart1, gstate1),
+    )
+    kgrad, vgrad = run(
+        partial(last_kernel, True), 2 * unit, [VMEM] * 7, [HBM, HBM], [whole, whole],
+        (k2, v2, kpart2, vpart2, gstate2, *done),
+        [pltpu.VMEM((rows, half), BF16)] * 2 + [pltpu.SemaphoreType.DMA((2 * chunks + 2,))],
+    )
     return qgrads[0], kgrad, vgrad
 
 

time: 57.2 us -> 50 us (0.87)
  blocking collectives: 10.5 us -> 0 us
  waiting for transfers between devices: 8.1 us -> 11.5 us
  Pallas kernels: 22.9 us -> 23.6 us
  starting transfers between devices: 14.3 us -> 13.7 us
    all_to_all x1 -> x0, blocking collectives: 10.5 us -> none  [shards(): sums = lax.all_to_all(sums, 'head', 0, 0)]
    ppermute x8, starting transfers between devices: 14.3 us -> 8.56 us  [move(): return lax.ppermute(value, 'seq', pairs)]
    ppermute x0 -> x3, starting transfers between devices: none -> 5.17 us  [shards(): lax.ppermute(sums, 'head', [(r, (r + shift) % peers) for r in range(peers)])]
    ppermute x0 -> x3, waiting for transfers between devices: none -> 4.61 us  [shards(): lax.ppermute(sums, 'head', [(r, (r + shift) % peers) for r in range(peers)])]
    ppermute x8, waiting for transfers between devices: 8.1 us -> 6.88 us  [move(): return lax.ppermute(value, 'seq', pairs)]
    pallas_call x18, Pallas kernels: 22.9 us -> 23.6 us  [run(): pl.pallas_call(kernel, in_specs=in_specs, out_specs=out_specs, out_shape=...]
  transfers between devices with their start and end apart: 8 -> 11, of which waited for: 7 -> 10; matrix products, arithmetic and copies ran while one was open for 0% -> 0% of each run, Pallas kernels for 31% -> 36%
where the time goes in v3:
time: 50 us; the launch traced here: 49.8 us
  Pallas kernels  23.6 us (47%)
  starting transfers between devices  13.7 us (27%)
  waiting for transfers between devices  11.5 us (23%)
  between operations  0.94 us (2%)
    pallas_call x18, Pallas kernels, run(): pl.pallas_call(kernel, in_specs=in_specs, out_specs=out_specs, out_shape=...  23.6 us
    ppermute x8, starting transfers between devices, move(): return lax.ppermute(value, 'seq', pairs)  8.56 us
    ppermute x8, waiting for transfers between devices, move(): return lax.ppermute(value, 'seq', pairs)  6.88 us
    ppermute x3, starting transfers between devices, shards(): lax.ppermute(sums, 'head', [(r, (r + shift) % peers) for r in range(peers)])  5.17 us
    ppermute x3, waiting for transfers between devices, shards(): lax.ppermute(sums, 'head', [(r, (r + shift) % peers) for r in range(peers)])  4.61 us
  transfers between devices with their start and end apart: 11, of which 10 were waited for; matrix products, arithmetic and copies ran while one was open for 0% of the time, Pallas kernels for 36%

profile of v3, /device:TPU:0, one launch (start us, length us, event | category | flops | bytes accessed | tf_op | source)
XLA Modules:
  0.0 49.8 jit_solution(5336358431389976856)
XLA Ops:
  0.6 1.9 %shard_map.77 = (bf16[768,512]{1,0:T(8,128)(2,1)S(1)}, bf16[768,512]{1,0:T(8,128)(2,1)S(1)}, f32[4,128,128]{2,1,0:T(8,128)S(1)}, bf16[3,4,128,128]{3,2,1,0:T(8,128)(2,1)S(1)}) custom-call(bf16[768,1024]{1,0:T(8,128)(2,1)} %k_hbm.3, bf16[768,1024]{1,0:T(8,128)(2,1)} %v_hbm.3), custom_call_target="tpu_custom_call" | custom-call | flops 100663296 | bytes 3145728 | tf_op jit(solution)/shard_map/pallas_call | solution.py:50
  3.1 1.9 %shard_map.76 = (bf16[768,512]{1,0:T(8,128)(2,1)S(1)}, bf16[768,512]{1,0:T(8,128)(2,1)S(1)}, f32[4,128,128]{2,1,0:T(8,128)S(1)}, bf16[3,4,128,128]{3,2,1,0:T(8,128)(2,1)S(1)}) custom-call(bf16[768,1024]{1,0:T(8,128)(2,1)} %k_hbm.3, bf16[768,1024]{1,0:T(8,128)(2,1)} %v_hbm.3), custom_call_target="tpu_custom_call" | custom-call | flops 100663296 | bytes 3145728 | tf_op jit(solution)/shard_map/pallas_call | solution.py:50
  5.1 2.6 %collective-permute-start.1 = (f32[4,128,128]{2,1,0:T(8,128)S(1)}, f32[4,128,128]{2,1,0:T(8,128)S(1)}, u32[]{:S(2)}, u32[]{:S(2)}) collective-permute-start(f32[4,128,128]{2,1,0:T(8,128)S(1)} %shard_map.78.after_ref), channel_id=1, source_target_pairs={{0,8},{4,20},{8,0},{12,28},{16,24},{20,4},{24,16},{28,12},{1,9},{5... | collective-permute-start | bytes 786440 | tf_op jit(solution)/shard_map/ppermute | solution.py:321
  7.7 3.3 %shard_map.79 = (bf16[768,512]{1,0:T(8,128)(2,1)S(1)}, f32[768,512]{1,0:T(8,128)S(1)}, f32[768,512]{1,0:T(8,128)S(1)}, bf16[512,768]{1,0:T(8,128)(2,1)S(1)}, bf16[4,768,256]{2,1,0:T(8,128)(2,1)S(1)}) custom-call(bf16[768,1024]{1,0:T(8,128)(2,1)} %q_hbm.3, bf16[768,1024]{1,0:T(8,128)(2,1)} %og_hbm.3, bf16[768,512]{1,0:T(8,128)(2,1)S(1)} %get-tuple-element.48.k_ref.refs_0_, ...), custom_call_target="tpu_custom_call" | custom-call | flops 603979776 | bytes 5378048 | tf_op jit(solution)/shard_map/pallas_call | solution.py:50
  11.0 1.0 %collective-permute-done.1.refs_2_ = f32[4,128,128]{2,1,0:T(8,128)S(1)} collective-permute-done((f32[4,128,128]{2,1,0:T(8,128)S(1)}, f32[4,128,128]{2,1,0:T(8,128)S(1)}, u32[]{:S(2)}, u32[]{:S(2)}) %collective-permute-start.1) | collective-permute-done | bytes 262176 | tf_op jit(solution)/shard_map/ppermute | solution.py:321
  12.1 2.1 %collective-permute-start.2 = (f32[4,128,128]{2,1,0:T(8,128)S(1)}, f32[4,128,128]{2,1,0:T(8,128)S(1)}, u32[]{:S(2)}, u32[]{:S(2)}) collective-permute-start(f32[4,128,128]{2,1,0:T(8,128)S(1)} %shard_map.80.after_ref), channel_id=1, source_target_pairs={{0,16},{4,12},{8,24},{12,4},{16,0},{20,28},{24,8},{28,20},{1,17},{... | collective-permute-start | bytes 786440 | tf_op jit(solution)/shard_map/ppermute | solution.py:321
  14.2 3.3 %shard_map.81 = (bf16[768,512]{1,0:T(8,128)(2,1)S(1)}, f32[768,512]{1,0:T(8,128)S(1)}, f32[768,512]{1,0:T(8,128)S(1)}, bf16[512,768]{1,0:T(8,128)(2,1)S(1)}, bf16[4,768,256]{2,1,0:T(8,128)(2,1)S(1)}) custom-call(bf16[768,1024]{1,0:T(8,128)(2,1)} %q_hbm.3, bf16[768,1024]{1,0:T(8,128)(2,1)} %og_hbm.3, bf16[768,512]{1,0:T(8,128)(2,1)S(1)} %get-tuple-element.54.k_ref.refs_0_, ...), custom_call_target="tpu_custom_call" | custom-call | flops 603979776 | bytes 5378048 | tf_op jit(solution)/shard_map/pallas_call | solution.py:50
  17.5 1.0 %collective-permute-done.2.refs_3_ = f32[4,128,128]{2,1,0:T(8,128)S(1)} collective-permute-done((f32[4,128,128]{2,1,0:T(8,128)S(1)}, f32[4,128,128]{2,1,0:T(8,128)S(1)}, u32[]{:S(2)}, u32[]{:S(2)}) %collective-permute-start.2) | collective-permute-done | bytes 262176 | tf_op jit(solution)/shard_map/ppermute | solution.py:321
  19.2 1.1 %collective-permute-done.3.state_ref = f32[4,128,128]{2,1,0:T(8,128)S(1)} collective-permute-done((f32[4,128,128]{2,1,0:T(8,128)S(1)}, f32[4,128,128]{2,1,0:T(8,128)S(1)}, u32[]{:S(2)}, u32[]{:S(2)}) %collective-permute-start.3) | collective-permute-done | bytes 262176 | tf_op jit(solution)/shard_map/ppermute | solution.py:321
  20.3 0.6 %shard_map.84 = (f32[768,512]{1,0:T(8,128)S(1)}, f32[8,768]{1,0:T(8,128)S(1)}) custom-call(bf16[768,512]{1,0:T(8,128)(2,1)S(1)} %get-tuple-element.58.q_ref, f32[768,512]{1,0:T(8,128)S(1)} %get-tuple-element.59.inner_ref, f32[768,512]{1,0:T(8,128)S(1)} %get-tuple-element.60.scaled_ref.refs_3_, f32[4,128,128]{2,1,0:T(8,128)S(1)} %collective-permute-done.3.state_ref, ...), custom_call_target="tpu_custom_call" | custom-call | flops 100663296 | bytes 4980736 | tf_op jit(solution)/shard_map/pallas_call | solution.py:50
  20.9 4.2 %collective-permute-start.6 = (f32[8,768]{1,0:T(8,128)S(1)}, f32[8,768]{1,0:T(8,128)S(1)}, u32[]{:S(2)}, u32[]{:S(2)}) collective-permute-start(f32[8,768]{1,0:T(8,128)S(1)} %get-tuple-element.68.refs_0_), channel_id=1, source_target_pairs={{0,3},{1,0},{2,1},{3,2},{4,7},{5,4},{6,5},{7,6},{8,11},{9,8},{10,9... | collective-permute-start | bytes 73736 | tf_op jit(solution)/shard_map/ppermute | solution.py:386
  25.1 1.0 %collective-permute-start.4 = (f32[8,768]{1,0:T(8,128)S(1)}, f32[8,768]{1,0:T(8,128)S(1)}, u32[]{:S(2)}, u32[]{:S(2)}) collective-permute-start(f32[8,768]{1,0:T(8,128)S(1)} %get-tuple-element.68.refs_0_), channel_id=1, source_target_pairs={{0,1},{1,2},{2,3},{3,0},{4,5},{5,6},{6,7},{7,4},{8,9},{9,10},{10,1... | collective-permute-start | bytes 73736 | tf_op jit(solution)/shard_map/ppermute | solution.py:386
  26.6 3.3 %collective-permute-done.5.refs_2_ = f32[8,768]{1,0:T(8,128)S(1)} collective-permute-done((f32[8,768]{1,0:T(8,128)S(1)}, f32[8,768]{1,0:T(8,128)S(1)}, u32[]{:S(2)}, u32[]{:S(2)}) %collective-permute-start.5) | collective-permute-done | bytes 24608 | tf_op jit(solution)/shard_map/ppermute | solution.py:386
  29.8 0.9 %collective-permute-done.4.refs_1_ = f32[8,768]{1,0:T(8,128)S(1)} collective-permute-done((f32[8,768]{1,0:T(8,128)S(1)}, f32[8,768]{1,0:T(8,128)S(1)}, u32[]{:S(2)}, u32[]{:S(2)}) %collective-permute-start.4) | collective-permute-done | bytes 24608 | tf_op jit(solution)/shard_map/ppermute | solution.py:386
  30.7 0.9 %shard_map.85 = (bf16[768,512]{1,0:T(8,128)(2,1)S(1)}, f32[4,128,128]{2,1,0:T(8,128)S(1)}, bf16[3,4,128,128]{3,2,1,0:T(8,128)(2,1)S(1)}, f32[768,128]{1,0:T(8,128)S(1)}, f32[768,128]{1,0:T(8,128)S(1)}) custom-call(f32[8,768]{1,0:T(8,128)S(1)} %get-tuple-element.68.refs_0_, f32[8,768]{1,0:T(8,128)S(1)} %collective-permute-done.4.refs_1_, ...), custom_call_target="tpu_custom_call" | custom-call | flops 100663296 | bytes 4030464 | tf_op jit(solution)/shard_map/pallas_call | solution.py:50
  32.2 1.0 %collective-permute-done.7.refs_1_ = f32[4,128,128]{2,1,0:T(8,128)S(1)} collective-permute-done((f32[4,128,128]{2,1,0:T(8,128)S(1)}, f32[4,128,128]{2,1,0:T(8,128)S(1)}, u32[]{:S(2)}, u32[]{:S(2)}) %collective-permute-start.7) | collective-permute-done | bytes 262176 | tf_op jit(solution)/shard_map/ppermute | solution.py:321
  33.2 1.6 %collective-permute-start.8 = (f32[4,128,128]{2,1,0:T(8,128)S(1)}, f32[4,128,128]{2,1,0:T(8,128)S(1)}, u32[]{:S(2)}, u32[]{:S(2)}) collective-permute-start(f32[4,128,128]{2,1,0:T(8,128)S(1)} %shard_map.87.refs_0_), channel_id=1, source_target_pairs={{28,20},{24,8},{20,28},{16,0},{12,4},{8,24},{4,12},{0,16},{29,21},... | collective-permute-start | bytes 786440 | tf_op jit(solution)/shard_map/ppermute | solution.py:321
  34.8 4.0 %shard_map.88 = (bf16[768,1024]{1,0:T(8,128)(2,1)}, f32[768,512]{1,0:T(8,128)S(1)}, f32[768,512]{1,0:T(8,128)S(1)}) custom-call(bf16[768,512]{1,0:T(8,128)(2,1)S(1)} %get-tuple-element.58.q_ref, bf16[768,512]{1,0:T(8,128)(2,1)S(1)} %get-tuple-element.54.k_ref.refs_0_, bf16[768,512]{1,0:T(8,128)(2,1)S(1)} %get-tuple-element.55.v_ref.refs_1_, ...), custom_call_target="tpu_custom_call" | custom-call | flops 905969664 | bytes 6029312 | tf_op jit(solution)/shard_map/pallas_call | solution.py:50
  38.8 0.9 %collective-permute-done.8.refs_2_ = f32[4,128,128]{2,1,0:T(8,128)S(1)} collective-permute-done((f32[4,128,128]{2,1,0:T(8,128)S(1)}, f32[4,128,128]{2,1,0:T(8,128)S(1)}, u32[]{:S(2)}, u32[]{:S(2)}) %collective-permute-start.8) | collective-permute-done | bytes 262176 | tf_op jit(solution)/shard_map/ppermute | solution.py:321
  39.7 1.6 %collective-permute-start.9 = (f32[4,128,128]{2,1,0:T(8,128)S(1)}, f32[4,128,128]{2,1,0:T(8,128)S(1)}, u32[]{:S(2)}, u32[]{:S(2)}) collective-permute-start(f32[4,128,128]{2,1,0:T(8,128)S(1)} %shard_map.89.refs_0_), channel_id=1, source_target_pairs={{28,12},{24,16},{20,4},{16,24},{12,28},{8,0},{4,20},{0,8},{29,13},... | collective-permute-start | bytes 786440 | tf_op jit(solution)/shard_map/ppermute | solution.py:321
  41.3 4.0 %shard_map.90 = (bf16[768,1024]{1,0:T(8,128)(2,1)}, f32[768,512]{1,0:T(8,128)S(1)}, f32[768,512]{1,0:T(8,128)S(1)}) custom-call(bf16[768,512]{1,0:T(8,128)(2,1)S(1)} %get-tuple-element.53.q_ref, bf16[768,512]{1,0:T(8,128)(2,1)S(1)} %get-tuple-element.48.k_ref.refs_0_, ...), custom_call_target="tpu_custom_call", output_to_operand_aliasing={{0}: (9, {})} | custom-call | flops 905969664 | bytes 7602176 | tf_op jit(solution)/shard_map/pallas_call | solution.py:50
  45.3 0.9 %collective-permute-done.9.refs_3_ = f32[4,128,128]{2,1,0:T(8,128)S(1)} collective-permute-done((f32[4,128,128]{2,1,0:T(8,128)S(1)}, f32[4,128,128]{2,1,0:T(8,128)S(1)}, u32[]{:S(2)}, u32[]{:S(2)}) %collective-permute-start.9) | collective-permute-done | bytes 262176 | tf_op jit(solution)/shard_map/ppermute | solution.py:321
  46.9 0.9 %collective-permute-done.10.refs_4_ = f32[4,128,128]{2,1,0:T(8,128)S(1)} collective-permute-done((f32[4,128,128]{2,1,0:T(8,128)S(1)}, f32[4,128,128]{2,1,0:T(8,128)S(1)}, u32[]{:S(2)}, u32[]{:S(2)}) %collective-permute-start.10) | collective-permute-done | bytes 262176 | tf_op jit(solution)/shard_map/ppermute | solution.py:321
  47.9 1.7 %shard_map.93 = (bf16[768,1024]{1,0:T(8,128)(2,1)}, bf16[768,1024]{1,0:T(8,128)(2,1)}) custom-call(bf16[768,512]{1,0:T(8,128)(2,1)S(1)} %get-tuple-element.48.k_ref.refs_0_, bf16[768,512]{1,0:T(8,128)(2,1)S(1)} %get-tuple-element.49.v_ref.refs_1_, f32[768,512]{1,0:T(8,128)S(1)} %get-tuple-element.84.refs_2_, ...), custom_call_target="tpu_custom_call" | custom-call | flops 201326592 | bytes 6553600 | tf_op jit(solution)/shard_map/pallas_call | solution.py:50
  (18 shorter events, 3.2 us)
Async XLA Ops:
  2.6 5.1 %copy-start = (f32[1024]{0:T(1024)S(1)}, f32[1024]{0:T(1024)}, u32[]{:S(2)}) copy-start(f32[1024]{0:T(1024)} %param.9) | copy-start | bytes 12292
  2.6 2.4 %collective-permute-start = (f32[4,128,128]{2,1,0:T(8,128)S(1)}, f32[4,128,128]{2,1,0:T(8,128)S(1)}, u32[]{:S(2)}, u32[]{:S(2)}) collective-permute-start(f32[4,128,128]{2,1,0:T(8,128)S(1)} %get-tuple-element.52), channel_id=1, source_target_pairs={{0,4},{4,0},{8,12},{12,8},{16,20},{20,16},{24,28},{28,24},{1,5},{5... | collective-permute-start | bytes 786440 | tf_op jit(solution)/shard_map/ppermute | solution.py:321
  5.1 6.9 %collective-permute-start.1 = (f32[4,128,128]{2,1,0:T(8,128)S(1)}, f32[4,128,128]{2,1,0:T(8,128)S(1)}, u32[]{:S(2)}, u32[]{:S(2)}) collective-permute-start(f32[4,128,128]{2,1,0:T(8,128)S(1)} %shard_map.78.after_ref), channel_id=1, source_target_pairs={{0,8},{4,20},{8,0},{12,28},{16,24},{20,4},{24,16},{28,12},{1,9},{5... | collective-permute-start | bytes 786440 | tf_op jit(solution)/shard_map/ppermute | solution.py:321
  12.1 6.5 %collective-permute-start.2 = (f32[4,128,128]{2,1,0:T(8,128)S(1)}, f32[4,128,128]{2,1,0:T(8,128)S(1)}, u32[]{:S(2)}, u32[]{:S(2)}) collective-permute-start(f32[4,128,128]{2,1,0:T(8,128)S(1)} %shard_map.80.after_ref), channel_id=1, source_target_pairs={{0,16},{4,12},{8,24},{12,4},{16,0},{20,28},{24,8},{28,20},{1,17},{... | collective-permute-start | bytes 786440 | tf_op jit(solution)/shard_map/ppermute | solution.py:321
  18.7 1.6 %collective-permute-start.3 = (f32[4,128,128]{2,1,0:T(8,128)S(1)}, f32[4,128,128]{2,1,0:T(8,128)S(1)}, u32[]{:S(2)}, u32[]{:S(2)}) collective-permute-start(f32[4,128,128]{2,1,0:T(8,128)S(1)} %get-tuple-element.62), channel_id=1, source_target_pairs={{0,4},{4,0},{8,12},{12,8},{16,20},{20,16},{24,28},{28,24},{1,5},{5... | collective-permute-start | bytes 786440 | tf_op jit(solution)/shard_map/ppermute | solution.py:321
  20.9 5.7 %collective-permute-start.6 = (f32[8,768]{1,0:T(8,128)S(1)}, f32[8,768]{1,0:T(8,128)S(1)}, u32[]{:S(2)}, u32[]{:S(2)}) collective-permute-start(f32[8,768]{1,0:T(8,128)S(1)} %get-tuple-element.68.refs_0_), channel_id=1, source_target_pairs={{0,3},{1,0},{2,1},{3,2},{4,7},{5,4},{6,5},{7,6},{8,11},{9,8},{10,9... | collective-permute-start | bytes 73736 | tf_op jit(solution)/shard_map/ppermute | solution.py:386
  25.1 4.8 %collective-permute-start.5 = (f32[8,768]{1,0:T(8,128)S(1)}, f32[8,768]{1,0:T(8,128)S(1)}, u32[]{:S(2)}, u32[]{:S(2)}) collective-permute-start(f32[8,768]{1,0:T(8,128)S(1)} %get-tuple-element.68.refs_0_), channel_id=1, source_target_pairs={{0,2},{1,3},{2,0},{3,1},{4,6},{5,7},{6,4},{7,5},{8,10},{9,11},{10,... | collective-permute-start | bytes 73736 | tf_op jit(solution)/shard_map/ppermute | solution.py:386
  25.1 5.6 %collective-permute-start.4 = (f32[8,768]{1,0:T(8,128)S(1)}, f32[8,768]{1,0:T(8,128)S(1)}, u32[]{:S(2)}, u32[]{:S(2)}) collective-permute-start(f32[8,768]{1,0:T(8,128)S(1)} %get-tuple-element.68.refs_0_), channel_id=1, source_target_pairs={{0,1},{1,2},{2,3},{3,0},{4,5},{5,6},{6,7},{7,4},{8,9},{9,10},{10,1... | collective-permute-start | bytes 73736 | tf_op jit(solution)/shard_map/ppermute | solution.py:386
  31.6 1.6 %collective-permute-start.7 = (f32[4,128,128]{2,1,0:T(8,128)S(1)}, f32[4,128,128]{2,1,0:T(8,128)S(1)}, u32[]{:S(2)}, u32[]{:S(2)}) collective-permute-start(f32[4,128,128]{2,1,0:T(8,128)S(1)} %get-tuple-element.78), channel_id=1, source_target_pairs={{28,24},{24,28},{20,16},{16,20},{12,8},{8,12},{4,0},{0,4},{29,25},... | collective-permute-start | bytes 786440 | tf_op jit(solution)/shard_map/ppermute | solution.py:321
  33.2 6.4 %collective-permute-start.8 = (f32[4,128,128]{2,1,0:T(8,128)S(1)}, f32[4,128,128]{2,1,0:T(8,128)S(1)}, u32[]{:S(2)}, u32[]{:S(2)}) collective-permute-start(f32[4,128,128]{2,1,0:T(8,128)S(1)} %shard_map.87.refs_0_), channel_id=1, source_target_pairs={{28,20},{24,8},{20,28},{16,0},{12,4},{8,24},{4,12},{0,16},{29,21},... | collective-permute-start | bytes 786440 | tf_op jit(solution)/shard_map/ppermute | solution.py:321
  39.7 6.4 %collective-permute-start.9 = (f32[4,128,128]{2,1,0:T(8,128)S(1)}, f32[4,128,128]{2,1,0:T(8,128)S(1)}, u32[]{:S(2)}, u32[]{:S(2)}) collective-permute-start(f32[4,128,128]{2,1,0:T(8,128)S(1)} %shard_map.89.refs_0_), channel_id=1, source_target_pairs={{28,12},{24,16},{20,4},{16,24},{12,28},{8,0},{4,20},{0,8},{29,13},... | collective-permute-start | bytes 786440 | tf_op jit(solution)/shard_map/ppermute | solution.py:321
  46.3 1.6 %collective-permute-start.10 = (f32[4,128,128]{2,1,0:T(8,128)S(1)}, f32[4,128,128]{2,1,0:T(8,128)S(1)}, u32[]{:S(2)}, u32[]{:S(2)}) collective-permute-start(f32[4,128,128]{2,1,0:T(8,128)S(1)} %get-tuple-element.86), channel_id=1, source_target_pairs={{28,24},{24,28},{20,16},{16,20},{12,8},{8,12},{4,0},{0,4},{29,25},... | collective-permute-start | bytes 786440 | tf_op jit(solution)/shard_map/ppermute | solution.py:321

commit v4 on v3

--- a/solution.py
+++ b/solution.py
@@ -383,8 +383,8 @@
         (q1, inner1, scaled1, state1, square, cross),
     )
     parts = [sums] + [
-        lax.ppermute(sums, "head", [(r, (r + shift) % peers) for r in range(peers)])
-        for shift in range(1, peers)
+        lax.ppermute(sums, "head", [(r, r ^ other) for r in range(peers)])
+        for other in range(1, peers)
     ]
 
     g2, gsend, post2, inv, slope = run(

time: 50 us -> 49.1 us (0.982)
  waiting for transfers between devices: 11.5 us -> 10.8 us
    ppermute x3, waiting for transfers between devices: 4.61 us -> 4.08 us  [shards(): lax.ppermute(sums, 'head', [(r, r ^ other) for r in range(peers)])]
  transfers between devices with their start and end apart: 11 -> 11, of which waited for: 10 -> 9; matrix products, arithmetic and copies ran while one was open for 0% -> 0% of each run, Pallas kernels for 36% -> 37%
where the time goes in v4:
time: 49.1 us; the launch traced here: 48.9 us
  Pallas kernels  23.8 us (48%)
  starting transfers between devices  13.4 us (27%)
  waiting for transfers between devices  10.8 us (22%)
  between operations  0.94 us (2%)
    pallas_call x18, Pallas kernels, run(): pl.pallas_call(kernel, in_specs=in_specs, out_specs=out_specs, out_shape=...  23.8 us
    ppermute x8, starting transfers between devices, move(): return lax.ppermute(value, 'seq', pairs)  8.56 us
    ppermute x8, waiting for transfers between devices, move(): return lax.ppermute(value, 'seq', pairs)  6.68 us
    ppermute x3, starting transfers between devices, shards(): lax.ppermute(sums, 'head', [(r, r ^ other) for r in range(peers)])  4.81 us
    ppermute x3, waiting for transfers between devices, shards(): lax.ppermute(sums, 'head', [(r, r ^ other) for r in range(peers)])  4.08 us
  transfers between devices with their start and end apart: 11, of which 9 were waited for; matrix products, arithmetic and copies ran while one was open for 0% of the time, Pallas kernels for 37%

profile of v4, /device:TPU:0, one launch (start us, length us, event | category | flops | bytes accessed | tf_op | source)
XLA Modules:
  0.0 48.9 jit_solution(3623587999949255130)
XLA Ops:
  0.6 1.9 %shard_map.77 = (bf16[768,512]{1,0:T(8,128)(2,1)S(1)}, bf16[768,512]{1,0:T(8,128)(2,1)S(1)}, f32[4,128,128]{2,1,0:T(8,128)S(1)}, bf16[3,4,128,128]{3,2,1,0:T(8,128)(2,1)S(1)}) custom-call(bf16[768,1024]{1,0:T(8,128)(2,1)} %k_hbm.3, bf16[768,1024]{1,0:T(8,128)(2,1)} %v_hbm.3), custom_call_target="tpu_custom_call" | custom-call | flops 100663296 | bytes 3145728 | tf_op jit(solution)/shard_map/pallas_call | solution.py:50
  3.1 1.9 %shard_map.76 = (bf16[768,512]{1,0:T(8,128)(2,1)S(1)}, bf16[768,512]{1,0:T(8,128)(2,1)S(1)}, f32[4,128,128]{2,1,0:T(8,128)S(1)}, bf16[3,4,128,128]{3,2,1,0:T(8,128)(2,1)S(1)}) custom-call(bf16[768,1024]{1,0:T(8,128)(2,1)} %k_hbm.3, bf16[768,1024]{1,0:T(8,128)(2,1)} %v_hbm.3), custom_call_target="tpu_custom_call" | custom-call | flops 100663296 | bytes 3145728 | tf_op jit(solution)/shard_map/pallas_call | solution.py:50
  5.1 2.6 %collective-permute-start.1 = (f32[4,128,128]{2,1,0:T(8,128)S(1)}, f32[4,128,128]{2,1,0:T(8,128)S(1)}, u32[]{:S(2)}, u32[]{:S(2)}) collective-permute-start(f32[4,128,128]{2,1,0:T(8,128)S(1)} %shard_map.78.after_ref), channel_id=1, source_target_pairs={{0,8},{4,20},{8,0},{12,28},{16,24},{20,4},{24,16},{28,12},{1,9},{5... | collective-permute-start | bytes 786440 | tf_op jit(solution)/shard_map/ppermute | solution.py:321
  7.7 3.3 %shard_map.79 = (bf16[768,512]{1,0:T(8,128)(2,1)S(1)}, f32[768,512]{1,0:T(8,128)S(1)}, f32[768,512]{1,0:T(8,128)S(1)}, bf16[512,768]{1,0:T(8,128)(2,1)S(1)}, bf16[4,768,256]{2,1,0:T(8,128)(2,1)S(1)}) custom-call(bf16[768,1024]{1,0:T(8,128)(2,1)} %q_hbm.3, bf16[768,1024]{1,0:T(8,128)(2,1)} %og_hbm.3, bf16[768,512]{1,0:T(8,128)(2,1)S(1)} %get-tuple-element.48.k_ref.refs_0_, ...), custom_call_target="tpu_custom_call" | custom-call | flops 603979776 | bytes 5378048 | tf_op jit(solution)/shard_map/pallas_call | solution.py:50
  11.0 1.0 %collective-permute-done.1.refs_2_ = f32[4,128,128]{2,1,0:T(8,128)S(1)} collective-permute-done((f32[4,128,128]{2,1,0:T(8,128)S(1)}, f32[4,128,128]{2,1,0:T(8,128)S(1)}, u32[]{:S(2)}, u32[]{:S(2)}) %collective-permute-start.1) | collective-permute-done | bytes 262176 | tf_op jit(solution)/shard_map/ppermute | solution.py:321
  12.1 2.1 %collective-permute-start.2 = (f32[4,128,128]{2,1,0:T(8,128)S(1)}, f32[4,128,128]{2,1,0:T(8,128)S(1)}, u32[]{:S(2)}, u32[]{:S(2)}) collective-permute-start(f32[4,128,128]{2,1,0:T(8,128)S(1)} %shard_map.80.after_ref), channel_id=1, source_target_pairs={{0,16},{4,12},{8,24},{12,4},{16,0},{20,28},{24,8},{28,20},{1,17},{... | collective-permute-start | bytes 786440 | tf_op jit(solution)/shard_map/ppermute | solution.py:321
  14.2 3.3 %shard_map.81 = (bf16[768,512]{1,0:T(8,128)(2,1)S(1)}, f32[768,512]{1,0:T(8,128)S(1)}, f32[768,512]{1,0:T(8,128)S(1)}, bf16[512,768]{1,0:T(8,128)(2,1)S(1)}, bf16[4,768,256]{2,1,0:T(8,128)(2,1)S(1)}) custom-call(bf16[768,1024]{1,0:T(8,128)(2,1)} %q_hbm.3, bf16[768,1024]{1,0:T(8,128)(2,1)} %og_hbm.3, bf16[768,512]{1,0:T(8,128)(2,1)S(1)} %get-tuple-element.54.k_ref.refs_0_, ...), custom_call_target="tpu_custom_call" | custom-call | flops 603979776 | bytes 5378048 | tf_op jit(solution)/shard_map/pallas_call | solution.py:50
  17.5 1.0 %collective-permute-done.2.refs_3_ = f32[4,128,128]{2,1,0:T(8,128)S(1)} collective-permute-done((f32[4,128,128]{2,1,0:T(8,128)S(1)}, f32[4,128,128]{2,1,0:T(8,128)S(1)}, u32[]{:S(2)}, u32[]{:S(2)}) %collective-permute-start.2) | collective-permute-done | bytes 262176 | tf_op jit(solution)/shard_map/ppermute | solution.py:321
  19.2 1.1 %collective-permute-done.3.state_ref = f32[4,128,128]{2,1,0:T(8,128)S(1)} collective-permute-done((f32[4,128,128]{2,1,0:T(8,128)S(1)}, f32[4,128,128]{2,1,0:T(8,128)S(1)}, u32[]{:S(2)}, u32[]{:S(2)}) %collective-permute-start.3) | collective-permute-done | bytes 262176 | tf_op jit(solution)/shard_map/ppermute | solution.py:321
  20.3 0.6 %shard_map.84 = (f32[768,512]{1,0:T(8,128)S(1)}, f32[8,768]{1,0:T(8,128)S(1)}) custom-call(bf16[768,512]{1,0:T(8,128)(2,1)S(1)} %get-tuple-element.58.q_ref, f32[768,512]{1,0:T(8,128)S(1)} %get-tuple-element.59.inner_ref, f32[768,512]{1,0:T(8,128)S(1)} %get-tuple-element.60.scaled_ref.refs_3_, f32[4,128,128]{2,1,0:T(8,128)S(1)} %collective-permute-done.3.state_ref, ...), custom_call_target="tpu_custom_call" | custom-call | flops 100663296 | bytes 4980736 | tf_op jit(solution)/shard_map/pallas_call | solution.py:50
  20.9 4.2 %collective-permute-start.6 = (f32[8,768]{1,0:T(8,128)S(1)}, f32[8,768]{1,0:T(8,128)S(1)}, u32[]{:S(2)}, u32[]{:S(2)}) collective-permute-start(f32[8,768]{1,0:T(8,128)S(1)} %get-tuple-element.68.refs_0_), channel_id=1, source_target_pairs={{0,3},{1,2},{2,1},{3,0},{4,7},{5,6},{6,5},{7,4},{8,11},{9,10},{10,... | collective-permute-start | bytes 73736 | tf_op jit(solution)/shard_map/ppermute | solution.py:386
  25.1 0.6 %collective-permute-start.4 = (f32[8,768]{1,0:T(8,128)S(1)}, f32[8,768]{1,0:T(8,128)S(1)}, u32[]{:S(2)}, u32[]{:S(2)}) collective-permute-start(f32[8,768]{1,0:T(8,128)S(1)} %get-tuple-element.68.refs_0_), channel_id=1, source_target_pairs={{0,1},{1,0},{2,3},{3,2},{4,5},{5,4},{6,7},{7,6},{8,9},{9,8},{10,11... | collective-permute-start | bytes 73736 | tf_op jit(solution)/shard_map/ppermute | solution.py:386
  25.7 1.2 %collective-permute-done.6.refs_3_ = f32[8,768]{1,0:T(8,128)S(1)} collective-permute-done((f32[8,768]{1,0:T(8,128)S(1)}, f32[8,768]{1,0:T(8,128)S(1)}, u32[]{:S(2)}, u32[]{:S(2)}) %collective-permute-start.6) | collective-permute-done | bytes 24608 | tf_op jit(solution)/shard_map/ppermute | solution.py:386
  26.9 2.9 %collective-permute-done.5.refs_2_ = f32[8,768]{1,0:T(8,128)S(1)} collective-permute-done((f32[8,768]{1,0:T(8,128)S(1)}, f32[8,768]{1,0:T(8,128)S(1)}, u32[]{:S(2)}, u32[]{:S(2)}) %collective-permute-start.5) | collective-permute-done | bytes 24608 | tf_op jit(solution)/shard_map/ppermute | solution.py:386
  29.8 0.9 %shard_map.85 = (bf16[768,512]{1,0:T(8,128)(2,1)S(1)}, f32[4,128,128]{2,1,0:T(8,128)S(1)}, bf16[3,4,128,128]{3,2,1,0:T(8,128)(2,1)S(1)}, f32[768,128]{1,0:T(8,128)S(1)}, f32[768,128]{1,0:T(8,128)S(1)}) custom-call(f32[8,768]{1,0:T(8,128)S(1)} %get-tuple-element.68.refs_0_, f32[8,768]{1,0:T(8,128)S(1)} %collective-permute-done.4.refs_1_, ...), custom_call_target="tpu_custom_call" | custom-call | flops 100663296 | bytes 4030464 | tf_op jit(solution)/shard_map/pallas_call | solution.py:50
  31.3 1.0 %collective-permute-done.7.refs_1_ = f32[4,128,128]{2,1,0:T(8,128)S(1)} collective-permute-done((f32[4,128,128]{2,1,0:T(8,128)S(1)}, f32[4,128,128]{2,1,0:T(8,128)S(1)}, u32[]{:S(2)}, u32[]{:S(2)}) %collective-permute-start.7) | collective-permute-done | bytes 262176 | tf_op jit(solution)/shard_map/ppermute | solution.py:321
  32.3 1.6 %collective-permute-start.8 = (f32[4,128,128]{2,1,0:T(8,128)S(1)}, f32[4,128,128]{2,1,0:T(8,128)S(1)}, u32[]{:S(2)}, u32[]{:S(2)}) collective-permute-start(f32[4,128,128]{2,1,0:T(8,128)S(1)} %shard_map.87.refs_0_), channel_id=1, source_target_pairs={{28,20},{24,8},{20,28},{16,0},{12,4},{8,24},{4,12},{0,16},{29,21},... | collective-permute-start | bytes 786440 | tf_op jit(solution)/shard_map/ppermute | solution.py:321
  33.9 4.0 %shard_map.88 = (bf16[768,1024]{1,0:T(8,128)(2,1)}, f32[768,512]{1,0:T(8,128)S(1)}, f32[768,512]{1,0:T(8,128)S(1)}) custom-call(bf16[768,512]{1,0:T(8,128)(2,1)S(1)} %get-tuple-element.58.q_ref, bf16[768,512]{1,0:T(8,128)(2,1)S(1)} %get-tuple-element.54.k_ref.refs_0_, bf16[768,512]{1,0:T(8,128)(2,1)S(1)} %get-tuple-element.55.v_ref.refs_1_, ...), custom_call_target="tpu_custom_call" | custom-call | flops 905969664 | bytes 6029312 | tf_op jit(solution)/shard_map/pallas_call | solution.py:50
  37.9 0.9 %collective-permute-done.8.refs_2_ = f32[4,128,128]{2,1,0:T(8,128)S(1)} collective-permute-done((f32[4,128,128]{2,1,0:T(8,128)S(1)}, f32[4,128,128]{2,1,0:T(8,128)S(1)}, u32[]{:S(2)}, u32[]{:S(2)}) %collective-permute-start.8) | collective-permute-done | bytes 262176 | tf_op jit(solution)/shard_map/ppermute | solution.py:321
  38.9 1.6 %collective-permute-start.9 = (f32[4,128,128]{2,1,0:T(8,128)S(1)}, f32[4,128,128]{2,1,0:T(8,128)S(1)}, u32[]{:S(2)}, u32[]{:S(2)}) collective-permute-start(f32[4,128,128]{2,1,0:T(8,128)S(1)} %shard_map.89.refs_0_), channel_id=1, source_target_pairs={{28,12},{24,16},{20,4},{16,24},{12,28},{8,0},{4,20},{0,8},{29,13},... | collective-permute-start | bytes 786440 | tf_op jit(solution)/shard_map/ppermute | solution.py:321
  40.4 4.2 %shard_map.90 = (bf16[768,1024]{1,0:T(8,128)(2,1)}, f32[768,512]{1,0:T(8,128)S(1)}, f32[768,512]{1,0:T(8,128)S(1)}) custom-call(bf16[768,512]{1,0:T(8,128)(2,1)S(1)} %get-tuple-element.53.q_ref, bf16[768,512]{1,0:T(8,128)(2,1)S(1)} %get-tuple-element.48.k_ref.refs_0_, ...), custom_call_target="tpu_custom_call", output_to_operand_aliasing={{0}: (9, {})} | custom-call | flops 905969664 | bytes 7602176 | tf_op jit(solution)/shard_map/pallas_call | solution.py:50
  44.6 0.7 %collective-permute-done.9.refs_3_ = f32[4,128,128]{2,1,0:T(8,128)S(1)} collective-permute-done((f32[4,128,128]{2,1,0:T(8,128)S(1)}, f32[4,128,128]{2,1,0:T(8,128)S(1)}, u32[]{:S(2)}, u32[]{:S(2)}) %collective-permute-start.9) | collective-permute-done | bytes 262176 | tf_op jit(solution)/shard_map/ppermute | solution.py:321
  46.0 0.9 %collective-permute-done.10.refs_4_ = f32[4,128,128]{2,1,0:T(8,128)S(1)} collective-permute-done((f32[4,128,128]{2,1,0:T(8,128)S(1)}, f32[4,128,128]{2,1,0:T(8,128)S(1)}, u32[]{:S(2)}, u32[]{:S(2)}) %collective-permute-start.10) | collective-permute-done | bytes 262176 | tf_op jit(solution)/shard_map/ppermute | solution.py:321
  47.0 1.7 %shard_map.93 = (bf16[768,1024]{1,0:T(8,128)(2,1)}, bf16[768,1024]{1,0:T(8,128)(2,1)}) custom-call(bf16[768,512]{1,0:T(8,128)(2,1)S(1)} %get-tuple-element.48.k_ref.refs_0_, bf16[768,512]{1,0:T(8,128)(2,1)S(1)} %get-tuple-element.49.v_ref.refs_1_, f32[768,512]{1,0:T(8,128)S(1)} %get-tuple-element.84.refs_2_, ...), custom_call_target="tpu_custom_call" | custom-call | flops 201326592 | bytes 6553600 | tf_op jit(solution)/shard_map/pallas_call | solution.py:50
  (18 shorter events, 2.7 us)
Async XLA Ops:
  2.6 5.1 %copy-start = (f32[1024]{0:T(1024)S(1)}, f32[1024]{0:T(1024)}, u32[]{:S(2)}) copy-start(f32[1024]{0:T(1024)} %param.9) | copy-start | bytes 12292
  2.6 2.4 %collective-permute-start = (f32[4,128,128]{2,1,0:T(8,128)S(1)}, f32[4,128,128]{2,1,0:T(8,128)S(1)}, u32[]{:S(2)}, u32[]{:S(2)}) collective-permute-start(f32[4,128,128]{2,1,0:T(8,128)S(1)} %get-tuple-element.52), channel_id=1, source_target_pairs={{0,4},{4,0},{8,12},{12,8},{16,20},{20,16},{24,28},{28,24},{1,5},{5... | collective-permute-start | bytes 786440 | tf_op jit(solution)/shard_map/ppermute | solution.py:321
  5.1 6.9 %collective-permute-start.1 = (f32[4,128,128]{2,1,0:T(8,128)S(1)}, f32[4,128,128]{2,1,0:T(8,128)S(1)}, u32[]{:S(2)}, u32[]{:S(2)}) collective-permute-start(f32[4,128,128]{2,1,0:T(8,128)S(1)} %shard_map.78.after_ref), channel_id=1, source_target_pairs={{0,8},{4,20},{8,0},{12,28},{16,24},{20,4},{24,16},{28,12},{1,9},{5... | collective-permute-start | bytes 786440 | tf_op jit(solution)/shard_map/ppermute | solution.py:321
  12.1 6.5 %collective-permute-start.2 = (f32[4,128,128]{2,1,0:T(8,128)S(1)}, f32[4,128,128]{2,1,0:T(8,128)S(1)}, u32[]{:S(2)}, u32[]{:S(2)}) collective-permute-start(f32[4,128,128]{2,1,0:T(8,128)S(1)} %shard_map.80.after_ref), channel_id=1, source_target_pairs={{0,16},{4,12},{8,24},{12,4},{16,0},{20,28},{24,8},{28,20},{1,17},{... | collective-permute-start | bytes 786440 | tf_op jit(solution)/shard_map/ppermute | solution.py:321
  18.7 1.6 %collective-permute-start.3 = (f32[4,128,128]{2,1,0:T(8,128)S(1)}, f32[4,128,128]{2,1,0:T(8,128)S(1)}, u32[]{:S(2)}, u32[]{:S(2)}) collective-permute-start(f32[4,128,128]{2,1,0:T(8,128)S(1)} %get-tuple-element.62), channel_id=1, source_target_pairs={{0,4},{4,0},{8,12},{12,8},{16,20},{20,16},{24,28},{28,24},{1,5},{5... | collective-permute-start | bytes 786440 | tf_op jit(solution)/shard_map/ppermute | solution.py:321
  20.9 6.0 %collective-permute-start.6 = (f32[8,768]{1,0:T(8,128)S(1)}, f32[8,768]{1,0:T(8,128)S(1)}, u32[]{:S(2)}, u32[]{:S(2)}) collective-permute-start(f32[8,768]{1,0:T(8,128)S(1)} %get-tuple-element.68.refs_0_), channel_id=1, source_target_pairs={{0,3},{1,2},{2,1},{3,0},{4,7},{5,6},{6,5},{7,4},{8,11},{9,10},{10,... | collective-permute-start | bytes 73736 | tf_op jit(solution)/shard_map/ppermute | solution.py:386
  25.1 4.7 %collective-permute-start.5 = (f32[8,768]{1,0:T(8,128)S(1)}, f32[8,768]{1,0:T(8,128)S(1)}, u32[]{:S(2)}, u32[]{:S(2)}) collective-permute-start(f32[8,768]{1,0:T(8,128)S(1)} %get-tuple-element.68.refs_0_), channel_id=1, source_target_pairs={{0,2},{1,3},{2,0},{3,1},{4,6},{5,7},{6,4},{7,5},{8,10},{9,11},{10,... | collective-permute-start | bytes 73736 | tf_op jit(solution)/shard_map/ppermute | solution.py:386
  25.1 4.7 %collective-permute-start.4 = (f32[8,768]{1,0:T(8,128)S(1)}, f32[8,768]{1,0:T(8,128)S(1)}, u32[]{:S(2)}, u32[]{:S(2)}) collective-permute-start(f32[8,768]{1,0:T(8,128)S(1)} %get-tuple-element.68.refs_0_), channel_id=1, source_target_pairs={{0,1},{1,0},{2,3},{3,2},{4,5},{5,4},{6,7},{7,6},{8,9},{9,8},{10,11... | collective-permute-start | bytes 73736 | tf_op jit(solution)/shard_map/ppermute | solution.py:386
  30.7 1.6 %collective-permute-start.7 = (f32[4,128,128]{2,1,0:T(8,128)S(1)}, f32[4,128,128]{2,1,0:T(8,128)S(1)}, u32[]{:S(2)}, u32[]{:S(2)}) collective-permute-start(f32[4,128,128]{2,1,0:T(8,128)S(1)} %get-tuple-element.78), channel_id=1, source_target_pairs={{28,24},{24,28},{20,16},{16,20},{12,8},{8,12},{4,0},{0,4},{29,25},... | collective-permute-start | bytes 786440 | tf_op jit(solution)/shard_map/ppermute | solution.py:321
  32.3 6.4 %collective-permute-start.8 = (f32[4,128,128]{2,1,0:T(8,128)S(1)}, f32[4,128,128]{2,1,0:T(8,128)S(1)}, u32[]{:S(2)}, u32[]{:S(2)}) collective-permute-start(f32[4,128,128]{2,1,0:T(8,128)S(1)} %shard_map.87.refs_0_), channel_id=1, source_target_pairs={{28,20},{24,8},{20,28},{16,0},{12,4},{8,24},{4,12},{0,16},{29,21},... | collective-permute-start | bytes 786440 | tf_op jit(solution)/shard_map/ppermute | solution.py:321
  38.9 6.4 %collective-permute-start.9 = (f32[4,128,128]{2,1,0:T(8,128)S(1)}, f32[4,128,128]{2,1,0:T(8,128)S(1)}, u32[]{:S(2)}, u32[]{:S(2)}) collective-permute-start(f32[4,128,128]{2,1,0:T(8,128)S(1)} %shard_map.89.refs_0_), channel_id=1, source_target_pairs={{28,12},{24,16},{20,4},{16,24},{12,28},{8,0},{4,20},{0,8},{29,13},... | collective-permute-start | bytes 786440 | tf_op jit(solution)/shard_map/ppermute | solution.py:321
  45.4 1.6 %collective-permute-start.10 = (f32[4,128,128]{2,1,0:T(8,128)S(1)}, f32[4,128,128]{2,1,0:T(8,128)S(1)}, u32[]{:S(2)}, u32[]{:S(2)}) collective-permute-start(f32[4,128,128]{2,1,0:T(8,128)S(1)} %get-tuple-element.86), channel_id=1, source_target_pairs={{28,24},{24,28},{20,16},{16,20},{12,8},{8,12},{4,0},{0,4},{29,25},... | collective-permute-start | bytes 786440 | tf_op jit(solution)/shard_map/ppermute | solution.py:321

commit v5 on v4

--- a/solution.py
+++ b/solution.py
@@ -33,6 +33,25 @@
 
 def lanes_of(j):
     return slice(j * HEAD_DIM, (j + 1) * HEAD_DIM)
+
+
+def pairs_of(width):
+    return [slice(i, i + 2 * HEAD_DIM) for i in range(0, width, 2 * HEAD_DIM)]
+
+
+def diagonal(first, second):
+    zero = jnp.zeros_like(first)
+    top = jnp.concatenate([first, zero], axis=1)
+    return jnp.concatenate([top, jnp.concatenate([zero, second], axis=1)], axis=0)
+
+
+def diagonals(states):
+    states = [state.astype(BF16) for state in states]
+    return [diagonal(*states[i:i + 2]) for i in range(0, len(states), 2)]
+
+
+def heads_in(pieces):
+    return [ref[j] for ref in pieces for j in range(ref.shape[0])]
 
 
 def lower(size):
@@ -96,8 +115,8 @@
         sum_ref[j] = totals[j]
 
 
-def inner_kernel(same, q_hbm, og_hbm, k_ref, v_ref, gain_ref, pre_ref, after_ref, *outs):
-    q_ref, inner_ref, scaled_ref, qturned_ref, turned_ref, og_ref, sems = outs
+def inner_kernel(same, q_hbm, og_hbm, k_ref, v_ref, gain_ref, pre_ref, *refs):
+    q_ref, inner_ref, scaled_ref, qturned_ref, turned_ref, og_ref, sems = refs[-7:]
     rows, width = q_ref.shape
     copies = fetches((q_hbm, og_hbm), (q_ref, og_ref), sems, same)
     for copy in copies:
@@ -106,6 +125,10 @@
     for i, part in enumerate(chunks_of(rows)):
         for copy in copies[2 * i:2 * i + 2]:
             copy.wait()
+        if i:
+            earlier = diagonals([pre_ref[i, j] for j in range(width // HEAD_DIM)])
+            for lanes, states in zip(pairs_of(width), earlier):
+                inner_ref[part, lanes] = dot(q_ref[part, lanes], states)
         for j in range(width // HEAD_DIM):
             lanes = lanes_of(j)
             q, k = q_ref[part, lanes], k_ref[part, lanes]
@@ -113,24 +136,25 @@
             scores = jnp.where(lower(size), dot(q, k, 1, 1), 0.0).astype(BF16)
             turned_ref[j, part] = jnp.where(upper(size), dot(k, q, 1, 1), 0.0).astype(BF16)
             inner = dot(scores, v_ref[part, lanes])
-            inner_ref[part, lanes] = inner + dot(q, pre_ref[i, j]) if i else inner
+            inner_ref[part, lanes] = inner_ref[part, lanes] + inner if i else inner
             scaled_ref[part, lanes] = gain[:, lanes] * og_ref[part, lanes].astype(F32)
             qturned_ref[lanes, part] = q.T
 
 
-def attn_kernel(last, q_ref, inner_ref, scaled_ref, state_ref, *refs):
-    attn_ref = refs[-3] if not last else refs[-2]
+def attn_kernel(last, pieces, q_ref, inner_ref, scaled_ref, *refs):
+    states = diagonals(heads_in(refs[:pieces]))
+    refs = refs[pieces:]
+    attn_ref = refs[2] if last else refs[0]
     rows, width = q_ref.shape
-    states = [state_ref[j].astype(BF16) for j in range(width // HEAD_DIM)]
     for part in chunks_of(rows):
         square, cross = (refs[0][part], refs[1][part]) if last else (None, None)
-        for j, state in enumerate(states):
-            lanes = lanes_of(j)
+        for lanes, state in zip(pairs_of(width), states):
             attn = inner_ref[part, lanes] + dot(q_ref[part, lanes], state)
             attn_ref[part, lanes] = attn
             more, crossed = attn * attn, scaled_ref[part, lanes] * attn
-            square = more if square is None else square + more
-            cross = crossed if cross is None else cross + crossed
+            for i in range(2):
+                square = more[:, lanes_of(i)] if square is None else square + more[:, lanes_of(i)]
+                cross = crossed[:, lanes_of(i)] if cross is None else cross + crossed[:, lanes_of(i)]
         if last:
             square = jnp.sum(square.T, axis=0, keepdims=True)
             cross = jnp.sum(cross.T, axis=0, keepdims=True)
@@ -182,54 +206,58 @@
         sum_ref[j] = totals[j]
 
 
-def local_kernel(same, q_ref, k_ref, v_ref, g_ref, turned_ref, state_ref, pre_ref, post_ref, *refs):
-    qgrad_hbm, kpart_ref, vpart_ref, qgrad_ref, sems = refs[-5:]
+def local_kernel(same, pieces, q_ref, k_ref, v_ref, g_ref, turned_ref, pre_ref, post_ref, *refs):
+    qgrad_hbm, kpart_ref, vpart_ref, qgrad_ref, out_ref, sems = refs[-6:]
+    state = heads_in(refs[:pieces])
     rows, width = q_ref.shape
     target = columns(same, width)
     parts = chunks_of(rows)
     copies = []
     for i, part in enumerate(parts):
-        for j in range(width // HEAD_DIM):
+        heads = range(width // HEAD_DIM)
+        before = [state[j] + pre_ref[i, j].astype(F32) if i else state[j] for j in heads]
+        for lanes, both in zip(pairs_of(width), diagonals(before)):
+            qgrad_ref[part, lanes] = dot(g_ref[part, lanes], both, 1, 1)
+        last = i == len(parts) - 1
+        if not last:
+            later = diagonals([post_ref[i, j] for j in heads])
+            for lanes, both in zip(pairs_of(width), later):
+                kpart_ref[part, lanes] = dot(v_ref[part, lanes], both, 1, 1)
+                vpart_ref[part, lanes] = dot(k_ref[part, lanes], both)
+        for j in heads:
             lanes = lanes_of(j)
             q, k, v, g = (ref[part, lanes] for ref in (q_ref, k_ref, v_ref, g_ref))
             size = q.shape[0]
             gscores = jnp.where(lower(size), dot(g, v, 1, 1), 0.0).astype(BF16)
             gturned = jnp.where(upper(size), dot(v, g, 1, 1), 0.0).astype(BF16)
-            qgrad = dot(gscores, k) + dot(g, state_ref[j].astype(BF16), 1, 1)
-            kgrad = dot(gturned, q)
-            vgrad = dot(turned_ref[j, part], g)
-            if i:
-                qgrad = qgrad + dot(g, pre_ref[i, j], 1, 1)
-            if i < len(parts) - 1:
-                kgrad = kgrad + dot(v, post_ref[i, j], 1, 1)
-                vgrad = vgrad + dot(k, post_ref[i, j])
-            qgrad_ref[part, lanes] = qgrad.astype(BF16)
-            kpart_ref[part, lanes] = kgrad
-            vpart_ref[part, lanes] = vgrad
-        copy = pltpu.make_async_copy(qgrad_ref.at[part], qgrad_hbm.at[part, target], sems.at[i])
+            kgrad, vgrad = dot(gturned, q), dot(turned_ref[j, part], g)
+            out_ref[part, lanes] = (qgrad_ref[part, lanes] + dot(gscores, k)).astype(BF16)
+            kpart_ref[part, lanes] = kgrad if last else kpart_ref[part, lanes] + kgrad
+            vpart_ref[part, lanes] = vgrad if last else vpart_ref[part, lanes] + vgrad
+        copy = pltpu.make_async_copy(out_ref.at[part], qgrad_hbm.at[part, target], sems.at[i])
         copy.start()
         copies.append(copy)
     for copy in copies:
         copy.wait()
 
 
-def final_parts(k_ref, v_ref, kpart_ref, vpart_ref, state_ref, kgrad_ref, vgrad_ref, part):
-    for j in range(state_ref.shape[0]):
-        lanes = lanes_of(j)
-        state = state_ref[j].astype(BF16)
+def final_parts(k_ref, v_ref, kpart_ref, vpart_ref, states, kgrad_ref, vgrad_ref, part):
+    for lanes, state in zip(pairs_of(k_ref.shape[1]), states):
         kgrad = kpart_ref[part, lanes] + dot(v_ref[part, lanes], state, 1, 1)
         vgrad = vpart_ref[part, lanes] + dot(k_ref[part, lanes], state)
         kgrad_ref[part, lanes] = kgrad.astype(BF16)
         vgrad_ref[part, lanes] = vgrad.astype(BF16)
 
 
-def near_kernel(*refs):
+def near_kernel(pieces, *refs):
+    states = diagonals(heads_in(refs[4:4 + pieces]))
     for part in chunks_of(refs[0].shape[0]):
-        final_parts(*refs, part)
-
-
-def last_kernel(same, *refs):
-    kdone_ref, vdone_ref, kgrad_hbm, vgrad_hbm, kgrad_ref, vgrad_ref, sems = refs[5:]
+        final_parts(*refs[:4], states, *refs[4 + pieces:], part)
+
+
+def last_kernel(same, pieces, *refs):
+    states = diagonals(heads_in(refs[4:4 + pieces]))
+    kdone_ref, vdone_ref, kgrad_hbm, vgrad_hbm, kgrad_ref, vgrad_ref, sems = refs[4 + pieces:]
     rows, width = kgrad_ref.shape
     copies = []
 
@@ -243,7 +271,7 @@
     send(kdone_ref, kgrad_hbm, slice(0, rows), not same)
     send(vdone_ref, vgrad_hbm, slice(0, rows), not same)
     for part in chunks_of(rows):
-        final_parts(*refs[:5], kgrad_ref, vgrad_ref, part)
+        final_parts(*refs[:4], states, kgrad_ref, vgrad_ref, part)
         send(kgrad_ref, kgrad_hbm, part, same)
         send(vgrad_ref, vgrad_hbm, part, same)
     for copy in copies:
@@ -260,16 +288,16 @@
     return stages
 
 
-def join_kernel(backward, done, final, *refs):
+def join_kernel(backward, piece, done, final, *refs):
     count = lax.axis_size("seq")
     rank = lax.axis_index("seq")
     if backward:
         rank = count - 1 - rank
     odd = (rank & 1) == 1
     plan = scan_plan(count)
-    keep_ref, extra_ref = refs[:2]
+    keep, extra = (ref[piece] for ref in refs[:2])
     came = refs[2:2 + done]
-    total = keep_ref[...] + extra_ref[...]
+    total = keep + extra
     before = jnp.zeros_like(total)
     for (rising, falling, _), ref in zip(plan, came):
         high = (jnp.where(odd, rank >> falling, rank >> rising) & 1) == 1
@@ -278,18 +306,18 @@
         total = total + jnp.where(odd, 0.0, value)
     if final:
         message_ref, state_ref = refs[-2:]
-        message_ref[...] = before + jnp.where(odd, 0.0, keep_ref[...])
-        state_ref[...] = before + jnp.where(odd, extra_ref[...], 0.0)
+        message_ref[...] = before + jnp.where(odd, 0.0, keep)
+        state_ref[...] = before + jnp.where(odd, extra, 0.0)
     else:
         rising, falling, _ = plan[done]
         high = (jnp.where(odd, rank >> falling, rank >> rising) & 1) == 1
         refs[-1][...] = jnp.where(odd, before + jnp.where(high, 0.0, total), total)
 
 
-def join(backward, keep, extra, came, final, after=()):
-    like = shape(keep.shape, F32)
+def join(backward, piece, keep, extra, came, final, after):
+    like = shape((piece.stop - piece.start,) + keep.shape[1:], F32)
     return run(
-        functools.partial(join_kernel, backward, len(came), final), 4 * keep.size,
+        functools.partial(join_kernel, backward, piece, len(came), final), 4 * like.size,
         [VMEM] * (2 + len(came)) + [ANYWHERE] * len(after),
         [VMEM, VMEM] if final else VMEM,
         [like, like] if final else like,
@@ -298,20 +326,27 @@
 
 
 def scan_states(keep, extra, backward, beside):
-    count = lax.axis_size("seq")
-    plan = scan_plan(count)
-    came, results = [], []
-    message = join(backward, keep, extra, came, not plan)
+    plan = scan_plan(lax.axis_size("seq"))
+    pieces = [slice(i, i + 2) for i in range(0, keep.shape[0], 2)]
+    came = [[] for _ in pieces]
+    results, after = [], []
     for stage, (_, _, pairs) in enumerate(plan):
-        arrived = move(message, pairs, backward)
-        mine = beside[stage::len(plan)] if stage < len(beside) else []
-        made = [work(message) for work in mine]
+        messages = []
+        for piece, arrived in zip(pieces, came):
+            message = join(backward, piece, keep, extra, arrived, False, after + messages)
+            messages.append(message)
+            arrived.append(move(message, pairs, backward))
+        mine = beside[stage:] if stage == len(plan) - 1 else beside[stage:stage + 1]
+        made = [work(messages) for work in mine]
+        after = [item[-1] for item in made]
         results += made
-        came = came + [arrived]
-        after = [leaf for item in made for leaf in item[-1:]]
-        message = join(backward, keep, extra, came, stage == len(plan) - 1, after)
-    message, state = message
-    return state, nearby(message, backward), results
+    states, others, last = [], [], []
+    for piece, arrived in zip(pieces, came):
+        message, state = join(backward, piece, keep, extra, arrived, True, after + last)
+        last = [message]
+        states.append(state)
+        others.append(nearby(message, backward))
+    return states, others, results
 
 
 def move(value, pairs, backward):
@@ -357,14 +392,14 @@
     k2, v2, keep, pre2 = states_of(True)
 
     def inner_of(same, k, v, pre):
-        return lambda message: run(
+        return lambda messages: run(
             partial(inner_kernel, same), 6 * unit,
-            [HBM, HBM, VMEM, VMEM, VMEM, VMEM, ANYWHERE], [VMEM] * 5,
+            [HBM, HBM, VMEM, VMEM, VMEM, VMEM] + [ANYWHERE] * len(messages), [VMEM] * 5,
             [
                 thin, wide, wide,
                 shape((half, rows), BF16), shape((heads, rows, rows // chunks), BF16),
             ],
-            (query, out_grad, k, v, gain, pre, message),
+            (query, out_grad, k, v, gain, pre, *messages),
             [pltpu.VMEM((rows, half), BF16), sems],
         )
 
@@ -374,13 +409,14 @@
     )
     (q2, inner2, scaled2, qturned2, turned2), (q1, inner1, scaled1, qturned1, turned1) = made
 
+    count = len(state2)
     attn2, square, cross = run(
-        partial(attn_kernel, False), unit, [VMEM] * 4, [VMEM] * 3, [wide, lane_sums, lane_sums],
-        (q2, inner2, scaled2, state2),
+        partial(attn_kernel, False, count), unit, [VMEM] * (3 + count), [VMEM] * 3,
+        [wide, lane_sums, lane_sums], (q2, inner2, scaled2, *state2),
     )
     attn1, sums = run(
-        partial(attn_kernel, True), unit, [VMEM] * 6, [VMEM] * 2, [wide, shape((8, rows), F32)],
-        (q1, inner1, scaled1, state1, square, cross),
+        partial(attn_kernel, True, count), unit, [VMEM] * (5 + count), [VMEM] * 2,
+        [wide, shape((8, rows), F32)], (q1, inner1, scaled1, *state1, square, cross),
     )
     parts = [sums] + [
         lax.ppermute(sums, "head", [(r, r ^ other) for r in range(peers)])
@@ -401,14 +437,14 @@
     qgrads = []
 
     def local_of(same, *args):
-        def work(message):
-            more = [message] + qgrads
+        def work(messages):
+            more = list(messages) + qgrads
             qgrad, kpart, vpart = run(
-                partial(local_kernel, same), 9 * unit,
-                [VMEM] * len(args) + [ANYWHERE] + [HBM] * len(qgrads), [HBM, VMEM, VMEM],
-                [whole, wide, wide], (*args, *more),
-                [pltpu.VMEM((rows, half), BF16), sems],
-                {len(args) + 1: 0} if qgrads else None,
+                partial(local_kernel, same, count), 9 * unit,
+                [VMEM] * len(args) + [ANYWHERE] * len(messages) + [HBM] * len(qgrads),
+                [HBM, VMEM, VMEM], [whole, wide, wide], (*args, *more),
+                [pltpu.VMEM((rows, half), F32), pltpu.VMEM((rows, half), BF16), sems],
+                {len(args) + len(messages): 0} if qgrads else None,
             )
             qgrads[:] = [qgrad]
             return kpart, vpart
@@ -418,19 +454,19 @@
     gstate1, gstate2, made = scan_states(
         gkeep, gextra, True,
         [
-            local_of(False, q1, k1, v1, g1, turned1, state1, pre1, post1),
-            local_of(True, q2, k2, v2, g2, turned2, state2, pre2, post2),
+            local_of(False, q1, k1, v1, g1, turned1, pre1, post1, *state1),
+            local_of(True, q2, k2, v2, g2, turned2, pre2, post2, *state2),
         ],
     )
     (kpart1, vpart1), (kpart2, vpart2) = made
 
     done = run(
-        near_kernel, 2 * unit, [VMEM] * 5, [VMEM] * 2, [thin, thin],
-        (k1, v1, kpart1, vpart1, gstate1),
+        partial(near_kernel, count), 2 * unit, [VMEM] * (4 + count), [VMEM] * 2, [thin, thin],
+        (k1, v1, kpart1, vpart1, *gstate1),
     )
     kgrad, vgrad = run(
-        partial(last_kernel, True), 2 * unit, [VMEM] * 7, [HBM, HBM], [whole, whole],
-        (k2, v2, kpart2, vpart2, gstate2, *done),
+        partial(last_kernel, True, count), 2 * unit, [VMEM] * (6 + count), [HBM, HBM],
+        [whole, whole], (k2, v2, kpart2, vpart2, *gstate2, *done),
         [pltpu.VMEM((rows, half), BF16)] * 2 + [pltpu.SemaphoreType.DMA((2 * chunks + 2,))],
     )
     return qgrads[0], kgrad, vgrad

time: 49.1 us -> 49.3 us (level)
  waiting for transfers between devices: 10.8 us -> 6.6 us
  starting transfers between devices: 13.4 us -> 16.2 us
  Pallas kernels: 23.8 us -> 25.3 us
    ppermute x8 -> x14, waiting for transfers between devices: 6.68 us -> 2.66 us  [move(): return lax.ppermute(value, 'seq', pairs)]
    ppermute x8 -> x14, starting transfers between devices: 8.56 us -> 11.7 us  [move(): return lax.ppermute(value, 'seq', pairs)]
    pallas_call x18 -> x24, Pallas kernels: 23.8 us -> 25.3 us  [run(): pl.pallas_call(kernel, in_specs=in_specs, out_specs=out_specs, out_shape=...]
  transfers between devices with their start and end apart: 11 -> 17, of which waited for: 9 -> 8; matrix products, arithmetic and copies ran while one was open for 0% -> 0% of each run, Pallas kernels for 37% -> 41%
where the time goes in v5:
time: 49.3 us; the launch traced here: 49.1 us
  Pallas kernels  25.3 us (51%)
  starting transfers between devices  16.2 us (33%)
  waiting for transfers between devices  6.6 us (13%)
  between operations  1.03 us (2%)
    pallas_call x24, Pallas kernels, run(): pl.pallas_call(kernel, in_specs=in_specs, out_specs=out_specs, out_shape=...  25.3 us
    ppermute x14, starting transfers between devices, move(): return lax.ppermute(value, 'seq', pairs)  11.7 us
    ppermute x3, starting transfers between devices, shards(): lax.ppermute(sums, 'head', [(r, r ^ other) for r in range(peers)])  4.45 us
    ppermute x3, waiting for transfers between devices, shards(): lax.ppermute(sums, 'head', [(r, r ^ other) for r in range(peers)])  3.94 us
    ppermute x14, waiting for transfers between devices, move(): return lax.ppermute(value, 'seq', pairs)  2.66 us
  transfers between devices with their start and end apart: 17, of which 8 were waited for; matrix products, arithmetic and copies ran while one was open for 0% of the time, Pallas kernels for 41%

profile of v5, /device:TPU:0, one launch (start us, length us, event | category | flops | bytes accessed | tf_op | source)
XLA Modules:
  0.0 49.1 jit_solution(3610676888504416347)
XLA Ops:
  0.6 1.9 %shard_map.77 = (bf16[768,512]{1,0:T(8,128)(2,1)S(1)}, bf16[768,512]{1,0:T(8,128)(2,1)S(1)}, f32[4,128,128]{2,1,0:T(8,128)S(1)}, bf16[3,4,128,128]{3,2,1,0:T(8,128)(2,1)S(1)}) custom-call(bf16[768,1024]{1,0:T(8,128)(2,1)} %k_hbm.3, bf16[768,1024]{1,0:T(8,128)(2,1)} %v_hbm.3), custom_call_target="tpu_custom_call" | custom-call | flops 100663296 | bytes 3145728 | tf_op jit(solution)/shard_map/pallas_call | solution.py:69
  2.6 0.5 %collective-permute-start = (f32[4,128,128]{2,1,0:T(8,128)S(1)}, f32[4,128,128]{2,1,0:T(8,128)S(1)}, u32[]{:S(2)}, u32[]{:S(2)}) collective-permute-start(f32[4,128,128]{2,1,0:T(8,128)S(1)} %get-tuple-element.56), channel_id=1, source_target_pairs={{0,4},{4,0},{8,12},{12,8},{16,20},{20,16},{24,28},{28,24},{1,5},{5... | collective-permute-start | bytes 786440 | tf_op jit(solution)/shard_map/ppermute | solution.py:356
  3.1 1.9 %shard_map.76 = (bf16[768,512]{1,0:T(8,128)(2,1)S(1)}, bf16[768,512]{1,0:T(8,128)(2,1)S(1)}, f32[4,128,128]{2,1,0:T(8,128)S(1)}, bf16[3,4,128,128]{3,2,1,0:T(8,128)(2,1)S(1)}) custom-call(bf16[768,1024]{1,0:T(8,128)(2,1)} %k_hbm.3, bf16[768,1024]{1,0:T(8,128)(2,1)} %v_hbm.3), custom_call_target="tpu_custom_call" | custom-call | flops 100663296 | bytes 3145728 | tf_op jit(solution)/shard_map/pallas_call | solution.py:69
  5.1 2.6 %collective-permute-start.1 = (f32[2,128,128]{2,1,0:T(8,128)S(1)}, f32[2,128,128]{2,1,0:T(8,128)S(1)}, u32[]{:S(2)}, u32[]{:S(2)}) collective-permute-start(f32[2,128,128]{2,1,0:T(8,128)S(1)} %shard_map.78.refs_2_.refs_0_), channel_id=1, source_target_pairs={{0,8},{4,20},{8,0},{12,28},{16,24},{20,4},{24,16},{28,12},{1,9},{5... | collective-permute-start | bytes 393224 | tf_op jit(solution)/shard_map/ppermute | solution.py:356
  7.8 3.4 %shard_map.80 = (bf16[768,512]{1,0:T(8,128)(2,1)S(1)}, f32[768,512]{1,0:T(8,128)S(1)}, f32[768,512]{1,0:T(8,128)S(1)}, bf16[512,768]{1,0:T(8,128)(2,1)S(1)}, bf16[4,768,256]{2,1,0:T(8,128)(2,1)S(1)}) custom-call(bf16[768,1024]{1,0:T(8,128)(2,1)} %q_hbm.3, bf16[768,1024]{1,0:T(8,128)(2,1)} %og_hbm.3, bf16[768,512]{1,0:T(8,128)(2,1)S(1)} %get-tuple-element.52.k_ref.refs_0_, ...), custom_call_target="tpu_custom_call" | custom-call | flops 603979776 | bytes 5378048 | tf_op jit(solution)/shard_map/pallas_call | solution.py:69
  11.3 2.1 %collective-permute-start.3 = (f32[2,128,128]{2,1,0:T(8,128)S(1)}, f32[2,128,128]{2,1,0:T(8,128)S(1)}, u32[]{:S(2)}, u32[]{:S(2)}) collective-permute-start(f32[2,128,128]{2,1,0:T(8,128)S(1)} %shard_map.81.refs_4_.refs_0_), channel_id=1, source_target_pairs={{0,16},{4,12},{8,24},{12,4},{16,0},{20,28},{24,8},{28,20},{1,17},{... | collective-permute-start | bytes 393224 | tf_op jit(solution)/shard_map/ppermute | solution.py:356
  13.4 0.9 %collective-permute-start.5 = (f32[2,128,128]{2,1,0:T(8,128)S(1)}, f32[2,128,128]{2,1,0:T(8,128)S(1)}, u32[]{:S(2)}, u32[]{:S(2)}) collective-permute-start(f32[2,128,128]{2,1,0:T(8,128)S(1)} %shard_map.82.refs_1_), channel_id=1, source_target_pairs={{0,16},{4,12},{8,24},{12,4},{16,0},{20,28},{24,8},{28,20},{1,17},{... | collective-permute-start | bytes 393224 | tf_op jit(solution)/shard_map/ppermute | solution.py:356
  14.3 3.4 %shard_map.83 = (bf16[768,512]{1,0:T(8,128)(2,1)S(1)}, f32[768,512]{1,0:T(8,128)S(1)}, f32[768,512]{1,0:T(8,128)S(1)}, bf16[512,768]{1,0:T(8,128)(2,1)S(1)}, bf16[4,768,256]{2,1,0:T(8,128)(2,1)S(1)}) custom-call(bf16[768,1024]{1,0:T(8,128)(2,1)} %q_hbm.3, bf16[768,1024]{1,0:T(8,128)(2,1)} %og_hbm.3, bf16[768,512]{1,0:T(8,128)(2,1)S(1)} %get-tuple-element.58.k_ref.refs_0_, ...), custom_call_target="tpu_custom_call" | custom-call | flops 603979776 | bytes 5378048 | tf_op jit(solution)/shard_map/pallas_call | solution.py:69
  17.9 0.6 %collective-permute-done.5.refs_3_ = f32[2,128,128]{2,1,0:T(8,128)S(1)} collective-permute-done((f32[2,128,128]{2,1,0:T(8,128)S(1)}, f32[2,128,128]{2,1,0:T(8,128)S(1)}, u32[]{:S(2)}, u32[]{:S(2)}) %collective-permute-start.5) | collective-permute-done | bytes 131104 | tf_op jit(solution)/shard_map/ppermute | solution.py:356
  20.1 0.6 %shard_map.87 = (f32[768,512]{1,0:T(8,128)S(1)}, f32[8,768]{1,0:T(8,128)S(1)}) custom-call(bf16[768,512]{1,0:T(8,128)(2,1)S(1)} %get-tuple-element.62.q_ref, f32[768,512]{1,0:T(8,128)S(1)} %get-tuple-element.63.inner_ref, f32[768,512]{1,0:T(8,128)S(1)} %get-tuple-element.64.scaled_ref.refs_3_, f32[2,128,128]{2,1,0:T(8,128)S(1)} %collective-permute-done.4.refs_0_, ...), custom_call_target="tpu_custom_call" | custom-call | flops 100663296 | bytes 4980736 | tf_op jit(solution)/shard_map/pallas_call | solution.py:69
  20.7 3.7 %collective-permute-start.9 = (f32[8,768]{1,0:T(8,128)S(1)}, f32[8,768]{1,0:T(8,128)S(1)}, u32[]{:S(2)}, u32[]{:S(2)}) collective-permute-start(f32[8,768]{1,0:T(8,128)S(1)} %get-tuple-element.74.refs_0_), channel_id=1, source_target_pairs={{0,3},{1,2},{2,1},{3,0},{4,7},{5,6},{6,5},{7,4},{8,11},{9,10},{10,... | collective-permute-start | bytes 73736 | tf_op jit(solution)/shard_map/ppermute | solution.py:422
  24.4 0.8 %collective-permute-start.7 = (f32[8,768]{1,0:T(8,128)S(1)}, f32[8,768]{1,0:T(8,128)S(1)}, u32[]{:S(2)}, u32[]{:S(2)}) collective-permute-start(f32[8,768]{1,0:T(8,128)S(1)} %get-tuple-element.74.refs_0_), channel_id=1, source_target_pairs={{0,1},{1,0},{2,3},{3,2},{4,5},{5,4},{6,7},{7,6},{8,9},{9,8},{10,11... | collective-permute-start | bytes 73736 | tf_op jit(solution)/shard_map/ppermute | solution.py:422
  25.2 1.2 %collective-permute-done.9.refs_3_ = f32[8,768]{1,0:T(8,128)S(1)} collective-permute-done((f32[8,768]{1,0:T(8,128)S(1)}, f32[8,768]{1,0:T(8,128)S(1)}, u32[]{:S(2)}, u32[]{:S(2)}) %collective-permute-start.9) | collective-permute-done | bytes 24608 | tf_op jit(solution)/shard_map/ppermute | solution.py:422
  26.4 2.7 %collective-permute-done.8.refs_2_ = f32[8,768]{1,0:T(8,128)S(1)} collective-permute-done((f32[8,768]{1,0:T(8,128)S(1)}, f32[8,768]{1,0:T(8,128)S(1)}, u32[]{:S(2)}, u32[]{:S(2)}) %collective-permute-start.8) | collective-permute-done | bytes 24608 | tf_op jit(solution)/shard_map/ppermute | solution.py:422
  29.1 0.9 %shard_map.88 = (bf16[768,512]{1,0:T(8,128)(2,1)S(1)}, f32[4,128,128]{2,1,0:T(8,128)S(1)}, bf16[3,4,128,128]{3,2,1,0:T(8,128)(2,1)S(1)}, f32[768,128]{1,0:T(8,128)S(1)}, f32[768,128]{1,0:T(8,128)S(1)}) custom-call(f32[8,768]{1,0:T(8,128)S(1)} %get-tuple-element.74.refs_0_, f32[8,768]{1,0:T(8,128)S(1)} %collective-permute-done.7.refs_1_, ...), custom_call_target="tpu_custom_call" | custom-call | flops 100663296 | bytes 4030464 | tf_op jit(solution)/shard_map/pallas_call | solution.py:69
  30.5 1.0 %collective-permute-done.10.refs_1_ = f32[4,128,128]{2,1,0:T(8,128)S(1)} collective-permute-done((f32[4,128,128]{2,1,0:T(8,128)S(1)}, f32[4,128,128]{2,1,0:T(8,128)S(1)}, u32[]{:S(2)}, u32[]{:S(2)}) %collective-permute-start.10) | collective-permute-done | bytes 262176 | tf_op jit(solution)/shard_map/ppermute | solution.py:356
  31.6 1.4 %collective-permute-start.11 = (f32[2,128,128]{2,1,0:T(8,128)S(1)}, f32[2,128,128]{2,1,0:T(8,128)S(1)}, u32[]{:S(2)}, u32[]{:S(2)}) collective-permute-start(f32[2,128,128]{2,1,0:T(8,128)S(1)} %shard_map.90.refs_2_), channel_id=1, source_target_pairs={{28,20},{24,8},{20,28},{16,0},{12,4},{8,24},{4,12},{0,16},{29,21},... | collective-permute-start | bytes 393224 | tf_op jit(solution)/shard_map/ppermute | solution.py:356
  33.0 0.8 %collective-permute-start.12 = (f32[2,128,128]{2,1,0:T(8,128)S(1)}, f32[2,128,128]{2,1,0:T(8,128)S(1)}, u32[]{:S(2)}, u32[]{:S(2)}) collective-permute-start(f32[2,128,128]{2,1,0:T(8,128)S(1)} %shard_map.91.refs_3_), channel_id=1, source_target_pairs={{28,20},{24,8},{20,28},{16,0},{12,4},{8,24},{4,12},{0,16},{29,21},... | collective-permute-start | bytes 393224 | tf_op jit(solution)/shard_map/ppermute | solution.py:356
  33.8 4.7 %shard_map.92 = (bf16[768,1024]{1,0:T(8,128)(2,1)}, f32[768,512]{1,0:T(8,128)S(1)}, f32[768,512]{1,0:T(8,128)S(1)}) custom-call(bf16[768,512]{1,0:T(8,128)(2,1)S(1)} %get-tuple-element.62.q_ref, bf16[768,512]{1,0:T(8,128)(2,1)S(1)} %get-tuple-element.58.k_ref.refs_0_, bf16[768,512]{1,0:T(8,128)(2,1)S(1)} %get-tuple-element.59.v_ref.refs_1_, ...), custom_call_target="tpu_custom_call" | custom-call | flops 905969664 | bytes 6029312 | tf_op jit(solution)/shard_map/pallas_call | solution.py:69
  38.6 1.6 %collective-permute-start.13 = (f32[2,128,128]{2,1,0:T(8,128)S(1)}, f32[2,128,128]{2,1,0:T(8,128)S(1)}, u32[]{:S(2)}, u32[]{:S(2)}) collective-permute-start(f32[2,128,128]{2,1,0:T(8,128)S(1)} %shard_map.93.refs_4_.refs_2_), channel_id=1, source_target_pairs={{28,12},{24,16},{20,4},{16,24},{12,28},{8,0},{4,20},{0,8},{29,13},... | collective-permute-start | bytes 393224 | tf_op jit(solution)/shard_map/ppermute | solution.py:356
  40.2 0.6 %collective-permute-start.15 = (f32[2,128,128]{2,1,0:T(8,128)S(1)}, f32[2,128,128]{2,1,0:T(8,128)S(1)}, u32[]{:S(2)}, u32[]{:S(2)}) collective-permute-start(f32[2,128,128]{2,1,0:T(8,128)S(1)} %shard_map.94.refs_3_), channel_id=1, source_target_pairs={{28,12},{24,16},{20,4},{16,24},{12,28},{8,0},{4,20},{0,8},{29,13},... | collective-permute-start | bytes 393224 | tf_op jit(solution)/shard_map/ppermute | solution.py:356
  40.8 4.6 %shard_map.95 = (bf16[768,1024]{1,0:T(8,128)(2,1)}, f32[768,512]{1,0:T(8,128)S(1)}, f32[768,512]{1,0:T(8,128)S(1)}) custom-call(bf16[768,512]{1,0:T(8,128)(2,1)S(1)} %get-tuple-element.57.q_ref, bf16[768,512]{1,0:T(8,128)(2,1)S(1)} %get-tuple-element.52.k_ref.refs_0_, ...), custom_call_target="tpu_custom_call", output_to_operand_aliasing={{0}: (11, {})} | custom-call | flops 905969664 | bytes 7602176 | tf_op jit(solution)/shard_map/pallas_call | solution.py:69
  46.1 0.6 %shard_map.98 = (bf16[768,512]{1,0:T(8,128)(2,1)S(1)}, bf16[768,512]{1,0:T(8,128)(2,1)S(1)}) custom-call(bf16[768,512]{1,0:T(8,128)(2,1)S(1)} %get-tuple-element.58.k_ref.refs_0_, bf16[768,512]{1,0:T(8,128)(2,1)S(1)} %get-tuple-element.59.v_ref.refs_1_, f32[768,512]{1,0:T(8,128)S(1)} %get-tuple-element.94.refs_2_, f32[768,512]{1,0:T(8,128)S(1)} %get-tuple-element.87.refs_3_, ...), custom_call_target="tpu_custom_call" | custom-call | flops 201326592 | bytes 4980736 | tf_op jit(solution)/shard_map/pallas_call | solution.py:69
  47.1 1.8 %shard_map.99 = (bf16[768,1024]{1,0:T(8,128)(2,1)}, bf16[768,1024]{1,0:T(8,128)(2,1)}) custom-call(bf16[768,512]{1,0:T(8,128)(2,1)S(1)} %get-tuple-element.52.k_ref.refs_0_, bf16[768,512]{1,0:T(8,128)(2,1)S(1)} %get-tuple-element.53.v_ref.refs_1_, f32[768,512]{1,0:T(8,128)S(1)} %get-tuple-element.90.refs_2_, ...), custom_call_target="tpu_custom_call" | custom-call | flops 201326592 | bytes 6553600 | tf_op jit(solution)/shard_map/pallas_call | solution.py:69
  (36 shorter events, 3.8 us)
Async XLA Ops:
  2.6 5.2 %copy-start = (f32[1024]{0:T(1024)S(1)}, f32[1024]{0:T(1024)}, u32[]{:S(2)}) copy-start(f32[1024]{0:T(1024)} %param.9) | copy-start | bytes 12292
  2.6 2.4 %collective-permute-start = (f32[4,128,128]{2,1,0:T(8,128)S(1)}, f32[4,128,128]{2,1,0:T(8,128)S(1)}, u32[]{:S(2)}, u32[]{:S(2)}) collective-permute-start(f32[4,128,128]{2,1,0:T(8,128)S(1)} %get-tuple-element.56), channel_id=1, source_target_pairs={{0,4},{4,0},{8,12},{12,8},{16,20},{20,16},{24,28},{28,24},{1,5},{5... | collective-permute-start | bytes 786440 | tf_op jit(solution)/shard_map/ppermute | solution.py:356
  5.1 6.2 %collective-permute-start.1 = (f32[2,128,128]{2,1,0:T(8,128)S(1)}, f32[2,128,128]{2,1,0:T(8,128)S(1)}, u32[]{:S(2)}, u32[]{:S(2)}) collective-permute-start(f32[2,128,128]{2,1,0:T(8,128)S(1)} %shard_map.78.refs_2_.refs_0_), channel_id=1, source_target_pairs={{0,8},{4,20},{8,0},{12,28},{16,24},{20,4},{24,16},{28,12},{1,9},{5... | collective-permute-start | bytes 393224 | tf_op jit(solution)/shard_map/ppermute | solution.py:356
  7.7 5.7 %collective-permute-start.2 = (f32[2,128,128]{2,1,0:T(8,128)S(1)}, f32[2,128,128]{2,1,0:T(8,128)S(1)}, u32[]{:S(2)}, u32[]{:S(2)}) collective-permute-start(f32[2,128,128]{2,1,0:T(8,128)S(1)} %shard_map.79.refs_1_), channel_id=1, source_target_pairs={{0,8},{4,20},{8,0},{12,28},{16,24},{20,4},{24,16},{28,12},{1,9},{5... | collective-permute-start | bytes 393224 | tf_op jit(solution)/shard_map/ppermute | solution.py:356
  11.3 6.5 %collective-permute-start.3 = (f32[2,128,128]{2,1,0:T(8,128)S(1)}, f32[2,128,128]{2,1,0:T(8,128)S(1)}, u32[]{:S(2)}, u32[]{:S(2)}) collective-permute-start(f32[2,128,128]{2,1,0:T(8,128)S(1)} %shard_map.81.refs_4_.refs_0_), channel_id=1, source_target_pairs={{0,16},{4,12},{8,24},{12,4},{16,0},{20,28},{24,8},{28,20},{1,17},{... | collective-permute-start | bytes 393224 | tf_op jit(solution)/shard_map/ppermute | solution.py:356
  13.4 5.0 %collective-permute-start.5 = (f32[2,128,128]{2,1,0:T(8,128)S(1)}, f32[2,128,128]{2,1,0:T(8,128)S(1)}, u32[]{:S(2)}, u32[]{:S(2)}) collective-permute-start(f32[2,128,128]{2,1,0:T(8,128)S(1)} %shard_map.82.refs_1_), channel_id=1, source_target_pairs={{0,16},{4,12},{8,24},{12,4},{16,0},{20,28},{24,8},{28,20},{1,17},{... | collective-permute-start | bytes 393224 | tf_op jit(solution)/shard_map/ppermute | solution.py:356
  18.5 1.4 %collective-permute-start.6 = (f32[2,128,128]{2,1,0:T(8,128)S(1)}, f32[2,128,128]{2,1,0:T(8,128)S(1)}, u32[]{:S(2)}, u32[]{:S(2)}) collective-permute-start(f32[2,128,128]{2,1,0:T(8,128)S(1)} %get-tuple-element.67), channel_id=1, source_target_pairs={{0,4},{4,0},{8,12},{12,8},{16,20},{20,16},{24,28},{28,24},{1,5},{5... | collective-permute-start | bytes 393224 | tf_op jit(solution)/shard_map/ppermute | solution.py:356
  18.6 1.5 %collective-permute-start.4 = (f32[2,128,128]{2,1,0:T(8,128)S(1)}, f32[2,128,128]{2,1,0:T(8,128)S(1)}, u32[]{:S(2)}, u32[]{:S(2)}) collective-permute-start(f32[2,128,128]{2,1,0:T(8,128)S(1)} %get-tuple-element.66.refs_5_), channel_id=1, source_target_pairs={{0,4},{4,0},{8,12},{12,8},{16,20},{20,16},{24,28},{28,24},{1,5},{5... | collective-permute-start | bytes 393224 | tf_op jit(solution)/shard_map/ppermute | solution.py:356
  20.7 5.7 %collective-permute-start.9 = (f32[8,768]{1,0:T(8,128)S(1)}, f32[8,768]{1,0:T(8,128)S(1)}, u32[]{:S(2)}, u32[]{:S(2)}) collective-permute-start(f32[8,768]{1,0:T(8,128)S(1)} %get-tuple-element.74.refs_0_), channel_id=1, source_target_pairs={{0,3},{1,2},{2,1},{3,0},{4,7},{5,6},{6,5},{7,4},{8,11},{9,10},{10,... | collective-permute-start | bytes 73736 | tf_op jit(solution)/shard_map/ppermute | solution.py:422
  24.4 4.7 %collective-permute-start.8 = (f32[8,768]{1,0:T(8,128)S(1)}, f32[8,768]{1,0:T(8,128)S(1)}, u32[]{:S(2)}, u32[]{:S(2)}) collective-permute-start(f32[8,768]{1,0:T(8,128)S(1)} %get-tuple-element.74.refs_0_), channel_id=1, source_target_pairs={{0,2},{1,3},{2,0},{3,1},{4,6},{5,7},{6,4},{7,5},{8,10},{9,11},{10,... | collective-permute-start | bytes 73736 | tf_op jit(solution)/shard_map/ppermute | solution.py:422
  24.4 4.7 %collective-permute-start.7 = (f32[8,768]{1,0:T(8,128)S(1)}, f32[8,768]{1,0:T(8,128)S(1)}, u32[]{:S(2)}, u32[]{:S(2)}) collective-permute-start(f32[8,768]{1,0:T(8,128)S(1)} %get-tuple-element.74.refs_0_), channel_id=1, source_target_pairs={{0,1},{1,0},{2,3},{3,2},{4,5},{5,4},{6,7},{7,6},{8,9},{9,8},{10,11... | collective-permute-start | bytes 73736 | tf_op jit(solution)/shard_map/ppermute | solution.py:422
  30.0 1.6 %collective-permute-start.10 = (f32[4,128,128]{2,1,0:T(8,128)S(1)}, f32[4,128,128]{2,1,0:T(8,128)S(1)}, u32[]{:S(2)}, u32[]{:S(2)}) collective-permute-start(f32[4,128,128]{2,1,0:T(8,128)S(1)} %get-tuple-element.84), channel_id=1, source_target_pairs={{28,24},{24,28},{20,16},{16,20},{12,8},{8,12},{4,0},{0,4},{29,25},... | collective-permute-start | bytes 786440 | tf_op jit(solution)/shard_map/ppermute | solution.py:356
  31.6 6.9 %collective-permute-start.11 = (f32[2,128,128]{2,1,0:T(8,128)S(1)}, f32[2,128,128]{2,1,0:T(8,128)S(1)}, u32[]{:S(2)}, u32[]{:S(2)}) collective-permute-start(f32[2,128,128]{2,1,0:T(8,128)S(1)} %shard_map.90.refs_2_), channel_id=1, source_target_pairs={{28,20},{24,8},{20,28},{16,0},{12,4},{8,24},{4,12},{0,16},{29,21},... | collective-permute-start | bytes 393224 | tf_op jit(solution)/shard_map/ppermute | solution.py:356
  33.0 7.2 %collective-permute-start.12 = (f32[2,128,128]{2,1,0:T(8,128)S(1)}, f32[2,128,128]{2,1,0:T(8,128)S(1)}, u32[]{:S(2)}, u32[]{:S(2)}) collective-permute-start(f32[2,128,128]{2,1,0:T(8,128)S(1)} %shard_map.91.refs_3_), channel_id=1, source_target_pairs={{28,20},{24,8},{20,28},{16,0},{12,4},{8,24},{4,12},{0,16},{29,21},... | collective-permute-start | bytes 393224 | tf_op jit(solution)/shard_map/ppermute | solution.py:356
  38.6 6.8 %collective-permute-start.13 = (f32[2,128,128]{2,1,0:T(8,128)S(1)}, f32[2,128,128]{2,1,0:T(8,128)S(1)}, u32[]{:S(2)}, u32[]{:S(2)}) collective-permute-start(f32[2,128,128]{2,1,0:T(8,128)S(1)} %shard_map.93.refs_4_.refs_2_), channel_id=1, source_target_pairs={{28,12},{24,16},{20,4},{16,24},{12,28},{8,0},{4,20},{0,8},{29,13},... | collective-permute-start | bytes 393224 | tf_op jit(solution)/shard_map/ppermute | solution.py:356
  40.2 5.2 %collective-permute-start.15 = (f32[2,128,128]{2,1,0:T(8,128)S(1)}, f32[2,128,128]{2,1,0:T(8,128)S(1)}, u32[]{:S(2)}, u32[]{:S(2)}) collective-permute-start(f32[2,128,128]{2,1,0:T(8,128)S(1)} %shard_map.94.refs_3_), channel_id=1, source_target_pairs={{28,12},{24,16},{20,4},{16,24},{12,28},{8,0},{4,20},{0,8},{29,13},... | collective-permute-start | bytes 393224 | tf_op jit(solution)/shard_map/ppermute | solution.py:356
  45.5 1.4 %collective-permute-start.16 = (f32[2,128,128]{2,1,0:T(8,128)S(1)}, f32[2,128,128]{2,1,0:T(8,128)S(1)}, u32[]{:S(2)}, u32[]{:S(2)}) collective-permute-start(f32[2,128,128]{2,1,0:T(8,128)S(1)} %get-tuple-element.93), channel_id=1, source_target_pairs={{28,24},{24,28},{20,16},{16,20},{12,8},{8,12},{4,0},{0,4},{29,25},... | collective-permute-start | bytes 393224 | tf_op jit(solution)/shard_map/ppermute | solution.py:356
  45.6 1.5 %collective-permute-start.14 = (f32[2,128,128]{2,1,0:T(8,128)S(1)}, f32[2,128,128]{2,1,0:T(8,128)S(1)}, u32[]{:S(2)}, u32[]{:S(2)}) collective-permute-start(f32[2,128,128]{2,1,0:T(8,128)S(1)} %get-tuple-element.92.refs_5_), channel_id=1, source_target_pairs={{28,24},{24,28},{20,16},{16,20},{12,8},{8,12},{4,0},{0,4},{29,25},... | collective-permute-start | bytes 393224 | tf_op jit(solution)/shard_map/ppermute | solution.py:356

commit v6 on v5

--- a/solution.py
+++ b/solution.py
@@ -8,7 +8,7 @@
 from jax.sharding import PartitionSpec as P
 
 HEAD_DIM = 128
-CHUNK = 256
+CHUNK = 128
 VMEM_BYTES = 12 * 2**20
 F32 = jnp.float32
 BF16 = jnp.bfloat16
@@ -33,21 +33,6 @@
 
 def lanes_of(j):
     return slice(j * HEAD_DIM, (j + 1) * HEAD_DIM)
-
-
-def pairs_of(width):
-    return [slice(i, i + 2 * HEAD_DIM) for i in range(0, width, 2 * HEAD_DIM)]
-
-
-def diagonal(first, second):
-    zero = jnp.zeros_like(first)
-    top = jnp.concatenate([first, zero], axis=1)
-    return jnp.concatenate([top, jnp.concatenate([zero, second], axis=1)], axis=0)
-
-
-def diagonals(states):
-    states = [state.astype(BF16) for state in states]
-    return [diagonal(*states[i:i + 2]) for i in range(0, len(states), 2)]
 
 
 def heads_in(pieces):
@@ -125,10 +110,6 @@
     for i, part in enumerate(chunks_of(rows)):
         for copy in copies[2 * i:2 * i + 2]:
             copy.wait()
-        if i:
-            earlier = diagonals([pre_ref[i, j] for j in range(width // HEAD_DIM)])
-            for lanes, states in zip(pairs_of(width), earlier):
-                inner_ref[part, lanes] = dot(q_ref[part, lanes], states)
         for j in range(width // HEAD_DIM):
             lanes = lanes_of(j)
             q, k = q_ref[part, lanes], k_ref[part, lanes]
@@ -136,25 +117,25 @@
             scores = jnp.where(lower(size), dot(q, k, 1, 1), 0.0).astype(BF16)
             turned_ref[j, part] = jnp.where(upper(size), dot(k, q, 1, 1), 0.0).astype(BF16)
             inner = dot(scores, v_ref[part, lanes])
-            inner_ref[part, lanes] = inner_ref[part, lanes] + inner if i else inner
+            inner_ref[part, lanes] = inner + dot(q, pre_ref[i, j]) if i else inner
             scaled_ref[part, lanes] = gain[:, lanes] * og_ref[part, lanes].astype(F32)
             qturned_ref[lanes, part] = q.T
 
 
 def attn_kernel(last, pieces, q_ref, inner_ref, scaled_ref, *refs):
-    states = diagonals(heads_in(refs[:pieces]))
+    states = [state.astype(BF16) for state in heads_in(refs[:pieces])]
     refs = refs[pieces:]
     attn_ref = refs[2] if last else refs[0]
     rows, width = q_ref.shape
     for part in chunks_of(rows):
         square, cross = (refs[0][part], refs[1][part]) if last else (None, None)
-        for lanes, state in zip(pairs_of(width), states):
+        for j, state in enumerate(states):
+            lanes = lanes_of(j)
             attn = inner_ref[part, lanes] + dot(q_ref[part, lanes], state)
             attn_ref[part, lanes] = attn
             more, crossed = attn * attn, scaled_ref[part, lanes] * attn
-            for i in range(2):
-                square = more[:, lanes_of(i)] if square is None else square + more[:, lanes_of(i)]
-                cross = crossed[:, lanes_of(i)] if cross is None else cross + crossed[:, lanes_of(i)]
+            square = more if square is None else square + more
+            cross = crossed if cross is None else cross + crossed
         if last:
             square = jnp.sum(square.T, axis=0, keepdims=True)
             cross = jnp.sum(cross.T, axis=0, keepdims=True)
@@ -207,34 +188,30 @@
 
 
 def local_kernel(same, pieces, q_ref, k_ref, v_ref, g_ref, turned_ref, pre_ref, post_ref, *refs):
-    qgrad_hbm, kpart_ref, vpart_ref, qgrad_ref, out_ref, sems = refs[-6:]
+    qgrad_hbm, kpart_ref, vpart_ref, qgrad_ref, sems = refs[-5:]
     state = heads_in(refs[:pieces])
     rows, width = q_ref.shape
     target = columns(same, width)
     parts = chunks_of(rows)
     copies = []
     for i, part in enumerate(parts):
-        heads = range(width // HEAD_DIM)
-        before = [state[j] + pre_ref[i, j].astype(F32) if i else state[j] for j in heads]
-        for lanes, both in zip(pairs_of(width), diagonals(before)):
-            qgrad_ref[part, lanes] = dot(g_ref[part, lanes], both, 1, 1)
-        last = i == len(parts) - 1
-        if not last:
-            later = diagonals([post_ref[i, j] for j in heads])
-            for lanes, both in zip(pairs_of(width), later):
-                kpart_ref[part, lanes] = dot(v_ref[part, lanes], both, 1, 1)
-                vpart_ref[part, lanes] = dot(k_ref[part, lanes], both)
-        for j in heads:
+        for j in range(width // HEAD_DIM):
             lanes = lanes_of(j)
             q, k, v, g = (ref[part, lanes] for ref in (q_ref, k_ref, v_ref, g_ref))
             size = q.shape[0]
             gscores = jnp.where(lower(size), dot(g, v, 1, 1), 0.0).astype(BF16)
             gturned = jnp.where(upper(size), dot(v, g, 1, 1), 0.0).astype(BF16)
-            kgrad, vgrad = dot(gturned, q), dot(turned_ref[j, part], g)
-            out_ref[part, lanes] = (qgrad_ref[part, lanes] + dot(gscores, k)).astype(BF16)
-            kpart_ref[part, lanes] = kgrad if last else kpart_ref[part, lanes] + kgrad
-            vpart_ref[part, lanes] = vgrad if last else vpart_ref[part, lanes] + vgrad
-        copy = pltpu.make_async_copy(out_ref.at[part], qgrad_hbm.at[part, target], sems.at[i])
+            before = state[j] + pre_ref[i, j].astype(F32) if i else state[j]
+            qgrad = dot(gscores, k) + dot(g, before.astype(BF16), 1, 1)
+            kgrad = dot(gturned, q)
+            vgrad = dot(turned_ref[j, part], g)
+            if i < len(parts) - 1:
+                kgrad = kgrad + dot(v, post_ref[i, j], 1, 1)
+                vgrad = vgrad + dot(k, post_ref[i, j])
+            qgrad_ref[part, lanes] = qgrad.astype(BF16)
+            kpart_ref[part, lanes] = kgrad
+            vpart_ref[part, lanes] = vgrad
+        copy = pltpu.make_async_copy(qgrad_ref.at[part], qgrad_hbm.at[part, target], sems.at[i])
         copy.start()
         copies.append(copy)
     for copy in copies:
@@ -242,7 +219,8 @@
 
 
 def final_parts(k_ref, v_ref, kpart_ref, vpart_ref, states, kgrad_ref, vgrad_ref, part):
-    for lanes, state in zip(pairs_of(k_ref.shape[1]), states):
+    for j, state in enumerate(states):
+        lanes = lanes_of(j)
         kgrad = kpart_ref[part, lanes] + dot(v_ref[part, lanes], state, 1, 1)
         vgrad = vpart_ref[part, lanes] + dot(k_ref[part, lanes], state)
         kgrad_ref[part, lanes] = kgrad.astype(BF16)
@@ -250,13 +228,13 @@
 
 
 def near_kernel(pieces, *refs):
-    states = diagonals(heads_in(refs[4:4 + pieces]))
+    states = [state.astype(BF16) for state in heads_in(refs[4:4 + pieces])]
     for part in chunks_of(refs[0].shape[0]):
         final_parts(*refs[:4], states, *refs[4 + pieces:], part)
 
 
 def last_kernel(same, pieces, *refs):
-    states = diagonals(heads_in(refs[4:4 + pieces]))
+    states = [state.astype(BF16) for state in heads_in(refs[4:4 + pieces])]
     kdone_ref, vdone_ref, kgrad_hbm, vgrad_hbm, kgrad_ref, vgrad_ref, sems = refs[4 + pieces:]
     rows, width = kgrad_ref.shape
     copies = []
@@ -443,7 +421,7 @@
                 partial(local_kernel, same, count), 9 * unit,
                 [VMEM] * len(args) + [ANYWHERE] * len(messages) + [HBM] * len(qgrads),
                 [HBM, VMEM, VMEM], [whole, wide, wide], (*args, *more),
-                [pltpu.VMEM((rows, half), F32), pltpu.VMEM((rows, half), BF16), sems],
+                [pltpu.VMEM((rows, half), BF16), sems],
                 {len(args) + len(messages): 0} if qgrads else None,
             )
             qgrads[:] = [qgrad]

time: 49.3 us -> 52.5 us (1.065)
  Pallas kernels: 25.3 us -> 29.7 us
  starting transfers between devices: 16.2 us -> 15.3 us
    pallas_call x24, Pallas kernels: 25.3 us -> 29.7 us  [run(): pl.pallas_call(kernel, in_specs=in_specs, out_specs=out_specs, out_shape=...]
    ppermute x14, starting transfers between devices: 11.7 us -> 10.9 us  [move(): return lax.ppermute(value, 'seq', pairs)]
  transfers between devices with their start and end apart: 17 -> 17, of which waited for: 8 -> 7; matrix products, arithmetic and copies ran while one was open for 0% -> 0% of each run, Pallas kernels for 41% -> 45%
where the time goes in v6:
time: 52.5 us; the launch traced here: 52.3 us
  Pallas kernels  29.7 us (57%)
  starting transfers between devices  15.3 us (29%)
  waiting for transfers between devices  6.23 us (12%)
  between operations  1.03 us (2%)
    pallas_call x24, Pallas kernels, run(): pl.pallas_call(kernel, in_specs=in_specs, out_specs=out_specs, out_shape=...  29.7 us
    ppermute x14, starting transfers between devices, move(): return lax.ppermute(value, 'seq', pairs)  10.9 us
    ppermute x3, starting transfers between devices, shards(): lax.ppermute(sums, 'head', [(r, r ^ other) for r in range(peers)])  4.45 us
    ppermute x3, waiting for transfers between devices, shards(): lax.ppermute(sums, 'head', [(r, r ^ other) for r in range(peers)])  3.99 us
    ppermute x14, waiting for transfers between devices, move(): return lax.ppermute(value, 'seq', pairs)  2.23 us
  transfers between devices with their start and end apart: 17, of which 7 were waited for; matrix products, arithmetic and copies ran while one was open for 0% of the time, Pallas kernels for 45%

profile of v6, /device:TPU:0, one launch (start us, length us, event | category | flops | bytes accessed | tf_op | source)
XLA Modules:
  0.0 52.3 jit_solution(17711608614612227765)
XLA Ops:
  0.6 2.4 %shard_map.77 = (bf16[768,512]{1,0:T(8,128)(2,1)S(1)}, bf16[768,512]{1,0:T(8,128)(2,1)S(1)}, f32[4,128,128]{2,1,0:T(8,128)S(1)}, bf16[6,4,128,128]{3,2,1,0:T(8,128)(2,1)S(1)}) custom-call(bf16[768,1024]{1,0:T(8,128)(2,1)} %k_hbm.3, bf16[768,1024]{1,0:T(8,128)(2,1)} %v_hbm.3), custom_call_target="tpu_custom_call" | custom-call | flops 100663296 | bytes 3145728 | tf_op jit(solution)/shard_map/pallas_call | solution.py:54
  3.1 0.5 collective-permute-start
  3.6 2.4 %shard_map.76 = (bf16[768,512]{1,0:T(8,128)(2,1)S(1)}, bf16[768,512]{1,0:T(8,128)(2,1)S(1)}, f32[4,128,128]{2,1,0:T(8,128)S(1)}, bf16[6,4,128,128]{3,2,1,0:T(8,128)(2,1)S(1)}) custom-call(bf16[768,1024]{1,0:T(8,128)(2,1)} %k_hbm.3, bf16[768,1024]{1,0:T(8,128)(2,1)} %v_hbm.3), custom_call_target="tpu_custom_call" | custom-call | flops 100663296 | bytes 3145728 | tf_op jit(solution)/shard_map/pallas_call | solution.py:54
  6.0 2.6 %collective-permute-start.1 = (f32[2,128,128]{2,1,0:T(8,128)S(1)}, f32[2,128,128]{2,1,0:T(8,128)S(1)}, u32[]{:S(2)}, u32[]{:S(2)}) collective-permute-start(f32[2,128,128]{2,1,0:T(8,128)S(1)} %shard_map.78.refs_2_.refs_0_), channel_id=1, source_target_pairs={{0,8},{4,20},{8,0},{12,28},{16,24},{20,4},{24,16},{28,12},{1,9},{5... | collective-permute-start | bytes 393224 | tf_op jit(solution)/shard_map/ppermute | solution.py:334
  8.7 4.4 %shard_map.80 = (bf16[768,512]{1,0:T(8,128)(2,1)S(1)}, f32[768,512]{1,0:T(8,128)S(1)}, f32[768,512]{1,0:T(8,128)S(1)}, bf16[512,768]{1,0:T(8,128)(2,1)S(1)}, bf16[4,768,128]{2,1,0:T(8,128)(2,1)S(1)}) custom-call(bf16[768,1024]{1,0:T(8,128)(2,1)} %q_hbm.3, bf16[768,1024]{1,0:T(8,128)(2,1)} %og_hbm.3, bf16[768,512]{1,0:T(8,128)(2,1)S(1)} %get-tuple-element.52.k_ref.refs_0_, ...), custom_call_target="tpu_custom_call" | custom-call | flops 603979776 | bytes 5771264 | tf_op jit(solution)/shard_map/pallas_call | solution.py:54
  13.2 2.1 %collective-permute-start.3 = (f32[2,128,128]{2,1,0:T(8,128)S(1)}, f32[2,128,128]{2,1,0:T(8,128)S(1)}, u32[]{:S(2)}, u32[]{:S(2)}) collective-permute-start(f32[2,128,128]{2,1,0:T(8,128)S(1)} %shard_map.81.refs_4_.refs_0_), channel_id=1, source_target_pairs={{0,16},{4,12},{8,24},{12,4},{16,0},{20,28},{24,8},{28,20},{1,17},{... | collective-permute-start | bytes 393224 | tf_op jit(solution)/shard_map/ppermute | solution.py:334
  15.4 4.4 %shard_map.83 = (bf16[768,512]{1,0:T(8,128)(2,1)S(1)}, f32[768,512]{1,0:T(8,128)S(1)}, f32[768,512]{1,0:T(8,128)S(1)}, bf16[512,768]{1,0:T(8,128)(2,1)S(1)}, bf16[4,768,128]{2,1,0:T(8,128)(2,1)S(1)}) custom-call(bf16[768,1024]{1,0:T(8,128)(2,1)} %q_hbm.3, bf16[768,1024]{1,0:T(8,128)(2,1)} %og_hbm.3, bf16[768,512]{1,0:T(8,128)(2,1)S(1)} %get-tuple-element.58.k_ref.refs_0_, ...), custom_call_target="tpu_custom_call" | custom-call | flops 603979776 | bytes 5771264 | tf_op jit(solution)/shard_map/pallas_call | solution.py:54
  20.5 0.5 collective-permute-start.4
  22.0 0.7 %shard_map.87 = (f32[768,512]{1,0:T(8,128)S(1)}, f32[8,768]{1,0:T(8,128)S(1)}) custom-call(bf16[768,512]{1,0:T(8,128)(2,1)S(1)} %get-tuple-element.62.q_ref, f32[768,512]{1,0:T(8,128)S(1)} %get-tuple-element.63.inner_ref, f32[768,512]{1,0:T(8,128)S(1)} %get-tuple-element.64.scaled_ref.refs_3_, f32[2,128,128]{2,1,0:T(8,128)S(1)} %collective-permute-done.4.refs_0_, ...), custom_call_target="tpu_custom_call" | custom-call | flops 100663296 | bytes 4980736 | tf_op jit(solution)/shard_map/pallas_call | solution.py:54
  22.7 3.7 %collective-permute-start.9 = (f32[8,768]{1,0:T(8,128)S(1)}, f32[8,768]{1,0:T(8,128)S(1)}, u32[]{:S(2)}, u32[]{:S(2)}) collective-permute-start(f32[8,768]{1,0:T(8,128)S(1)} %get-tuple-element.74.refs_0_), channel_id=1, source_target_pairs={{0,3},{1,2},{2,1},{3,0},{4,7},{5,6},{6,5},{7,4},{8,11},{9,10},{10,... | collective-permute-start | bytes 73736 | tf_op jit(solution)/shard_map/ppermute | solution.py:400
  26.5 0.7 %collective-permute-start.7 = (f32[8,768]{1,0:T(8,128)S(1)}, f32[8,768]{1,0:T(8,128)S(1)}, u32[]{:S(2)}, u32[]{:S(2)}) collective-permute-start(f32[8,768]{1,0:T(8,128)S(1)} %get-tuple-element.74.refs_0_), channel_id=1, source_target_pairs={{0,1},{1,0},{2,3},{3,2},{4,5},{5,4},{6,7},{7,6},{8,9},{9,8},{10,11... | collective-permute-start | bytes 73736 | tf_op jit(solution)/shard_map/ppermute | solution.py:400
  27.2 1.2 %collective-permute-done.9.refs_3_ = f32[8,768]{1,0:T(8,128)S(1)} collective-permute-done((f32[8,768]{1,0:T(8,128)S(1)}, f32[8,768]{1,0:T(8,128)S(1)}, u32[]{:S(2)}, u32[]{:S(2)}) %collective-permute-start.9) | collective-permute-done | bytes 24608 | tf_op jit(solution)/shard_map/ppermute | solution.py:400
  28.4 2.8 %collective-permute-done.8.refs_2_ = f32[8,768]{1,0:T(8,128)S(1)} collective-permute-done((f32[8,768]{1,0:T(8,128)S(1)}, f32[8,768]{1,0:T(8,128)S(1)}, u32[]{:S(2)}, u32[]{:S(2)}) %collective-permute-start.8) | collective-permute-done | bytes 24608 | tf_op jit(solution)/shard_map/ppermute | solution.py:400
  31.2 0.9 %shard_map.88 = (bf16[768,512]{1,0:T(8,128)(2,1)S(1)}, f32[4,128,128]{2,1,0:T(8,128)S(1)}, bf16[6,4,128,128]{3,2,1,0:T(8,128)(2,1)S(1)}, f32[768,128]{1,0:T(8,128)S(1)}, f32[768,128]{1,0:T(8,128)S(1)}) custom-call(f32[8,768]{1,0:T(8,128)S(1)} %get-tuple-element.74.refs_0_, f32[8,768]{1,0:T(8,128)S(1)} %collective-permute-done.7.refs_1_, ...), custom_call_target="tpu_custom_call" | custom-call | flops 100663296 | bytes 4030464 | tf_op jit(solution)/shard_map/pallas_call | solution.py:54
  32.2 0.6 %shard_map.89 = (bf16[768,512]{1,0:T(8,128)(2,1)S(1)}, f32[4,128,128]{2,1,0:T(8,128)S(1)}, bf16[6,4,128,128]{3,2,1,0:T(8,128)(2,1)S(1)}) custom-call(f32[768,128]{1,0:T(8,128)S(1)} %get-tuple-element.79.refs_0_, f32[768,128]{1,0:T(8,128)S(1)} %get-tuple-element.80.refs_1_, f32[768,512]{1,0:T(8,128)S(1)} %get-tuple-element.81.refs_2_, ...), custom_call_target="tpu_custom_call" | custom-call | flops 100663296 | bytes 4718592 | tf_op jit(solution)/shard_map/pallas_call | solution.py:54
  32.7 1.0 %collective-permute-done.10.refs_1_ = f32[4,128,128]{2,1,0:T(8,128)S(1)} collective-permute-done((f32[4,128,128]{2,1,0:T(8,128)S(1)}, f32[4,128,128]{2,1,0:T(8,128)S(1)}, u32[]{:S(2)}, u32[]{:S(2)}) %collective-permute-start.10) | collective-permute-done | bytes 262176 | tf_op jit(solution)/shard_map/ppermute | solution.py:334
  33.7 1.6 %collective-permute-start.11 = (f32[2,128,128]{2,1,0:T(8,128)S(1)}, f32[2,128,128]{2,1,0:T(8,128)S(1)}, u32[]{:S(2)}, u32[]{:S(2)}) collective-permute-start(f32[2,128,128]{2,1,0:T(8,128)S(1)} %shard_map.90.refs_2_), channel_id=1, source_target_pairs={{28,20},{24,8},{20,28},{16,0},{12,4},{8,24},{4,12},{0,16},{29,21},... | collective-permute-start | bytes 393224 | tf_op jit(solution)/shard_map/ppermute | solution.py:334
  35.3 0.6 %collective-permute-start.12 = (f32[2,128,128]{2,1,0:T(8,128)S(1)}, f32[2,128,128]{2,1,0:T(8,128)S(1)}, u32[]{:S(2)}, u32[]{:S(2)}) collective-permute-start(f32[2,128,128]{2,1,0:T(8,128)S(1)} %shard_map.91.refs_3_), channel_id=1, source_target_pairs={{28,20},{24,8},{20,28},{16,0},{12,4},{8,24},{4,12},{0,16},{29,21},... | collective-permute-start | bytes 393224 | tf_op jit(solution)/shard_map/ppermute | solution.py:334
  35.9 5.1 %shard_map.92 = (bf16[768,1024]{1,0:T(8,128)(2,1)}, f32[768,512]{1,0:T(8,128)S(1)}, f32[768,512]{1,0:T(8,128)S(1)}) custom-call(bf16[768,512]{1,0:T(8,128)(2,1)S(1)} %get-tuple-element.62.q_ref, bf16[768,512]{1,0:T(8,128)(2,1)S(1)} %get-tuple-element.58.k_ref.refs_0_, bf16[768,512]{1,0:T(8,128)(2,1)S(1)} %get-tuple-element.59.v_ref.refs_1_, ...), custom_call_target="tpu_custom_call" | custom-call | flops 905969664 | bytes 6029312 | tf_op jit(solution)/shard_map/pallas_call | solution.py:54
  41.1 1.6 %collective-permute-start.13 = (f32[2,128,128]{2,1,0:T(8,128)S(1)}, f32[2,128,128]{2,1,0:T(8,128)S(1)}, u32[]{:S(2)}, u32[]{:S(2)}) collective-permute-start(f32[2,128,128]{2,1,0:T(8,128)S(1)} %shard_map.93.refs_4_.refs_2_), channel_id=1, source_target_pairs={{28,12},{24,16},{20,4},{16,24},{12,28},{8,0},{4,20},{0,8},{29,13},... | collective-permute-start | bytes 393224 | tf_op jit(solution)/shard_map/ppermute | solution.py:334
  42.7 0.6 %collective-permute-start.15 = (f32[2,128,128]{2,1,0:T(8,128)S(1)}, f32[2,128,128]{2,1,0:T(8,128)S(1)}, u32[]{:S(2)}, u32[]{:S(2)}) collective-permute-start(f32[2,128,128]{2,1,0:T(8,128)S(1)} %shard_map.94.refs_3_), channel_id=1, source_target_pairs={{28,12},{24,16},{20,4},{16,24},{12,28},{8,0},{4,20},{0,8},{29,13},... | collective-permute-start | bytes 393224 | tf_op jit(solution)/shard_map/ppermute | solution.py:334
  43.3 5.3 %shard_map.95 = (bf16[768,1024]{1,0:T(8,128)(2,1)}, f32[768,512]{1,0:T(8,128)S(1)}, f32[768,512]{1,0:T(8,128)S(1)}) custom-call(bf16[768,512]{1,0:T(8,128)(2,1)S(1)} %get-tuple-element.57.q_ref, bf16[768,512]{1,0:T(8,128)(2,1)S(1)} %get-tuple-element.52.k_ref.refs_0_, ...), custom_call_target="tpu_custom_call", output_to_operand_aliasing={{0}: (11, {})} | custom-call | flops 905969664 | bytes 7602176 | tf_op jit(solution)/shard_map/pallas_call | solution.py:54
  49.3 0.8 %shard_map.98 = (bf16[768,512]{1,0:T(8,128)(2,1)S(1)}, bf16[768,512]{1,0:T(8,128)(2,1)S(1)}) custom-call(bf16[768,512]{1,0:T(8,128)(2,1)S(1)} %get-tuple-element.58.k_ref.refs_0_, bf16[768,512]{1,0:T(8,128)(2,1)S(1)} %get-tuple-element.59.v_ref.refs_1_, f32[768,512]{1,0:T(8,128)S(1)} %get-tuple-element.94.refs_2_, f32[768,512]{1,0:T(8,128)S(1)} %get-tuple-element.87.refs_3_, ...), custom_call_target="tpu_custom_call" | custom-call | flops 201326592 | bytes 4980736 | tf_op jit(solution)/shard_map/pallas_call | solution.py:54
  50.3 1.8 %shard_map.99 = (bf16[768,1024]{1,0:T(8,128)(2,1)}, bf16[768,1024]{1,0:T(8,128)(2,1)}) custom-call(bf16[768,512]{1,0:T(8,128)(2,1)S(1)} %get-tuple-element.52.k_ref.refs_0_, bf16[768,512]{1,0:T(8,128)(2,1)S(1)} %get-tuple-element.53.v_ref.refs_1_, f32[768,512]{1,0:T(8,128)S(1)} %get-tuple-element.90.refs_2_, ...), custom_call_target="tpu_custom_call" | custom-call | flops 201326592 | bytes 6553600 | tf_op jit(solution)/shard_map/pallas_call | solution.py:54
  (36 shorter events, 3.1 us)
Async XLA Ops:
  3.1 5.7 %copy-start = (f32[1024]{0:T(1024)S(1)}, f32[1024]{0:T(1024)}, u32[]{:S(2)}) copy-start(f32[1024]{0:T(1024)} %param.9) | copy-start | bytes 12292
  3.1 2.9 %collective-permute-start = (f32[4,128,128]{2,1,0:T(8,128)S(1)}, f32[4,128,128]{2,1,0:T(8,128)S(1)}, u32[]{:S(2)}, u32[]{:S(2)}) collective-permute-start(f32[4,128,128]{2,1,0:T(8,128)S(1)} %get-tuple-element.56), channel_id=1, source_target_pairs={{0,4},{4,0},{8,12},{12,8},{16,20},{20,16},{24,28},{28,24},{1,5},{5... | collective-permute-start | bytes 786440 | tf_op jit(solution)/shard_map/ppermute | solution.py:334
  6.0 7.1 %collective-permute-start.1 = (f32[2,128,128]{2,1,0:T(8,128)S(1)}, f32[2,128,128]{2,1,0:T(8,128)S(1)}, u32[]{:S(2)}, u32[]{:S(2)}) collective-permute-start(f32[2,128,128]{2,1,0:T(8,128)S(1)} %shard_map.78.refs_2_.refs_0_), channel_id=1, source_target_pairs={{0,8},{4,20},{8,0},{12,28},{16,24},{20,4},{24,16},{28,12},{1,9},{5... | collective-permute-start | bytes 393224 | tf_op jit(solution)/shard_map/ppermute | solution.py:334
  8.6 6.7 %collective-permute-start.2 = (f32[2,128,128]{2,1,0:T(8,128)S(1)}, f32[2,128,128]{2,1,0:T(8,128)S(1)}, u32[]{:S(2)}, u32[]{:S(2)}) collective-permute-start(f32[2,128,128]{2,1,0:T(8,128)S(1)} %shard_map.79.refs_1_), channel_id=1, source_target_pairs={{0,8},{4,20},{8,0},{12,28},{16,24},{20,4},{24,16},{28,12},{1,9},{5... | collective-permute-start | bytes 393224 | tf_op jit(solution)/shard_map/ppermute | solution.py:334
  13.2 6.6 %collective-permute-start.3 = (f32[2,128,128]{2,1,0:T(8,128)S(1)}, f32[2,128,128]{2,1,0:T(8,128)S(1)}, u32[]{:S(2)}, u32[]{:S(2)}) collective-permute-start(f32[2,128,128]{2,1,0:T(8,128)S(1)} %shard_map.81.refs_4_.refs_0_), channel_id=1, source_target_pairs={{0,16},{4,12},{8,24},{12,4},{16,0},{20,28},{24,8},{28,20},{1,17},{... | collective-permute-start | bytes 393224 | tf_op jit(solution)/shard_map/ppermute | solution.py:334
  15.4 5.0 %collective-permute-start.5 = (f32[2,128,128]{2,1,0:T(8,128)S(1)}, f32[2,128,128]{2,1,0:T(8,128)S(1)}, u32[]{:S(2)}, u32[]{:S(2)}) collective-permute-start(f32[2,128,128]{2,1,0:T(8,128)S(1)} %shard_map.82.refs_1_), channel_id=1, source_target_pairs={{0,16},{4,12},{8,24},{12,4},{16,0},{20,28},{24,8},{28,20},{1,17},{... | collective-permute-start | bytes 393224 | tf_op jit(solution)/shard_map/ppermute | solution.py:334
  20.4 1.4 %collective-permute-start.6 = (f32[2,128,128]{2,1,0:T(8,128)S(1)}, f32[2,128,128]{2,1,0:T(8,128)S(1)}, u32[]{:S(2)}, u32[]{:S(2)}) collective-permute-start(f32[2,128,128]{2,1,0:T(8,128)S(1)} %get-tuple-element.67), channel_id=1, source_target_pairs={{0,4},{4,0},{8,12},{12,8},{16,20},{20,16},{24,28},{28,24},{1,5},{5... | collective-permute-start | bytes 393224 | tf_op jit(solution)/shard_map/ppermute | solution.py:334
  20.5 1.5 %collective-permute-start.4 = (f32[2,128,128]{2,1,0:T(8,128)S(1)}, f32[2,128,128]{2,1,0:T(8,128)S(1)}, u32[]{:S(2)}, u32[]{:S(2)}) collective-permute-start(f32[2,128,128]{2,1,0:T(8,128)S(1)} %get-tuple-element.66.refs_5_), channel_id=1, source_target_pairs={{0,4},{4,0},{8,12},{12,8},{16,20},{20,16},{24,28},{28,24},{1,5},{5... | collective-permute-start | bytes 393224 | tf_op jit(solution)/shard_map/ppermute | solution.py:334
  22.7 5.7 %collective-permute-start.9 = (f32[8,768]{1,0:T(8,128)S(1)}, f32[8,768]{1,0:T(8,128)S(1)}, u32[]{:S(2)}, u32[]{:S(2)}) collective-permute-start(f32[8,768]{1,0:T(8,128)S(1)} %get-tuple-element.74.refs_0_), channel_id=1, source_target_pairs={{0,3},{1,2},{2,1},{3,0},{4,7},{5,6},{6,5},{7,4},{8,11},{9,10},{10,... | collective-permute-start | bytes 73736 | tf_op jit(solution)/shard_map/ppermute | solution.py:400
  26.5 4.7 %collective-permute-start.8 = (f32[8,768]{1,0:T(8,128)S(1)}, f32[8,768]{1,0:T(8,128)S(1)}, u32[]{:S(2)}, u32[]{:S(2)}) collective-permute-start(f32[8,768]{1,0:T(8,128)S(1)} %get-tuple-element.74.refs_0_), channel_id=1, source_target_pairs={{0,2},{1,3},{2,0},{3,1},{4,6},{5,7},{6,4},{7,5},{8,10},{9,11},{10,... | collective-permute-start | bytes 73736 | tf_op jit(solution)/shard_map/ppermute | solution.py:400
  26.5 4.7 %collective-permute-start.7 = (f32[8,768]{1,0:T(8,128)S(1)}, f32[8,768]{1,0:T(8,128)S(1)}, u32[]{:S(2)}, u32[]{:S(2)}) collective-permute-start(f32[8,768]{1,0:T(8,128)S(1)} %get-tuple-element.74.refs_0_), channel_id=1, source_target_pairs={{0,1},{1,0},{2,3},{3,2},{4,5},{5,4},{6,7},{7,6},{8,9},{9,8},{10,11... | collective-permute-start | bytes 73736 | tf_op jit(solution)/shard_map/ppermute | solution.py:400
  32.1 1.6 %collective-permute-start.10 = (f32[4,128,128]{2,1,0:T(8,128)S(1)}, f32[4,128,128]{2,1,0:T(8,128)S(1)}, u32[]{:S(2)}, u32[]{:S(2)}) collective-permute-start(f32[4,128,128]{2,1,0:T(8,128)S(1)} %get-tuple-element.84), channel_id=1, source_target_pairs={{28,24},{24,28},{20,16},{16,20},{12,8},{8,12},{4,0},{0,4},{29,25},... | collective-permute-start | bytes 786440 | tf_op jit(solution)/shard_map/ppermute | solution.py:334
  33.7 7.3 %collective-permute-start.11 = (f32[2,128,128]{2,1,0:T(8,128)S(1)}, f32[2,128,128]{2,1,0:T(8,128)S(1)}, u32[]{:S(2)}, u32[]{:S(2)}) collective-permute-start(f32[2,128,128]{2,1,0:T(8,128)S(1)} %shard_map.90.refs_2_), channel_id=1, source_target_pairs={{28,20},{24,8},{20,28},{16,0},{12,4},{8,24},{4,12},{0,16},{29,21},... | collective-permute-start | bytes 393224 | tf_op jit(solution)/shard_map/ppermute | solution.py:334
  35.3 7.3 %collective-permute-start.12 = (f32[2,128,128]{2,1,0:T(8,128)S(1)}, f32[2,128,128]{2,1,0:T(8,128)S(1)}, u32[]{:S(2)}, u32[]{:S(2)}) collective-permute-start(f32[2,128,128]{2,1,0:T(8,128)S(1)} %shard_map.91.refs_3_), channel_id=1, source_target_pairs={{28,20},{24,8},{20,28},{16,0},{12,4},{8,24},{4,12},{0,16},{29,21},... | collective-permute-start | bytes 393224 | tf_op jit(solution)/shard_map/ppermute | solution.py:334
  41.1 7.5 %collective-permute-start.13 = (f32[2,128,128]{2,1,0:T(8,128)S(1)}, f32[2,128,128]{2,1,0:T(8,128)S(1)}, u32[]{:S(2)}, u32[]{:S(2)}) collective-permute-start(f32[2,128,128]{2,1,0:T(8,128)S(1)} %shard_map.93.refs_4_.refs_2_), channel_id=1, source_target_pairs={{28,12},{24,16},{20,4},{16,24},{12,28},{8,0},{4,20},{0,8},{29,13},... | collective-permute-start | bytes 393224 | tf_op jit(solution)/shard_map/ppermute | solution.py:334
  42.7 6.0 %collective-permute-start.15 = (f32[2,128,128]{2,1,0:T(8,128)S(1)}, f32[2,128,128]{2,1,0:T(8,128)S(1)}, u32[]{:S(2)}, u32[]{:S(2)}) collective-permute-start(f32[2,128,128]{2,1,0:T(8,128)S(1)} %shard_map.94.refs_3_), channel_id=1, source_target_pairs={{28,12},{24,16},{20,4},{16,24},{12,28},{8,0},{4,20},{0,8},{29,13},... | collective-permute-start | bytes 393224 | tf_op jit(solution)/shard_map/ppermute | solution.py:334
  48.7 1.4 %collective-permute-start.16 = (f32[2,128,128]{2,1,0:T(8,128)S(1)}, f32[2,128,128]{2,1,0:T(8,128)S(1)}, u32[]{:S(2)}, u32[]{:S(2)}) collective-permute-start(f32[2,128,128]{2,1,0:T(8,128)S(1)} %get-tuple-element.93), channel_id=1, source_target_pairs={{28,24},{24,28},{20,16},{16,20},{12,8},{8,12},{4,0},{0,4},{29,25},... | collective-permute-start | bytes 393224 | tf_op jit(solution)/shard_map/ppermute | solution.py:334
  48.8 1.5 %collective-permute-start.14 = (f32[2,128,128]{2,1,0:T(8,128)S(1)}, f32[2,128,128]{2,1,0:T(8,128)S(1)}, u32[]{:S(2)}, u32[]{:S(2)}) collective-permute-start(f32[2,128,128]{2,1,0:T(8,128)S(1)} %get-tuple-element.92.refs_5_), channel_id=1, source_target_pairs={{28,24},{24,28},{20,16},{16,20},{12,8},{8,12},{4,0},{0,4},{29,25},... | collective-permute-start | bytes 393224 | tf_op jit(solution)/shard_map/ppermute | solution.py:334

commit v7 on v6

--- a/solution.py
+++ b/solution.py
@@ -8,7 +8,7 @@
 from jax.sharding import PartitionSpec as P
 
 HEAD_DIM = 128
-CHUNK = 128
+CHUNK = 256
 VMEM_BYTES = 12 * 2**20
 F32 = jnp.float32
 BF16 = jnp.bfloat16
@@ -80,10 +80,7 @@
     return copies
 
 
-def state_kernel(same, k_hbm, v_hbm, k_ref, v_ref, sum_ref, pre_ref, sems):
-    copies = fetches((k_hbm, v_hbm), (k_ref, v_ref), sems, same)
-    for copy in copies:
-        copy.start()
+def sum_states(k_ref, v_ref, sum_ref, pre_ref, copies=()):
     heads = sum_ref.shape[0]
     totals = [None] * heads
     for i, part in enumerate(chunks_of(k_ref.shape[0])):
@@ -98,6 +95,16 @@
             totals[j] = totals[j] + term if i else term
     for j in range(heads):
         sum_ref[j] = totals[j]
+
+
+def first_kernel(k_hbm, v_hbm, k1, v1, k2, v2, sum_ref, pre_ref, sems1, sems2):
+    now = fetches((k_hbm, v_hbm), (k1, v1), sems1, False)
+    later = fetches((k_hbm, v_hbm), (k2, v2), sems2, True)
+    for copy in now + later:
+        copy.start()
+    sum_states(k1, v1, sum_ref, pre_ref, now)
+    for copy in later:
+        copy.wait()
 
 
 def inner_kernel(same, q_hbm, og_hbm, k_ref, v_ref, gain_ref, pre_ref, *refs):
@@ -194,26 +201,40 @@
     target = columns(same, width)
     parts = chunks_of(rows)
     copies = []
-    for i, part in enumerate(parts):
-        for j in range(width // HEAD_DIM):
-            lanes = lanes_of(j)
-            q, k, v, g = (ref[part, lanes] for ref in (q_ref, k_ref, v_ref, g_ref))
-            size = q.shape[0]
-            gscores = jnp.where(lower(size), dot(g, v, 1, 1), 0.0).astype(BF16)
-            gturned = jnp.where(upper(size), dot(v, g, 1, 1), 0.0).astype(BF16)
-            before = state[j] + pre_ref[i, j].astype(F32) if i else state[j]
-            qgrad = dot(gscores, k) + dot(g, before.astype(BF16), 1, 1)
-            kgrad = dot(gturned, q)
-            vgrad = dot(turned_ref[j, part], g)
-            if i < len(parts) - 1:
-                kgrad = kgrad + dot(v, post_ref[i, j], 1, 1)
-                vgrad = vgrad + dot(k, post_ref[i, j])
-            qgrad_ref[part, lanes] = qgrad.astype(BF16)
-            kpart_ref[part, lanes] = kgrad
-            vpart_ref[part, lanes] = vgrad
-        copy = pltpu.make_async_copy(qgrad_ref.at[part], qgrad_hbm.at[part, target], sems.at[i])
-        copy.start()
-        copies.append(copy)
+
+    def scores(i, j):
+        part, lanes = parts[i], lanes_of(j)
+        v, g = v_ref[part, lanes], g_ref[part, lanes]
+        size = g.shape[0]
+        gscores = jnp.where(lower(size), dot(g, v, 1, 1), 0.0).astype(BF16)
+        gturned = jnp.where(upper(size), dot(v, g, 1, 1), 0.0).astype(BF16)
+        return gscores, gturned
+
+    def products(i, j, gscores, gturned):
+        part, lanes = parts[i], lanes_of(j)
+        q, k, v, g = (ref[part, lanes] for ref in (q_ref, k_ref, v_ref, g_ref))
+        before = state[j] + pre_ref[i, j].astype(F32) if i else state[j]
+        qgrad = dot(g, before.astype(BF16), 1, 1) + dot(gscores, k)
+        kgrad = dot(gturned, q)
+        vgrad = dot(turned_ref[j, part], g)
+        if i < len(parts) - 1:
+            kgrad = kgrad + dot(v, post_ref[i, j], 1, 1)
+            vgrad = vgrad + dot(k, post_ref[i, j])
+        qgrad_ref[part, lanes] = qgrad.astype(BF16)
+        kpart_ref[part, lanes] = kgrad
+        vpart_ref[part, lanes] = vgrad
+
+    places = [(i, j) for i in range(len(parts)) for j in range(width // HEAD_DIM)]
+    ready = scores(*places[0])
+    for place, following in zip(places, places[1:] + [None]):
+        coming = scores(*following) if following else None
+        products(*place, *ready)
+        ready = coming
+        i = place[0]
+        if following is None or following[0] != i:
+            source, out = qgrad_ref.at[parts[i]], qgrad_hbm.at[parts[i], target]
+            copies.append(pltpu.make_async_copy(source, out, sems.at[i]))
+            copies[-1].start()
     for copy in copies:
         copy.wait()
 
@@ -359,15 +380,12 @@
     whole = shape((rows, width), BF16)
     sems = pltpu.SemaphoreType.DMA((2 * chunks,))
 
-    def states_of(same):
-        return run(
-            partial(state_kernel, same), unit, [HBM, HBM], [VMEM] * 4, [thin, thin, states, inside],
-            (key_in, value), [sems],
-        )
-
-    k1, v1, send, pre1 = states_of(False)
+    k1, v1, k2, v2, send, pre1 = run(
+        first_kernel, unit, [HBM, HBM], [VMEM] * 6, [thin] * 4 + [states, inside],
+        (key_in, value), [sems, sems],
+    )
     extra = nearby(send, False)
-    k2, v2, keep, pre2 = states_of(True)
+    keep, pre2 = run(sum_states, unit, [VMEM, VMEM], [VMEM] * 2, [states, inside], (k2, v2))
 
     def inner_of(same, k, v, pre):
         return lambda messages: run(

time: 52.5 us -> 47.3 us (0.901)
  Pallas kernels: 29.7 us -> 21.4 us
  waiting for transfers between devices: 6.23 us -> 7.9 us
  starting transfers between devices: 15.3 us -> 16.8 us
    pallas_call x24, Pallas kernels: 29.7 us -> 21.4 us  [run(): pl.pallas_call(kernel, in_specs=in_specs, out_specs=out_specs, out_shape=...]
    ppermute x14, waiting for transfers between devices: 2.23 us -> 3.95 us  [move(): return lax.ppermute(value, 'seq', pairs)]
    ppermute x14, starting transfers between devices: 10.9 us -> 12.4 us  [move(): return lax.ppermute(value, 'seq', pairs)]
  transfers between devices with their start and end apart: 17 -> 17, of which waited for: 7 -> 10; matrix products, arithmetic and copies ran while one was open for 0% -> 0% of each run, Pallas kernels for 45% -> 34%
where the time goes in v7:
time: 47.3 us; the launch traced here: 47.1 us
  Pallas kernels  21.4 us (45%)
  starting transfers between devices  16.8 us (36%)
  waiting for transfers between devices  7.9 us (17%)
  between operations  1 us (2%)
    pallas_call x24, Pallas kernels, run(): pl.pallas_call(kernel, in_specs=in_specs, out_specs=out_specs, out_shape=...  21.4 us
    ppermute x14, starting transfers between devices, move(): return lax.ppermute(value, 'seq', pairs)  12.4 us
    ppermute x3, starting transfers between devices, shards(): lax.ppermute(sums, 'head', [(r, r ^ other) for r in range(peers)])  4.45 us
    ppermute x14, waiting for transfers between devices, move(): return lax.ppermute(value, 'seq', pairs)  3.95 us
    ppermute x3, waiting for transfers between devices, shards(): lax.ppermute(sums, 'head', [(r, r ^ other) for r in range(peers)])  3.94 us
  transfers between devices with their start and end apart: 17, of which 10 were waited for; matrix products, arithmetic and copies ran while one was open for 0% of the time, Pallas kernels for 34%

profile of v7, /device:TPU:0, one launch (start us, length us, event | category | flops | bytes accessed | tf_op | source)
XLA Modules:
  0.0 47.1 jit_solution(1824561149573898246)
XLA Ops:
  0.6 2.1 %shard_map.76 = (bf16[768,512]{1,0:T(8,128)(2,1)S(1)}, bf16[768,512]{1,0:T(8,128)(2,1)S(1)}, bf16[768,512]{1,0:T(8,128)(2,1)S(1)}, bf16[768,512]{1,0:T(8,128)(2,...) custom-call(bf16[768,1024]{1,0:T(8,128)(2,1)} %k_hbm.1, bf16[768,1024]{1,0:T(8,128)(2,1)} %v_hbm.1), custom_call_target="tpu_custom_call" | custom-call | flops 100663296 | bytes 3145728 | tf_op jit(solution)/shard_map/pallas_call | solution.py:54
  3.7 0.7 %collective-permute-done.refs_1_ = f32[4,128,128]{2,1,0:T(8,128)S(1)} collective-permute-done((f32[4,128,128]{2,1,0:T(8,128)S(1)}, f32[4,128,128]{2,1,0:T(8,128)S(1)}, u32[]{:S(2)}, u32[]{:S(2)}) %collective-permute-start) | collective-permute-done | bytes 262176 | tf_op jit(solution)/shard_map/ppermute | solution.py:355
  4.5 2.9 %collective-permute-start.1 = (f32[2,128,128]{2,1,0:T(8,128)S(1)}, f32[2,128,128]{2,1,0:T(8,128)S(1)}, u32[]{:S(2)}, u32[]{:S(2)}) collective-permute-start(f32[2,128,128]{2,1,0:T(8,128)S(1)} %shard_map.78.refs_2_.refs_0_), channel_id=1, source_target_pairs={{0,8},{4,20},{8,0},{12,28},{16,24},{20,4},{24,16},{28,12},{1,9},{5... | collective-permute-start | bytes 393224 | tf_op jit(solution)/shard_map/ppermute | solution.py:355
  7.5 3.3 %shard_map.80 = (bf16[768,512]{1,0:T(8,128)(2,1)S(1)}, f32[768,512]{1,0:T(8,128)S(1)}, f32[768,512]{1,0:T(8,128)S(1)}, bf16[512,768]{1,0:T(8,128)(2,1)S(1)}, bf16[4,768,256]{2,1,0:T(8,128)(2,1)S(1)}) custom-call(bf16[768,1024]{1,0:T(8,128)(2,1)} %q_hbm.3, bf16[768,1024]{1,0:T(8,128)(2,1)} %og_hbm.3, bf16[768,512]{1,0:T(8,128)(2,1)S(1)} %get-tuple-element.52.k_ref.refs_0_, ...), custom_call_target="tpu_custom_call" | custom-call | flops 603979776 | bytes 5378048 | tf_op jit(solution)/shard_map/pallas_call | solution.py:54
  10.9 2.1 %collective-permute-start.3 = (f32[2,128,128]{2,1,0:T(8,128)S(1)}, f32[2,128,128]{2,1,0:T(8,128)S(1)}, u32[]{:S(2)}, u32[]{:S(2)}) collective-permute-start(f32[2,128,128]{2,1,0:T(8,128)S(1)} %shard_map.81.refs_4_.refs_0_), channel_id=1, source_target_pairs={{0,16},{4,12},{8,24},{12,4},{16,0},{20,28},{24,8},{28,20},{1,17},{... | collective-permute-start | bytes 393224 | tf_op jit(solution)/shard_map/ppermute | solution.py:355
  13.1 1.0 %collective-permute-start.5 = (f32[2,128,128]{2,1,0:T(8,128)S(1)}, f32[2,128,128]{2,1,0:T(8,128)S(1)}, u32[]{:S(2)}, u32[]{:S(2)}) collective-permute-start(f32[2,128,128]{2,1,0:T(8,128)S(1)} %shard_map.82.refs_1_), channel_id=1, source_target_pairs={{0,16},{4,12},{8,24},{12,4},{16,0},{20,28},{24,8},{28,20},{1,17},{... | collective-permute-start | bytes 393224 | tf_op jit(solution)/shard_map/ppermute | solution.py:355
  14.1 3.3 %shard_map.83 = (bf16[768,512]{1,0:T(8,128)(2,1)S(1)}, f32[768,512]{1,0:T(8,128)S(1)}, f32[768,512]{1,0:T(8,128)S(1)}, bf16[512,768]{1,0:T(8,128)(2,1)S(1)}, bf16[4,768,256]{2,1,0:T(8,128)(2,1)S(1)}) custom-call(bf16[768,1024]{1,0:T(8,128)(2,1)} %q_hbm.3, bf16[768,1024]{1,0:T(8,128)(2,1)} %og_hbm.3, bf16[768,512]{1,0:T(8,128)(2,1)S(1)} %get-tuple-element.58.k_ref.refs_0_, ...), custom_call_target="tpu_custom_call" | custom-call | flops 603979776 | bytes 5378048 | tf_op jit(solution)/shard_map/pallas_call | solution.py:54
  17.5 0.6 %collective-permute-done.5.refs_3_ = f32[2,128,128]{2,1,0:T(8,128)S(1)} collective-permute-done((f32[2,128,128]{2,1,0:T(8,128)S(1)}, f32[2,128,128]{2,1,0:T(8,128)S(1)}, u32[]{:S(2)}, u32[]{:S(2)}) %collective-permute-start.5) | collective-permute-done | bytes 131104 | tf_op jit(solution)/shard_map/ppermute | solution.py:355
  19.8 0.6 %shard_map.87 = (f32[768,512]{1,0:T(8,128)S(1)}, f32[8,768]{1,0:T(8,128)S(1)}) custom-call(bf16[768,512]{1,0:T(8,128)(2,1)S(1)} %get-tuple-element.62.q_ref, f32[768,512]{1,0:T(8,128)S(1)} %get-tuple-element.63.inner_ref, f32[768,512]{1,0:T(8,128)S(1)} %get-tuple-element.64.scaled_ref.refs_3_, f32[2,128,128]{2,1,0:T(8,128)S(1)} %collective-permute-done.4.refs_0_, ...), custom_call_target="tpu_custom_call" | custom-call | flops 100663296 | bytes 4980736 | tf_op jit(solution)/shard_map/pallas_call | solution.py:54
  20.4 3.7 %collective-permute-start.9 = (f32[8,768]{1,0:T(8,128)S(1)}, f32[8,768]{1,0:T(8,128)S(1)}, u32[]{:S(2)}, u32[]{:S(2)}) collective-permute-start(f32[8,768]{1,0:T(8,128)S(1)} %get-tuple-element.74.refs_0_), channel_id=1, source_target_pairs={{0,3},{1,2},{2,1},{3,0},{4,7},{5,6},{6,5},{7,4},{8,11},{9,10},{10,... | collective-permute-start | bytes 73736 | tf_op jit(solution)/shard_map/ppermute | solution.py:418
  24.1 0.8 %collective-permute-start.7 = (f32[8,768]{1,0:T(8,128)S(1)}, f32[8,768]{1,0:T(8,128)S(1)}, u32[]{:S(2)}, u32[]{:S(2)}) collective-permute-start(f32[8,768]{1,0:T(8,128)S(1)} %get-tuple-element.74.refs_0_), channel_id=1, source_target_pairs={{0,1},{1,0},{2,3},{3,2},{4,5},{5,4},{6,7},{7,6},{8,9},{9,8},{10,11... | collective-permute-start | bytes 73736 | tf_op jit(solution)/shard_map/ppermute | solution.py:418
  24.9 1.2 %collective-permute-done.9.refs_3_ = f32[8,768]{1,0:T(8,128)S(1)} collective-permute-done((f32[8,768]{1,0:T(8,128)S(1)}, f32[8,768]{1,0:T(8,128)S(1)}, u32[]{:S(2)}, u32[]{:S(2)}) %collective-permute-start.9) | collective-permute-done | bytes 24608 | tf_op jit(solution)/shard_map/ppermute | solution.py:418
  26.1 2.7 %collective-permute-done.8.refs_2_ = f32[8,768]{1,0:T(8,128)S(1)} collective-permute-done((f32[8,768]{1,0:T(8,128)S(1)}, f32[8,768]{1,0:T(8,128)S(1)}, u32[]{:S(2)}, u32[]{:S(2)}) %collective-permute-start.8) | collective-permute-done | bytes 24608 | tf_op jit(solution)/shard_map/ppermute | solution.py:418
  28.8 0.9 %shard_map.88 = (bf16[768,512]{1,0:T(8,128)(2,1)S(1)}, f32[4,128,128]{2,1,0:T(8,128)S(1)}, bf16[3,4,128,128]{3,2,1,0:T(8,128)(2,1)S(1)}, f32[768,128]{1,0:T(8,128)S(1)}, f32[768,128]{1,0:T(8,128)S(1)}) custom-call(f32[8,768]{1,0:T(8,128)S(1)} %get-tuple-element.74.refs_0_, f32[8,768]{1,0:T(8,128)S(1)} %collective-permute-done.7.refs_1_, ...), custom_call_target="tpu_custom_call" | custom-call | flops 100663296 | bytes 4030464 | tf_op jit(solution)/shard_map/pallas_call | solution.py:54
  30.2 1.0 %collective-permute-done.10.refs_1_ = f32[4,128,128]{2,1,0:T(8,128)S(1)} collective-permute-done((f32[4,128,128]{2,1,0:T(8,128)S(1)}, f32[4,128,128]{2,1,0:T(8,128)S(1)}, u32[]{:S(2)}, u32[]{:S(2)}) %collective-permute-start.10) | collective-permute-done | bytes 262176 | tf_op jit(solution)/shard_map/ppermute | solution.py:355
  31.3 1.4 %collective-permute-start.11 = (f32[2,128,128]{2,1,0:T(8,128)S(1)}, f32[2,128,128]{2,1,0:T(8,128)S(1)}, u32[]{:S(2)}, u32[]{:S(2)}) collective-permute-start(f32[2,128,128]{2,1,0:T(8,128)S(1)} %shard_map.90.refs_2_), channel_id=1, source_target_pairs={{28,20},{24,8},{20,28},{16,0},{12,4},{8,24},{4,12},{0,16},{29,21},... | collective-permute-start | bytes 393224 | tf_op jit(solution)/shard_map/ppermute | solution.py:355
  32.7 0.8 %collective-permute-start.12 = (f32[2,128,128]{2,1,0:T(8,128)S(1)}, f32[2,128,128]{2,1,0:T(8,128)S(1)}, u32[]{:S(2)}, u32[]{:S(2)}) collective-permute-start(f32[2,128,128]{2,1,0:T(8,128)S(1)} %shard_map.91.refs_3_), channel_id=1, source_target_pairs={{28,20},{24,8},{20,28},{16,0},{12,4},{8,24},{4,12},{0,16},{29,21},... | collective-permute-start | bytes 393224 | tf_op jit(solution)/shard_map/ppermute | solution.py:355
  33.5 3.4 %shard_map.92 = (bf16[768,1024]{1,0:T(8,128)(2,1)}, f32[768,512]{1,0:T(8,128)S(1)}, f32[768,512]{1,0:T(8,128)S(1)}) custom-call(bf16[768,512]{1,0:T(8,128)(2,1)S(1)} %get-tuple-element.62.q_ref, bf16[768,512]{1,0:T(8,128)(2,1)S(1)} %get-tuple-element.58.k_ref.refs_0_, bf16[768,512]{1,0:T(8,128)(2,1)S(1)} %get-tuple-element.59.v_ref.refs_1_, ...), custom_call_target="tpu_custom_call" | custom-call | flops 905969664 | bytes 6029312 | tf_op jit(solution)/shard_map/pallas_call | solution.py:54
  36.9 1.6 %collective-permute-start.13 = (f32[2,128,128]{2,1,0:T(8,128)S(1)}, f32[2,128,128]{2,1,0:T(8,128)S(1)}, u32[]{:S(2)}, u32[]{:S(2)}) collective-permute-start(f32[2,128,128]{2,1,0:T(8,128)S(1)} %shard_map.93.refs_4_.refs_2_), channel_id=1, source_target_pairs={{28,12},{24,16},{20,4},{16,24},{12,28},{8,0},{4,20},{0,8},{29,13},... | collective-permute-start | bytes 393224 | tf_op jit(solution)/shard_map/ppermute | solution.py:355
  38.5 0.8 %collective-permute-start.15 = (f32[2,128,128]{2,1,0:T(8,128)S(1)}, f32[2,128,128]{2,1,0:T(8,128)S(1)}, u32[]{:S(2)}, u32[]{:S(2)}) collective-permute-start(f32[2,128,128]{2,1,0:T(8,128)S(1)} %shard_map.94.refs_3_), channel_id=1, source_target_pairs={{28,12},{24,16},{20,4},{16,24},{12,28},{8,0},{4,20},{0,8},{29,13},... | collective-permute-start | bytes 393224 | tf_op jit(solution)/shard_map/ppermute | solution.py:355
  39.3 3.6 %shard_map.95 = (bf16[768,1024]{1,0:T(8,128)(2,1)}, f32[768,512]{1,0:T(8,128)S(1)}, f32[768,512]{1,0:T(8,128)S(1)}) custom-call(bf16[768,512]{1,0:T(8,128)(2,1)S(1)} %get-tuple-element.57.q_ref, bf16[768,512]{1,0:T(8,128)(2,1)S(1)} %get-tuple-element.52.k_ref.refs_0_, ...), custom_call_target="tpu_custom_call", output_to_operand_aliasing={{0}: (11, {})} | custom-call | flops 905969664 | bytes 7602176 | tf_op jit(solution)/shard_map/pallas_call | solution.py:54
  43.0 0.5 %collective-permute-done.15.refs_3_ = f32[2,128,128]{2,1,0:T(8,128)S(1)} collective-permute-done((f32[2,128,128]{2,1,0:T(8,128)S(1)}, f32[2,128,128]{2,1,0:T(8,128)S(1)}, u32[]{:S(2)}, u32[]{:S(2)}) %collective-permute-start.15) | collective-permute-done | bytes 131104 | tf_op jit(solution)/shard_map/ppermute | solution.py:355
  44.2 0.6 %shard_map.98 = (bf16[768,512]{1,0:T(8,128)(2,1)S(1)}, bf16[768,512]{1,0:T(8,128)(2,1)S(1)}) custom-call(bf16[768,512]{1,0:T(8,128)(2,1)S(1)} %get-tuple-element.58.k_ref.refs_0_, bf16[768,512]{1,0:T(8,128)(2,1)S(1)} %get-tuple-element.59.v_ref.refs_1_, f32[768,512]{1,0:T(8,128)S(1)} %get-tuple-element.94.refs_2_, f32[768,512]{1,0:T(8,128)S(1)} %get-tuple-element.87.refs_3_, ...), custom_call_target="tpu_custom_call" | custom-call | flops 201326592 | bytes 4980736 | tf_op jit(solution)/shard_map/pallas_call | solution.py:54
  45.2 1.7 %shard_map.99 = (bf16[768,1024]{1,0:T(8,128)(2,1)}, bf16[768,1024]{1,0:T(8,128)(2,1)}) custom-call(bf16[768,512]{1,0:T(8,128)(2,1)S(1)} %get-tuple-element.52.k_ref.refs_0_, bf16[768,512]{1,0:T(8,128)(2,1)S(1)} %get-tuple-element.53.v_ref.refs_1_, f32[768,512]{1,0:T(8,128)S(1)} %get-tuple-element.90.refs_2_, ...), custom_call_target="tpu_custom_call" | custom-call | flops 201326592 | bytes 6553600 | tf_op jit(solution)/shard_map/pallas_call | solution.py:54
  (36 shorter events, 4.7 us)
Async XLA Ops:
  2.8 4.8 %copy-start = (f32[1024]{0:T(1024)S(1)}, f32[1024]{0:T(1024)}, u32[]{:S(2)}) copy-start(f32[1024]{0:T(1024)} %param.9) | copy-start | bytes 12292
  2.8 1.7 %collective-permute-start = (f32[4,128,128]{2,1,0:T(8,128)S(1)}, f32[4,128,128]{2,1,0:T(8,128)S(1)}, u32[]{:S(2)}, u32[]{:S(2)}) collective-permute-start(f32[4,128,128]{2,1,0:T(8,128)S(1)} %get-tuple-element.56), channel_id=1, source_target_pairs={{0,4},{4,0},{8,12},{12,8},{16,20},{20,16},{24,28},{28,24},{1,5},{5... | collective-permute-start | bytes 786440 | tf_op jit(solution)/shard_map/ppermute | solution.py:355
  4.5 6.4 %collective-permute-start.1 = (f32[2,128,128]{2,1,0:T(8,128)S(1)}, f32[2,128,128]{2,1,0:T(8,128)S(1)}, u32[]{:S(2)}, u32[]{:S(2)}) collective-permute-start(f32[2,128,128]{2,1,0:T(8,128)S(1)} %shard_map.78.refs_2_.refs_0_), channel_id=1, source_target_pairs={{0,8},{4,20},{8,0},{12,28},{16,24},{20,4},{24,16},{28,12},{1,9},{5... | collective-permute-start | bytes 393224 | tf_op jit(solution)/shard_map/ppermute | solution.py:355
  7.5 5.6 %collective-permute-start.2 = (f32[2,128,128]{2,1,0:T(8,128)S(1)}, f32[2,128,128]{2,1,0:T(8,128)S(1)}, u32[]{:S(2)}, u32[]{:S(2)}) collective-permute-start(f32[2,128,128]{2,1,0:T(8,128)S(1)} %shard_map.79.refs_1_), channel_id=1, source_target_pairs={{0,8},{4,20},{8,0},{12,28},{16,24},{20,4},{24,16},{28,12},{1,9},{5... | collective-permute-start | bytes 393224 | tf_op jit(solution)/shard_map/ppermute | solution.py:355
  10.9 6.5 %collective-permute-start.3 = (f32[2,128,128]{2,1,0:T(8,128)S(1)}, f32[2,128,128]{2,1,0:T(8,128)S(1)}, u32[]{:S(2)}, u32[]{:S(2)}) collective-permute-start(f32[2,128,128]{2,1,0:T(8,128)S(1)} %shard_map.81.refs_4_.refs_0_), channel_id=1, source_target_pairs={{0,16},{4,12},{8,24},{12,4},{16,0},{20,28},{24,8},{28,20},{1,17},{... | collective-permute-start | bytes 393224 | tf_op jit(solution)/shard_map/ppermute | solution.py:355
  13.1 5.0 %collective-permute-start.5 = (f32[2,128,128]{2,1,0:T(8,128)S(1)}, f32[2,128,128]{2,1,0:T(8,128)S(1)}, u32[]{:S(2)}, u32[]{:S(2)}) collective-permute-start(f32[2,128,128]{2,1,0:T(8,128)S(1)} %shard_map.82.refs_1_), channel_id=1, source_target_pairs={{0,16},{4,12},{8,24},{12,4},{16,0},{20,28},{24,8},{28,20},{1,17},{... | collective-permute-start | bytes 393224 | tf_op jit(solution)/shard_map/ppermute | solution.py:355
  18.2 1.4 %collective-permute-start.6 = (f32[2,128,128]{2,1,0:T(8,128)S(1)}, f32[2,128,128]{2,1,0:T(8,128)S(1)}, u32[]{:S(2)}, u32[]{:S(2)}) collective-permute-start(f32[2,128,128]{2,1,0:T(8,128)S(1)} %get-tuple-element.67), channel_id=1, source_target_pairs={{0,4},{4,0},{8,12},{12,8},{16,20},{20,16},{24,28},{28,24},{1,5},{5... | collective-permute-start | bytes 393224 | tf_op jit(solution)/shard_map/ppermute | solution.py:355
  18.2 1.5 %collective-permute-start.4 = (f32[2,128,128]{2,1,0:T(8,128)S(1)}, f32[2,128,128]{2,1,0:T(8,128)S(1)}, u32[]{:S(2)}, u32[]{:S(2)}) collective-permute-start(f32[2,128,128]{2,1,0:T(8,128)S(1)} %get-tuple-element.66.refs_5_), channel_id=1, source_target_pairs={{0,4},{4,0},{8,12},{12,8},{16,20},{20,16},{24,28},{28,24},{1,5},{5... | collective-permute-start | bytes 393224 | tf_op jit(solution)/shard_map/ppermute | solution.py:355
  20.4 5.7 %collective-permute-start.9 = (f32[8,768]{1,0:T(8,128)S(1)}, f32[8,768]{1,0:T(8,128)S(1)}, u32[]{:S(2)}, u32[]{:S(2)}) collective-permute-start(f32[8,768]{1,0:T(8,128)S(1)} %get-tuple-element.74.refs_0_), channel_id=1, source_target_pairs={{0,3},{1,2},{2,1},{3,0},{4,7},{5,6},{6,5},{7,4},{8,11},{9,10},{10,... | collective-permute-start | bytes 73736 | tf_op jit(solution)/shard_map/ppermute | solution.py:418
  24.1 4.7 %collective-permute-start.8 = (f32[8,768]{1,0:T(8,128)S(1)}, f32[8,768]{1,0:T(8,128)S(1)}, u32[]{:S(2)}, u32[]{:S(2)}) collective-permute-start(f32[8,768]{1,0:T(8,128)S(1)} %get-tuple-element.74.refs_0_), channel_id=1, source_target_pairs={{0,2},{1,3},{2,0},{3,1},{4,6},{5,7},{6,4},{7,5},{8,10},{9,11},{10,... | collective-permute-start | bytes 73736 | tf_op jit(solution)/shard_map/ppermute | solution.py:418
  24.1 4.7 %collective-permute-start.7 = (f32[8,768]{1,0:T(8,128)S(1)}, f32[8,768]{1,0:T(8,128)S(1)}, u32[]{:S(2)}, u32[]{:S(2)}) collective-permute-start(f32[8,768]{1,0:T(8,128)S(1)} %get-tuple-element.74.refs_0_), channel_id=1, source_target_pairs={{0,1},{1,0},{2,3},{3,2},{4,5},{5,4},{6,7},{7,6},{8,9},{9,8},{10,11... | collective-permute-start | bytes 73736 | tf_op jit(solution)/shard_map/ppermute | solution.py:418
  29.7 1.6 %collective-permute-start.10 = (f32[4,128,128]{2,1,0:T(8,128)S(1)}, f32[4,128,128]{2,1,0:T(8,128)S(1)}, u32[]{:S(2)}, u32[]{:S(2)}) collective-permute-start(f32[4,128,128]{2,1,0:T(8,128)S(1)} %get-tuple-element.84), channel_id=1, source_target_pairs={{28,24},{24,28},{20,16},{16,20},{12,8},{8,12},{4,0},{0,4},{29,25},... | collective-permute-start | bytes 786440 | tf_op jit(solution)/shard_map/ppermute | solution.py:355
  31.3 5.6 %collective-permute-start.11 = (f32[2,128,128]{2,1,0:T(8,128)S(1)}, f32[2,128,128]{2,1,0:T(8,128)S(1)}, u32[]{:S(2)}, u32[]{:S(2)}) collective-permute-start(f32[2,128,128]{2,1,0:T(8,128)S(1)} %shard_map.90.refs_2_), channel_id=1, source_target_pairs={{28,20},{24,8},{20,28},{16,0},{12,4},{8,24},{4,12},{0,16},{29,21},... | collective-permute-start | bytes 393224 | tf_op jit(solution)/shard_map/ppermute | solution.py:355
  32.7 5.8 %collective-permute-start.12 = (f32[2,128,128]{2,1,0:T(8,128)S(1)}, f32[2,128,128]{2,1,0:T(8,128)S(1)}, u32[]{:S(2)}, u32[]{:S(2)}) collective-permute-start(f32[2,128,128]{2,1,0:T(8,128)S(1)} %shard_map.91.refs_3_), channel_id=1, source_target_pairs={{28,20},{24,8},{20,28},{16,0},{12,4},{8,24},{4,12},{0,16},{29,21},... | collective-permute-start | bytes 393224 | tf_op jit(solution)/shard_map/ppermute | solution.py:355
  36.9 6.0 %collective-permute-start.13 = (f32[2,128,128]{2,1,0:T(8,128)S(1)}, f32[2,128,128]{2,1,0:T(8,128)S(1)}, u32[]{:S(2)}, u32[]{:S(2)}) collective-permute-start(f32[2,128,128]{2,1,0:T(8,128)S(1)} %shard_map.93.refs_4_.refs_2_), channel_id=1, source_target_pairs={{28,12},{24,16},{20,4},{16,24},{12,28},{8,0},{4,20},{0,8},{29,13},... | collective-permute-start | bytes 393224 | tf_op jit(solution)/shard_map/ppermute | solution.py:355
  38.5 5.0 %collective-permute-start.15 = (f32[2,128,128]{2,1,0:T(8,128)S(1)}, f32[2,128,128]{2,1,0:T(8,128)S(1)}, u32[]{:S(2)}, u32[]{:S(2)}) collective-permute-start(f32[2,128,128]{2,1,0:T(8,128)S(1)} %shard_map.94.refs_3_), channel_id=1, source_target_pairs={{28,12},{24,16},{20,4},{16,24},{12,28},{8,0},{4,20},{0,8},{29,13},... | collective-permute-start | bytes 393224 | tf_op jit(solution)/shard_map/ppermute | solution.py:355
  43.6 1.4 %collective-permute-start.16 = (f32[2,128,128]{2,1,0:T(8,128)S(1)}, f32[2,128,128]{2,1,0:T(8,128)S(1)}, u32[]{:S(2)}, u32[]{:S(2)}) collective-permute-start(f32[2,128,128]{2,1,0:T(8,128)S(1)} %get-tuple-element.93), channel_id=1, source_target_pairs={{28,24},{24,28},{20,16},{16,20},{12,8},{8,12},{4,0},{0,4},{29,25},... | collective-permute-start | bytes 393224 | tf_op jit(solution)/shard_map/ppermute | solution.py:355
  43.7 1.5 %collective-permute-start.14 = (f32[2,128,128]{2,1,0:T(8,128)S(1)}, f32[2,128,128]{2,1,0:T(8,128)S(1)}, u32[]{:S(2)}, u32[]{:S(2)}) collective-permute-start(f32[2,128,128]{2,1,0:T(8,128)S(1)} %get-tuple-element.92.refs_5_), channel_id=1, source_target_pairs={{28,24},{24,28},{20,16},{16,20},{12,8},{8,12},{4,0},{0,4},{29,25},... | collective-permute-start | bytes 393224 | tf_op jit(solution)/shard_map/ppermute | solution.py:355

commit v8 on v7

--- a/solution.py
+++ b/solution.py
@@ -9,6 +9,7 @@
 
 HEAD_DIM = 128
 CHUNK = 256
+PIECE = 2
 VMEM_BYTES = 12 * 2**20
 F32 = jnp.float32
 BF16 = jnp.bfloat16
@@ -50,7 +51,7 @@
 
 
 def run(kernel, flops, in_specs, out_specs, out_shape, args, scratch=(), aliases=None):
-    nbytes = sum(a.size * a.dtype.itemsize for a in args)
+    nbytes = sum(a.size * a.dtype.itemsize for a, spec in zip(args, in_specs) if spec is HBM)
     return pl.pallas_call(
         kernel,
         in_specs=in_specs,
@@ -63,10 +64,13 @@
     )(*args)
 
 
-def columns(same, width):
+def columns(same, width, piece=None):
     odd = lax.rem(lax.axis_index("seq"), 2)
     half = odd if same else 1 - odd
-    return pl.ds(pl.multiple_of(half * width, width), width)
+    if piece is None:
+        return pl.ds(pl.multiple_of(half * width, width), width)
+    size = PIECE * HEAD_DIM
+    return pl.ds(pl.multiple_of(half * width + piece * size, size), size)
 
 
 def fetches(sources, targets, sems, same):
@@ -80,8 +84,8 @@
     return copies
 
 
-def sum_states(k_ref, v_ref, sum_ref, pre_ref, copies=()):
-    heads = sum_ref.shape[0]
+def sum_states(k_ref, v_ref, pre_ref, *sum_refs, copies=()):
+    heads = pre_ref.shape[1]
     totals = [None] * heads
     for i, part in enumerate(chunks_of(k_ref.shape[0])):
         for copy in copies[2 * i:2 * i + 2]:
@@ -94,15 +98,16 @@
                 pre_ref[i, j] = jnp.zeros_like(pre_ref[i, j])
             totals[j] = totals[j] + term if i else term
     for j in range(heads):
-        sum_ref[j] = totals[j]
-
-
-def first_kernel(k_hbm, v_hbm, k1, v1, k2, v2, sum_ref, pre_ref, sems1, sems2):
+        sum_refs[j // PIECE][j % PIECE] = totals[j]
+
+
+def first_kernel(k_hbm, v_hbm, k1, v1, k2, v2, pre_ref, *refs):
+    *sum_refs, sems1, sems2 = refs
     now = fetches((k_hbm, v_hbm), (k1, v1), sems1, False)
     later = fetches((k_hbm, v_hbm), (k2, v2), sems2, True)
     for copy in now + later:
         copy.start()
-    sum_states(k1, v1, sum_ref, pre_ref, now)
+    sum_states(k1, v1, pre_ref, *sum_refs, copies=now)
     for copy in later:
         copy.wait()
 
@@ -129,17 +134,15 @@
             qturned_ref[lanes, part] = q.T
 
 
-def attn_kernel(last, pieces, q_ref, inner_ref, scaled_ref, *refs):
-    states = [state.astype(BF16) for state in heads_in(refs[:pieces])]
-    refs = refs[pieces:]
-    attn_ref = refs[2] if last else refs[0]
-    rows, width = q_ref.shape
-    for part in chunks_of(rows):
-        square, cross = (refs[0][part], refs[1][part]) if last else (None, None)
-        for j, state in enumerate(states):
-            lanes = lanes_of(j)
+def attn_kernel(piece, first, last, q_ref, inner_ref, scaled_ref, state_ref, *refs):
+    attn_ref = refs[0] if first else refs[2]
+    for part in chunks_of(q_ref.shape[0]):
+        square, cross = (None, None) if first else (refs[0][part], refs[1][part])
+        for j in range(PIECE):
+            lanes = lanes_of(piece * PIECE + j)
+            state = state_ref[j].astype(BF16)
             attn = inner_ref[part, lanes] + dot(q_ref[part, lanes], state)
-            attn_ref[part, lanes] = attn
+            attn_ref[part, lanes_of(j)] = attn
             more, crossed = attn * attn, scaled_ref[part, lanes] * attn
             square = more if square is None else square + more
             cross = crossed if cross is None else cross + crossed
@@ -166,23 +169,23 @@
     return jnp.broadcast_to(both[:, 0:1], wide), jnp.broadcast_to(both[:, 1:2], wide)
 
 
-def grad_kernel(full, parts, *refs):
+def grad_kernel(piece, full, parts, *refs):
     if parts:
         inv, slope = factors_kernel(full, parts, refs)
         refs[-2][...] = inv
         refs[-1][...] = slope
         inv_ref, slope_ref = refs[-2:]
-        attn_ref, scaled_ref, qturned_ref, g_ref, sum_ref, post_ref = refs[parts:-2]
+        attn_ref, scaled_ref, qturned_ref, g_ref, post_ref, sum_ref = refs[parts:-2]
     else:
-        inv_ref, slope_ref, attn_ref, scaled_ref, qturned_ref, g_ref, sum_ref, post_ref = refs
-    heads = sum_ref.shape[0]
-    totals = [None] * heads
+        inv_ref, slope_ref, attn_ref, scaled_ref, qturned_ref, g_ref, post_ref, sum_ref = refs
+    totals = [None] * PIECE
     for i, part in reversed(list(enumerate(chunks_of(g_ref.shape[0])))):
-        for j in range(heads):
-            lanes = lanes_of(j)
-            grad = inv_ref[part] * scaled_ref[part, lanes] - attn_ref[part, lanes] * slope_ref[part]
+        for j in range(PIECE):
+            lanes = lanes_of(piece * PIECE + j)
+            attn = attn_ref[part, lanes_of(j)]
+            grad = inv_ref[part] * scaled_ref[part, lanes] - attn * slope_ref[part]
             grad = grad.astype(BF16)
-            g_ref[part, lanes] = grad
+            g_ref[part, lanes_of(j)] = grad
             term = dot(qturned_ref[lanes, part], grad)
             if totals[j] is None:
                 post_ref[i, j] = jnp.zeros_like(post_ref[i, j])
@@ -190,13 +193,14 @@
             else:
                 post_ref[i, j] = totals[j].astype(BF16)
                 totals[j] = totals[j] + term
-    for j in range(heads):
+    for j in range(PIECE):
         sum_ref[j] = totals[j]
 
 
-def local_kernel(same, pieces, q_ref, k_ref, v_ref, g_ref, turned_ref, pre_ref, post_ref, *refs):
+def local_kernel(same, pieces, q_ref, k_ref, v_ref, turned_ref, pre_ref, *refs):
     qgrad_hbm, kpart_ref, vpart_ref, qgrad_ref, sems = refs[-5:]
     state = heads_in(refs[:pieces])
+    g_refs, post_refs = refs[pieces:2 * pieces], refs[2 * pieces:3 * pieces]
     rows, width = q_ref.shape
     target = columns(same, width)
     parts = chunks_of(rows)
@@ -204,7 +208,7 @@
 
     def scores(i, j):
         part, lanes = parts[i], lanes_of(j)
-        v, g = v_ref[part, lanes], g_ref[part, lanes]
+        v, g = v_ref[part, lanes], g_refs[j // PIECE][part, lanes_of(j % PIECE)]
         size = g.shape[0]
         gscores = jnp.where(lower(size), dot(g, v, 1, 1), 0.0).astype(BF16)
         gturned = jnp.where(upper(size), dot(v, g, 1, 1), 0.0).astype(BF16)
@@ -212,14 +216,16 @@
 
     def products(i, j, gscores, gturned):
         part, lanes = parts[i], lanes_of(j)
-        q, k, v, g = (ref[part, lanes] for ref in (q_ref, k_ref, v_ref, g_ref))
+        q, k, v = (ref[part, lanes] for ref in (q_ref, k_ref, v_ref))
+        g = g_refs[j // PIECE][part, lanes_of(j % PIECE)]
         before = state[j] + pre_ref[i, j].astype(F32) if i else state[j]
         qgrad = dot(g, before.astype(BF16), 1, 1) + dot(gscores, k)
         kgrad = dot(gturned, q)
         vgrad = dot(turned_ref[j, part], g)
         if i < len(parts) - 1:
-            kgrad = kgrad + dot(v, post_ref[i, j], 1, 1)
-            vgrad = vgrad + dot(k, post_ref[i, j])
+            post = post_refs[j // PIECE][i, j % PIECE]
+            kgrad = kgrad + dot(v, post, 1, 1)
+            vgrad = vgrad + dot(k, post)
         qgrad_ref[part, lanes] = qgrad.astype(BF16)
         kpart_ref[part, lanes] = kgrad
         vpart_ref[part, lanes] = vgrad
@@ -239,40 +245,39 @@
         copy.wait()
 
 
-def final_parts(k_ref, v_ref, kpart_ref, vpart_ref, states, kgrad_ref, vgrad_ref, part):
-    for j, state in enumerate(states):
-        lanes = lanes_of(j)
+def final_part(piece, part, k_ref, v_ref, kpart_ref, vpart_ref, state_ref, kgrad_ref, vgrad_ref):
+    for j in range(PIECE):
+        lanes = lanes_of(piece * PIECE + j)
+        state = state_ref[j].astype(BF16)
         kgrad = kpart_ref[part, lanes] + dot(v_ref[part, lanes], state, 1, 1)
         vgrad = vpart_ref[part, lanes] + dot(k_ref[part, lanes], state)
-        kgrad_ref[part, lanes] = kgrad.astype(BF16)
-        vgrad_ref[part, lanes] = vgrad.astype(BF16)
-
-
-def near_kernel(pieces, *refs):
-    states = [state.astype(BF16) for state in heads_in(refs[4:4 + pieces])]
+        kgrad_ref[part, lanes_of(j)] = kgrad.astype(BF16)
+        vgrad_ref[part, lanes_of(j)] = vgrad.astype(BF16)
+
+
+def final_kernel(piece, *refs):
     for part in chunks_of(refs[0].shape[0]):
-        final_parts(*refs[:4], states, *refs[4 + pieces:], part)
-
-
-def last_kernel(same, pieces, *refs):
-    states = [state.astype(BF16) for state in heads_in(refs[4:4 + pieces])]
-    kdone_ref, vdone_ref, kgrad_hbm, vgrad_hbm, kgrad_ref, vgrad_ref, sems = refs[4 + pieces:]
-    rows, width = kgrad_ref.shape
+        final_part(piece, part, *refs)
+
+
+def write_kernel(same, piece, *refs):
+    kgrad_hbm, vgrad_hbm, kgrad_ref, vgrad_ref, sems = refs[-5:]
+    done = refs[5:5 + 2 * piece]
+    rows, width = refs[0].shape
     copies = []
 
-    def send(source, out, part, half):
-        sem = sems.at[len(copies)]
-        target = out.at[part, columns(half, width)]
-        copy = pltpu.make_async_copy(source.at[part], target, sem)
-        copy.start()
-        copies.append(copy)
-
-    send(kdone_ref, kgrad_hbm, slice(0, rows), not same)
-    send(vdone_ref, vgrad_hbm, slice(0, rows), not same)
+    def send(source, out, part, number):
+        target = out.at[part, columns(same, width, number)]
+        copies.append(pltpu.make_async_copy(source.at[part], target, sems.at[len(copies)]))
+        copies[-1].start()
+
+    for number in range(piece):
+        send(done[2 * number], kgrad_hbm, slice(0, rows), number)
+        send(done[2 * number + 1], vgrad_hbm, slice(0, rows), number)
     for part in chunks_of(rows):
-        final_parts(*refs[:4], states, kgrad_ref, vgrad_ref, part)
-        send(kgrad_ref, kgrad_hbm, part, same)
-        send(vgrad_ref, vgrad_hbm, part, same)
+        final_part(piece, part, *refs[:5], kgrad_ref, vgrad_ref)
+        send(kgrad_ref, kgrad_hbm, part, piece)
+        send(vgrad_ref, vgrad_hbm, part, piece)
     for copy in copies:
         copy.wait()
 
@@ -287,14 +292,14 @@
     return stages
 
 
-def join_kernel(backward, piece, done, final, *refs):
+def join_kernel(backward, done, final, *refs):
     count = lax.axis_size("seq")
     rank = lax.axis_index("seq")
     if backward:
         rank = count - 1 - rank
     odd = (rank & 1) == 1
     plan = scan_plan(count)
-    keep, extra = (ref[piece] for ref in refs[:2])
+    keep, extra = (ref[...] for ref in refs[:2])
     came = refs[2:2 + done]
     total = keep + extra
     before = jnp.zeros_like(total)
@@ -313,10 +318,10 @@
         refs[-1][...] = jnp.where(odd, before + jnp.where(high, 0.0, total), total)
 
 
-def join(backward, piece, keep, extra, came, final, after):
-    like = shape((piece.stop - piece.start,) + keep.shape[1:], F32)
+def join(backward, keep, extra, came, final, after):
+    like = shape(keep.shape, F32)
     return run(
-        functools.partial(join_kernel, backward, piece, len(came), final), 4 * like.size,
+        functools.partial(join_kernel, backward, len(came), final), 4 * like.size,
         [VMEM] * (2 + len(came)) + [ANYWHERE] * len(after),
         [VMEM, VMEM] if final else VMEM,
         [like, like] if final else like,
@@ -324,27 +329,26 @@
     )
 
 
-def scan_states(keep, extra, backward, beside):
+def scan_states(keeps, extras, backward, beside):
     plan = scan_plan(lax.axis_size("seq"))
-    pieces = [slice(i, i + 2) for i in range(0, keep.shape[0], 2)]
-    came = [[] for _ in pieces]
+    came = [[] for _ in keeps]
     results, after = [], []
     for stage, (_, _, pairs) in enumerate(plan):
         messages = []
-        for piece, arrived in zip(pieces, came):
-            message = join(backward, piece, keep, extra, arrived, False, after + messages)
+        for keep, extra, arrived in zip(keeps, extras, came):
+            message = join(backward, keep, extra, arrived, False, after + messages)
             messages.append(message)
             arrived.append(move(message, pairs, backward))
         mine = beside[stage:] if stage == len(plan) - 1 else beside[stage:stage + 1]
         made = [work(messages) for work in mine]
         after = [item[-1] for item in made]
         results += made
-    states, others, last = [], [], []
-    for piece, arrived in zip(pieces, came):
-        message, state = join(backward, piece, keep, extra, arrived, True, after + last)
-        last = [message]
+    states, messages = [], []
+    for keep, extra, arrived in zip(keeps, extras, came):
+        message, state = join(backward, keep, extra, arrived, True, after + messages)
         states.append(state)
-        others.append(nearby(message, backward))
+        messages.append(message)
+    others = [nearby(message, backward) for message in messages[::-1]][::-1]
     return states, others, results
 
 
@@ -372,7 +376,8 @@
     unit = 2 * rows * half * HEAD_DIM
     partial = functools.partial
 
-    states = shape((heads, HEAD_DIM, HEAD_DIM), F32)
+    count = heads // PIECE
+    states = shape((PIECE, HEAD_DIM, HEAD_DIM), F32)
     inside = shape((chunks, heads, HEAD_DIM, HEAD_DIM), BF16)
     wide = shape((rows, half), F32)
     thin = shape((rows, half), BF16)
@@ -380,12 +385,14 @@
     whole = shape((rows, width), BF16)
     sems = pltpu.SemaphoreType.DMA((2 * chunks,))
 
-    k1, v1, k2, v2, send, pre1 = run(
-        first_kernel, unit, [HBM, HBM], [VMEM] * 6, [thin] * 4 + [states, inside],
+    k1, v1, k2, v2, pre1, *sends = run(
+        first_kernel, unit, [HBM, HBM], [VMEM] * (5 + count), [thin] * 4 + [inside] + [states] * count,
         (key_in, value), [sems, sems],
     )
-    extra = nearby(send, False)
-    keep, pre2 = run(sum_states, unit, [VMEM, VMEM], [VMEM] * 2, [states, inside], (k2, v2))
+    extras = [nearby(send, False) for send in sends]
+    pre2, *keeps = run(
+        sum_states, unit, [VMEM, VMEM], [VMEM] * (1 + count), [inside] + [states] * count, (k2, v2)
+    )
 
     def inner_of(same, k, v, pre):
         return lambda messages: run(
@@ -400,35 +407,51 @@
         )
 
     state2, state1, made = scan_states(
-        keep, extra, False,
+        keeps, extras, False,
         [inner_of(True, k2, v2, pre2), inner_of(False, k1, v1, pre1)],
     )
     (q2, inner2, scaled2, qturned2, turned2), (q1, inner1, scaled1, qturned1, turned1) = made
 
-    count = len(state2)
-    attn2, square, cross = run(
-        partial(attn_kernel, False, count), unit, [VMEM] * (3 + count), [VMEM] * 3,
-        [wide, lane_sums, lane_sums], (q2, inner2, scaled2, *state2),
-    )
-    attn1, sums = run(
-        partial(attn_kernel, True, count), unit, [VMEM] * (5 + count), [VMEM] * 2,
-        [wide, shape((8, rows), F32)], (q1, inner1, scaled1, *state1, square, cross),
-    )
+    attns, sums = [], ()
+    piece_wide = shape((rows, PIECE * HEAD_DIM), F32)
+    for number, state in enumerate([*state2, *state1]):
+        args = (q2, inner2, scaled2) if number < count else (q1, inner1, scaled1)
+        last = number == 2 * count - 1
+        attn, *sums = run(
+            partial(attn_kernel, number % count, number == 0, last), unit // count,
+            [VMEM] * (4 + len(sums)), [VMEM] * (2 if last else 3),
+            [piece_wide] + ([shape((8, rows), F32)] if last else [lane_sums] * 2),
+            (*args, state, *sums),
+        )
+        attns.append(attn)
+    sums = sums[0]
     parts = [sums] + [
         lax.ppermute(sums, "head", [(r, r ^ other) for r in range(peers)])
         for other in range(1, peers)
     ]
 
-    g2, gsend, post2, inv, slope = run(
-        partial(grad_kernel, full, peers), unit,
-        [VMEM] * (peers + 3), [VMEM] * 5, [thin, states, inside, lane_sums, lane_sums],
-        (*parts, attn2, scaled2, qturned2),
-    )
-    gextra = nearby(gsend, True)
-    g1, gkeep, post1 = run(
-        partial(grad_kernel, full, 0), unit, [VMEM] * 5, [VMEM] * 3, [thin, states, inside],
-        (inv, slope, attn1, scaled1, qturned1),
-    )
+    factors = []
+
+    def grads_of(attns, scaled, qturned):
+        made = []
+        for piece, attn in enumerate(attns):
+            peers_in = 0 if factors else len(parts)
+            first = factors or parts
+            g, post, total, *more = run(
+                partial(grad_kernel, piece, full, peers_in), unit // count,
+                [VMEM] * (len(first) + 3), [VMEM] * (3 if factors else 5),
+                [shape((rows, PIECE * HEAD_DIM), BF16), posts, states]
+                + ([] if factors else [lane_sums] * 2),
+                (*first, attn, scaled, qturned),
+            )
+            factors.extend(more)
+            made.append((g, post, total))
+        return zip(*made)
+
+    posts = shape((chunks, PIECE, HEAD_DIM, HEAD_DIM), BF16)
+    gs2, posts2, gsends = grads_of(attns[:count], scaled2, qturned2)
+    gextras = [nearby(gsend, True) for gsend in gsends]
+    gs1, posts1, gkeeps = grads_of(attns[count:], scaled1, qturned1)
 
     qgrads = []
 
@@ -448,23 +471,34 @@
         return work
 
     gstate1, gstate2, made = scan_states(
-        gkeep, gextra, True,
+        gkeeps, gextras, True,
         [
-            local_of(False, q1, k1, v1, g1, turned1, pre1, post1, *state1),
-            local_of(True, q2, k2, v2, g2, turned2, pre2, post2, *state2),
+            local_of(False, q1, k1, v1, turned1, pre1, *state1, *gs1, *posts1),
+            local_of(True, q2, k2, v2, turned2, pre2, *state2, *gs2, *posts2),
         ],
     )
     (kpart1, vpart1), (kpart2, vpart2) = made
 
-    done = run(
-        partial(near_kernel, count), 2 * unit, [VMEM] * (4 + count), [VMEM] * 2, [thin, thin],
-        (k1, v1, kpart1, vpart1, *gstate1),
-    )
-    kgrad, vgrad = run(
-        partial(last_kernel, True, count), 2 * unit, [VMEM] * (6 + count), [HBM, HBM],
-        [whole, whole], (k2, v2, kpart2, vpart2, *gstate2, *done),
-        [pltpu.VMEM((rows, half), BF16)] * 2 + [pltpu.SemaphoreType.DMA((2 * chunks + 2,))],
-    )
+    piece_thin = shape((rows, PIECE * HEAD_DIM), BF16)
+
+    def finals_of(same, k, v, kpart, vpart, found, outs):
+        done = []
+        for piece, state in enumerate(found[:-1]):
+            done += run(
+                partial(final_kernel, piece), 2 * unit // count, [VMEM] * 5, [VMEM] * 2,
+                [piece_thin] * 2, (k, v, kpart, vpart, state),
+            )
+        args = (k, v, kpart, vpart, found[-1], *done)
+        return run(
+            partial(write_kernel, same, count - 1), 2 * unit // count,
+            [VMEM] * len(args) + [HBM] * len(outs), [HBM, HBM], [whole, whole], (*args, *outs),
+            [pltpu.VMEM(piece_thin.shape, BF16)] * 2
+            + [pltpu.SemaphoreType.DMA((2 * (chunks + count - 1),))],
+            {len(args) + i: i for i in range(len(outs))},
+        )
+
+    outs = finals_of(False, k1, v1, kpart1, vpart1, gstate1, ())
+    kgrad, vgrad = finals_of(True, k2, v2, kpart2, vpart2, gstate2, outs)
     return qgrads[0], kgrad, vgrad
 
 

time: 47.3 us -> 46.9 us (level)
  waiting for transfers between devices: 7.9 us -> 5.88 us
  Pallas kernels: 21.4 us -> 23.2 us
    ppermute x14 -> x16, waiting for transfers between devices: 3.95 us -> 1.93 us  [move(): return lax.ppermute(value, 'seq', pairs)]
    pallas_call x24 -> x30, Pallas kernels: 21.4 us -> 23.2 us  [run(): pl.pallas_call(kernel, in_specs=in_specs, out_specs=out_specs, out_shape=...]
    ppermute x14 -> x16, starting transfers between devices: 12.4 us -> 12.1 us  [move(): return lax.ppermute(value, 'seq', pairs)]
  transfers between devices with their start and end apart: 17 -> 19, of which waited for: 10 -> 8; matrix products, arithmetic and copies ran while one was open for 0% -> 0% of each run, Pallas kernels for 34% -> 40%
where the time goes in v8:
time: 46.9 us; the launch traced here: 46.7 us
  Pallas kernels  23.2 us (49%)
  starting transfers between devices  16.5 us (35%)
  waiting for transfers between devices  5.88 us (13%)
  between operations  1.09 us (2%)
    pallas_call x30, Pallas kernels, run(): pl.pallas_call(kernel, in_specs=in_specs, out_specs=out_specs, out_shape=...  23.2 us
    ppermute x16, starting transfers between devices, move(): return lax.ppermute(value, 'seq', pairs)  12.1 us
    ppermute x3, starting transfers between devices, shards(): lax.ppermute(sums, 'head', [(r, r ^ other) for r in range(peers)])  4.45 us
    ppermute x3, waiting for transfers between devices, shards(): lax.ppermute(sums, 'head', [(r, r ^ other) for r in range(peers)])  3.94 us
    ppermute x16, waiting for transfers between devices, move(): return lax.ppermute(value, 'seq', pairs)  1.93 us
  transfers between devices with their start and end apart: 19, of which 8 were waited for; matrix products, arithmetic and copies ran while one was open for 0% of the time, Pallas kernels for 40%

profile of v8, /device:TPU:0, one launch (start us, length us, event | category | flops | bytes accessed | tf_op | source)
XLA Modules:
  0.0 46.7 jit_solution(8834363379200818366)
XLA Ops:
  0.6 2.1 %shard_map.76 = (bf16[768,512]{1,0:T(8,128)(2,1)S(1)}, bf16[768,512]{1,0:T(8,128)(2,1)S(1)}, bf16[768,512]{1,0:T(8,128)(2,1)S(1)}, bf16[768,512]{1,0:T(8,128)(2,...) custom-call(bf16[768,1024]{1,0:T(8,128)(2,1)} %k_hbm.1, ...), custom_call_target="tpu_custom_call" | custom-call | flops 100663296 | bytes 3145728 | tf_op jit(solution)/shard_map/pallas_call | solution.py:55
  2.8 0.5 %collective-permute-start = (f32[2,128,128]{2,1,0:T(8,128)S(1)}, f32[2,128,128]{2,1,0:T(8,128)S(1)}, u32[]{:S(2)}, u32[]{:S(2)}) collective-permute-start(f32[2,128,128]{2,1,0:T(8,128)S(1)} %get-tuple-element.74), channel_id=1, source_target_pairs={{0,4},{4,0},{8,12},{12,8},{16,20},{20,16},{24,28},{28,24},{1,5},{5... | collective-permute-start | bytes 393224 | tf_op jit(solution)/shard_map/ppermute | solution.py:359
  3.8 0.5 %collective-permute-done.refs_1_ = f32[2,128,128]{2,1,0:T(8,128)S(1)} collective-permute-done((f32[2,128,128]{2,1,0:T(8,128)S(1)}, f32[2,128,128]{2,1,0:T(8,128)S(1)}, u32[]{:S(2)}, u32[]{:S(2)}) %collective-permute-start) | collective-permute-done | bytes 131104 | tf_op jit(solution)/shard_map/ppermute | solution.py:359
  4.3 2.9 %collective-permute-start.2 = (f32[2,128,128]{2,1,0:T(8,128)S(1)}, f32[2,128,128]{2,1,0:T(8,128)S(1)}, u32[]{:S(2)}, u32[]{:S(2)}) collective-permute-start(f32[2,128,128]{2,1,0:T(8,128)S(1)} %shard_map.78.refs_2_.refs_0_), channel_id=1, source_target_pairs={{0,8},{4,20},{8,0},{12,28},{16,24},{20,4},{24,16},{28,12},{1,9},{5... | collective-permute-start | bytes 393224 | tf_op jit(solution)/shard_map/ppermute | solution.py:359
  7.4 3.3 %shard_map.80 = (bf16[768,512]{1,0:T(8,128)(2,1)S(1)}, f32[768,512]{1,0:T(8,128)S(1)}, f32[768,512]{1,0:T(8,128)S(1)}, bf16[512,768]{1,0:T(8,128)(2,1)S(1)}, bf16[4,768,256]{2,1,0:T(8,128)(2,1)S(1)}) custom-call(bf16[768,1024]{1,0:T(8,128)(2,1)} %q_hbm.3, bf16[768,1024]{1,0:T(8,128)(2,1)} %og_hbm.3, bf16[768,512]{1,0:T(8,128)(2,1)S(1)} %get-tuple-element.70.k_ref.refs_0_, ...), custom_call_target="tpu_custom_call" | custom-call | flops 603979776 | bytes 3145728 | tf_op jit(solution)/shard_map/pallas_call | solution.py:55
  10.8 2.0 %collective-permute-start.3 = (f32[2,128,128]{2,1,0:T(8,128)S(1)}, f32[2,128,128]{2,1,0:T(8,128)S(1)}, u32[]{:S(2)}, u32[]{:S(2)}) collective-permute-start(f32[2,128,128]{2,1,0:T(8,128)S(1)} %shard_map.81.refs_4_.refs_0_), channel_id=1, source_target_pairs={{0,16},{4,12},{8,24},{12,4},{16,0},{20,28},{24,8},{28,20},{1,17},{... | collective-permute-start | bytes 393224 | tf_op jit(solution)/shard_map/ppermute | solution.py:359
  12.9 1.0 %collective-permute-start.5 = (f32[2,128,128]{2,1,0:T(8,128)S(1)}, f32[2,128,128]{2,1,0:T(8,128)S(1)}, u32[]{:S(2)}, u32[]{:S(2)}) collective-permute-start(f32[2,128,128]{2,1,0:T(8,128)S(1)} %shard_map.82.refs_1_), channel_id=1, source_target_pairs={{0,16},{4,12},{8,24},{12,4},{16,0},{20,28},{24,8},{28,20},{1,17},{... | collective-permute-start | bytes 393224 | tf_op jit(solution)/shard_map/ppermute | solution.py:359
  13.9 3.3 %shard_map.83 = (bf16[768,512]{1,0:T(8,128)(2,1)S(1)}, f32[768,512]{1,0:T(8,128)S(1)}, f32[768,512]{1,0:T(8,128)S(1)}, bf16[512,768]{1,0:T(8,128)(2,1)S(1)}, bf16[4,768,256]{2,1,0:T(8,128)(2,1)S(1)}) custom-call(bf16[768,1024]{1,0:T(8,128)(2,1)} %q_hbm.3, bf16[768,1024]{1,0:T(8,128)(2,1)} %og_hbm.3, bf16[768,512]{1,0:T(8,128)(2,1)S(1)} %get-tuple-element.79.k_ref.refs_0_, ...), custom_call_target="tpu_custom_call" | custom-call | flops 603979776 | bytes 3145728 | tf_op jit(solution)/shard_map/pallas_call | solution.py:55
  17.4 0.5 %collective-permute-done.5.refs_3_ = f32[2,128,128]{2,1,0:T(8,128)S(1)} collective-permute-done((f32[2,128,128]{2,1,0:T(8,128)S(1)}, f32[2,128,128]{2,1,0:T(8,128)S(1)}, u32[]{:S(2)}, u32[]{:S(2)}) %collective-permute-start.5) | collective-permute-done | bytes 131104 | tf_op jit(solution)/shard_map/ppermute | solution.py:359
  19.4 0.5 %shard_map.89 = (f32[768,256]{1,0:T(8,128)S(1)}, f32[8,768]{1,0:T(8,128)S(1)}) custom-call(bf16[768,512]{1,0:T(8,128)(2,1)S(1)} %get-tuple-element.86.q_ref, f32[768,512]{1,0:T(8,128)S(1)} %get-tuple-element.87.inner_ref, f32[768,512]{1,0:T(8,128)S(1)} %get-tuple-element.88.scaled_ref.refs_3_, f32[2,128,128]{2,1,0:T(8,128)S(1)} %collective-permute-done.6.state_ref.refs_1_, ...), custom_call_target="tpu_custom_call" | custom-call | flops 50331648 | tf_op jit(solution)/shard_map/pallas_call | solution.py:55
  19.9 3.7 %collective-permute-start.10 = (f32[8,768]{1,0:T(8,128)S(1)}, f32[8,768]{1,0:T(8,128)S(1)}, u32[]{:S(2)}, u32[]{:S(2)}) collective-permute-start(f32[8,768]{1,0:T(8,128)S(1)} %get-tuple-element.98.refs_0_), channel_id=1, source_target_pairs={{0,3},{1,2},{2,1},{3,0},{4,7},{5,6},{6,5},{7,4},{8,11},{9,10},{10,... | collective-permute-start | bytes 73736 | tf_op jit(solution)/shard_map/ppermute | solution.py:429
  23.6 0.8 %collective-permute-start.8 = (f32[8,768]{1,0:T(8,128)S(1)}, f32[8,768]{1,0:T(8,128)S(1)}, u32[]{:S(2)}, u32[]{:S(2)}) collective-permute-start(f32[8,768]{1,0:T(8,128)S(1)} %get-tuple-element.98.refs_0_), channel_id=1, source_target_pairs={{0,1},{1,0},{2,3},{3,2},{4,5},{5,4},{6,7},{7,6},{8,9},{9,8},{10,11... | collective-permute-start | bytes 73736 | tf_op jit(solution)/shard_map/ppermute | solution.py:429
  24.4 1.2 %collective-permute-done.10.refs_3_ = f32[8,768]{1,0:T(8,128)S(1)} collective-permute-done((f32[8,768]{1,0:T(8,128)S(1)}, f32[8,768]{1,0:T(8,128)S(1)}, u32[]{:S(2)}, u32[]{:S(2)}) %collective-permute-start.10) | collective-permute-done | bytes 24608 | tf_op jit(solution)/shard_map/ppermute | solution.py:429
  25.6 2.7 %collective-permute-done.9.refs_2_ = f32[8,768]{1,0:T(8,128)S(1)} collective-permute-done((f32[8,768]{1,0:T(8,128)S(1)}, f32[8,768]{1,0:T(8,128)S(1)}, u32[]{:S(2)}, u32[]{:S(2)}) %collective-permute-start.9) | collective-permute-done | bytes 24608 | tf_op jit(solution)/shard_map/ppermute | solution.py:429
  28.3 0.7 %shard_map.90 = (bf16[768,256]{1,0:T(8,128)(2,1)S(1)}, bf16[3,2,128,128]{3,2,1,0:T(8,128)(2,1)S(1)}, f32[2,128,128]{2,1,0:T(8,128)S(1)}, f32[768,128]{1,0:T(8,128)S(1)}, f32[768,128]{1,0:T(8,128)S(1)}) custom-call(f32[8,768]{1,0:T(8,128)S(1)} %get-tuple-element.98.refs_0_, f32[8,768]{1,0:T(8,128)S(1)} %collective-permute-done.8.refs_1_, ...), custom_call_target="tpu_custom_call" | custom-call | flops 50331648 | tf_op jit(solution)/shard_map/pallas_call | solution.py:55
  29.5 0.6 %collective-permute-start.13 = (f32[2,128,128]{2,1,0:T(8,128)S(1)}, f32[2,128,128]{2,1,0:T(8,128)S(1)}, u32[]{:S(2)}, u32[]{:S(2)}) collective-permute-start(f32[2,128,128]{2,1,0:T(8,128)S(1)} %get-tuple-element.118), channel_id=1, source_target_pairs={{28,24},{24,28},{20,16},{16,20},{12,8},{8,12},{4,0},{0,4},{29,25},... | collective-permute-start | bytes 393224 | tf_op jit(solution)/shard_map/ppermute | solution.py:359
  30.5 1.4 %collective-permute-start.12 = (f32[2,128,128]{2,1,0:T(8,128)S(1)}, f32[2,128,128]{2,1,0:T(8,128)S(1)}, u32[]{:S(2)}, u32[]{:S(2)}) collective-permute-start(f32[2,128,128]{2,1,0:T(8,128)S(1)} %shard_map.93.refs_2_.refs_6_), channel_id=1, source_target_pairs={{28,20},{24,8},{20,28},{16,0},{12,4},{8,24},{4,12},{0,16},{29,21},... | collective-permute-start | bytes 393224 | tf_op jit(solution)/shard_map/ppermute | solution.py:359
  32.2 0.8 %collective-permute-start.14 = (f32[2,128,128]{2,1,0:T(8,128)S(1)}, f32[2,128,128]{2,1,0:T(8,128)S(1)}, u32[]{:S(2)}, u32[]{:S(2)}) collective-permute-start(f32[2,128,128]{2,1,0:T(8,128)S(1)} %shard_map.95.refs_7_), channel_id=1, source_target_pairs={{28,20},{24,8},{20,28},{16,0},{12,4},{8,24},{4,12},{0,16},{29,21},... | collective-permute-start | bytes 393224 | tf_op jit(solution)/shard_map/ppermute | solution.py:359
  33.0 3.4 %shard_map.96 = (bf16[768,1024]{1,0:T(8,128)(2,1)}, f32[768,512]{1,0:T(8,128)S(1)}, f32[768,512]{1,0:T(8,128)S(1)}) custom-call(bf16[768,512]{1,0:T(8,128)(2,1)S(1)} %get-tuple-element.86.q_ref, bf16[768,512]{1,0:T(8,128)(2,1)S(1)} %get-tuple-element.79.k_ref.refs_0_, bf16[768,512]{1,0:T(8,128)(2,1)S(1)} %get-tuple-element.80.v_ref.refs_1_, ...), custom_call_target="tpu_custom_call" | custom-call | flops 905969664 | tf_op jit(solution)/shard_map/pallas_call | solution.py:55
  36.5 1.6 %collective-permute-start.16 = (f32[2,128,128]{2,1,0:T(8,128)S(1)}, f32[2,128,128]{2,1,0:T(8,128)S(1)}, u32[]{:S(2)}, u32[]{:S(2)}) collective-permute-start(f32[2,128,128]{2,1,0:T(8,128)S(1)} %shard_map.97.refs_4_.refs_6_), channel_id=1, source_target_pairs={{28,12},{24,16},{20,4},{16,24},{12,28},{8,0},{4,20},{0,8},{29,13},... | collective-permute-start | bytes 393224 | tf_op jit(solution)/shard_map/ppermute | solution.py:359
  38.1 0.7 %collective-permute-start.15 = (f32[2,128,128]{2,1,0:T(8,128)S(1)}, f32[2,128,128]{2,1,0:T(8,128)S(1)}, u32[]{:S(2)}, u32[]{:S(2)}) collective-permute-start(f32[2,128,128]{2,1,0:T(8,128)S(1)} %shard_map.98.refs_7_), channel_id=1, source_target_pairs={{28,12},{24,16},{20,4},{16,24},{12,28},{8,0},{4,20},{0,8},{29,13},... | collective-permute-start | bytes 393224 | tf_op jit(solution)/shard_map/ppermute | solution.py:359
  38.8 3.7 %shard_map.99 = (bf16[768,1024]{1,0:T(8,128)(2,1)}, f32[768,512]{1,0:T(8,128)S(1)}, f32[768,512]{1,0:T(8,128)S(1)}) custom-call(bf16[768,512]{1,0:T(8,128)(2,1)S(1)} %get-tuple-element.77.q_ref, bf16[768,512]{1,0:T(8,128)(2,1)S(1)} %get-tuple-element.70.k_ref.refs_0_, ...), custom_call_target="tpu_custom_call", output_to_operand_aliasing={{0}: (13, {})} | custom-call | flops 905969664 | bytes 1572864 | tf_op jit(solution)/shard_map/pallas_call | solution.py:55
  43.7 1.2 %shard_map.104 = (bf16[768,1024]{1,0:T(8,128)(2,1)}, bf16[768,1024]{1,0:T(8,128)(2,1)}) custom-call(bf16[768,512]{1,0:T(8,128)(2,1)S(1)} %get-tuple-element.79.k_ref.refs_0_, bf16[768,512]{1,0:T(8,128)(2,1)S(1)} %get-tuple-element.80.v_ref.refs_1_, f32[768,512]{1,0:T(8,128)S(1)} %get-tuple-element.128.refs_2_, f32[768,512]{1,0:T(8,128)S(1)} %get-tuple-element.119.refs_3_, ...), custom_call_target="tpu_custom_call" | custom-call | flops 100663296 | tf_op jit(solution)/shard_map/pallas_call | solution.py:55
  45.3 1.2 %shard_map.105 = (bf16[768,1024]{1,0:T(8,128)(2,1)}, bf16[768,1024]{1,0:T(8,128)(2,1)}) custom-call(bf16[768,512]{1,0:T(8,128)(2,1)S(1)} %get-tuple-element.70.k_ref.refs_0_, bf16[768,512]{1,0:T(8,128)(2,1)S(1)} %get-tuple-element.71.v_ref.refs_1_, f32[768,512]{1,0:T(8,128)S(1)} %get-tuple-element.122.refs_2_, ...), custom_call_target="tpu_custom_call", output_to_operand_aliasing={{0}: (7, {}), {1}: (8, {})} | custom-call | flops 100663296 | bytes 3145728 | tf_op jit(solution)/shard_map/pallas_call | solution.py:55
  (46 shorter events, 5.2 us)
Async XLA Ops:
  2.8 4.6 %copy-start = (f32[1024]{0:T(1024)S(1)}, f32[1024]{0:T(1024)}, u32[]{:S(2)}) copy-start(f32[1024]{0:T(1024)} %param.9) | copy-start | bytes 12292
  2.8 1.5 %collective-permute-start = (f32[2,128,128]{2,1,0:T(8,128)S(1)}, f32[2,128,128]{2,1,0:T(8,128)S(1)}, u32[]{:S(2)}, u32[]{:S(2)}) collective-permute-start(f32[2,128,128]{2,1,0:T(8,128)S(1)} %get-tuple-element.74), channel_id=1, source_target_pairs={{0,4},{4,0},{8,12},{12,8},{16,20},{20,16},{24,28},{28,24},{1,5},{5... | collective-permute-start | bytes 393224 | tf_op jit(solution)/shard_map/ppermute | solution.py:359
  3.3 3.9 %collective-permute-start.1 = (f32[2,128,128]{2,1,0:T(8,128)S(1)}, f32[2,128,128]{2,1,0:T(8,128)S(1)}, u32[]{:S(2)}, u32[]{:S(2)}) collective-permute-start(f32[2,128,128]{2,1,0:T(8,128)S(1)} %get-tuple-element.76), channel_id=1, source_target_pairs={{0,4},{4,0},{8,12},{12,8},{16,20},{20,16},{24,28},{28,24},{1,5},{5... | collective-permute-start | bytes 393224 | tf_op jit(solution)/shard_map/ppermute | solution.py:359
  4.3 6.4 %collective-permute-start.2 = (f32[2,128,128]{2,1,0:T(8,128)S(1)}, f32[2,128,128]{2,1,0:T(8,128)S(1)}, u32[]{:S(2)}, u32[]{:S(2)}) collective-permute-start(f32[2,128,128]{2,1,0:T(8,128)S(1)} %shard_map.78.refs_2_.refs_0_), channel_id=1, source_target_pairs={{0,8},{4,20},{8,0},{12,28},{16,24},{20,4},{24,16},{28,12},{1,9},{5... | collective-permute-start | bytes 393224 | tf_op jit(solution)/shard_map/ppermute | solution.py:359
  7.3 5.6 %collective-permute-start.4 = (f32[2,128,128]{2,1,0:T(8,128)S(1)}, f32[2,128,128]{2,1,0:T(8,128)S(1)}, u32[]{:S(2)}, u32[]{:S(2)}) collective-permute-start(f32[2,128,128]{2,1,0:T(8,128)S(1)} %shard_map.79.refs_1_), channel_id=1, source_target_pairs={{0,8},{4,20},{8,0},{12,28},{16,24},{20,4},{24,16},{28,12},{1,9},{5... | collective-permute-start | bytes 393224 | tf_op jit(solution)/shard_map/ppermute | solution.py:359
  10.8 6.4 %collective-permute-start.3 = (f32[2,128,128]{2,1,0:T(8,128)S(1)}, f32[2,128,128]{2,1,0:T(8,128)S(1)}, u32[]{:S(2)}, u32[]{:S(2)}) collective-permute-start(f32[2,128,128]{2,1,0:T(8,128)S(1)} %shard_map.81.refs_4_.refs_0_), channel_id=1, source_target_pairs={{0,16},{4,12},{8,24},{12,4},{16,0},{20,28},{24,8},{28,20},{1,17},{... | collective-permute-start | bytes 393224 | tf_op jit(solution)/shard_map/ppermute | solution.py:359
  12.9 5.0 %collective-permute-start.5 = (f32[2,128,128]{2,1,0:T(8,128)S(1)}, f32[2,128,128]{2,1,0:T(8,128)S(1)}, u32[]{:S(2)}, u32[]{:S(2)}) collective-permute-start(f32[2,128,128]{2,1,0:T(8,128)S(1)} %shard_map.82.refs_1_), channel_id=1, source_target_pairs={{0,16},{4,12},{8,24},{12,4},{16,0},{20,28},{24,8},{28,20},{1,17},{... | collective-permute-start | bytes 393224 | tf_op jit(solution)/shard_map/ppermute | solution.py:359
  17.4 1.4 %collective-permute-start.7 = (f32[2,128,128]{2,1,0:T(8,128)S(1)}, f32[2,128,128]{2,1,0:T(8,128)S(1)}, u32[]{:S(2)}, u32[]{:S(2)}) collective-permute-start(f32[2,128,128]{2,1,0:T(8,128)S(1)} %get-tuple-element.84.refs_5_), channel_id=1, source_target_pairs={{0,4},{4,0},{8,12},{12,8},{16,20},{20,16},{24,28},{28,24},{1,5},{5... | collective-permute-start | bytes 393224 | tf_op jit(solution)/shard_map/ppermute | solution.py:359
  18.0 1.4 %collective-permute-start.6 = (f32[2,128,128]{2,1,0:T(8,128)S(1)}, f32[2,128,128]{2,1,0:T(8,128)S(1)}, u32[]{:S(2)}, u32[]{:S(2)}) collective-permute-start(f32[2,128,128]{2,1,0:T(8,128)S(1)} %get-tuple-element.89), channel_id=1, source_target_pairs={{0,4},{4,0},{8,12},{12,8},{16,20},{20,16},{24,28},{28,24},{1,5},{5... | collective-permute-start | bytes 393224 | tf_op jit(solution)/shard_map/ppermute | solution.py:359
  19.9 5.7 %collective-permute-start.10 = (f32[8,768]{1,0:T(8,128)S(1)}, f32[8,768]{1,0:T(8,128)S(1)}, u32[]{:S(2)}, u32[]{:S(2)}) collective-permute-start(f32[8,768]{1,0:T(8,128)S(1)} %get-tuple-element.98.refs_0_), channel_id=1, source_target_pairs={{0,3},{1,2},{2,1},{3,0},{4,7},{5,6},{6,5},{7,4},{8,11},{9,10},{10,... | collective-permute-start | bytes 73736 | tf_op jit(solution)/shard_map/ppermute | solution.py:429
  23.6 4.7 %collective-permute-start.9 = (f32[8,768]{1,0:T(8,128)S(1)}, f32[8,768]{1,0:T(8,128)S(1)}, u32[]{:S(2)}, u32[]{:S(2)}) collective-permute-start(f32[8,768]{1,0:T(8,128)S(1)} %get-tuple-element.98.refs_0_), channel_id=1, source_target_pairs={{0,2},{1,3},{2,0},{3,1},{4,6},{5,7},{6,4},{7,5},{8,10},{9,11},{10,... | collective-permute-start | bytes 73736 | tf_op jit(solution)/shard_map/ppermute | solution.py:429
  23.6 4.7 %collective-permute-start.8 = (f32[8,768]{1,0:T(8,128)S(1)}, f32[8,768]{1,0:T(8,128)S(1)}, u32[]{:S(2)}, u32[]{:S(2)}) collective-permute-start(f32[8,768]{1,0:T(8,128)S(1)} %get-tuple-element.98.refs_0_), channel_id=1, source_target_pairs={{0,1},{1,0},{2,3},{3,2},{4,5},{5,4},{6,7},{7,6},{8,9},{9,8},{10,11... | collective-permute-start | bytes 73736 | tf_op jit(solution)/shard_map/ppermute | solution.py:429
  29.0 1.4 %collective-permute-start.11 = (f32[2,128,128]{2,1,0:T(8,128)S(1)}, f32[2,128,128]{2,1,0:T(8,128)S(1)}, u32[]{:S(2)}, u32[]{:S(2)}) collective-permute-start(f32[2,128,128]{2,1,0:T(8,128)S(1)} %get-tuple-element.111), channel_id=1, source_target_pairs={{28,24},{24,28},{20,16},{16,20},{12,8},{8,12},{4,0},{0,4},{29,25},... | collective-permute-start | bytes 393224 | tf_op jit(solution)/shard_map/ppermute | solution.py:359
  29.5 2.7 %collective-permute-start.13 = (f32[2,128,128]{2,1,0:T(8,128)S(1)}, f32[2,128,128]{2,1,0:T(8,128)S(1)}, u32[]{:S(2)}, u32[]{:S(2)}) collective-permute-start(f32[2,128,128]{2,1,0:T(8,128)S(1)} %get-tuple-element.118), channel_id=1, source_target_pairs={{28,24},{24,28},{20,16},{16,20},{12,8},{8,12},{4,0},{0,4},{29,25},... | collective-permute-start | bytes 393224 | tf_op jit(solution)/shard_map/ppermute | solution.py:359
  30.5 6.0 %collective-permute-start.12 = (f32[2,128,128]{2,1,0:T(8,128)S(1)}, f32[2,128,128]{2,1,0:T(8,128)S(1)}, u32[]{:S(2)}, u32[]{:S(2)}) collective-permute-start(f32[2,128,128]{2,1,0:T(8,128)S(1)} %shard_map.93.refs_2_.refs_6_), channel_id=1, source_target_pairs={{28,20},{24,8},{20,28},{16,0},{12,4},{8,24},{4,12},{0,16},{29,21},... | collective-permute-start | bytes 393224 | tf_op jit(solution)/shard_map/ppermute | solution.py:359
  32.2 5.9 %collective-permute-start.14 = (f32[2,128,128]{2,1,0:T(8,128)S(1)}, f32[2,128,128]{2,1,0:T(8,128)S(1)}, u32[]{:S(2)}, u32[]{:S(2)}) collective-permute-start(f32[2,128,128]{2,1,0:T(8,128)S(1)} %shard_map.95.refs_7_), channel_id=1, source_target_pairs={{28,20},{24,8},{20,28},{16,0},{12,4},{8,24},{4,12},{0,16},{29,21},... | collective-permute-start | bytes 393224 | tf_op jit(solution)/shard_map/ppermute | solution.py:359
  36.5 6.0 %collective-permute-start.16 = (f32[2,128,128]{2,1,0:T(8,128)S(1)}, f32[2,128,128]{2,1,0:T(8,128)S(1)}, u32[]{:S(2)}, u32[]{:S(2)}) collective-permute-start(f32[2,128,128]{2,1,0:T(8,128)S(1)} %shard_map.97.refs_4_.refs_6_), channel_id=1, source_target_pairs={{28,12},{24,16},{20,4},{16,24},{12,28},{8,0},{4,20},{0,8},{29,13},... | collective-permute-start | bytes 393224 | tf_op jit(solution)/shard_map/ppermute | solution.py:359
  38.1 5.0 %collective-permute-start.15 = (f32[2,128,128]{2,1,0:T(8,128)S(1)}, f32[2,128,128]{2,1,0:T(8,128)S(1)}, u32[]{:S(2)}, u32[]{:S(2)}) collective-permute-start(f32[2,128,128]{2,1,0:T(8,128)S(1)} %shard_map.98.refs_7_), channel_id=1, source_target_pairs={{28,12},{24,16},{20,4},{16,24},{12,28},{8,0},{4,20},{0,8},{29,13},... | collective-permute-start | bytes 393224 | tf_op jit(solution)/shard_map/ppermute | solution.py:359
  42.6 2.3 %collective-permute-start.18 = (f32[2,128,128]{2,1,0:T(8,128)S(1)}, f32[2,128,128]{2,1,0:T(8,128)S(1)}, u32[]{:S(2)}, u32[]{:S(2)}) collective-permute-start(f32[2,128,128]{2,1,0:T(8,128)S(1)} %get-tuple-element.124.refs_5_), channel_id=1, source_target_pairs={{28,24},{24,28},{20,16},{16,20},{12,8},{8,12},{4,0},{0,4},{29,25},... | collective-permute-start | bytes 393224 | tf_op jit(solution)/shard_map/ppermute | solution.py:359
  43.2 2.1 %collective-permute-start.17 = (f32[2,128,128]{2,1,0:T(8,128)S(1)}, f32[2,128,128]{2,1,0:T(8,128)S(1)}, u32[]{:S(2)}, u32[]{:S(2)}) collective-permute-start(f32[2,128,128]{2,1,0:T(8,128)S(1)} %get-tuple-element.125), channel_id=1, source_target_pairs={{28,24},{24,28},{20,16},{16,20},{12,8},{8,12},{4,0},{0,4},{29,25},... | collective-permute-start | bytes 393224 | tf_op jit(solution)/shard_map/ppermute | solution.py:359

commit v9 on v8

--- a/solution.py
+++ b/solution.py
@@ -197,14 +197,24 @@
         sum_ref[j] = totals[j]
 
 
-def local_kernel(same, pieces, q_ref, k_ref, v_ref, turned_ref, pre_ref, *refs):
-    qgrad_hbm, kpart_ref, vpart_ref, qgrad_ref, sems = refs[-5:]
+def local_kernel(pieces, second, q_ref, k_ref, v_ref, turned_ref, pre_ref, *refs):
+    if second:
+        qgrad_hbm, tail_ref, kpart_ref, vpart_ref, qgrad_ref, sems = refs[-6:]
+        first_ref = refs[3 * pieces]
+    else:
+        qgrad_ref, kpart_ref, vpart_ref = refs[-3:]
     state = heads_in(refs[:pieces])
     g_refs, post_refs = refs[pieces:2 * pieces], refs[2 * pieces:3 * pieces]
     rows, width = q_ref.shape
-    target = columns(same, width)
     parts = chunks_of(rows)
     copies = []
+
+    def send(source, lanes, part):
+        copies.append(pltpu.make_async_copy(source, qgrad_hbm.at[part, lanes], sems.at[len(copies)]))
+        copies[-1].start()
+
+    if second:
+        send(first_ref, columns(False, width), slice(0, rows))
 
     def scores(i, j):
         part, lanes = parts[i], lanes_of(j)
@@ -226,7 +236,10 @@
             post = post_refs[j // PIECE][i, j % PIECE]
             kgrad = kgrad + dot(v, post, 1, 1)
             vgrad = vgrad + dot(k, post)
-        qgrad_ref[part, lanes] = qgrad.astype(BF16)
+        if second and i == len(parts) - 1:
+            tail_ref[:, lanes] = qgrad.astype(BF16)
+        else:
+            qgrad_ref[part, lanes] = qgrad.astype(BF16)
         kpart_ref[part, lanes] = kgrad
         vpart_ref[part, lanes] = vgrad
 
@@ -236,11 +249,9 @@
         coming = scores(*following) if following else None
         products(*place, *ready)
         ready = coming
-        i = place[0]
-        if following is None or following[0] != i:
-            source, out = qgrad_ref.at[parts[i]], qgrad_hbm.at[parts[i], target]
-            copies.append(pltpu.make_async_copy(source, out, sems.at[i]))
-            copies[-1].start()
+        if second and following and following[0] != place[0]:
+            part = parts[place[0]]
+            send(qgrad_ref.at[part], columns(True, width), part)
     for copy in copies:
         copy.wait()
 
@@ -260,24 +271,26 @@
         final_part(piece, part, *refs)
 
 
-def write_kernel(same, piece, *refs):
-    kgrad_hbm, vgrad_hbm, kgrad_ref, vgrad_ref, sems = refs[-5:]
-    done = refs[5:5 + 2 * piece]
+def last_kernel(count, *refs):
+    qgrad_hbm, kgrad_hbm, vgrad_hbm, kgrad_ref, vgrad_ref, sems = refs[-6:]
+    near, far, tail_ref = refs[5:5 + 2 * count], refs[5 + 2 * count:3 + 4 * count], refs[3 + 4 * count]
     rows, width = refs[0].shape
-    copies = []
-
-    def send(source, out, part, number):
-        target = out.at[part, columns(same, width, number)]
-        copies.append(pltpu.make_async_copy(source.at[part], target, sems.at[len(copies)]))
+    everything, copies = slice(0, rows), []
+
+    def send(source, out, part, lanes):
+        copies.append(pltpu.make_async_copy(source, out.at[part, lanes], sems.at[len(copies)]))
         copies[-1].start()
 
-    for number in range(piece):
-        send(done[2 * number], kgrad_hbm, slice(0, rows), number)
-        send(done[2 * number + 1], vgrad_hbm, slice(0, rows), number)
+    for same, done in ((False, near), (True, far)):
+        for i, source in enumerate(done):
+            out = vgrad_hbm if i % 2 else kgrad_hbm
+            send(source, out, everything, columns(same, width, i // 2))
+    send(tail_ref, qgrad_hbm, chunks_of(rows)[-1], columns(True, width))
     for part in chunks_of(rows):
-        final_part(piece, part, *refs[:5], kgrad_ref, vgrad_ref)
-        send(kgrad_ref, kgrad_hbm, part, piece)
-        send(vgrad_ref, vgrad_hbm, part, piece)
+        final_part(count - 1, part, *refs[:5], kgrad_ref, vgrad_ref)
+        lanes = columns(True, width, count - 1)
+        send(kgrad_ref.at[part], kgrad_hbm, part, lanes)
+        send(vgrad_ref.at[part], vgrad_hbm, part, lanes)
     for copy in copies:
         copy.wait()
 
@@ -329,7 +342,7 @@
     )
 
 
-def scan_states(keeps, extras, backward, beside):
+def scan_states(keeps, extras, backward, beside, between):
     plan = scan_plan(lax.axis_size("seq"))
     came = [[] for _ in keeps]
     results, after = [], []
@@ -343,13 +356,15 @@
         made = [work(messages) for work in mine]
         after = [item[-1] for item in made]
         results += made
-    states, messages = [], []
+    states, messages, early = [], [], ()
     for keep, extra, arrived in zip(keeps, extras, came):
-        message, state = join(backward, keep, extra, arrived, True, after + messages)
+        token = [*after, *messages, *early[-1:]]
+        message, state = join(backward, keep, extra, arrived, True, token)
         states.append(state)
         messages.append(message)
+        early = early or between(state, results)
     others = [nearby(message, backward) for message in messages[::-1]][::-1]
-    return states, others, results
+    return states, others, results, early
 
 
 def move(value, pairs, backward):
@@ -406,28 +421,34 @@
             [pltpu.VMEM((rows, half), BF16), sems],
         )
 
-    state2, state1, made = scan_states(
-        keeps, extras, False,
-        [inner_of(True, k2, v2, pre2), inner_of(False, k1, v1, pre1)],
-    )
-    (q2, inner2, scaled2, qturned2, turned2), (q1, inner1, scaled1, qturned1, turned1) = made
-
-    attns, sums = [], ()
     piece_wide = shape((rows, PIECE * HEAD_DIM), F32)
-    for number, state in enumerate([*state2, *state1]):
-        args = (q2, inner2, scaled2) if number < count else (q1, inner1, scaled1)
+
+    def attn_of(number, inner, state, sums):
         last = number == 2 * count - 1
-        attn, *sums = run(
+        return run(
             partial(attn_kernel, number % count, number == 0, last), unit // count,
             [VMEM] * (4 + len(sums)), [VMEM] * (2 if last else 3),
             [piece_wide] + ([shape((8, rows), F32)] if last else [lane_sums] * 2),
-            (*args, state, *sums),
+            (*inner, state, *sums),
         )
+
+    state2, state1, made, early = scan_states(
+        keeps, extras, False,
+        [inner_of(True, k2, v2, pre2), inner_of(False, k1, v1, pre1)],
+        lambda state, made: attn_of(0, made[0][:3], state, ()),
+    )
+    (q2, inner2, scaled2, qturned2, turned2), (q1, inner1, scaled1, qturned1, turned1) = made
+
+    attn, *sums = early
+    attns = [attn]
+    for number, state in list(enumerate([*state2, *state1]))[1:]:
+        inner = (q2, inner2, scaled2) if number < count else (q1, inner1, scaled1)
+        attn, *sums = attn_of(number, inner, state, sums)
         attns.append(attn)
     sums = sums[0]
     parts = [sums] + [
         lax.ppermute(sums, "head", [(r, r ^ other) for r in range(peers)])
-        for other in range(1, peers)
+        for other in [*range(2, peers), 1][:peers - 1]
     ]
 
     factors = []
@@ -453,53 +474,59 @@
     gextras = [nearby(gsend, True) for gsend in gsends]
     gs1, posts1, gkeeps = grads_of(attns[count:], scaled1, qturned1)
 
-    qgrads = []
-
-    def local_of(same, *args):
+    def local_of(second, *args):
         def work(messages):
-            more = list(messages) + qgrads
-            qgrad, kpart, vpart = run(
-                partial(local_kernel, same, count), 9 * unit,
-                [VMEM] * len(args) + [ANYWHERE] * len(messages) + [HBM] * len(qgrads),
-                [HBM, VMEM, VMEM], [whole, wide, wide], (*args, *more),
-                [pltpu.VMEM((rows, half), BF16), sems],
-                {len(args) + len(messages): 0} if qgrads else None,
+            more = (*first_grads, *messages)
+            outs = [VMEM] * 3, [thin, wide, wide], ()
+            if second:
+                tail = shape((rows // chunks, half), BF16)
+                outs = (
+                    [HBM] + [VMEM] * 3, [whole, tail, wide, wide],
+                    [pltpu.VMEM((rows, half), BF16), sems],
+                )
+            qgrad, *others = run(
+                partial(local_kernel, count, second), 9 * unit,
+                [VMEM] * (len(args) + len(first_grads)) + [ANYWHERE] * len(messages), outs[0], outs[1],
+                (*args, *more), outs[2],
             )
-            qgrads[:] = [qgrad]
-            return kpart, vpart
+            first_grads.append(qgrad)
+            return (qgrad, *others)
 
         return work
 
-    gstate1, gstate2, made = scan_states(
+    piece_thin = shape((rows, PIECE * HEAD_DIM), BF16)
+
+    def final_of(piece, args, state):
+        return run(
+            partial(final_kernel, piece), 2 * unit // count, [VMEM] * 5, [VMEM] * 2,
+            [piece_thin] * 2, (*args, state),
+        )
+
+    first_grads = []
+    gstate1, gstate2, made, early = scan_states(
         gkeeps, gextras, True,
         [
             local_of(False, q1, k1, v1, turned1, pre1, *state1, *gs1, *posts1),
             local_of(True, q2, k2, v2, turned2, pre2, *state2, *gs2, *posts2),
         ],
-    )
-    (kpart1, vpart1), (kpart2, vpart2) = made
-
-    piece_thin = shape((rows, PIECE * HEAD_DIM), BF16)
-
-    def finals_of(same, k, v, kpart, vpart, found, outs):
-        done = []
-        for piece, state in enumerate(found[:-1]):
-            done += run(
-                partial(final_kernel, piece), 2 * unit // count, [VMEM] * 5, [VMEM] * 2,
-                [piece_thin] * 2, (k, v, kpart, vpart, state),
-            )
-        args = (k, v, kpart, vpart, found[-1], *done)
-        return run(
-            partial(write_kernel, same, count - 1), 2 * unit // count,
-            [VMEM] * len(args) + [HBM] * len(outs), [HBM, HBM], [whole, whole], (*args, *outs),
-            [pltpu.VMEM(piece_thin.shape, BF16)] * 2
-            + [pltpu.SemaphoreType.DMA((2 * (chunks + count - 1),))],
-            {len(args) + i: i for i in range(len(outs))},
-        )
-
-    outs = finals_of(False, k1, v1, kpart1, vpart1, gstate1, ())
-    kgrad, vgrad = finals_of(True, k2, v2, kpart2, vpart2, gstate2, outs)
-    return qgrads[0], kgrad, vgrad
+        lambda state, made: final_of(0, (k1, v1, *made[0][1:]), state),
+    )
+    (_, kpart1, vpart1), (qgrad, tail, kpart2, vpart2) = made
+
+    done = list(early)
+    for piece in range(1, count):
+        done += final_of(piece, (k1, v1, kpart1, vpart1), gstate1[piece])
+    for piece in range(count - 1):
+        done += final_of(piece, (k2, v2, kpart2, vpart2), gstate2[piece])
+    args = (k2, v2, kpart2, vpart2, gstate2[-1], *done, tail)
+    qgrad, kgrad, vgrad = run(
+        partial(last_kernel, count), 2 * unit // count, [VMEM] * len(args) + [HBM],
+        [HBM] * 3, [whole] * 3, (*args, qgrad),
+        [pltpu.VMEM(piece_thin.shape, BF16)] * 2
+        + [pltpu.SemaphoreType.DMA((2 * (chunks + 2 * count - 1) + 1,))],
+        {len(args): 0},
+    )
+    return qgrad, kgrad, vgrad
 
 
 def solution(mesh):

time: 46.9 us -> 47.3 us (level)
  Pallas kernels: 23.2 us -> 21.9 us
  starting transfers between devices: 16.5 us -> 17.8 us
    ppermute x16, starting transfers between devices: 12.1 us -> 13.6 us  [move(): return lax.ppermute(value, 'seq', pairs)]
    pallas_call x30, Pallas kernels: 23.2 us -> 21.9 us  [run(): pl.pallas_call(kernel, in_specs=in_specs, out_specs=out_specs, out_shape=...]
    ppermute x3, waiting for transfers between devices: 3.94 us -> 4.87 us  [shards(): lax.ppermute(sums, 'head', [(r, r ^ other) for r in range(peers)])]
    ppermute x16, waiting for transfers between devices: 1.93 us -> 1.42 us  [move(): return lax.ppermute(value, 'seq', pairs)]
  transfers between devices with their start and end apart: 19 -> 19, of which waited for: 8 -> 7; matrix products, arithmetic and copies ran while one was open for 0% -> 0% of each run, Pallas kernels for 40% -> 35%
where the time goes in v9:
time: 47.3 us; the launch traced here: 47.1 us
  Pallas kernels  21.9 us (46%)
  starting transfers between devices  17.8 us (38%)
  waiting for transfers between devices  6.28 us (13%)
  between operations  1.09 us (2%)
    pallas_call x30, Pallas kernels, run(): pl.pallas_call(kernel, in_specs=in_specs, out_specs=out_specs, out_shape=...  21.9 us
    ppermute x16, starting transfers between devices, move(): return lax.ppermute(value, 'seq', pairs)  13.6 us
    ppermute x3, waiting for transfers between devices, shards(): lax.ppermute(sums, 'head', [(r, r ^ other) for r in range(peers)])  4.87 us
    ppermute x3, starting transfers between devices, shards(): lax.ppermute(sums, 'head', [(r, r ^ other) for r in range(peers)])  4.24 us
    ppermute x16, waiting for transfers between devices, move(): return lax.ppermute(value, 'seq', pairs)  1.42 us
  transfers between devices with their start and end apart: 19, of which 7 were waited for; matrix products, arithmetic and copies ran while one was open for 0% of the time, Pallas kernels for 35%

profile of v9, /device:TPU:0, one launch (start us, length us, event | category | flops | bytes accessed | tf_op | source)
XLA Modules:
  0.0 47.1 jit_solution(12224554189862955634)
XLA Ops:
  0.6 2.1 %shard_map.76 = (bf16[768,512]{1,0:T(8,128)(2,1)S(1)}, bf16[768,512]{1,0:T(8,128)(2,1)S(1)}, bf16[768,512]{1,0:T(8,128)(2,1)S(1)}, bf16[768,512]{1,0:T(8,128)(2,...) custom-call(bf16[768,1024]{1,0:T(8,128)(2,1)} %k_hbm.1, ...), custom_call_target="tpu_custom_call" | custom-call | flops 100663296 | bytes 3145728 | tf_op jit(solution)/shard_map/pallas_call | solution.py:55
  2.8 0.5 %collective-permute-start = (f32[2,128,128]{2,1,0:T(8,128)S(1)}, f32[2,128,128]{2,1,0:T(8,128)S(1)}, u32[]{:S(2)}, u32[]{:S(2)}) collective-permute-start(f32[2,128,128]{2,1,0:T(8,128)S(1)} %get-tuple-element.73), channel_id=1, source_target_pairs={{0,4},{4,0},{8,12},{12,8},{16,20},{20,16},{24,28},{28,24},{1,5},{5... | collective-permute-start | bytes 393224 | tf_op jit(solution)/shard_map/ppermute | solution.py:374
  3.4 0.4 shard_map.77
  3.8 0.5 %collective-permute-done.refs_1_ = f32[2,128,128]{2,1,0:T(8,128)S(1)} collective-permute-done((f32[2,128,128]{2,1,0:T(8,128)S(1)}, f32[2,128,128]{2,1,0:T(8,128)S(1)}, u32[]{:S(2)}, u32[]{:S(2)}) %collective-permute-start) | collective-permute-done | bytes 131104 | tf_op jit(solution)/shard_map/ppermute | solution.py:374
  4.3 2.9 %collective-permute-start.2 = (f32[2,128,128]{2,1,0:T(8,128)S(1)}, f32[2,128,128]{2,1,0:T(8,128)S(1)}, u32[]{:S(2)}, u32[]{:S(2)}) collective-permute-start(f32[2,128,128]{2,1,0:T(8,128)S(1)} %shard_map.78.refs_2_.refs_0_), channel_id=1, source_target_pairs={{0,8},{4,20},{8,0},{12,28},{16,24},{20,4},{24,16},{28,12},{1,9},{5... | collective-permute-start | bytes 393224 | tf_op jit(solution)/shard_map/ppermute | solution.py:374
  7.4 3.3 %shard_map.80 = (bf16[768,512]{1,0:T(8,128)(2,1)S(1)}, f32[768,512]{1,0:T(8,128)S(1)}, f32[768,512]{1,0:T(8,128)S(1)}, bf16[512,768]{1,0:T(8,128)(2,1)S(1)}, bf16[4,768,256]{2,1,0:T(8,128)(2,1)S(1)}) custom-call(bf16[768,1024]{1,0:T(8,128)(2,1)} %q_hbm.3, bf16[768,1024]{1,0:T(8,128)(2,1)} %og_hbm.3, bf16[768,512]{1,0:T(8,128)(2,1)S(1)} %get-tuple-element.69.k_ref.refs_0_, ...), custom_call_target="tpu_custom_call" | custom-call | flops 603979776 | bytes 3145728 | tf_op jit(solution)/shard_map/pallas_call | solution.py:55
  10.8 2.0 %collective-permute-start.3 = (f32[2,128,128]{2,1,0:T(8,128)S(1)}, f32[2,128,128]{2,1,0:T(8,128)S(1)}, u32[]{:S(2)}, u32[]{:S(2)}) collective-permute-start(f32[2,128,128]{2,1,0:T(8,128)S(1)} %shard_map.81.refs_4_.refs_0_), channel_id=1, source_target_pairs={{0,16},{4,12},{8,24},{12,4},{16,0},{20,28},{24,8},{28,20},{1,17},{... | collective-permute-start | bytes 393224 | tf_op jit(solution)/shard_map/ppermute | solution.py:374
  12.9 1.0 %collective-permute-start.5 = (f32[2,128,128]{2,1,0:T(8,128)S(1)}, f32[2,128,128]{2,1,0:T(8,128)S(1)}, u32[]{:S(2)}, u32[]{:S(2)}) collective-permute-start(f32[2,128,128]{2,1,0:T(8,128)S(1)} %shard_map.82.refs_1_), channel_id=1, source_target_pairs={{0,16},{4,12},{8,24},{12,4},{16,0},{20,28},{24,8},{28,20},{1,17},{... | collective-permute-start | bytes 393224 | tf_op jit(solution)/shard_map/ppermute | solution.py:374
  13.9 3.3 %shard_map.83 = (bf16[768,512]{1,0:T(8,128)(2,1)S(1)}, f32[768,512]{1,0:T(8,128)S(1)}, f32[768,512]{1,0:T(8,128)S(1)}, bf16[512,768]{1,0:T(8,128)(2,1)S(1)}, bf16[4,768,256]{2,1,0:T(8,128)(2,1)S(1)}) custom-call(bf16[768,1024]{1,0:T(8,128)(2,1)} %q_hbm.3, bf16[768,1024]{1,0:T(8,128)(2,1)} %og_hbm.3, bf16[768,512]{1,0:T(8,128)(2,1)S(1)} %get-tuple-element.78.k_ref.refs_0_, ...), custom_call_target="tpu_custom_call" | custom-call | flops 603979776 | bytes 3145728 | tf_op jit(solution)/shard_map/pallas_call | solution.py:55
  19.4 0.5 %shard_map.89 = (f32[768,256]{1,0:T(8,128)S(1)}, f32[8,768]{1,0:T(8,128)S(1)}) custom-call(bf16[768,512]{1,0:T(8,128)(2,1)S(1)} %get-tuple-element.88.q_ref, f32[768,512]{1,0:T(8,128)S(1)} %get-tuple-element.89.inner_ref, f32[768,512]{1,0:T(8,128)S(1)} %get-tuple-element.90.scaled_ref.refs_3_, f32[2,128,128]{2,1,0:T(8,128)S(1)} %collective-permute-done.6.state_ref.refs_1_, ...), custom_call_target="tpu_custom_call" | custom-call | flops 50331648 | tf_op jit(solution)/shard_map/pallas_call | solution.py:55
  19.9 1.6 %collective-permute-start.10 = (f32[8,768]{1,0:T(8,128)S(1)}, f32[8,768]{1,0:T(8,128)S(1)}, u32[]{:S(2)}, u32[]{:S(2)}) collective-permute-start(f32[8,768]{1,0:T(8,128)S(1)} %get-tuple-element.97.refs_0_), channel_id=1, source_target_pairs={{0,1},{1,0},{2,3},{3,2},{4,5},{5,4},{6,7},{7,6},{8,9},{9,8},{10,11... | collective-permute-start | bytes 73736 | tf_op jit(solution)/shard_map/ppermute | solution.py:450
  21.6 2.5 %collective-permute-start.9 = (f32[8,768]{1,0:T(8,128)S(1)}, f32[8,768]{1,0:T(8,128)S(1)}, u32[]{:S(2)}, u32[]{:S(2)}) collective-permute-start(f32[8,768]{1,0:T(8,128)S(1)} %get-tuple-element.97.refs_0_), channel_id=1, source_target_pairs={{0,3},{1,2},{2,1},{3,0},{4,7},{5,6},{6,5},{7,4},{8,11},{9,10},{10,... | collective-permute-start | bytes 73736 | tf_op jit(solution)/shard_map/ppermute | solution.py:450
  24.2 3.0 %collective-permute-done.9.refs_2_ = f32[8,768]{1,0:T(8,128)S(1)} collective-permute-done((f32[8,768]{1,0:T(8,128)S(1)}, f32[8,768]{1,0:T(8,128)S(1)}, u32[]{:S(2)}, u32[]{:S(2)}) %collective-permute-start.9) | collective-permute-done | bytes 24608 | tf_op jit(solution)/shard_map/ppermute | solution.py:450
  27.2 1.8 %collective-permute-done.8.refs_1_ = f32[8,768]{1,0:T(8,128)S(1)} collective-permute-done((f32[8,768]{1,0:T(8,128)S(1)}, f32[8,768]{1,0:T(8,128)S(1)}, u32[]{:S(2)}, u32[]{:S(2)}) %collective-permute-start.8) | collective-permute-done | bytes 24608 | tf_op jit(solution)/shard_map/ppermute | solution.py:450
  29.0 0.7 %shard_map.90 = (bf16[768,256]{1,0:T(8,128)(2,1)S(1)}, bf16[3,2,128,128]{3,2,1,0:T(8,128)(2,1)S(1)}, f32[2,128,128]{2,1,0:T(8,128)S(1)}, f32[768,128]{1,0:T(8,128)S(1)}, f32[768,128]{1,0:T(8,128)S(1)}) custom-call(f32[8,768]{1,0:T(8,128)S(1)} %get-tuple-element.97.refs_0_, f32[8,768]{1,0:T(8,128)S(1)} %collective-permute-done.8.refs_1_, ...), custom_call_target="tpu_custom_call" | custom-call | flops 50331648 | tf_op jit(solution)/shard_map/pallas_call | solution.py:55
  30.2 0.6 %collective-permute-start.12 = (f32[2,128,128]{2,1,0:T(8,128)S(1)}, f32[2,128,128]{2,1,0:T(8,128)S(1)}, u32[]{:S(2)}, u32[]{:S(2)}) collective-permute-start(f32[2,128,128]{2,1,0:T(8,128)S(1)} %get-tuple-element.117), channel_id=1, source_target_pairs={{28,24},{24,28},{20,16},{16,20},{12,8},{8,12},{4,0},{0,4},{29,25},... | collective-permute-start | bytes 393224 | tf_op jit(solution)/shard_map/ppermute | solution.py:374
  31.2 1.4 %collective-permute-start.13 = (f32[2,128,128]{2,1,0:T(8,128)S(1)}, f32[2,128,128]{2,1,0:T(8,128)S(1)}, u32[]{:S(2)}, u32[]{:S(2)}) collective-permute-start(f32[2,128,128]{2,1,0:T(8,128)S(1)} %shard_map.94.refs_2_.refs_6_), channel_id=1, source_target_pairs={{28,20},{24,8},{20,28},{16,0},{12,4},{8,24},{4,12},{0,16},{29,21},... | collective-permute-start | bytes 393224 | tf_op jit(solution)/shard_map/ppermute | solution.py:374
  32.9 0.8 %collective-permute-start.14 = (f32[2,128,128]{2,1,0:T(8,128)S(1)}, f32[2,128,128]{2,1,0:T(8,128)S(1)}, u32[]{:S(2)}, u32[]{:S(2)}) collective-permute-start(f32[2,128,128]{2,1,0:T(8,128)S(1)} %shard_map.95.refs_7_), channel_id=1, source_target_pairs={{28,20},{24,8},{20,28},{16,0},{12,4},{8,24},{4,12},{0,16},{29,21},... | collective-permute-start | bytes 393224 | tf_op jit(solution)/shard_map/ppermute | solution.py:374
  33.7 2.7 %shard_map.96 = (bf16[768,512]{1,0:T(8,128)(2,1)S(1)}, f32[768,512]{1,0:T(8,128)S(1)}, f32[768,512]{1,0:T(8,128)S(1)}) custom-call(bf16[768,512]{1,0:T(8,128)(2,1)S(1)} %get-tuple-element.88.q_ref, bf16[768,512]{1,0:T(8,128)(2,1)S(1)} %get-tuple-element.78.k_ref.refs_0_, bf16[768,512]{1,0:T(8,128)(2,1)S(1)} %get-tuple-element.79.v_ref.refs_1_, ...), custom_call_target="tpu_custom_call" | custom-call | flops 905969664 | tf_op jit(solution)/shard_map/pallas_call | solution.py:55
  36.5 1.6 %collective-permute-start.16 = (f32[2,128,128]{2,1,0:T(8,128)S(1)}, f32[2,128,128]{2,1,0:T(8,128)S(1)}, u32[]{:S(2)}, u32[]{:S(2)}) collective-permute-start(f32[2,128,128]{2,1,0:T(8,128)S(1)} %shard_map.97.refs_4_.refs_7_), channel_id=1, source_target_pairs={{28,12},{24,16},{20,4},{16,24},{12,28},{8,0},{4,20},{0,8},{29,13},... | collective-permute-start | bytes 393224 | tf_op jit(solution)/shard_map/ppermute | solution.py:374
  38.1 1.5 %collective-permute-start.15 = (f32[2,128,128]{2,1,0:T(8,128)S(1)}, f32[2,128,128]{2,1,0:T(8,128)S(1)}, u32[]{:S(2)}, u32[]{:S(2)}) collective-permute-start(f32[2,128,128]{2,1,0:T(8,128)S(1)} %shard_map.98.refs_8_), channel_id=1, source_target_pairs={{28,12},{24,16},{20,4},{16,24},{12,28},{8,0},{4,20},{0,8},{29,13},... | collective-permute-start | bytes 393224 | tf_op jit(solution)/shard_map/ppermute | solution.py:374
  39.5 3.3 %shard_map.99 = (bf16[768,1024]{1,0:T(8,128)(2,1)}, bf16[256,512]{1,0:T(8,128)(2,1)S(1)}, f32[768,512]{1,0:T(8,128)S(1)}, f32[768,512]{1,0:T(8,128)S(1)}) custom-call(bf16[768,512]{1,0:T(8,128)(2,1)S(1)} %get-tuple-element.76.q_ref, bf16[768,512]{1,0:T(8,128)(2,1)S(1)} %get-tuple-element.69.k_ref.refs_0_, ...), custom_call_target="tpu_custom_call" | custom-call | flops 905969664 | tf_op jit(solution)/shard_map/pallas_call | solution.py:55
  43.5 0.6 %collective-permute-start.17 = (f32[2,128,128]{2,1,0:T(8,128)S(1)}, f32[2,128,128]{2,1,0:T(8,128)S(1)}, u32[]{:S(2)}, u32[]{:S(2)}) collective-permute-start(f32[2,128,128]{2,1,0:T(8,128)S(1)} %get-tuple-element.126), channel_id=1, source_target_pairs={{28,24},{24,28},{20,16},{16,20},{12,8},{8,12},{4,0},{0,4},{29,25},... | collective-permute-start | bytes 393224 | tf_op jit(solution)/shard_map/ppermute | solution.py:374
  45.1 1.9 %shard_map.105 = (bf16[768,1024]{1,0:T(8,128)(2,1)}, bf16[768,1024]{1,0:T(8,128)(2,1)}, bf16[768,1024]{1,0:T(8,128)(2,1)}) custom-call(bf16[768,512]{1,0:T(8,128)(2,1)S(1)} %get-tuple-element.69.k_ref.refs_0_, bf16[768,512]{1,0:T(8,128)(2,1)S(1)} %get-tuple-element.70.v_ref.refs_1_, ...), custom_call_target="tpu_custom_call", output_to_operand_aliasing={{0}: (12, {})} | custom-call | flops 100663296 | bytes 1572864 | tf_op jit(solution)/shard_map/pallas_call | solution.py:55
  (46 shorter events, 5.4 us)
Async XLA Ops:
  2.8 4.6 %copy-start = (f32[1024]{0:T(1024)S(1)}, f32[1024]{0:T(1024)}, u32[]{:S(2)}) copy-start(f32[1024]{0:T(1024)} %param.9) | copy-start | bytes 12292
  2.8 1.5 %collective-permute-start = (f32[2,128,128]{2,1,0:T(8,128)S(1)}, f32[2,128,128]{2,1,0:T(8,128)S(1)}, u32[]{:S(2)}, u32[]{:S(2)}) collective-permute-start(f32[2,128,128]{2,1,0:T(8,128)S(1)} %get-tuple-element.73), channel_id=1, source_target_pairs={{0,4},{4,0},{8,12},{12,8},{16,20},{20,16},{24,28},{28,24},{1,5},{5... | collective-permute-start | bytes 393224 | tf_op jit(solution)/shard_map/ppermute | solution.py:374
  3.3 3.9 %collective-permute-start.1 = (f32[2,128,128]{2,1,0:T(8,128)S(1)}, f32[2,128,128]{2,1,0:T(8,128)S(1)}, u32[]{:S(2)}, u32[]{:S(2)}) collective-permute-start(f32[2,128,128]{2,1,0:T(8,128)S(1)} %get-tuple-element.75), channel_id=1, source_target_pairs={{0,4},{4,0},{8,12},{12,8},{16,20},{20,16},{24,28},{28,24},{1,5},{5... | collective-permute-start | bytes 393224 | tf_op jit(solution)/shard_map/ppermute | solution.py:374
  4.3 6.4 %collective-permute-start.2 = (f32[2,128,128]{2,1,0:T(8,128)S(1)}, f32[2,128,128]{2,1,0:T(8,128)S(1)}, u32[]{:S(2)}, u32[]{:S(2)}) collective-permute-start(f32[2,128,128]{2,1,0:T(8,128)S(1)} %shard_map.78.refs_2_.refs_0_), channel_id=1, source_target_pairs={{0,8},{4,20},{8,0},{12,28},{16,24},{20,4},{24,16},{28,12},{1,9},{5... | collective-permute-start | bytes 393224 | tf_op jit(solution)/shard_map/ppermute | solution.py:374
  7.3 5.6 %collective-permute-start.4 = (f32[2,128,128]{2,1,0:T(8,128)S(1)}, f32[2,128,128]{2,1,0:T(8,128)S(1)}, u32[]{:S(2)}, u32[]{:S(2)}) collective-permute-start(f32[2,128,128]{2,1,0:T(8,128)S(1)} %shard_map.79.refs_1_), channel_id=1, source_target_pairs={{0,8},{4,20},{8,0},{12,28},{16,24},{20,4},{24,16},{28,12},{1,9},{5... | collective-permute-start | bytes 393224 | tf_op jit(solution)/shard_map/ppermute | solution.py:374
  10.8 6.4 %collective-permute-start.3 = (f32[2,128,128]{2,1,0:T(8,128)S(1)}, f32[2,128,128]{2,1,0:T(8,128)S(1)}, u32[]{:S(2)}, u32[]{:S(2)}) collective-permute-start(f32[2,128,128]{2,1,0:T(8,128)S(1)} %shard_map.81.refs_4_.refs_0_), channel_id=1, source_target_pairs={{0,16},{4,12},{8,24},{12,4},{16,0},{20,28},{24,8},{28,20},{1,17},{... | collective-permute-start | bytes 393224 | tf_op jit(solution)/shard_map/ppermute | solution.py:374
  12.9 5.0 %collective-permute-start.5 = (f32[2,128,128]{2,1,0:T(8,128)S(1)}, f32[2,128,128]{2,1,0:T(8,128)S(1)}, u32[]{:S(2)}, u32[]{:S(2)}) collective-permute-start(f32[2,128,128]{2,1,0:T(8,128)S(1)} %shard_map.82.refs_1_), channel_id=1, source_target_pairs={{0,16},{4,12},{8,24},{12,4},{16,0},{20,28},{24,8},{28,20},{1,17},{... | collective-permute-start | bytes 393224 | tf_op jit(solution)/shard_map/ppermute | solution.py:374
  17.3 1.4 %collective-permute-start.7 = (f32[2,128,128]{2,1,0:T(8,128)S(1)}, f32[2,128,128]{2,1,0:T(8,128)S(1)}, u32[]{:S(2)}, u32[]{:S(2)}) collective-permute-start(f32[2,128,128]{2,1,0:T(8,128)S(1)} %get-tuple-element.83.refs_5_), channel_id=1, source_target_pairs={{0,4},{4,0},{8,12},{12,8},{16,20},{20,16},{24,28},{28,24},{1,5},{5... | collective-permute-start | bytes 393224 | tf_op jit(solution)/shard_map/ppermute | solution.py:374
  18.0 1.4 %collective-permute-start.6 = (f32[2,128,128]{2,1,0:T(8,128)S(1)}, f32[2,128,128]{2,1,0:T(8,128)S(1)}, u32[]{:S(2)}, u32[]{:S(2)}) collective-permute-start(f32[2,128,128]{2,1,0:T(8,128)S(1)} %get-tuple-element.91), channel_id=1, source_target_pairs={{0,4},{4,0},{8,12},{12,8},{16,20},{20,16},{24,28},{28,24},{1,5},{5... | collective-permute-start | bytes 393224 | tf_op jit(solution)/shard_map/ppermute | solution.py:374
  19.9 4.2 %collective-permute-start.10 = (f32[8,768]{1,0:T(8,128)S(1)}, f32[8,768]{1,0:T(8,128)S(1)}, u32[]{:S(2)}, u32[]{:S(2)}) collective-permute-start(f32[8,768]{1,0:T(8,128)S(1)} %get-tuple-element.97.refs_0_), channel_id=1, source_target_pairs={{0,1},{1,0},{2,3},{3,2},{4,5},{5,4},{6,7},{7,6},{8,9},{9,8},{10,11... | collective-permute-start | bytes 73736 | tf_op jit(solution)/shard_map/ppermute | solution.py:450
  21.6 5.6 %collective-permute-start.9 = (f32[8,768]{1,0:T(8,128)S(1)}, f32[8,768]{1,0:T(8,128)S(1)}, u32[]{:S(2)}, u32[]{:S(2)}) collective-permute-start(f32[8,768]{1,0:T(8,128)S(1)} %get-tuple-element.97.refs_0_), channel_id=1, source_target_pairs={{0,3},{1,2},{2,1},{3,0},{4,7},{5,6},{6,5},{7,4},{8,11},{9,10},{10,... | collective-permute-start | bytes 73736 | tf_op jit(solution)/shard_map/ppermute | solution.py:450
  24.0 5.0 %collective-permute-start.8 = (f32[8,768]{1,0:T(8,128)S(1)}, f32[8,768]{1,0:T(8,128)S(1)}, u32[]{:S(2)}, u32[]{:S(2)}) collective-permute-start(f32[8,768]{1,0:T(8,128)S(1)} %get-tuple-element.97.refs_0_), channel_id=1, source_target_pairs={{0,2},{1,3},{2,0},{3,1},{4,6},{5,7},{6,4},{7,5},{8,10},{9,11},{10,... | collective-permute-start | bytes 73736 | tf_op jit(solution)/shard_map/ppermute | solution.py:450
  29.7 1.4 %collective-permute-start.11 = (f32[2,128,128]{2,1,0:T(8,128)S(1)}, f32[2,128,128]{2,1,0:T(8,128)S(1)}, u32[]{:S(2)}, u32[]{:S(2)}) collective-permute-start(f32[2,128,128]{2,1,0:T(8,128)S(1)} %get-tuple-element.115), channel_id=1, source_target_pairs={{28,24},{24,28},{20,16},{16,20},{12,8},{8,12},{4,0},{0,4},{29,25},... | collective-permute-start | bytes 393224 | tf_op jit(solution)/shard_map/ppermute | solution.py:374
  30.2 2.7 %collective-permute-start.12 = (f32[2,128,128]{2,1,0:T(8,128)S(1)}, f32[2,128,128]{2,1,0:T(8,128)S(1)}, u32[]{:S(2)}, u32[]{:S(2)}) collective-permute-start(f32[2,128,128]{2,1,0:T(8,128)S(1)} %get-tuple-element.117), channel_id=1, source_target_pairs={{28,24},{24,28},{20,16},{16,20},{12,8},{8,12},{4,0},{0,4},{29,25},... | collective-permute-start | bytes 393224 | tf_op jit(solution)/shard_map/ppermute | solution.py:374
  31.2 5.3 %collective-permute-start.13 = (f32[2,128,128]{2,1,0:T(8,128)S(1)}, f32[2,128,128]{2,1,0:T(8,128)S(1)}, u32[]{:S(2)}, u32[]{:S(2)}) collective-permute-start(f32[2,128,128]{2,1,0:T(8,128)S(1)} %shard_map.94.refs_2_.refs_6_), channel_id=1, source_target_pairs={{28,20},{24,8},{20,28},{16,0},{12,4},{8,24},{4,12},{0,16},{29,21},... | collective-permute-start | bytes 393224 | tf_op jit(solution)/shard_map/ppermute | solution.py:374
  32.9 5.1 %collective-permute-start.14 = (f32[2,128,128]{2,1,0:T(8,128)S(1)}, f32[2,128,128]{2,1,0:T(8,128)S(1)}, u32[]{:S(2)}, u32[]{:S(2)}) collective-permute-start(f32[2,128,128]{2,1,0:T(8,128)S(1)} %shard_map.95.refs_7_), channel_id=1, source_target_pairs={{28,20},{24,8},{20,28},{16,0},{12,4},{8,24},{4,12},{0,16},{29,21},... | collective-permute-start | bytes 393224 | tf_op jit(solution)/shard_map/ppermute | solution.py:374
  36.5 6.4 %collective-permute-start.16 = (f32[2,128,128]{2,1,0:T(8,128)S(1)}, f32[2,128,128]{2,1,0:T(8,128)S(1)}, u32[]{:S(2)}, u32[]{:S(2)}) collective-permute-start(f32[2,128,128]{2,1,0:T(8,128)S(1)} %shard_map.97.refs_4_.refs_7_), channel_id=1, source_target_pairs={{28,12},{24,16},{20,4},{16,24},{12,28},{8,0},{4,20},{0,8},{29,13},... | collective-permute-start | bytes 393224 | tf_op jit(solution)/shard_map/ppermute | solution.py:374
  38.1 5.4 %collective-permute-start.15 = (f32[2,128,128]{2,1,0:T(8,128)S(1)}, f32[2,128,128]{2,1,0:T(8,128)S(1)}, u32[]{:S(2)}, u32[]{:S(2)}) collective-permute-start(f32[2,128,128]{2,1,0:T(8,128)S(1)} %shard_map.98.refs_8_), channel_id=1, source_target_pairs={{28,12},{24,16},{20,4},{16,24},{12,28},{8,0},{4,20},{0,8},{29,13},... | collective-permute-start | bytes 393224 | tf_op jit(solution)/shard_map/ppermute | solution.py:374
  43.0 1.5 %collective-permute-start.18 = (f32[2,128,128]{2,1,0:T(8,128)S(1)}, f32[2,128,128]{2,1,0:T(8,128)S(1)}, u32[]{:S(2)}, u32[]{:S(2)}) collective-permute-start(f32[2,128,128]{2,1,0:T(8,128)S(1)} %get-tuple-element.122.refs_5_), channel_id=1, source_target_pairs={{28,24},{24,28},{20,16},{16,20},{12,8},{8,12},{4,0},{0,4},{29,25},... | collective-permute-start | bytes 393224 | tf_op jit(solution)/shard_map/ppermute | solution.py:374
  43.5 1.5 %collective-permute-start.17 = (f32[2,128,128]{2,1,0:T(8,128)S(1)}, f32[2,128,128]{2,1,0:T(8,128)S(1)}, u32[]{:S(2)}, u32[]{:S(2)}) collective-permute-start(f32[2,128,128]{2,1,0:T(8,128)S(1)} %get-tuple-element.126), channel_id=1, source_target_pairs={{28,24},{24,28},{20,16},{16,20},{12,8},{8,12},{4,0},{0,4},{29,25},... | collective-permute-start | bytes 393224 | tf_op jit(solution)/shard_map/ppermute | solution.py:374

commit v10 on v9

--- a/solution.py
+++ b/solution.py
@@ -169,52 +169,53 @@
     return jnp.broadcast_to(both[:, 0:1], wide), jnp.broadcast_to(both[:, 1:2], wide)
 
 
-def grad_kernel(piece, full, parts, *refs):
+def grad_kernel(pieces, full, parts, *refs):
     if parts:
         inv, slope = factors_kernel(full, parts, refs)
         refs[-2][...] = inv
         refs[-1][...] = slope
         inv_ref, slope_ref = refs[-2:]
-        attn_ref, scaled_ref, qturned_ref, g_ref, post_ref, sum_ref = refs[parts:-2]
+        refs = refs[parts:-2]
     else:
-        inv_ref, slope_ref, attn_ref, scaled_ref, qturned_ref, g_ref, post_ref, sum_ref = refs
-    totals = [None] * PIECE
-    for i, part in reversed(list(enumerate(chunks_of(g_ref.shape[0])))):
+        inv_ref, slope_ref = refs[:2]
+        refs = refs[2:]
+    scaled_ref, qturned_ref = refs[:2]
+    count = len(pieces)
+    attns, outs = refs[2:2 + count], refs[2 + count:]
+    for attn_ref, piece, at in zip(attns, pieces, range(0, 3 * count, 3)):
+        g_ref, post_ref, sum_ref = outs[at:at + 3]
+        totals = [None] * PIECE
+        for i, part in reversed(list(enumerate(chunks_of(g_ref.shape[0])))):
+            for j in range(PIECE):
+                lanes = lanes_of(piece * PIECE + j)
+                attn = attn_ref[part, lanes_of(j)]
+                grad = inv_ref[part] * scaled_ref[part, lanes] - attn * slope_ref[part]
+                grad = grad.astype(BF16)
+                g_ref[part, lanes_of(j)] = grad
+                term = dot(qturned_ref[lanes, part], grad)
+                if totals[j] is None:
+                    post_ref[i, j] = jnp.zeros_like(post_ref[i, j])
+                    totals[j] = term
+                else:
+                    post_ref[i, j] = totals[j].astype(BF16)
+                    totals[j] = totals[j] + term
         for j in range(PIECE):
-            lanes = lanes_of(piece * PIECE + j)
-            attn = attn_ref[part, lanes_of(j)]
-            grad = inv_ref[part] * scaled_ref[part, lanes] - attn * slope_ref[part]
-            grad = grad.astype(BF16)
-            g_ref[part, lanes_of(j)] = grad
-            term = dot(qturned_ref[lanes, part], grad)
-            if totals[j] is None:
-                post_ref[i, j] = jnp.zeros_like(post_ref[i, j])
-                totals[j] = term
-            else:
-                post_ref[i, j] = totals[j].astype(BF16)
-                totals[j] = totals[j] + term
-    for j in range(PIECE):
-        sum_ref[j] = totals[j]
+            sum_ref[j] = totals[j]
 
 
 def local_kernel(pieces, second, q_ref, k_ref, v_ref, turned_ref, pre_ref, *refs):
     if second:
-        qgrad_hbm, tail_ref, kpart_ref, vpart_ref, qgrad_ref, sems = refs[-6:]
-        first_ref = refs[3 * pieces]
+        qgrad_hbm, qgrad_ref, kpart_ref, vpart_ref, sem = refs[-5:]
     else:
         qgrad_ref, kpart_ref, vpart_ref = refs[-3:]
     state = heads_in(refs[:pieces])
     g_refs, post_refs = refs[pieces:2 * pieces], refs[2 * pieces:3 * pieces]
     rows, width = q_ref.shape
     parts = chunks_of(rows)
-    copies = []
-
-    def send(source, lanes, part):
-        copies.append(pltpu.make_async_copy(source, qgrad_hbm.at[part, lanes], sems.at[len(copies)]))
-        copies[-1].start()
-
     if second:
-        send(first_ref, columns(False, width), slice(0, rows))
+        target = qgrad_hbm.at[slice(0, rows), columns(False, width)]
+        copy = pltpu.make_async_copy(refs[3 * pieces], target, sem)
+        copy.start()
 
     def scores(i, j):
         part, lanes = parts[i], lanes_of(j)
@@ -236,10 +237,7 @@
             post = post_refs[j // PIECE][i, j % PIECE]
             kgrad = kgrad + dot(v, post, 1, 1)
             vgrad = vgrad + dot(k, post)
-        if second and i == len(parts) - 1:
-            tail_ref[:, lanes] = qgrad.astype(BF16)
-        else:
-            qgrad_ref[part, lanes] = qgrad.astype(BF16)
+        qgrad_ref[part, lanes] = qgrad.astype(BF16)
         kpart_ref[part, lanes] = kgrad
         vpart_ref[part, lanes] = vgrad
 
@@ -249,10 +247,7 @@
         coming = scores(*following) if following else None
         products(*place, *ready)
         ready = coming
-        if second and following and following[0] != place[0]:
-            part = parts[place[0]]
-            send(qgrad_ref.at[part], columns(True, width), part)
-    for copy in copies:
+    if second:
         copy.wait()
 
 
@@ -266,31 +261,24 @@
         vgrad_ref[part, lanes_of(j)] = vgrad.astype(BF16)
 
 
-def final_kernel(piece, *refs):
-    for part in chunks_of(refs[0].shape[0]):
-        final_part(piece, part, *refs)
-
-
-def last_kernel(count, *refs):
-    qgrad_hbm, kgrad_hbm, vgrad_hbm, kgrad_ref, vgrad_ref, sems = refs[-6:]
-    near, far, tail_ref = refs[5:5 + 2 * count], refs[5 + 2 * count:3 + 4 * count], refs[3 + 4 * count]
-    rows, width = refs[0].shape
-    everything, copies = slice(0, rows), []
-
-    def send(source, out, part, lanes):
-        copies.append(pltpu.make_async_copy(source, out.at[part, lanes], sems.at[len(copies)]))
+def final_kernel(piece, own, wholes, plan, *refs):
+    sources = refs[5:5 + len(plan)]
+    *outs, kgrad_ref, vgrad_ref, sems = refs[5 + len(plan):]
+    outs = outs[len(outs) - wholes:]
+    rows, copies = refs[0].shape[0], []
+
+    def send(source, out, part, place):
+        target = outs[out].at[part, columns(*place)]
+        copies.append(pltpu.make_async_copy(source, target, sems.at[len(copies)]))
         copies[-1].start()
 
-    for same, done in ((False, near), (True, far)):
-        for i, source in enumerate(done):
-            out = vgrad_hbm if i % 2 else kgrad_hbm
-            send(source, out, everything, columns(same, width, i // 2))
-    send(tail_ref, qgrad_hbm, chunks_of(rows)[-1], columns(True, width))
+    for source, (out, place) in zip(sources, plan):
+        send(source, out, slice(0, rows), place)
     for part in chunks_of(rows):
-        final_part(count - 1, part, *refs[:5], kgrad_ref, vgrad_ref)
-        lanes = columns(True, width, count - 1)
-        send(kgrad_ref.at[part], kgrad_hbm, part, lanes)
-        send(vgrad_ref.at[part], vgrad_hbm, part, lanes)
+        final_part(piece, part, *refs[:5], kgrad_ref, vgrad_ref)
+        if own:
+            send(kgrad_ref.at[part], 0, part, own)
+            send(vgrad_ref.at[part], 1, part, own)
     for copy in copies:
         copy.wait()
 
@@ -448,83 +436,86 @@
     sums = sums[0]
     parts = [sums] + [
         lax.ppermute(sums, "head", [(r, r ^ other) for r in range(peers)])
-        for other in [*range(2, peers), 1][:peers - 1]
+        for other in range(1, peers)
     ]
 
-    factors = []
-
-    def grads_of(attns, scaled, qturned):
-        made = []
-        for piece, attn in enumerate(attns):
-            peers_in = 0 if factors else len(parts)
-            first = factors or parts
-            g, post, total, *more = run(
-                partial(grad_kernel, piece, full, peers_in), unit // count,
-                [VMEM] * (len(first) + 3), [VMEM] * (3 if factors else 5),
-                [shape((rows, PIECE * HEAD_DIM), BF16), posts, states]
-                + ([] if factors else [lane_sums] * 2),
-                (*first, attn, scaled, qturned),
-            )
-            factors.extend(more)
-            made.append((g, post, total))
-        return zip(*made)
-
     posts = shape((chunks, PIECE, HEAD_DIM, HEAD_DIM), BF16)
-    gs2, posts2, gsends = grads_of(attns[:count], scaled2, qturned2)
+    piece_out = [shape((rows, PIECE * HEAD_DIM), BF16), posts, states]
+
+    def grads_of(pieces, first, attns, scaled, qturned):
+        fresh = len(first) if first is parts else 0
+        shapes = piece_out * len(pieces) + [lane_sums] * (2 if fresh else 0)
+        made = run(
+            partial(grad_kernel, pieces, full, fresh), unit * len(pieces) // count,
+            [VMEM] * (len(first) + 2 + len(pieces)), [VMEM] * len(shapes), shapes,
+            (*first, scaled, qturned, *attns),
+        )
+        return [made[i:i + 3] for i in range(0, 3 * len(pieces), 3)], made[3 * len(pieces):]
+
+    made, factors = grads_of([0], parts, attns[:1], scaled2, qturned2)
+    for piece in range(1, count):
+        made += grads_of([piece], factors, attns[piece:piece + 1], scaled2, qturned2)[0]
+    gs2, posts2, gsends = zip(*made)
     gextras = [nearby(gsend, True) for gsend in gsends]
-    gs1, posts1, gkeeps = grads_of(attns[count:], scaled1, qturned1)
+    made = grads_of(list(range(count)), factors, attns[count:], scaled1, qturned1)[0]
+    gs1, posts1, gkeeps = zip(*made)
+
+    first_grads = []
 
     def local_of(second, *args):
         def work(messages):
-            more = (*first_grads, *messages)
-            outs = [VMEM] * 3, [thin, wide, wide], ()
-            if second:
-                tail = shape((rows // chunks, half), BF16)
-                outs = (
-                    [HBM] + [VMEM] * 3, [whole, tail, wide, wide],
-                    [pltpu.VMEM((rows, half), BF16), sems],
-                )
-            qgrad, *others = run(
+            made = run(
                 partial(local_kernel, count, second), 9 * unit,
-                [VMEM] * (len(args) + len(first_grads)) + [ANYWHERE] * len(messages), outs[0], outs[1],
-                (*args, *more), outs[2],
+                [VMEM] * (len(args) + len(first_grads)) + [ANYWHERE] * len(messages),
+                [HBM] * second + [VMEM] * 3, [whole] * second + [thin, wide, wide],
+                (*args, *first_grads, *messages), [pltpu.SemaphoreType.DMA(())] * second,
             )
-            first_grads.append(qgrad)
-            return (qgrad, *others)
+            first_grads.append(made[0])
+            return made
 
         return work
 
     piece_thin = shape((rows, PIECE * HEAD_DIM), BF16)
 
-    def final_of(piece, args, state):
+    def final_of(piece, args, state, ready=(), outs=(), fresh=0, own=None):
+        sources = [source for source, _, _ in ready]
+        plan = [(out, place) for _, out, place in ready]
+        args = (*args, state, *sources)
+        wholes = len(outs) + fresh
+        last = [pltpu.VMEM(piece_thin.shape, BF16)] * 2 if own else []
         return run(
-            partial(final_kernel, piece), 2 * unit // count, [VMEM] * 5, [VMEM] * 2,
-            [piece_thin] * 2, (*args, state),
+            partial(final_kernel, piece, own, wholes, plan), 2 * unit // count,
+            [VMEM] * len(args) + [HBM] * len(outs),
+            [HBM] * wholes + ([] if own else [VMEM] * 2),
+            [whole] * wholes + ([] if own else [piece_thin] * 2), (*args, *outs),
+            last + [pltpu.SemaphoreType.DMA((len(plan) + 2 * chunks,))],
+            {len(args) + i: i for i in range(len(outs))},
         )
 
-    first_grads = []
     gstate1, gstate2, made, early = scan_states(
         gkeeps, gextras, True,
         [
-            local_of(False, q1, k1, v1, turned1, pre1, *state1, *gs1, *posts1),
-            local_of(True, q2, k2, v2, turned2, pre2, *state2, *gs2, *posts2),
+            local_of(0, q1, k1, v1, turned1, pre1, *state1, *gs1, *posts1),
+            local_of(1, q2, k2, v2, turned2, pre2, *state2, *gs2, *posts2),
         ],
-        lambda state, made: final_of(0, (k1, v1, *made[0][1:]), state),
-    )
-    (_, kpart1, vpart1), (qgrad, tail, kpart2, vpart2) = made
-
-    done = list(early)
+        lambda state, made: final_of(
+            0, (k1, v1, *made[0][1:]), state, [(made[1][1], 0, (True, half))], made[1][:1]
+        ),
+    )
+    near = (k1, v1, *made[0][1:])
+    far = (k2, v2, *made[1][2:])
+    qgrad, *done = early
     for piece in range(1, count):
-        done += final_of(piece, (k1, v1, kpart1, vpart1), gstate1[piece])
+        done += final_of(piece, near, gstate1[piece])
+    ready = [(array, i % 2, (False, half, i // 2)) for i, array in enumerate(done)]
+    outs, done = [], []
     for piece in range(count - 1):
-        done += final_of(piece, (k2, v2, kpart2, vpart2), gstate2[piece])
-    args = (k2, v2, kpart2, vpart2, gstate2[-1], *done, tail)
-    qgrad, kgrad, vgrad = run(
-        partial(last_kernel, count), 2 * unit // count, [VMEM] * len(args) + [HBM],
-        [HBM] * 3, [whole] * 3, (*args, qgrad),
-        [pltpu.VMEM(piece_thin.shape, BF16)] * 2
-        + [pltpu.SemaphoreType.DMA((2 * (chunks + 2 * count - 1) + 1,))],
-        {len(args): 0},
+        *outs, kdone, vdone = final_of(
+            piece, far, gstate2[piece], ready, outs, 0 if outs else 2
+        )
+        ready = [(kdone, 0, (True, half, piece)), (vdone, 1, (True, half, piece))]
+    kgrad, vgrad = final_of(
+        count - 1, far, gstate2[-1], ready, outs, 0 if outs else 2, (True, half, count - 1)
     )
     return qgrad, kgrad, vgrad
 

time: 47.3 us -> 47.9 us (1.013)
  Pallas kernels: 21.9 us -> 23.5 us
  waiting for transfers between devices: 6.28 us -> 5.23 us
    pallas_call x30 -> x29, Pallas kernels: 21.9 us -> 23.5 us  [run(): pl.pallas_call(kernel, in_specs=in_specs, out_specs=out_specs, out_shape=...]
    ppermute x3, waiting for transfers between devices: 4.87 us -> 3.94 us  [shards(): lax.ppermute(sums, 'head', [(r, r ^ other) for r in range(peers)])]
  transfers between devices with their start and end apart: 19 -> 19, of which waited for: 7 -> 7; matrix products, arithmetic and copies ran while one was open for 0% -> 0% of each run, Pallas kernels for 35% -> 40%
where the time goes in v10:
time: 47.9 us; the launch traced here: 47.7 us
  Pallas kernels  23.5 us (49%)
  starting transfers between devices  17.9 us (37%)
  waiting for transfers between devices  5.23 us (11%)
  between operations  1.07 us (2%)
    pallas_call x29, Pallas kernels, run(): pl.pallas_call(kernel, in_specs=in_specs, out_specs=out_specs, out_shape=...  23.5 us
    ppermute x16, starting transfers between devices, move(): return lax.ppermute(value, 'seq', pairs)  13.5 us
    ppermute x3, starting transfers between devices, shards(): lax.ppermute(sums, 'head', [(r, r ^ other) for r in range(peers)])  4.45 us
    ppermute x3, waiting for transfers between devices, shards(): lax.ppermute(sums, 'head', [(r, r ^ other) for r in range(peers)])  3.94 us
    ppermute x16, waiting for transfers between devices, move(): return lax.ppermute(value, 'seq', pairs)  1.28 us
  transfers between devices with their start and end apart: 19, of which 7 were waited for; matrix products, arithmetic and copies ran while one was open for 0% of the time, Pallas kernels for 40%

profile of v10, /device:TPU:0, one launch (start us, length us, event | category | flops | bytes accessed | tf_op | source)
XLA Modules:
  0.0 47.7 jit_solution(3197094201213216198)
XLA Ops:
  0.6 2.1 %shard_map.76 = (bf16[768,512]{1,0:T(8,128)(2,1)S(1)}, bf16[768,512]{1,0:T(8,128)(2,1)S(1)}, bf16[768,512]{1,0:T(8,128)(2,1)S(1)}, bf16[768,512]{1,0:T(8,128)(2,...) custom-call(bf16[768,1024]{1,0:T(8,128)(2,1)} %k_hbm.1, ...), custom_call_target="tpu_custom_call" | custom-call | flops 100663296 | bytes 3145728 | tf_op jit(solution)/shard_map/pallas_call | solution.py:55
  4.3 2.9 %collective-permute-start.1 = (f32[2,128,128]{2,1,0:T(8,128)S(1)}, f32[2,128,128]{2,1,0:T(8,128)S(1)}, u32[]{:S(2)}, u32[]{:S(2)}) collective-permute-start(f32[2,128,128]{2,1,0:T(8,128)S(1)} %shard_map.78.refs_2_.refs_0_), channel_id=1, source_target_pairs={{0,8},{4,20},{8,0},{12,28},{16,24},{20,4},{24,16},{28,12},{1,9},{5... | collective-permute-start | bytes 393224 | tf_op jit(solution)/shard_map/ppermute | solution.py:362
  7.4 3.3 %shard_map.80 = (bf16[768,512]{1,0:T(8,128)(2,1)S(1)}, f32[768,512]{1,0:T(8,128)S(1)}, f32[768,512]{1,0:T(8,128)S(1)}, bf16[512,768]{1,0:T(8,128)(2,1)S(1)}, bf16[4,768,256]{2,1,0:T(8,128)(2,1)S(1)}) custom-call(bf16[768,1024]{1,0:T(8,128)(2,1)} %q_hbm.3, bf16[768,1024]{1,0:T(8,128)(2,1)} %og_hbm.3, bf16[768,512]{1,0:T(8,128)(2,1)S(1)} %get-tuple-element.77.k_ref.refs_0_, ...), custom_call_target="tpu_custom_call" | custom-call | flops 603979776 | bytes 3145728 | tf_op jit(solution)/shard_map/pallas_call | solution.py:55
  10.8 2.0 %collective-permute-start.4 = (f32[2,128,128]{2,1,0:T(8,128)S(1)}, f32[2,128,128]{2,1,0:T(8,128)S(1)}, u32[]{:S(2)}, u32[]{:S(2)}) collective-permute-start(f32[2,128,128]{2,1,0:T(8,128)S(1)} %shard_map.81.refs_4_.refs_0_), channel_id=1, source_target_pairs={{0,16},{4,12},{8,24},{12,4},{16,0},{20,28},{24,8},{28,20},{1,17},{... | collective-permute-start | bytes 393224 | tf_op jit(solution)/shard_map/ppermute | solution.py:362
  12.9 1.0 %collective-permute-start.6 = (f32[2,128,128]{2,1,0:T(8,128)S(1)}, f32[2,128,128]{2,1,0:T(8,128)S(1)}, u32[]{:S(2)}, u32[]{:S(2)}) collective-permute-start(f32[2,128,128]{2,1,0:T(8,128)S(1)} %shard_map.82.refs_1_), channel_id=1, source_target_pairs={{0,16},{4,12},{8,24},{12,4},{16,0},{20,28},{24,8},{28,20},{1,17},{... | collective-permute-start | bytes 393224 | tf_op jit(solution)/shard_map/ppermute | solution.py:362
  13.9 3.3 %shard_map.83 = (bf16[768,512]{1,0:T(8,128)(2,1)S(1)}, f32[768,512]{1,0:T(8,128)S(1)}, f32[768,512]{1,0:T(8,128)S(1)}, bf16[512,768]{1,0:T(8,128)(2,1)S(1)}, bf16[4,768,256]{2,1,0:T(8,128)(2,1)S(1)}) custom-call(bf16[768,1024]{1,0:T(8,128)(2,1)} %q_hbm.3, bf16[768,1024]{1,0:T(8,128)(2,1)} %og_hbm.3, bf16[768,512]{1,0:T(8,128)(2,1)S(1)} %get-tuple-element.74.k_ref.refs_0_, ...), custom_call_target="tpu_custom_call" | custom-call | flops 603979776 | bytes 3145728 | tf_op jit(solution)/shard_map/pallas_call | solution.py:55
  19.4 0.5 %shard_map.89 = (f32[768,256]{1,0:T(8,128)S(1)}, f32[8,768]{1,0:T(8,128)S(1)}) custom-call(bf16[768,512]{1,0:T(8,128)(2,1)S(1)} %get-tuple-element.85.q_ref, f32[768,512]{1,0:T(8,128)S(1)} %get-tuple-element.94.inner_ref, f32[768,512]{1,0:T(8,128)S(1)} %get-tuple-element.95.scaled_ref.refs_2_, f32[2,128,128]{2,1,0:T(8,128)S(1)} %collective-permute-done.7.state_ref.refs_1_, ...), custom_call_target="tpu_custom_call" | custom-call | flops 50331648 | tf_op jit(solution)/shard_map/pallas_call | solution.py:55
  19.9 3.7 %collective-permute-start.10 = (f32[8,768]{1,0:T(8,128)S(1)}, f32[8,768]{1,0:T(8,128)S(1)}, u32[]{:S(2)}, u32[]{:S(2)}) collective-permute-start(f32[8,768]{1,0:T(8,128)S(1)} %get-tuple-element.102.refs_0_), channel_id=1, source_target_pairs={{0,3},{1,2},{2,1},{3,0},{4,7},{5,6},{6,5},{7,4},{8,11},{9,10},{10,... | collective-permute-start | bytes 73736 | tf_op jit(solution)/shard_map/ppermute | solution.py:438
  23.6 0.8 %collective-permute-start.8 = (f32[8,768]{1,0:T(8,128)S(1)}, f32[8,768]{1,0:T(8,128)S(1)}, u32[]{:S(2)}, u32[]{:S(2)}) collective-permute-start(f32[8,768]{1,0:T(8,128)S(1)} %get-tuple-element.102.refs_0_), channel_id=1, source_target_pairs={{0,1},{1,0},{2,3},{3,2},{4,5},{5,4},{6,7},{7,6},{8,9},{9,8},{10,11... | collective-permute-start | bytes 73736 | tf_op jit(solution)/shard_map/ppermute | solution.py:438
  24.4 1.2 %collective-permute-done.10.refs_3_ = f32[8,768]{1,0:T(8,128)S(1)} collective-permute-done((f32[8,768]{1,0:T(8,128)S(1)}, f32[8,768]{1,0:T(8,128)S(1)}, u32[]{:S(2)}, u32[]{:S(2)}) %collective-permute-start.10) | collective-permute-done | bytes 24608 | tf_op jit(solution)/shard_map/ppermute | solution.py:438
  25.6 2.7 %collective-permute-done.9.refs_2_ = f32[8,768]{1,0:T(8,128)S(1)} collective-permute-done((f32[8,768]{1,0:T(8,128)S(1)}, f32[8,768]{1,0:T(8,128)S(1)}, u32[]{:S(2)}, u32[]{:S(2)}) %collective-permute-start.9) | collective-permute-done | bytes 24608 | tf_op jit(solution)/shard_map/ppermute | solution.py:438
  28.3 0.7 %shard_map.90 = (bf16[768,256]{1,0:T(8,128)(2,1)S(1)}, bf16[3,2,128,128]{3,2,1,0:T(8,128)(2,1)S(1)}, f32[2,128,128]{2,1,0:T(8,128)S(1)}, f32[768,128]{1,0:T(8,128)S(1)}, f32[768,128]{1,0:T(8,128)S(1)}) custom-call(f32[8,768]{1,0:T(8,128)S(1)} %get-tuple-element.102.refs_0_, f32[8,768]{1,0:T(8,128)S(1)} %collective-permute-done.8.refs_1_, ...), custom_call_target="tpu_custom_call" | custom-call | flops 50331648 | tf_op jit(solution)/shard_map/pallas_call | solution.py:55
  29.5 0.6 %collective-permute-start.12 = (f32[2,128,128]{2,1,0:T(8,128)S(1)}, f32[2,128,128]{2,1,0:T(8,128)S(1)}, u32[]{:S(2)}, u32[]{:S(2)}) collective-permute-start(f32[2,128,128]{2,1,0:T(8,128)S(1)} %get-tuple-element.118), channel_id=1, source_target_pairs={{28,24},{24,28},{20,16},{16,20},{12,8},{8,12},{4,0},{0,4},{29,25},... | collective-permute-start | bytes 393224 | tf_op jit(solution)/shard_map/ppermute | solution.py:362
  30.0 0.6 %shard_map.91 = (bf16[768,256]{1,0:T(8,128)(2,1)S(1)}, bf16[3,2,128,128]{3,2,1,0:T(8,128)(2,1)S(1)}, f32[2,128,128]{2,1,0:T(8,128)S(1)}, bf16[768,256]{1,0:T(8,1...) custom-call(f32[768,128]{1,0:T(8,128)S(1)} %get-tuple-element.105.refs_0_, ...), custom_call_target="tpu_custom_call" | custom-call | flops 100663296 | tf_op jit(solution)/shard_map/pallas_call | solution.py:55
  30.6 1.4 %collective-permute-start.13 = (f32[2,128,128]{2,1,0:T(8,128)S(1)}, f32[2,128,128]{2,1,0:T(8,128)S(1)}, u32[]{:S(2)}, u32[]{:S(2)}) collective-permute-start(f32[2,128,128]{2,1,0:T(8,128)S(1)} %shard_map.92.refs_2_.refs_6_), channel_id=1, source_target_pairs={{28,20},{24,8},{20,28},{16,0},{12,4},{8,24},{4,12},{0,16},{29,21},... | collective-permute-start | bytes 393224 | tf_op jit(solution)/shard_map/ppermute | solution.py:362
  32.0 0.8 %collective-permute-start.15 = (f32[2,128,128]{2,1,0:T(8,128)S(1)}, f32[2,128,128]{2,1,0:T(8,128)S(1)}, u32[]{:S(2)}, u32[]{:S(2)}) collective-permute-start(f32[2,128,128]{2,1,0:T(8,128)S(1)} %shard_map.94.refs_7_), channel_id=1, source_target_pairs={{28,20},{24,8},{20,28},{16,0},{12,4},{8,24},{4,12},{0,16},{29,21},... | collective-permute-start | bytes 393224 | tf_op jit(solution)/shard_map/ppermute | solution.py:362
  32.8 2.7 %shard_map.95 = (bf16[768,512]{1,0:T(8,128)(2,1)S(1)}, f32[768,512]{1,0:T(8,128)S(1)}, f32[768,512]{1,0:T(8,128)S(1)}) custom-call(bf16[768,512]{1,0:T(8,128)(2,1)S(1)} %get-tuple-element.85.q_ref, bf16[768,512]{1,0:T(8,128)(2,1)S(1)} %get-tuple-element.74.k_ref.refs_0_, bf16[768,512]{1,0:T(8,128)(2,1)S(1)} %get-tuple-element.75.v_ref.refs_1_, ...), custom_call_target="tpu_custom_call" | custom-call | flops 905969664 | tf_op jit(solution)/shard_map/pallas_call | solution.py:55
  35.7 1.6 %collective-permute-start.14 = (f32[2,128,128]{2,1,0:T(8,128)S(1)}, f32[2,128,128]{2,1,0:T(8,128)S(1)}, u32[]{:S(2)}, u32[]{:S(2)}) collective-permute-start(f32[2,128,128]{2,1,0:T(8,128)S(1)} %shard_map.96.refs_4_.refs_7_), channel_id=1, source_target_pairs={{28,12},{24,16},{20,4},{16,24},{12,28},{8,0},{4,20},{0,8},{29,13},... | collective-permute-start | bytes 393224 | tf_op jit(solution)/shard_map/ppermute | solution.py:362
  37.3 1.4 %collective-permute-start.16 = (f32[2,128,128]{2,1,0:T(8,128)S(1)}, f32[2,128,128]{2,1,0:T(8,128)S(1)}, u32[]{:S(2)}, u32[]{:S(2)}) collective-permute-start(f32[2,128,128]{2,1,0:T(8,128)S(1)} %shard_map.97.refs_8_), channel_id=1, source_target_pairs={{28,12},{24,16},{20,4},{16,24},{12,28},{8,0},{4,20},{0,8},{29,13},... | collective-permute-start | bytes 393224 | tf_op jit(solution)/shard_map/ppermute | solution.py:362
  38.7 3.7 %shard_map.98 = (bf16[768,1024]{1,0:T(8,128)(2,1)}, bf16[768,512]{1,0:T(8,128)(2,1)S(1)}, f32[768,512]{1,0:T(8,128)S(1)}, f32[768,512]{1,0:T(8,128)S(1)}) custom-call(bf16[768,512]{1,0:T(8,128)(2,1)S(1)} %get-tuple-element.88.q_ref, bf16[768,512]{1,0:T(8,128)(2,1)S(1)} %get-tuple-element.77.k_ref.refs_0_, ...), custom_call_target="tpu_custom_call" | custom-call | flops 905969664 | tf_op jit(solution)/shard_map/pallas_call | solution.py:55
  42.5 1.2 %shard_map.100 = (bf16[768,1024]{1,0:T(8,128)(2,1)}, bf16[768,256]{1,0:T(8,128)(2,1)S(1)}, bf16[768,256]{1,0:T(8,128)(2,1)S(1)}) custom-call(bf16[768,512]{1,0:T(8,128)(2,1)S(1)} %get-tuple-element.74.k_ref.refs_0_, bf16[768,512]{1,0:T(8,128)(2,1)S(1)} %get-tuple-element.75.v_ref.refs_1_, ...), custom_call_target="tpu_custom_call", output_to_operand_aliasing={{0}: (6, {})} | custom-call | flops 100663296 | bytes 1572864 | tf_op jit(solution)/shard_map/pallas_call | solution.py:55
  43.8 0.6 %collective-permute-start.17 = (f32[2,128,128]{2,1,0:T(8,128)S(1)}, f32[2,128,128]{2,1,0:T(8,128)S(1)}, u32[]{:S(2)}, u32[]{:S(2)}) collective-permute-start(f32[2,128,128]{2,1,0:T(8,128)S(1)} %get-tuple-element.134), channel_id=1, source_target_pairs={{28,24},{24,28},{20,16},{16,20},{12,8},{8,12},{4,0},{0,4},{29,25},... | collective-permute-start | bytes 393224 | tf_op jit(solution)/shard_map/ppermute | solution.py:362
  44.8 1.5 %shard_map.103 = (bf16[768,1024]{1,0:T(8,128)(2,1)}, bf16[768,1024]{1,0:T(8,128)(2,1)}, bf16[768,256]{1,0:T(8,128)(2,1)S(1)}, bf16[768,256]{1,0:T(8,128)(2,1)S(1)}) custom-call(bf16[768,512]{1,0:T(8,128)(2,1)S(1)} %get-tuple-element.77.k_ref.refs_0_, bf16[768,512]{1,0:T(8,128)(2,1)S(1)} %get-tuple-element.78.v_ref.refs_1_, ...), custom_call_target="tpu_custom_call" | custom-call | flops 100663296 | tf_op jit(solution)/shard_map/pallas_call | solution.py:55
  46.3 1.2 %shard_map.104 = (bf16[768,1024]{1,0:T(8,128)(2,1)}, bf16[768,1024]{1,0:T(8,128)(2,1)}) custom-call(bf16[768,512]{1,0:T(8,128)(2,1)S(1)} %get-tuple-element.77.k_ref.refs_0_, bf16[768,512]{1,0:T(8,128)(2,1)S(1)} %get-tuple-element.78.v_ref.refs_1_, f32[768,512]{1,0:T(8,128)S(1)} %get-tuple-element.131.refs_2_, ...), custom_call_target="tpu_custom_call", output_to_operand_aliasing={{0}: (7, {}), {1}: (8, {})} | custom-call | flops 100663296 | bytes 3145728 | tf_op jit(solution)/shard_map/pallas_call | solution.py:55
  (45 shorter events, 5.2 us)
Async XLA Ops:
  2.8 4.6 %copy-start = (f32[1024]{0:T(1024)S(1)}, f32[1024]{0:T(1024)}, u32[]{:S(2)}) copy-start(f32[1024]{0:T(1024)} %param.9) | copy-start | bytes 12292
  2.8 1.5 %collective-permute-start = (f32[2,128,128]{2,1,0:T(8,128)S(1)}, f32[2,128,128]{2,1,0:T(8,128)S(1)}, u32[]{:S(2)}, u32[]{:S(2)}) collective-permute-start(f32[2,128,128]{2,1,0:T(8,128)S(1)} %get-tuple-element.80), channel_id=1, source_target_pairs={{0,4},{4,0},{8,12},{12,8},{16,20},{20,16},{24,28},{28,24},{1,5},{5... | collective-permute-start | bytes 393224 | tf_op jit(solution)/shard_map/ppermute | solution.py:362
  3.3 3.9 %collective-permute-start.2 = (f32[2,128,128]{2,1,0:T(8,128)S(1)}, f32[2,128,128]{2,1,0:T(8,128)S(1)}, u32[]{:S(2)}, u32[]{:S(2)}) collective-permute-start(f32[2,128,128]{2,1,0:T(8,128)S(1)} %get-tuple-element.83), channel_id=1, source_target_pairs={{0,4},{4,0},{8,12},{12,8},{16,20},{20,16},{24,28},{28,24},{1,5},{5... | collective-permute-start | bytes 393224 | tf_op jit(solution)/shard_map/ppermute | solution.py:362
  4.3 6.4 %collective-permute-start.1 = (f32[2,128,128]{2,1,0:T(8,128)S(1)}, f32[2,128,128]{2,1,0:T(8,128)S(1)}, u32[]{:S(2)}, u32[]{:S(2)}) collective-permute-start(f32[2,128,128]{2,1,0:T(8,128)S(1)} %shard_map.78.refs_2_.refs_0_), channel_id=1, source_target_pairs={{0,8},{4,20},{8,0},{12,28},{16,24},{20,4},{24,16},{28,12},{1,9},{5... | collective-permute-start | bytes 393224 | tf_op jit(solution)/shard_map/ppermute | solution.py:362
  7.3 5.6 %collective-permute-start.3 = (f32[2,128,128]{2,1,0:T(8,128)S(1)}, f32[2,128,128]{2,1,0:T(8,128)S(1)}, u32[]{:S(2)}, u32[]{:S(2)}) collective-permute-start(f32[2,128,128]{2,1,0:T(8,128)S(1)} %shard_map.79.refs_1_), channel_id=1, source_target_pairs={{0,8},{4,20},{8,0},{12,28},{16,24},{20,4},{24,16},{28,12},{1,9},{5... | collective-permute-start | bytes 393224 | tf_op jit(solution)/shard_map/ppermute | solution.py:362
  10.8 6.4 %collective-permute-start.4 = (f32[2,128,128]{2,1,0:T(8,128)S(1)}, f32[2,128,128]{2,1,0:T(8,128)S(1)}, u32[]{:S(2)}, u32[]{:S(2)}) collective-permute-start(f32[2,128,128]{2,1,0:T(8,128)S(1)} %shard_map.81.refs_4_.refs_0_), channel_id=1, source_target_pairs={{0,16},{4,12},{8,24},{12,4},{16,0},{20,28},{24,8},{28,20},{1,17},{... | collective-permute-start | bytes 393224 | tf_op jit(solution)/shard_map/ppermute | solution.py:362
  12.9 5.0 %collective-permute-start.6 = (f32[2,128,128]{2,1,0:T(8,128)S(1)}, f32[2,128,128]{2,1,0:T(8,128)S(1)}, u32[]{:S(2)}, u32[]{:S(2)}) collective-permute-start(f32[2,128,128]{2,1,0:T(8,128)S(1)} %shard_map.82.refs_1_), channel_id=1, source_target_pairs={{0,16},{4,12},{8,24},{12,4},{16,0},{20,28},{24,8},{28,20},{1,17},{... | collective-permute-start | bytes 393224 | tf_op jit(solution)/shard_map/ppermute | solution.py:362
  17.3 1.4 %collective-permute-start.5 = (f32[2,128,128]{2,1,0:T(8,128)S(1)}, f32[2,128,128]{2,1,0:T(8,128)S(1)}, u32[]{:S(2)}, u32[]{:S(2)}) collective-permute-start(f32[2,128,128]{2,1,0:T(8,128)S(1)} %get-tuple-element.87.refs_5_), channel_id=1, source_target_pairs={{0,4},{4,0},{8,12},{12,8},{16,20},{20,16},{24,28},{28,24},{1,5},{5... | collective-permute-start | bytes 393224 | tf_op jit(solution)/shard_map/ppermute | solution.py:362
  18.0 1.4 %collective-permute-start.7 = (f32[2,128,128]{2,1,0:T(8,128)S(1)}, f32[2,128,128]{2,1,0:T(8,128)S(1)}, u32[]{:S(2)}, u32[]{:S(2)}) collective-permute-start(f32[2,128,128]{2,1,0:T(8,128)S(1)} %get-tuple-element.93), channel_id=1, source_target_pairs={{0,4},{4,0},{8,12},{12,8},{16,20},{20,16},{24,28},{28,24},{1,5},{5... | collective-permute-start | bytes 393224 | tf_op jit(solution)/shard_map/ppermute | solution.py:362
  19.9 5.7 %collective-permute-start.10 = (f32[8,768]{1,0:T(8,128)S(1)}, f32[8,768]{1,0:T(8,128)S(1)}, u32[]{:S(2)}, u32[]{:S(2)}) collective-permute-start(f32[8,768]{1,0:T(8,128)S(1)} %get-tuple-element.102.refs_0_), channel_id=1, source_target_pairs={{0,3},{1,2},{2,1},{3,0},{4,7},{5,6},{6,5},{7,4},{8,11},{9,10},{10,... | collective-permute-start | bytes 73736 | tf_op jit(solution)/shard_map/ppermute | solution.py:438
  23.6 4.7 %collective-permute-start.9 = (f32[8,768]{1,0:T(8,128)S(1)}, f32[8,768]{1,0:T(8,128)S(1)}, u32[]{:S(2)}, u32[]{:S(2)}) collective-permute-start(f32[8,768]{1,0:T(8,128)S(1)} %get-tuple-element.102.refs_0_), channel_id=1, source_target_pairs={{0,2},{1,3},{2,0},{3,1},{4,6},{5,7},{6,4},{7,5},{8,10},{9,11},{10,... | collective-permute-start | bytes 73736 | tf_op jit(solution)/shard_map/ppermute | solution.py:438
  23.6 4.7 %collective-permute-start.8 = (f32[8,768]{1,0:T(8,128)S(1)}, f32[8,768]{1,0:T(8,128)S(1)}, u32[]{:S(2)}, u32[]{:S(2)}) collective-permute-start(f32[8,768]{1,0:T(8,128)S(1)} %get-tuple-element.102.refs_0_), channel_id=1, source_target_pairs={{0,1},{1,0},{2,3},{3,2},{4,5},{5,4},{6,7},{7,6},{8,9},{9,8},{10,11... | collective-permute-start | bytes 73736 | tf_op jit(solution)/shard_map/ppermute | solution.py:438
  29.0 1.6 %collective-permute-start.11 = (f32[2,128,128]{2,1,0:T(8,128)S(1)}, f32[2,128,128]{2,1,0:T(8,128)S(1)}, u32[]{:S(2)}, u32[]{:S(2)}) collective-permute-start(f32[2,128,128]{2,1,0:T(8,128)S(1)} %get-tuple-element.115), channel_id=1, source_target_pairs={{28,24},{24,28},{20,16},{16,20},{12,8},{8,12},{4,0},{0,4},{29,25},... | collective-permute-start | bytes 393224 | tf_op jit(solution)/shard_map/ppermute | solution.py:362
  29.5 2.5 %collective-permute-start.12 = (f32[2,128,128]{2,1,0:T(8,128)S(1)}, f32[2,128,128]{2,1,0:T(8,128)S(1)}, u32[]{:S(2)}, u32[]{:S(2)}) collective-permute-start(f32[2,128,128]{2,1,0:T(8,128)S(1)} %get-tuple-element.118), channel_id=1, source_target_pairs={{28,24},{24,28},{20,16},{16,20},{12,8},{8,12},{4,0},{0,4},{29,25},... | collective-permute-start | bytes 393224 | tf_op jit(solution)/shard_map/ppermute | solution.py:362
  30.6 5.0 %collective-permute-start.13 = (f32[2,128,128]{2,1,0:T(8,128)S(1)}, f32[2,128,128]{2,1,0:T(8,128)S(1)}, u32[]{:S(2)}, u32[]{:S(2)}) collective-permute-start(f32[2,128,128]{2,1,0:T(8,128)S(1)} %shard_map.92.refs_2_.refs_6_), channel_id=1, source_target_pairs={{28,20},{24,8},{20,28},{16,0},{12,4},{8,24},{4,12},{0,16},{29,21},... | collective-permute-start | bytes 393224 | tf_op jit(solution)/shard_map/ppermute | solution.py:362
  32.0 5.2 %collective-permute-start.15 = (f32[2,128,128]{2,1,0:T(8,128)S(1)}, f32[2,128,128]{2,1,0:T(8,128)S(1)}, u32[]{:S(2)}, u32[]{:S(2)}) collective-permute-start(f32[2,128,128]{2,1,0:T(8,128)S(1)} %shard_map.94.refs_7_), channel_id=1, source_target_pairs={{28,20},{24,8},{20,28},{16,0},{12,4},{8,24},{4,12},{0,16},{29,21},... | collective-permute-start | bytes 393224 | tf_op jit(solution)/shard_map/ppermute | solution.py:362
  35.7 6.6 %collective-permute-start.14 = (f32[2,128,128]{2,1,0:T(8,128)S(1)}, f32[2,128,128]{2,1,0:T(8,128)S(1)}, u32[]{:S(2)}, u32[]{:S(2)}) collective-permute-start(f32[2,128,128]{2,1,0:T(8,128)S(1)} %shard_map.96.refs_4_.refs_7_), channel_id=1, source_target_pairs={{28,12},{24,16},{20,4},{16,24},{12,28},{8,0},{4,20},{0,8},{29,13},... | collective-permute-start | bytes 393224 | tf_op jit(solution)/shard_map/ppermute | solution.py:362
  37.3 6.4 %collective-permute-start.16 = (f32[2,128,128]{2,1,0:T(8,128)S(1)}, f32[2,128,128]{2,1,0:T(8,128)S(1)}, u32[]{:S(2)}, u32[]{:S(2)}) collective-permute-start(f32[2,128,128]{2,1,0:T(8,128)S(1)} %shard_map.97.refs_8_), channel_id=1, source_target_pairs={{28,12},{24,16},{20,4},{16,24},{12,28},{8,0},{4,20},{0,8},{29,13},... | collective-permute-start | bytes 393224 | tf_op jit(solution)/shard_map/ppermute | solution.py:362
  42.4 2.4 %collective-permute-start.18 = (f32[2,128,128]{2,1,0:T(8,128)S(1)}, f32[2,128,128]{2,1,0:T(8,128)S(1)}, u32[]{:S(2)}, u32[]{:S(2)}) collective-permute-start(f32[2,128,128]{2,1,0:T(8,128)S(1)} %get-tuple-element.132.refs_5_), channel_id=1, source_target_pairs={{28,24},{24,28},{20,16},{16,20},{12,8},{8,12},{4,0},{0,4},{29,25},... | collective-permute-start | bytes 393224 | tf_op jit(solution)/shard_map/ppermute | solution.py:362
  43.8 2.5 %collective-permute-start.17 = (f32[2,128,128]{2,1,0:T(8,128)S(1)}, f32[2,128,128]{2,1,0:T(8,128)S(1)}, u32[]{:S(2)}, u32[]{:S(2)}) collective-permute-start(f32[2,128,128]{2,1,0:T(8,128)S(1)} %get-tuple-element.134), channel_id=1, source_target_pairs={{28,24},{24,28},{20,16},{16,20},{12,8},{8,12},{4,0},{0,4},{29,25},... | collective-permute-start | bytes 393224 | tf_op jit(solution)/shard_map/ppermute | solution.py:362

commit v11 on v10

--- a/solution.py
+++ b/solution.py
@@ -205,17 +205,22 @@
 
 def local_kernel(pieces, second, q_ref, k_ref, v_ref, turned_ref, pre_ref, *refs):
     if second:
-        qgrad_hbm, qgrad_ref, kpart_ref, vpart_ref, sem = refs[-5:]
+        qgrad_hbm, tail_ref, kpart_ref, vpart_ref, qgrad_ref, sems = refs[-6:]
     else:
         qgrad_ref, kpart_ref, vpart_ref = refs[-3:]
     state = heads_in(refs[:pieces])
     g_refs, post_refs = refs[pieces:2 * pieces], refs[2 * pieces:3 * pieces]
     rows, width = q_ref.shape
     parts = chunks_of(rows)
+    copies = []
+
+    def send(source, same, part):
+        target = qgrad_hbm.at[part, columns(same, width)]
+        copies.append(pltpu.make_async_copy(source, target, sems.at[len(copies)]))
+        copies[-1].start()
+
     if second:
-        target = qgrad_hbm.at[slice(0, rows), columns(False, width)]
-        copy = pltpu.make_async_copy(refs[3 * pieces], target, sem)
-        copy.start()
+        send(refs[3 * pieces], False, slice(0, rows))
 
     def scores(i, j):
         part, lanes = parts[i], lanes_of(j)
@@ -237,7 +242,10 @@
             post = post_refs[j // PIECE][i, j % PIECE]
             kgrad = kgrad + dot(v, post, 1, 1)
             vgrad = vgrad + dot(k, post)
-        qgrad_ref[part, lanes] = qgrad.astype(BF16)
+        if second and i == len(parts) - 1:
+            tail_ref[:, lanes] = qgrad.astype(BF16)
+        else:
+            qgrad_ref[part, lanes] = qgrad.astype(BF16)
         kpart_ref[part, lanes] = kgrad
         vpart_ref[part, lanes] = vgrad
 
@@ -247,7 +255,10 @@
         coming = scores(*following) if following else None
         products(*place, *ready)
         ready = coming
-    if second:
+        if second and following and following[0] != place[0]:
+            part = parts[place[0]]
+            send(qgrad_ref.at[part], True, part)
+    for copy in copies:
         copy.wait()
 
 
@@ -272,13 +283,13 @@
         copies.append(pltpu.make_async_copy(source, target, sems.at[len(copies)]))
         copies[-1].start()
 
-    for source, (out, place) in zip(sources, plan):
-        send(source, out, slice(0, rows), place)
+    for source, (out, part, place) in zip(sources, plan):
+        send(source, out, part, place)
     for part in chunks_of(rows):
         final_part(piece, part, *refs[:5], kgrad_ref, vgrad_ref)
         if own:
-            send(kgrad_ref.at[part], 0, part, own)
-            send(vgrad_ref.at[part], 1, part, own)
+            send(kgrad_ref.at[part], -2, part, own)
+            send(vgrad_ref.at[part], -1, part, own)
     for copy in copies:
         copy.wait()
 
@@ -464,11 +475,15 @@
 
     def local_of(second, *args):
         def work(messages):
+            if second:
+                specs, scratch = [HBM] + [VMEM] * 3, [pltpu.VMEM((rows, half), BF16), sems]
+                shapes = [whole, shape((rows // chunks, half), BF16), wide, wide]
+            else:
+                specs, scratch, shapes = [VMEM] * 3, [], [thin, wide, wide]
             made = run(
                 partial(local_kernel, count, second), 9 * unit,
                 [VMEM] * (len(args) + len(first_grads)) + [ANYWHERE] * len(messages),
-                [HBM] * second + [VMEM] * 3, [whole] * second + [thin, wide, wide],
-                (*args, *first_grads, *messages), [pltpu.SemaphoreType.DMA(())] * second,
+                specs, shapes, (*args, *first_grads, *messages), scratch,
             )
             first_grads.append(made[0])
             return made
@@ -478,8 +493,8 @@
     piece_thin = shape((rows, PIECE * HEAD_DIM), BF16)
 
     def final_of(piece, args, state, ready=(), outs=(), fresh=0, own=None):
-        sources = [source for source, _, _ in ready]
-        plan = [(out, place) for _, out, place in ready]
+        sources = [item[0] for item in ready]
+        plan = [item[1:] for item in ready]
         args = (*args, state, *sources)
         wholes = len(outs) + fresh
         last = [pltpu.VMEM(piece_thin.shape, BF16)] * 2 if own else []
@@ -498,24 +513,28 @@
             local_of(0, q1, k1, v1, turned1, pre1, *state1, *gs1, *posts1),
             local_of(1, q2, k2, v2, turned2, pre2, *state2, *gs2, *posts2),
         ],
-        lambda state, made: final_of(
-            0, (k1, v1, *made[0][1:]), state, [(made[1][1], 0, (True, half))], made[1][:1]
-        ),
+        lambda state, made: final_of(0, (k1, v1, *made[0][1:]), state),
     )
     near = (k1, v1, *made[0][1:])
-    far = (k2, v2, *made[1][2:])
-    qgrad, *done = early
+    qgrad, tail, *far = made[1]
+    far = (k2, v2, *far)
+    every = slice(0, rows)
+    ready, outs, done = [], [], list(early)
     for piece in range(1, count):
         done += final_of(piece, near, gstate1[piece])
-    ready = [(array, i % 2, (False, half, i // 2)) for i, array in enumerate(done)]
-    outs, done = [], []
+    for i, array in enumerate(done):
+        ready.append((array, i % 2, every, (False, half, i // 2)))
     for piece in range(count - 1):
-        *outs, kdone, vdone = final_of(
-            piece, far, gstate2[piece], ready, outs, 0 if outs else 2
-        )
-        ready = [(kdone, 0, (True, half, piece)), (vdone, 1, (True, half, piece))]
-    kgrad, vgrad = final_of(
-        count - 1, far, gstate2[-1], ready, outs, 0 if outs else 2, (True, half, count - 1)
+        now, ready = ready[:2], ready[2:]
+        fresh = 0 if outs else 2
+        *outs, kdone, vdone = final_of(piece, far, gstate2[piece], now, outs, fresh)
+        ready.append((kdone, 0, every, (True, half, piece)))
+        ready.append((vdone, 1, every, (True, half, piece)))
+    ready = [(array, out + 1, part, place) for array, out, part, place in ready]
+    ready.append((tail, 0, chunks_of(rows)[-1], (True, half)))
+    qgrad, kgrad, vgrad = final_of(
+        count - 1, far, gstate2[-1], ready, [qgrad, *outs], 0 if outs else 2,
+        (True, half, count - 1),
     )
     return qgrad, kgrad, vgrad
 

time: 47.9 us -> 46.9 us (0.979)
  Pallas kernels: 23.5 us -> 22.4 us
    pallas_call x29, Pallas kernels: 23.5 us -> 22.4 us  [run(): pl.pallas_call(kernel, in_specs=in_specs, out_specs=out_specs, out_shape=...]
  transfers between devices with their start and end apart: 19 -> 19, of which waited for: 7 -> 7; matrix products, arithmetic and copies ran while one was open for 0% -> 0% of each run, Pallas kernels for 40% -> 37%
where the time goes in v11:
time: 46.9 us; the launch traced here: 46.7 us
  Pallas kernels  22.4 us (48%)
  starting transfers between devices  17.9 us (38%)
  waiting for transfers between devices  5.22 us (11%)
  between operations  1.07 us (2%)
    pallas_call x29, Pallas kernels, run(): pl.pallas_call(kernel, in_specs=in_specs, out_specs=out_specs, out_shape=...  22.4 us
    ppermute x16, starting transfers between devices, move(): return lax.ppermute(value, 'seq', pairs)  13.5 us
    ppermute x3, starting transfers between devices, shards(): lax.ppermute(sums, 'head', [(r, r ^ other) for r in range(peers)])  4.45 us
    ppermute x3, waiting for transfers between devices, shards(): lax.ppermute(sums, 'head', [(r, r ^ other) for r in range(peers)])  3.94 us
    ppermute x16, waiting for transfers between devices, move(): return lax.ppermute(value, 'seq', pairs)  1.27 us
  transfers between devices with their start and end apart: 19, of which 7 were waited for; matrix products, arithmetic and copies ran while one was open for 0% of the time, Pallas kernels for 37%

profile of v11, /device:TPU:0, one launch (start us, length us, event | category | flops | bytes accessed | tf_op | source)
XLA Modules:
  0.0 46.7 jit_solution(1283945314124456660)
XLA Ops:
  0.6 2.1 %shard_map.76 = (bf16[768,512]{1,0:T(8,128)(2,1)S(1)}, bf16[768,512]{1,0:T(8,128)(2,1)S(1)}, bf16[768,512]{1,0:T(8,128)(2,1)S(1)}, bf16[768,512]{1,0:T(8,128)(2,...) custom-call(bf16[768,1024]{1,0:T(8,128)(2,1)} %k_hbm.1, ...), custom_call_target="tpu_custom_call" | custom-call | flops 100663296 | bytes 3145728 | tf_op jit(solution)/shard_map/pallas_call | solution.py:55
  2.8 0.5 %collective-permute-start = (f32[2,128,128]{2,1,0:T(8,128)S(1)}, f32[2,128,128]{2,1,0:T(8,128)S(1)}, u32[]{:S(2)}, u32[]{:S(2)}) collective-permute-start(f32[2,128,128]{2,1,0:T(8,128)S(1)} %get-tuple-element.75), channel_id=1, source_target_pairs={{0,4},{4,0},{8,12},{12,8},{16,20},{20,16},{24,28},{28,24},{1,5},{5... | collective-permute-start | bytes 393224 | tf_op jit(solution)/shard_map/ppermute | solution.py:373
  4.3 2.9 %collective-permute-start.2 = (f32[2,128,128]{2,1,0:T(8,128)S(1)}, f32[2,128,128]{2,1,0:T(8,128)S(1)}, u32[]{:S(2)}, u32[]{:S(2)}) collective-permute-start(f32[2,128,128]{2,1,0:T(8,128)S(1)} %shard_map.78.refs_2_.refs_0_), channel_id=1, source_target_pairs={{0,8},{4,20},{8,0},{12,28},{16,24},{20,4},{24,16},{28,12},{1,9},{5... | collective-permute-start | bytes 393224 | tf_op jit(solution)/shard_map/ppermute | solution.py:373
  7.4 3.3 %shard_map.80 = (bf16[768,512]{1,0:T(8,128)(2,1)S(1)}, f32[768,512]{1,0:T(8,128)S(1)}, f32[768,512]{1,0:T(8,128)S(1)}, bf16[512,768]{1,0:T(8,128)(2,1)S(1)}, bf16[4,768,256]{2,1,0:T(8,128)(2,1)S(1)}) custom-call(bf16[768,1024]{1,0:T(8,128)(2,1)} %q_hbm.3, bf16[768,1024]{1,0:T(8,128)(2,1)} %og_hbm.3, bf16[768,512]{1,0:T(8,128)(2,1)S(1)} %get-tuple-element.71.k_ref.refs_0_, ...), custom_call_target="tpu_custom_call" | custom-call | flops 603979776 | bytes 3145728 | tf_op jit(solution)/shard_map/pallas_call | solution.py:55
  10.8 2.0 %collective-permute-start.3 = (f32[2,128,128]{2,1,0:T(8,128)S(1)}, f32[2,128,128]{2,1,0:T(8,128)S(1)}, u32[]{:S(2)}, u32[]{:S(2)}) collective-permute-start(f32[2,128,128]{2,1,0:T(8,128)S(1)} %shard_map.81.refs_4_.refs_0_), channel_id=1, source_target_pairs={{0,16},{4,12},{8,24},{12,4},{16,0},{20,28},{24,8},{28,20},{1,17},{... | collective-permute-start | bytes 393224 | tf_op jit(solution)/shard_map/ppermute | solution.py:373
  12.9 1.0 %collective-permute-start.5 = (f32[2,128,128]{2,1,0:T(8,128)S(1)}, f32[2,128,128]{2,1,0:T(8,128)S(1)}, u32[]{:S(2)}, u32[]{:S(2)}) collective-permute-start(f32[2,128,128]{2,1,0:T(8,128)S(1)} %shard_map.82.refs_1_), channel_id=1, source_target_pairs={{0,16},{4,12},{8,24},{12,4},{16,0},{20,28},{24,8},{28,20},{1,17},{... | collective-permute-start | bytes 393224 | tf_op jit(solution)/shard_map/ppermute | solution.py:373
  13.9 3.3 %shard_map.83 = (bf16[768,512]{1,0:T(8,128)(2,1)S(1)}, f32[768,512]{1,0:T(8,128)S(1)}, f32[768,512]{1,0:T(8,128)S(1)}, bf16[512,768]{1,0:T(8,128)(2,1)S(1)}, bf16[4,768,256]{2,1,0:T(8,128)(2,1)S(1)}) custom-call(bf16[768,1024]{1,0:T(8,128)(2,1)} %q_hbm.3, bf16[768,1024]{1,0:T(8,128)(2,1)} %og_hbm.3, bf16[768,512]{1,0:T(8,128)(2,1)S(1)} %get-tuple-element.80.k_ref.refs_0_, ...), custom_call_target="tpu_custom_call" | custom-call | flops 603979776 | bytes 3145728 | tf_op jit(solution)/shard_map/pallas_call | solution.py:55
  19.4 0.5 %shard_map.89 = (f32[768,256]{1,0:T(8,128)S(1)}, f32[8,768]{1,0:T(8,128)S(1)}) custom-call(bf16[768,512]{1,0:T(8,128)(2,1)S(1)} %get-tuple-element.90.q_ref, f32[768,512]{1,0:T(8,128)S(1)} %get-tuple-element.91.inner_ref, f32[768,512]{1,0:T(8,128)S(1)} %get-tuple-element.92.scaled_ref.refs_2_, f32[2,128,128]{2,1,0:T(8,128)S(1)} %collective-permute-done.6.state_ref.refs_1_, ...), custom_call_target="tpu_custom_call" | custom-call | flops 50331648 | tf_op jit(solution)/shard_map/pallas_call | solution.py:55
  19.9 3.7 %collective-permute-start.10 = (f32[8,768]{1,0:T(8,128)S(1)}, f32[8,768]{1,0:T(8,128)S(1)}, u32[]{:S(2)}, u32[]{:S(2)}) collective-permute-start(f32[8,768]{1,0:T(8,128)S(1)} %get-tuple-element.99.refs_0_), channel_id=1, source_target_pairs={{0,3},{1,2},{2,1},{3,0},{4,7},{5,6},{6,5},{7,4},{8,11},{9,10},{10,... | collective-permute-start | bytes 73736 | tf_op jit(solution)/shard_map/ppermute | solution.py:449
  23.6 0.8 %collective-permute-start.8 = (f32[8,768]{1,0:T(8,128)S(1)}, f32[8,768]{1,0:T(8,128)S(1)}, u32[]{:S(2)}, u32[]{:S(2)}) collective-permute-start(f32[8,768]{1,0:T(8,128)S(1)} %get-tuple-element.99.refs_0_), channel_id=1, source_target_pairs={{0,1},{1,0},{2,3},{3,2},{4,5},{5,4},{6,7},{7,6},{8,9},{9,8},{10,11... | collective-permute-start | bytes 73736 | tf_op jit(solution)/shard_map/ppermute | solution.py:449
  24.4 1.2 %collective-permute-done.10.refs_3_ = f32[8,768]{1,0:T(8,128)S(1)} collective-permute-done((f32[8,768]{1,0:T(8,128)S(1)}, f32[8,768]{1,0:T(8,128)S(1)}, u32[]{:S(2)}, u32[]{:S(2)}) %collective-permute-start.10) | collective-permute-done | bytes 24608 | tf_op jit(solution)/shard_map/ppermute | solution.py:449
  25.6 2.7 %collective-permute-done.9.refs_2_ = f32[8,768]{1,0:T(8,128)S(1)} collective-permute-done((f32[8,768]{1,0:T(8,128)S(1)}, f32[8,768]{1,0:T(8,128)S(1)}, u32[]{:S(2)}, u32[]{:S(2)}) %collective-permute-start.9) | collective-permute-done | bytes 24608 | tf_op jit(solution)/shard_map/ppermute | solution.py:449
  28.3 0.7 %shard_map.90 = (bf16[768,256]{1,0:T(8,128)(2,1)S(1)}, bf16[3,2,128,128]{3,2,1,0:T(8,128)(2,1)S(1)}, f32[2,128,128]{2,1,0:T(8,128)S(1)}, f32[768,128]{1,0:T(8,128)S(1)}, f32[768,128]{1,0:T(8,128)S(1)}) custom-call(f32[8,768]{1,0:T(8,128)S(1)} %get-tuple-element.99.refs_0_, f32[8,768]{1,0:T(8,128)S(1)} %collective-permute-done.8.refs_1_, ...), custom_call_target="tpu_custom_call" | custom-call | flops 50331648 | tf_op jit(solution)/shard_map/pallas_call | solution.py:55
  29.4 0.6 %collective-permute-start.12 = (f32[2,128,128]{2,1,0:T(8,128)S(1)}, f32[2,128,128]{2,1,0:T(8,128)S(1)}, u32[]{:S(2)}, u32[]{:S(2)}) collective-permute-start(f32[2,128,128]{2,1,0:T(8,128)S(1)} %get-tuple-element.119), channel_id=1, source_target_pairs={{28,24},{24,28},{20,16},{16,20},{12,8},{8,12},{4,0},{0,4},{29,25},... | collective-permute-start | bytes 393224 | tf_op jit(solution)/shard_map/ppermute | solution.py:373
  30.0 0.6 %shard_map.92 = (bf16[768,256]{1,0:T(8,128)(2,1)S(1)}, bf16[3,2,128,128]{3,2,1,0:T(8,128)(2,1)S(1)}, f32[2,128,128]{2,1,0:T(8,128)S(1)}, bf16[768,256]{1,0:T(8,1...) custom-call(f32[768,128]{1,0:T(8,128)S(1)} %get-tuple-element.103.refs_0_, ...), custom_call_target="tpu_custom_call" | custom-call | flops 100663296 | tf_op jit(solution)/shard_map/pallas_call | solution.py:55
  30.6 1.4 %collective-permute-start.13 = (f32[2,128,128]{2,1,0:T(8,128)S(1)}, f32[2,128,128]{2,1,0:T(8,128)S(1)}, u32[]{:S(2)}, u32[]{:S(2)}) collective-permute-start(f32[2,128,128]{2,1,0:T(8,128)S(1)} %shard_map.93.refs_2_.refs_6_), channel_id=1, source_target_pairs={{28,20},{24,8},{20,28},{16,0},{12,4},{8,24},{4,12},{0,16},{29,21},... | collective-permute-start | bytes 393224 | tf_op jit(solution)/shard_map/ppermute | solution.py:373
  32.0 0.8 %collective-permute-start.14 = (f32[2,128,128]{2,1,0:T(8,128)S(1)}, f32[2,128,128]{2,1,0:T(8,128)S(1)}, u32[]{:S(2)}, u32[]{:S(2)}) collective-permute-start(f32[2,128,128]{2,1,0:T(8,128)S(1)} %shard_map.94.refs_7_), channel_id=1, source_target_pairs={{28,20},{24,8},{20,28},{16,0},{12,4},{8,24},{4,12},{0,16},{29,21},... | collective-permute-start | bytes 393224 | tf_op jit(solution)/shard_map/ppermute | solution.py:373
  32.8 2.7 %shard_map.95 = (bf16[768,512]{1,0:T(8,128)(2,1)S(1)}, f32[768,512]{1,0:T(8,128)S(1)}, f32[768,512]{1,0:T(8,128)S(1)}) custom-call(bf16[768,512]{1,0:T(8,128)(2,1)S(1)} %get-tuple-element.90.q_ref, bf16[768,512]{1,0:T(8,128)(2,1)S(1)} %get-tuple-element.80.k_ref.refs_0_, bf16[768,512]{1,0:T(8,128)(2,1)S(1)} %get-tuple-element.81.v_ref.refs_1_, ...), custom_call_target="tpu_custom_call" | custom-call | flops 905969664 | tf_op jit(solution)/shard_map/pallas_call | solution.py:55
  35.7 1.6 %collective-permute-start.16 = (f32[2,128,128]{2,1,0:T(8,128)S(1)}, f32[2,128,128]{2,1,0:T(8,128)S(1)}, u32[]{:S(2)}, u32[]{:S(2)}) collective-permute-start(f32[2,128,128]{2,1,0:T(8,128)S(1)} %shard_map.96.refs_4_.refs_7_), channel_id=1, source_target_pairs={{28,12},{24,16},{20,4},{16,24},{12,28},{8,0},{4,20},{0,8},{29,13},... | collective-permute-start | bytes 393224 | tf_op jit(solution)/shard_map/ppermute | solution.py:373
  37.3 1.4 %collective-permute-start.15 = (f32[2,128,128]{2,1,0:T(8,128)S(1)}, f32[2,128,128]{2,1,0:T(8,128)S(1)}, u32[]{:S(2)}, u32[]{:S(2)}) collective-permute-start(f32[2,128,128]{2,1,0:T(8,128)S(1)} %shard_map.97.refs_8_), channel_id=1, source_target_pairs={{28,12},{24,16},{20,4},{16,24},{12,28},{8,0},{4,20},{0,8},{29,13},... | collective-permute-start | bytes 393224 | tf_op jit(solution)/shard_map/ppermute | solution.py:373
  38.7 3.3 %shard_map.98 = (bf16[768,1024]{1,0:T(8,128)(2,1)}, bf16[256,512]{1,0:T(8,128)(2,1)S(1)}, f32[768,512]{1,0:T(8,128)S(1)}, f32[768,512]{1,0:T(8,128)S(1)}) custom-call(bf16[768,512]{1,0:T(8,128)(2,1)S(1)} %get-tuple-element.78.q_ref, bf16[768,512]{1,0:T(8,128)(2,1)S(1)} %get-tuple-element.71.k_ref.refs_0_, ...), custom_call_target="tpu_custom_call" | custom-call | flops 905969664 | tf_op jit(solution)/shard_map/pallas_call | solution.py:55
  42.7 0.6 %collective-permute-start.17 = (f32[2,128,128]{2,1,0:T(8,128)S(1)}, f32[2,128,128]{2,1,0:T(8,128)S(1)}, u32[]{:S(2)}, u32[]{:S(2)}) collective-permute-start(f32[2,128,128]{2,1,0:T(8,128)S(1)} %get-tuple-element.128), channel_id=1, source_target_pairs={{28,24},{24,28},{20,16},{16,20},{12,8},{8,12},{4,0},{0,4},{29,25},... | collective-permute-start | bytes 393224 | tf_op jit(solution)/shard_map/ppermute | solution.py:373
  43.7 1.2 %shard_map.103 = (bf16[768,1024]{1,0:T(8,128)(2,1)}, bf16[768,1024]{1,0:T(8,128)(2,1)}, bf16[768,256]{1,0:T(8,128)(2,1)S(1)}, bf16[768,256]{1,0:T(8,128)(2,1)S(1)}) custom-call(bf16[768,512]{1,0:T(8,128)(2,1)S(1)} %get-tuple-element.71.k_ref.refs_0_, bf16[768,512]{1,0:T(8,128)(2,1)S(1)} %get-tuple-element.72.v_ref.refs_1_, ...), custom_call_target="tpu_custom_call" | custom-call | flops 100663296 | tf_op jit(solution)/shard_map/pallas_call | solution.py:55
  44.9 1.6 %shard_map.104 = (bf16[768,1024]{1,0:T(8,128)(2,1)}, bf16[768,1024]{1,0:T(8,128)(2,1)}, bf16[768,1024]{1,0:T(8,128)(2,1)}) custom-call(bf16[768,512]{1,0:T(8,128)(2,1)S(1)} %get-tuple-element.71.k_ref.refs_0_, bf16[768,512]{1,0:T(8,128)(2,1)S(1)} %get-tuple-element.72.v_ref.refs_1_, ...), custom_call_target="tpu_custom_call", output_to_operand_aliasing={{0}: (10, {}), {1}: (11, {}), {2}: (12, {})} | custom-call | flops 100663296 | bytes 4718592 | tf_op jit(solution)/shard_map/pallas_call | solution.py:55
  (45 shorter events, 5.1 us)
Async XLA Ops:
  2.8 4.6 %copy-start = (f32[1024]{0:T(1024)S(1)}, f32[1024]{0:T(1024)}, u32[]{:S(2)}) copy-start(f32[1024]{0:T(1024)} %param.9) | copy-start | bytes 12292
  2.8 1.5 %collective-permute-start = (f32[2,128,128]{2,1,0:T(8,128)S(1)}, f32[2,128,128]{2,1,0:T(8,128)S(1)}, u32[]{:S(2)}, u32[]{:S(2)}) collective-permute-start(f32[2,128,128]{2,1,0:T(8,128)S(1)} %get-tuple-element.75), channel_id=1, source_target_pairs={{0,4},{4,0},{8,12},{12,8},{16,20},{20,16},{24,28},{28,24},{1,5},{5... | collective-permute-start | bytes 393224 | tf_op jit(solution)/shard_map/ppermute | solution.py:373
  3.3 3.9 %collective-permute-start.1 = (f32[2,128,128]{2,1,0:T(8,128)S(1)}, f32[2,128,128]{2,1,0:T(8,128)S(1)}, u32[]{:S(2)}, u32[]{:S(2)}) collective-permute-start(f32[2,128,128]{2,1,0:T(8,128)S(1)} %get-tuple-element.77), channel_id=1, source_target_pairs={{0,4},{4,0},{8,12},{12,8},{16,20},{20,16},{24,28},{28,24},{1,5},{5... | collective-permute-start | bytes 393224 | tf_op jit(solution)/shard_map/ppermute | solution.py:373
  4.3 6.4 %collective-permute-start.2 = (f32[2,128,128]{2,1,0:T(8,128)S(1)}, f32[2,128,128]{2,1,0:T(8,128)S(1)}, u32[]{:S(2)}, u32[]{:S(2)}) collective-permute-start(f32[2,128,128]{2,1,0:T(8,128)S(1)} %shard_map.78.refs_2_.refs_0_), channel_id=1, source_target_pairs={{0,8},{4,20},{8,0},{12,28},{16,24},{20,4},{24,16},{28,12},{1,9},{5... | collective-permute-start | bytes 393224 | tf_op jit(solution)/shard_map/ppermute | solution.py:373
  7.3 5.6 %collective-permute-start.4 = (f32[2,128,128]{2,1,0:T(8,128)S(1)}, f32[2,128,128]{2,1,0:T(8,128)S(1)}, u32[]{:S(2)}, u32[]{:S(2)}) collective-permute-start(f32[2,128,128]{2,1,0:T(8,128)S(1)} %shard_map.79.refs_1_), channel_id=1, source_target_pairs={{0,8},{4,20},{8,0},{12,28},{16,24},{20,4},{24,16},{28,12},{1,9},{5... | collective-permute-start | bytes 393224 | tf_op jit(solution)/shard_map/ppermute | solution.py:373
  10.8 6.4 %collective-permute-start.3 = (f32[2,128,128]{2,1,0:T(8,128)S(1)}, f32[2,128,128]{2,1,0:T(8,128)S(1)}, u32[]{:S(2)}, u32[]{:S(2)}) collective-permute-start(f32[2,128,128]{2,1,0:T(8,128)S(1)} %shard_map.81.refs_4_.refs_0_), channel_id=1, source_target_pairs={{0,16},{4,12},{8,24},{12,4},{16,0},{20,28},{24,8},{28,20},{1,17},{... | collective-permute-start | bytes 393224 | tf_op jit(solution)/shard_map/ppermute | solution.py:373
  12.9 5.0 %collective-permute-start.5 = (f32[2,128,128]{2,1,0:T(8,128)S(1)}, f32[2,128,128]{2,1,0:T(8,128)S(1)}, u32[]{:S(2)}, u32[]{:S(2)}) collective-permute-start(f32[2,128,128]{2,1,0:T(8,128)S(1)} %shard_map.82.refs_1_), channel_id=1, source_target_pairs={{0,16},{4,12},{8,24},{12,4},{16,0},{20,28},{24,8},{28,20},{1,17},{... | collective-permute-start | bytes 393224 | tf_op jit(solution)/shard_map/ppermute | solution.py:373
  17.3 1.4 %collective-permute-start.7 = (f32[2,128,128]{2,1,0:T(8,128)S(1)}, f32[2,128,128]{2,1,0:T(8,128)S(1)}, u32[]{:S(2)}, u32[]{:S(2)}) collective-permute-start(f32[2,128,128]{2,1,0:T(8,128)S(1)} %get-tuple-element.85.refs_5_), channel_id=1, source_target_pairs={{0,4},{4,0},{8,12},{12,8},{16,20},{20,16},{24,28},{28,24},{1,5},{5... | collective-permute-start | bytes 393224 | tf_op jit(solution)/shard_map/ppermute | solution.py:373
  18.0 1.4 %collective-permute-start.6 = (f32[2,128,128]{2,1,0:T(8,128)S(1)}, f32[2,128,128]{2,1,0:T(8,128)S(1)}, u32[]{:S(2)}, u32[]{:S(2)}) collective-permute-start(f32[2,128,128]{2,1,0:T(8,128)S(1)} %get-tuple-element.93), channel_id=1, source_target_pairs={{0,4},{4,0},{8,12},{12,8},{16,20},{20,16},{24,28},{28,24},{1,5},{5... | collective-permute-start | bytes 393224 | tf_op jit(solution)/shard_map/ppermute | solution.py:373
  19.9 5.7 %collective-permute-start.10 = (f32[8,768]{1,0:T(8,128)S(1)}, f32[8,768]{1,0:T(8,128)S(1)}, u32[]{:S(2)}, u32[]{:S(2)}) collective-permute-start(f32[8,768]{1,0:T(8,128)S(1)} %get-tuple-element.99.refs_0_), channel_id=1, source_target_pairs={{0,3},{1,2},{2,1},{3,0},{4,7},{5,6},{6,5},{7,4},{8,11},{9,10},{10,... | collective-permute-start | bytes 73736 | tf_op jit(solution)/shard_map/ppermute | solution.py:449
  23.6 4.7 %collective-permute-start.9 = (f32[8,768]{1,0:T(8,128)S(1)}, f32[8,768]{1,0:T(8,128)S(1)}, u32[]{:S(2)}, u32[]{:S(2)}) collective-permute-start(f32[8,768]{1,0:T(8,128)S(1)} %get-tuple-element.99.refs_0_), channel_id=1, source_target_pairs={{0,2},{1,3},{2,0},{3,1},{4,6},{5,7},{6,4},{7,5},{8,10},{9,11},{10,... | collective-permute-start | bytes 73736 | tf_op jit(solution)/shard_map/ppermute | solution.py:449
  23.6 4.7 %collective-permute-start.8 = (f32[8,768]{1,0:T(8,128)S(1)}, f32[8,768]{1,0:T(8,128)S(1)}, u32[]{:S(2)}, u32[]{:S(2)}) collective-permute-start(f32[8,768]{1,0:T(8,128)S(1)} %get-tuple-element.99.refs_0_), channel_id=1, source_target_pairs={{0,1},{1,0},{2,3},{3,2},{4,5},{5,4},{6,7},{7,6},{8,9},{9,8},{10,11... | collective-permute-start | bytes 73736 | tf_op jit(solution)/shard_map/ppermute | solution.py:449
  29.0 1.6 %collective-permute-start.11 = (f32[2,128,128]{2,1,0:T(8,128)S(1)}, f32[2,128,128]{2,1,0:T(8,128)S(1)}, u32[]{:S(2)}, u32[]{:S(2)}) collective-permute-start(f32[2,128,128]{2,1,0:T(8,128)S(1)} %get-tuple-element.117), channel_id=1, source_target_pairs={{28,24},{24,28},{20,16},{16,20},{12,8},{8,12},{4,0},{0,4},{29,25},... | collective-permute-start | bytes 393224 | tf_op jit(solution)/shard_map/ppermute | solution.py:373
  29.4 2.5 %collective-permute-start.12 = (f32[2,128,128]{2,1,0:T(8,128)S(1)}, f32[2,128,128]{2,1,0:T(8,128)S(1)}, u32[]{:S(2)}, u32[]{:S(2)}) collective-permute-start(f32[2,128,128]{2,1,0:T(8,128)S(1)} %get-tuple-element.119), channel_id=1, source_target_pairs={{28,24},{24,28},{20,16},{16,20},{12,8},{8,12},{4,0},{0,4},{29,25},... | collective-permute-start | bytes 393224 | tf_op jit(solution)/shard_map/ppermute | solution.py:373
  30.6 5.0 %collective-permute-start.13 = (f32[2,128,128]{2,1,0:T(8,128)S(1)}, f32[2,128,128]{2,1,0:T(8,128)S(1)}, u32[]{:S(2)}, u32[]{:S(2)}) collective-permute-start(f32[2,128,128]{2,1,0:T(8,128)S(1)} %shard_map.93.refs_2_.refs_6_), channel_id=1, source_target_pairs={{28,20},{24,8},{20,28},{16,0},{12,4},{8,24},{4,12},{0,16},{29,21},... | collective-permute-start | bytes 393224 | tf_op jit(solution)/shard_map/ppermute | solution.py:373
  32.0 5.3 %collective-permute-start.14 = (f32[2,128,128]{2,1,0:T(8,128)S(1)}, f32[2,128,128]{2,1,0:T(8,128)S(1)}, u32[]{:S(2)}, u32[]{:S(2)}) collective-permute-start(f32[2,128,128]{2,1,0:T(8,128)S(1)} %shard_map.94.refs_7_), channel_id=1, source_target_pairs={{28,20},{24,8},{20,28},{16,0},{12,4},{8,24},{4,12},{0,16},{29,21},... | collective-permute-start | bytes 393224 | tf_op jit(solution)/shard_map/ppermute | solution.py:373
  35.7 6.3 %collective-permute-start.16 = (f32[2,128,128]{2,1,0:T(8,128)S(1)}, f32[2,128,128]{2,1,0:T(8,128)S(1)}, u32[]{:S(2)}, u32[]{:S(2)}) collective-permute-start(f32[2,128,128]{2,1,0:T(8,128)S(1)} %shard_map.96.refs_4_.refs_7_), channel_id=1, source_target_pairs={{28,12},{24,16},{20,4},{16,24},{12,28},{8,0},{4,20},{0,8},{29,13},... | collective-permute-start | bytes 393224 | tf_op jit(solution)/shard_map/ppermute | solution.py:373
  37.3 5.3 %collective-permute-start.15 = (f32[2,128,128]{2,1,0:T(8,128)S(1)}, f32[2,128,128]{2,1,0:T(8,128)S(1)}, u32[]{:S(2)}, u32[]{:S(2)}) collective-permute-start(f32[2,128,128]{2,1,0:T(8,128)S(1)} %shard_map.97.refs_8_), channel_id=1, source_target_pairs={{28,12},{24,16},{20,4},{16,24},{12,28},{8,0},{4,20},{0,8},{29,13},... | collective-permute-start | bytes 393224 | tf_op jit(solution)/shard_map/ppermute | solution.py:373
  42.1 1.6 %collective-permute-start.18 = (f32[2,128,128]{2,1,0:T(8,128)S(1)}, f32[2,128,128]{2,1,0:T(8,128)S(1)}, u32[]{:S(2)}, u32[]{:S(2)}) collective-permute-start(f32[2,128,128]{2,1,0:T(8,128)S(1)} %get-tuple-element.124.refs_5_), channel_id=1, source_target_pairs={{28,24},{24,28},{20,16},{16,20},{12,8},{8,12},{4,0},{0,4},{29,25},... | collective-permute-start | bytes 393224 | tf_op jit(solution)/shard_map/ppermute | solution.py:373
  42.7 2.2 %collective-permute-start.17 = (f32[2,128,128]{2,1,0:T(8,128)S(1)}, f32[2,128,128]{2,1,0:T(8,128)S(1)}, u32[]{:S(2)}, u32[]{:S(2)}) collective-permute-start(f32[2,128,128]{2,1,0:T(8,128)S(1)} %get-tuple-element.128), channel_id=1, source_target_pairs={{28,24},{24,28},{20,16},{16,20},{12,8},{8,12},{4,0},{0,4},{29,25},... | collective-permute-start | bytes 393224 | tf_op jit(solution)/shard_map/ppermute | solution.py:373

commit v12 on v11

--- a/solution.py
+++ b/solution.py
@@ -272,11 +272,14 @@
         vgrad_ref[part, lanes_of(j)] = vgrad.astype(BF16)
 
 
-def final_kernel(piece, own, wholes, plan, *refs):
-    sources = refs[5:5 + len(plan)]
-    *outs, kgrad_ref, vgrad_ref, sems = refs[5 + len(plan):]
+def final_kernel(jobs, wholes, plan, *refs):
+    inputs = [refs[5 * i:5 * i + 5] for i in range(len(jobs))]
+    refs = refs[5 * len(jobs):]
+    sources, refs = refs[:len(plan)], refs[len(plan):]
+    results, sems = refs[-1 - 2 * len(jobs):-1], refs[-1]
+    outs = refs[:-1 - 2 * len(jobs)]
     outs = outs[len(outs) - wholes:]
-    rows, copies = refs[0].shape[0], []
+    rows, copies = inputs[0][0].shape[0], []
 
     def send(source, out, part, place):
         target = outs[out].at[part, columns(*place)]
@@ -285,11 +288,16 @@
 
     for source, (out, part, place) in zip(sources, plan):
         send(source, out, part, place)
-    for part in chunks_of(rows):
-        final_part(piece, part, *refs[:5], kgrad_ref, vgrad_ref)
-        if own:
-            send(kgrad_ref.at[part], -2, part, own)
-            send(vgrad_ref.at[part], -1, part, own)
+    kept = [i for i, (_, place) in enumerate(jobs) if place is None]
+    order = kept + [i for i in range(len(jobs)) if i not in kept]
+    for i, (piece, place) in enumerate(jobs):
+        at = 2 * order.index(i)
+        kgrad_ref, vgrad_ref = results[at:at + 2]
+        for part in chunks_of(rows):
+            final_part(piece, part, *inputs[i], kgrad_ref, vgrad_ref)
+            if place:
+                send(kgrad_ref.at[part], -2, part, place)
+                send(vgrad_ref.at[part], -1, part, place)
     for copy in copies:
         copy.wait()
 
@@ -492,18 +500,18 @@
 
     piece_thin = shape((rows, PIECE * HEAD_DIM), BF16)
 
-    def final_of(piece, args, state, ready=(), outs=(), fresh=0, own=None):
-        sources = [item[0] for item in ready]
+    def final_of(jobs, ready=(), outs=(), fresh=0):
         plan = [item[1:] for item in ready]
-        args = (*args, state, *sources)
+        args = [leaf for job in jobs for leaf in job[2]] + [item[0] for item in ready]
         wholes = len(outs) + fresh
-        last = [pltpu.VMEM(piece_thin.shape, BF16)] * 2 if own else []
+        kept = sum(job[1] is None for job in jobs)
+        buffers = [pltpu.VMEM(piece_thin.shape, BF16)] * (2 * (len(jobs) - kept))
         return run(
-            partial(final_kernel, piece, own, wholes, plan), 2 * unit // count,
-            [VMEM] * len(args) + [HBM] * len(outs),
-            [HBM] * wholes + ([] if own else [VMEM] * 2),
-            [whole] * wholes + ([] if own else [piece_thin] * 2), (*args, *outs),
-            last + [pltpu.SemaphoreType.DMA((len(plan) + 2 * chunks,))],
+            partial(final_kernel, [job[:2] for job in jobs], wholes, plan),
+            2 * unit * len(jobs) // count, [VMEM] * len(args) + [HBM] * len(outs),
+            [HBM] * wholes + [VMEM] * (2 * kept), [whole] * wholes + [piece_thin] * (2 * kept),
+            (*args, *outs),
+            buffers + [pltpu.SemaphoreType.DMA((len(plan) + 2 * chunks * (len(jobs) - kept) + 1,))],
             {len(args) + i: i for i in range(len(outs))},
         )
 
@@ -513,29 +521,20 @@
             local_of(0, q1, k1, v1, turned1, pre1, *state1, *gs1, *posts1),
             local_of(1, q2, k2, v2, turned2, pre2, *state2, *gs2, *posts2),
         ],
-        lambda state, made: final_of(0, (k1, v1, *made[0][1:]), state),
+        lambda state, made: final_of([(0, None, (k1, v1, *made[0][1:], state))]),
     )
     near = (k1, v1, *made[0][1:])
     qgrad, tail, *far = made[1]
     far = (k2, v2, *far)
     every = slice(0, rows)
-    ready, outs, done = [], [], list(early)
-    for piece in range(1, count):
-        done += final_of(piece, near, gstate1[piece])
-    for i, array in enumerate(done):
-        ready.append((array, i % 2, every, (False, half, i // 2)))
-    for piece in range(count - 1):
-        now, ready = ready[:2], ready[2:]
-        fresh = 0 if outs else 2
-        *outs, kdone, vdone = final_of(piece, far, gstate2[piece], now, outs, fresh)
-        ready.append((kdone, 0, every, (True, half, piece)))
-        ready.append((vdone, 1, every, (True, half, piece)))
-    ready = [(array, out + 1, part, place) for array, out, part, place in ready]
+    jobs = [(i, (False, half, i), (*near, gstate1[i])) for i in range(1, count)]
+    jobs += [(i, None, (*far, gstate2[i])) for i in range(count - 1)]
+    ready = [(early[i], i, every, (False, half, 0)) for i in range(2)]
+    kgrad, vgrad, *done = final_of(jobs, ready, (), 2)
+    jobs = [(count - 1, (True, half, count - 1), (*far, gstate2[-1]))]
+    ready = [(done[i], 1 + i % 2, every, (True, half, i // 2)) for i in range(len(done))]
     ready.append((tail, 0, chunks_of(rows)[-1], (True, half)))
-    qgrad, kgrad, vgrad = final_of(
-        count - 1, far, gstate2[-1], ready, [qgrad, *outs], 0 if outs else 2,
-        (True, half, count - 1),
-    )
+    qgrad, kgrad, vgrad = final_of(jobs, ready, (qgrad, kgrad, vgrad))
     return qgrad, kgrad, vgrad
 
 

time: 46.9 us -> 46.5 us (level)
  Pallas kernels: 22.4 us -> 21.8 us
    pallas_call x29 -> x28, Pallas kernels: 22.4 us -> 21.8 us  [run(): pl.pallas_call(kernel, in_specs=in_specs, out_specs=out_specs, out_shape=...]
  transfers between devices with their start and end apart: 19 -> 19, of which waited for: 7 -> 8; matrix products, arithmetic and copies ran while one was open for 0% -> 0% of each run, Pallas kernels for 37% -> 37%
where the time goes in v12:
time: 46.5 us; the launch traced here: 46.3 us
  Pallas kernels  21.8 us (47%)
  starting transfers between devices  17.9 us (38%)
  waiting for transfers between devices  5.52 us (12%)
  between operations  1.05 us (2%)
    pallas_call x28, Pallas kernels, run(): pl.pallas_call(kernel, in_specs=in_specs, out_specs=out_specs, out_shape=...  21.8 us
    ppermute x16, starting transfers between devices, move(): return lax.ppermute(value, 'seq', pairs)  13.5 us
    ppermute x3, starting transfers between devices, shards(): lax.ppermute(sums, 'head', [(r, r ^ other) for r in range(peers)])  4.45 us
    ppermute x3, waiting for transfers between devices, shards(): lax.ppermute(sums, 'head', [(r, r ^ other) for r in range(peers)])  3.94 us
    ppermute x16, waiting for transfers between devices, move(): return lax.ppermute(value, 'seq', pairs)  1.58 us
  transfers between devices with their start and end apart: 19, of which 8 were waited for; matrix products, arithmetic and copies ran while one was open for 0% of the time, Pallas kernels for 37%

profile of v12, /device:TPU:0, one launch (start us, length us, event | category | flops | bytes accessed | tf_op | source)
XLA Modules:
  0.0 46.3 jit_solution(6096788743345631705)
XLA Ops:
  0.6 2.1 %shard_map.76 = (bf16[768,512]{1,0:T(8,128)(2,1)S(1)}, bf16[768,512]{1,0:T(8,128)(2,1)S(1)}, bf16[768,512]{1,0:T(8,128)(2,1)S(1)}, bf16[768,512]{1,0:T(8,128)(2,...) custom-call(bf16[768,1024]{1,0:T(8,128)(2,1)} %k_hbm.1, ...), custom_call_target="tpu_custom_call" | custom-call | flops 100663296 | bytes 3145728 | tf_op jit(solution)/shard_map/pallas_call | solution.py:55
  2.8 0.5 %collective-permute-start = (f32[2,128,128]{2,1,0:T(8,128)S(1)}, f32[2,128,128]{2,1,0:T(8,128)S(1)}, u32[]{:S(2)}, u32[]{:S(2)}) collective-permute-start(f32[2,128,128]{2,1,0:T(8,128)S(1)} %get-tuple-element.73), channel_id=1, source_target_pairs={{0,4},{4,0},{8,12},{12,8},{16,20},{20,16},{24,28},{28,24},{1,5},{5... | collective-permute-start | bytes 393224 | tf_op jit(solution)/shard_map/ppermute | solution.py:381
  4.3 2.9 %collective-permute-start.2 = (f32[2,128,128]{2,1,0:T(8,128)S(1)}, f32[2,128,128]{2,1,0:T(8,128)S(1)}, u32[]{:S(2)}, u32[]{:S(2)}) collective-permute-start(f32[2,128,128]{2,1,0:T(8,128)S(1)} %shard_map.78.refs_2_.refs_0_), channel_id=1, source_target_pairs={{0,8},{4,20},{8,0},{12,28},{16,24},{20,4},{24,16},{28,12},{1,9},{5... | collective-permute-start | bytes 393224 | tf_op jit(solution)/shard_map/ppermute | solution.py:381
  7.4 3.3 %shard_map.80 = (bf16[768,512]{1,0:T(8,128)(2,1)S(1)}, f32[768,512]{1,0:T(8,128)S(1)}, f32[768,512]{1,0:T(8,128)S(1)}, bf16[512,768]{1,0:T(8,128)(2,1)S(1)}, bf16[4,768,256]{2,1,0:T(8,128)(2,1)S(1)}) custom-call(bf16[768,1024]{1,0:T(8,128)(2,1)} %q_hbm.3, bf16[768,1024]{1,0:T(8,128)(2,1)} %og_hbm.3, ...), custom_call_target="tpu_custom_call" | custom-call | flops 603979776 | bytes 3145728 | tf_op jit(solution)/shard_map/pallas_call | solution.py:55
  10.8 2.0 %collective-permute-start.3 = (f32[2,128,128]{2,1,0:T(8,128)S(1)}, f32[2,128,128]{2,1,0:T(8,128)S(1)}, u32[]{:S(2)}, u32[]{:S(2)}) collective-permute-start(f32[2,128,128]{2,1,0:T(8,128)S(1)} %shard_map.81.refs_4_.refs_0_), channel_id=1, source_target_pairs={{0,16},{4,12},{8,24},{12,4},{16,0},{20,28},{24,8},{28,20},{1,17},{... | collective-permute-start | bytes 393224 | tf_op jit(solution)/shard_map/ppermute | solution.py:381
  12.9 1.0 %collective-permute-start.5 = (f32[2,128,128]{2,1,0:T(8,128)S(1)}, f32[2,128,128]{2,1,0:T(8,128)S(1)}, u32[]{:S(2)}, u32[]{:S(2)}) collective-permute-start(f32[2,128,128]{2,1,0:T(8,128)S(1)} %shard_map.82.refs_1_), channel_id=1, source_target_pairs={{0,16},{4,12},{8,24},{12,4},{16,0},{20,28},{24,8},{28,20},{1,17},{... | collective-permute-start | bytes 393224 | tf_op jit(solution)/shard_map/ppermute | solution.py:381
  13.9 3.3 %shard_map.83 = (bf16[768,512]{1,0:T(8,128)(2,1)S(1)}, f32[768,512]{1,0:T(8,128)S(1)}, f32[768,512]{1,0:T(8,128)S(1)}, bf16[512,768]{1,0:T(8,128)(2,1)S(1)}, bf16[4,768,256]{2,1,0:T(8,128)(2,1)S(1)}) custom-call(bf16[768,1024]{1,0:T(8,128)(2,1)} %q_hbm.3, bf16[768,1024]{1,0:T(8,128)(2,1)} %og_hbm.3, bf16[768,512]{1,0:T(8,128)(2,1)S(1)} %get-tuple-element.78.k_ref.refs_0_, ...), custom_call_target="tpu_custom_call" | custom-call | flops 603979776 | bytes 3145728 | tf_op jit(solution)/shard_map/pallas_call | solution.py:55
  19.4 0.5 %shard_map.89 = (f32[768,256]{1,0:T(8,128)S(1)}, f32[8,768]{1,0:T(8,128)S(1)}) custom-call(bf16[768,512]{1,0:T(8,128)(2,1)S(1)} %get-tuple-element.88.q_ref, f32[768,512]{1,0:T(8,128)S(1)} %get-tuple-element.89.inner_ref, f32[768,512]{1,0:T(8,128)S(1)} %get-tuple-element.90.scaled_ref.refs_2_, f32[2,128,128]{2,1,0:T(8,128)S(1)} %collective-permute-done.6.state_ref.refs_1_, ...), custom_call_target="tpu_custom_call" | custom-call | flops 50331648 | tf_op jit(solution)/shard_map/pallas_call | solution.py:55
  19.9 3.7 %collective-permute-start.10 = (f32[8,768]{1,0:T(8,128)S(1)}, f32[8,768]{1,0:T(8,128)S(1)}, u32[]{:S(2)}, u32[]{:S(2)}) collective-permute-start(f32[8,768]{1,0:T(8,128)S(1)} %get-tuple-element.97.refs_0_), channel_id=1, source_target_pairs={{0,3},{1,2},{2,1},{3,0},{4,7},{5,6},{6,5},{7,4},{8,11},{9,10},{10,... | collective-permute-start | bytes 73736 | tf_op jit(solution)/shard_map/ppermute | solution.py:457
  23.6 0.8 %collective-permute-start.8 = (f32[8,768]{1,0:T(8,128)S(1)}, f32[8,768]{1,0:T(8,128)S(1)}, u32[]{:S(2)}, u32[]{:S(2)}) collective-permute-start(f32[8,768]{1,0:T(8,128)S(1)} %get-tuple-element.97.refs_0_), channel_id=1, source_target_pairs={{0,1},{1,0},{2,3},{3,2},{4,5},{5,4},{6,7},{7,6},{8,9},{9,8},{10,11... | collective-permute-start | bytes 73736 | tf_op jit(solution)/shard_map/ppermute | solution.py:457
  24.4 1.2 %collective-permute-done.10.refs_3_ = f32[8,768]{1,0:T(8,128)S(1)} collective-permute-done((f32[8,768]{1,0:T(8,128)S(1)}, f32[8,768]{1,0:T(8,128)S(1)}, u32[]{:S(2)}, u32[]{:S(2)}) %collective-permute-start.10) | collective-permute-done | bytes 24608 | tf_op jit(solution)/shard_map/ppermute | solution.py:457
  25.6 2.7 %collective-permute-done.9.refs_2_ = f32[8,768]{1,0:T(8,128)S(1)} collective-permute-done((f32[8,768]{1,0:T(8,128)S(1)}, f32[8,768]{1,0:T(8,128)S(1)}, u32[]{:S(2)}, u32[]{:S(2)}) %collective-permute-start.9) | collective-permute-done | bytes 24608 | tf_op jit(solution)/shard_map/ppermute | solution.py:457
  28.3 0.7 %shard_map.90 = (bf16[768,256]{1,0:T(8,128)(2,1)S(1)}, bf16[3,2,128,128]{3,2,1,0:T(8,128)(2,1)S(1)}, f32[2,128,128]{2,1,0:T(8,128)S(1)}, f32[768,128]{1,0:T(8,128)S(1)}, f32[768,128]{1,0:T(8,128)S(1)}) custom-call(f32[8,768]{1,0:T(8,128)S(1)} %get-tuple-element.97.refs_0_, f32[8,768]{1,0:T(8,128)S(1)} %collective-permute-done.8.refs_1_, ...), custom_call_target="tpu_custom_call" | custom-call | flops 50331648 | tf_op jit(solution)/shard_map/pallas_call | solution.py:55
  29.5 0.6 %collective-permute-start.12 = (f32[2,128,128]{2,1,0:T(8,128)S(1)}, f32[2,128,128]{2,1,0:T(8,128)S(1)}, u32[]{:S(2)}, u32[]{:S(2)}) collective-permute-start(f32[2,128,128]{2,1,0:T(8,128)S(1)} %get-tuple-element.117), channel_id=1, source_target_pairs={{28,24},{24,28},{20,16},{16,20},{12,8},{8,12},{4,0},{0,4},{29,25},... | collective-permute-start | bytes 393224 | tf_op jit(solution)/shard_map/ppermute | solution.py:381
  30.0 0.6 %shard_map.92 = (bf16[768,256]{1,0:T(8,128)(2,1)S(1)}, bf16[3,2,128,128]{3,2,1,0:T(8,128)(2,1)S(1)}, f32[2,128,128]{2,1,0:T(8,128)S(1)}, bf16[768,256]{1,0:T(8,1...) custom-call(f32[768,128]{1,0:T(8,128)S(1)} %get-tuple-element.101.refs_0_, ...), custom_call_target="tpu_custom_call" | custom-call | flops 100663296 | tf_op jit(solution)/shard_map/pallas_call | solution.py:55
  30.6 1.4 %collective-permute-start.13 = (f32[2,128,128]{2,1,0:T(8,128)S(1)}, f32[2,128,128]{2,1,0:T(8,128)S(1)}, u32[]{:S(2)}, u32[]{:S(2)}) collective-permute-start(f32[2,128,128]{2,1,0:T(8,128)S(1)} %shard_map.93.refs_2_.refs_6_), channel_id=1, source_target_pairs={{28,20},{24,8},{20,28},{16,0},{12,4},{8,24},{4,12},{0,16},{29,21},... | collective-permute-start | bytes 393224 | tf_op jit(solution)/shard_map/ppermute | solution.py:381
  32.0 0.8 %collective-permute-start.14 = (f32[2,128,128]{2,1,0:T(8,128)S(1)}, f32[2,128,128]{2,1,0:T(8,128)S(1)}, u32[]{:S(2)}, u32[]{:S(2)}) collective-permute-start(f32[2,128,128]{2,1,0:T(8,128)S(1)} %shard_map.94.refs_7_), channel_id=1, source_target_pairs={{28,20},{24,8},{20,28},{16,0},{12,4},{8,24},{4,12},{0,16},{29,21},... | collective-permute-start | bytes 393224 | tf_op jit(solution)/shard_map/ppermute | solution.py:381
  32.8 2.7 %shard_map.95 = (bf16[768,512]{1,0:T(8,128)(2,1)S(1)}, f32[768,512]{1,0:T(8,128)S(1)}, f32[768,512]{1,0:T(8,128)S(1)}) custom-call(bf16[768,512]{1,0:T(8,128)(2,1)S(1)} %get-tuple-element.88.q_ref, bf16[768,512]{1,0:T(8,128)(2,1)S(1)} %get-tuple-element.78.k_ref.refs_0_, bf16[768,512]{1,0:T(8,128)(2,1)S(1)} %get-tuple-element.79.v_ref.refs_1_, ...), custom_call_target="tpu_custom_call" | custom-call | flops 905969664 | tf_op jit(solution)/shard_map/pallas_call | solution.py:55
  35.7 1.6 %collective-permute-start.16 = (f32[2,128,128]{2,1,0:T(8,128)S(1)}, f32[2,128,128]{2,1,0:T(8,128)S(1)}, u32[]{:S(2)}, u32[]{:S(2)}) collective-permute-start(f32[2,128,128]{2,1,0:T(8,128)S(1)} %shard_map.96.refs_4_.refs_7_), channel_id=1, source_target_pairs={{28,12},{24,16},{20,4},{16,24},{12,28},{8,0},{4,20},{0,8},{29,13},... | collective-permute-start | bytes 393224 | tf_op jit(solution)/shard_map/ppermute | solution.py:381
  37.3 1.4 %collective-permute-start.15 = (f32[2,128,128]{2,1,0:T(8,128)S(1)}, f32[2,128,128]{2,1,0:T(8,128)S(1)}, u32[]{:S(2)}, u32[]{:S(2)}) collective-permute-start(f32[2,128,128]{2,1,0:T(8,128)S(1)} %shard_map.97.refs_8_), channel_id=1, source_target_pairs={{28,12},{24,16},{20,4},{16,24},{12,28},{8,0},{4,20},{0,8},{29,13},... | collective-permute-start | bytes 393224 | tf_op jit(solution)/shard_map/ppermute | solution.py:381
  38.7 3.3 %shard_map.98 = (bf16[768,1024]{1,0:T(8,128)(2,1)}, bf16[256,512]{1,0:T(8,128)(2,1)S(1)}, f32[768,512]{1,0:T(8,128)S(1)}, f32[768,512]{1,0:T(8,128)S(1)}) custom-call(bf16[768,512]{1,0:T(8,128)(2,1)S(1)} %get-tuple-element.76.q_ref, bf16[768,512]{1,0:T(8,128)(2,1)S(1)} %get-tuple-element.69.k_ref.refs_5_.refs_0_, ...), custom_call_target="tpu_custom_call" | custom-call | flops 905969664 | tf_op jit(solution)/shard_map/pallas_call | solution.py:55
  42.6 0.6 %collective-permute-start.17 = (f32[2,128,128]{2,1,0:T(8,128)S(1)}, f32[2,128,128]{2,1,0:T(8,128)S(1)}, u32[]{:S(2)}, u32[]{:S(2)}) collective-permute-start(f32[2,128,128]{2,1,0:T(8,128)S(1)} %get-tuple-element.126), channel_id=1, source_target_pairs={{28,24},{24,28},{20,16},{16,20},{12,8},{8,12},{4,0},{0,4},{29,25},... | collective-permute-start | bytes 393224 | tf_op jit(solution)/shard_map/ppermute | solution.py:381
  43.5 1.3 %shard_map.102 = (bf16[768,1024]{1,0:T(8,128)(2,1)}, bf16[768,1024]{1,0:T(8,128)(2,1)}, bf16[768,256]{1,0:T(8,128)(2,1)S(1)}, bf16[768,256]{1,0:T(8,128)(2,1)S(1)}) custom-call(bf16[768,512]{1,0:T(8,128)(2,1)S(1)} %get-tuple-element.78.k_ref.refs_0_, bf16[768,512]{1,0:T(8,128)(2,1)S(1)} %get-tuple-element.79.v_ref.refs_1_, ...), custom_call_target="tpu_custom_call" | custom-call | flops 201326592 | tf_op jit(solution)/shard_map/pallas_call | solution.py:55
  44.8 1.3 %shard_map.103 = (bf16[768,1024]{1,0:T(8,128)(2,1)}, bf16[768,1024]{1,0:T(8,128)(2,1)}, bf16[768,1024]{1,0:T(8,128)(2,1)}) custom-call(bf16[768,512]{1,0:T(8,128)(2,1)S(1)} %get-tuple-element.69.k_ref.refs_5_.refs_0_, bf16[768,512]{1,0:T(8,128)(2,1)S(1)} %get-tuple-element.70.v_ref.refs_6_.refs_1_, ...), custom_call_target="tpu_custom_call", output_to_operand_aliasing={{0}: (8, {}), {1}: (9, {}), {2}: (10, {})} | custom-call | flops 100663296 | bytes 4718592 | tf_op jit(solution)/shard_map/pallas_call | solution.py:55
  (44 shorter events, 5.0 us)
Async XLA Ops:
  2.8 4.6 %copy-start = (f32[1024]{0:T(1024)S(1)}, f32[1024]{0:T(1024)}, u32[]{:S(2)}) copy-start(f32[1024]{0:T(1024)} %param.9) | copy-start | bytes 12292
  2.8 1.5 %collective-permute-start = (f32[2,128,128]{2,1,0:T(8,128)S(1)}, f32[2,128,128]{2,1,0:T(8,128)S(1)}, u32[]{:S(2)}, u32[]{:S(2)}) collective-permute-start(f32[2,128,128]{2,1,0:T(8,128)S(1)} %get-tuple-element.73), channel_id=1, source_target_pairs={{0,4},{4,0},{8,12},{12,8},{16,20},{20,16},{24,28},{28,24},{1,5},{5... | collective-permute-start | bytes 393224 | tf_op jit(solution)/shard_map/ppermute | solution.py:381
  3.3 3.9 %collective-permute-start.1 = (f32[2,128,128]{2,1,0:T(8,128)S(1)}, f32[2,128,128]{2,1,0:T(8,128)S(1)}, u32[]{:S(2)}, u32[]{:S(2)}) collective-permute-start(f32[2,128,128]{2,1,0:T(8,128)S(1)} %get-tuple-element.75), channel_id=1, source_target_pairs={{0,4},{4,0},{8,12},{12,8},{16,20},{20,16},{24,28},{28,24},{1,5},{5... | collective-permute-start | bytes 393224 | tf_op jit(solution)/shard_map/ppermute | solution.py:381
  4.3 6.4 %collective-permute-start.2 = (f32[2,128,128]{2,1,0:T(8,128)S(1)}, f32[2,128,128]{2,1,0:T(8,128)S(1)}, u32[]{:S(2)}, u32[]{:S(2)}) collective-permute-start(f32[2,128,128]{2,1,0:T(8,128)S(1)} %shard_map.78.refs_2_.refs_0_), channel_id=1, source_target_pairs={{0,8},{4,20},{8,0},{12,28},{16,24},{20,4},{24,16},{28,12},{1,9},{5... | collective-permute-start | bytes 393224 | tf_op jit(solution)/shard_map/ppermute | solution.py:381
  7.3 5.6 %collective-permute-start.4 = (f32[2,128,128]{2,1,0:T(8,128)S(1)}, f32[2,128,128]{2,1,0:T(8,128)S(1)}, u32[]{:S(2)}, u32[]{:S(2)}) collective-permute-start(f32[2,128,128]{2,1,0:T(8,128)S(1)} %shard_map.79.refs_1_), channel_id=1, source_target_pairs={{0,8},{4,20},{8,0},{12,28},{16,24},{20,4},{24,16},{28,12},{1,9},{5... | collective-permute-start | bytes 393224 | tf_op jit(solution)/shard_map/ppermute | solution.py:381
  10.8 6.4 %collective-permute-start.3 = (f32[2,128,128]{2,1,0:T(8,128)S(1)}, f32[2,128,128]{2,1,0:T(8,128)S(1)}, u32[]{:S(2)}, u32[]{:S(2)}) collective-permute-start(f32[2,128,128]{2,1,0:T(8,128)S(1)} %shard_map.81.refs_4_.refs_0_), channel_id=1, source_target_pairs={{0,16},{4,12},{8,24},{12,4},{16,0},{20,28},{24,8},{28,20},{1,17},{... | collective-permute-start | bytes 393224 | tf_op jit(solution)/shard_map/ppermute | solution.py:381
  12.9 5.0 %collective-permute-start.5 = (f32[2,128,128]{2,1,0:T(8,128)S(1)}, f32[2,128,128]{2,1,0:T(8,128)S(1)}, u32[]{:S(2)}, u32[]{:S(2)}) collective-permute-start(f32[2,128,128]{2,1,0:T(8,128)S(1)} %shard_map.82.refs_1_), channel_id=1, source_target_pairs={{0,16},{4,12},{8,24},{12,4},{16,0},{20,28},{24,8},{28,20},{1,17},{... | collective-permute-start | bytes 393224 | tf_op jit(solution)/shard_map/ppermute | solution.py:381
  17.3 1.4 %collective-permute-start.7 = (f32[2,128,128]{2,1,0:T(8,128)S(1)}, f32[2,128,128]{2,1,0:T(8,128)S(1)}, u32[]{:S(2)}, u32[]{:S(2)}) collective-permute-start(f32[2,128,128]{2,1,0:T(8,128)S(1)} %get-tuple-element.83.refs_5_), channel_id=1, source_target_pairs={{0,4},{4,0},{8,12},{12,8},{16,20},{20,16},{24,28},{28,24},{1,5},{5... | collective-permute-start | bytes 393224 | tf_op jit(solution)/shard_map/ppermute | solution.py:381
  18.0 1.4 %collective-permute-start.6 = (f32[2,128,128]{2,1,0:T(8,128)S(1)}, f32[2,128,128]{2,1,0:T(8,128)S(1)}, u32[]{:S(2)}, u32[]{:S(2)}) collective-permute-start(f32[2,128,128]{2,1,0:T(8,128)S(1)} %get-tuple-element.91), channel_id=1, source_target_pairs={{0,4},{4,0},{8,12},{12,8},{16,20},{20,16},{24,28},{28,24},{1,5},{5... | collective-permute-start | bytes 393224 | tf_op jit(solution)/shard_map/ppermute | solution.py:381
  19.9 5.7 %collective-permute-start.10 = (f32[8,768]{1,0:T(8,128)S(1)}, f32[8,768]{1,0:T(8,128)S(1)}, u32[]{:S(2)}, u32[]{:S(2)}) collective-permute-start(f32[8,768]{1,0:T(8,128)S(1)} %get-tuple-element.97.refs_0_), channel_id=1, source_target_pairs={{0,3},{1,2},{2,1},{3,0},{4,7},{5,6},{6,5},{7,4},{8,11},{9,10},{10,... | collective-permute-start | bytes 73736 | tf_op jit(solution)/shard_map/ppermute | solution.py:457
  23.6 4.7 %collective-permute-start.9 = (f32[8,768]{1,0:T(8,128)S(1)}, f32[8,768]{1,0:T(8,128)S(1)}, u32[]{:S(2)}, u32[]{:S(2)}) collective-permute-start(f32[8,768]{1,0:T(8,128)S(1)} %get-tuple-element.97.refs_0_), channel_id=1, source_target_pairs={{0,2},{1,3},{2,0},{3,1},{4,6},{5,7},{6,4},{7,5},{8,10},{9,11},{10,... | collective-permute-start | bytes 73736 | tf_op jit(solution)/shard_map/ppermute | solution.py:457
  23.6 4.7 %collective-permute-start.8 = (f32[8,768]{1,0:T(8,128)S(1)}, f32[8,768]{1,0:T(8,128)S(1)}, u32[]{:S(2)}, u32[]{:S(2)}) collective-permute-start(f32[8,768]{1,0:T(8,128)S(1)} %get-tuple-element.97.refs_0_), channel_id=1, source_target_pairs={{0,1},{1,0},{2,3},{3,2},{4,5},{5,4},{6,7},{7,6},{8,9},{9,8},{10,11... | collective-permute-start | bytes 73736 | tf_op jit(solution)/shard_map/ppermute | solution.py:457
  29.0 1.6 %collective-permute-start.11 = (f32[2,128,128]{2,1,0:T(8,128)S(1)}, f32[2,128,128]{2,1,0:T(8,128)S(1)}, u32[]{:S(2)}, u32[]{:S(2)}) collective-permute-start(f32[2,128,128]{2,1,0:T(8,128)S(1)} %get-tuple-element.115), channel_id=1, source_target_pairs={{28,24},{24,28},{20,16},{16,20},{12,8},{8,12},{4,0},{0,4},{29,25},... | collective-permute-start | bytes 393224 | tf_op jit(solution)/shard_map/ppermute | solution.py:381
  29.5 2.5 %collective-permute-start.12 = (f32[2,128,128]{2,1,0:T(8,128)S(1)}, f32[2,128,128]{2,1,0:T(8,128)S(1)}, u32[]{:S(2)}, u32[]{:S(2)}) collective-permute-start(f32[2,128,128]{2,1,0:T(8,128)S(1)} %get-tuple-element.117), channel_id=1, source_target_pairs={{28,24},{24,28},{20,16},{16,20},{12,8},{8,12},{4,0},{0,4},{29,25},... | collective-permute-start | bytes 393224 | tf_op jit(solution)/shard_map/ppermute | solution.py:381
  30.6 5.0 %collective-permute-start.13 = (f32[2,128,128]{2,1,0:T(8,128)S(1)}, f32[2,128,128]{2,1,0:T(8,128)S(1)}, u32[]{:S(2)}, u32[]{:S(2)}) collective-permute-start(f32[2,128,128]{2,1,0:T(8,128)S(1)} %shard_map.93.refs_2_.refs_6_), channel_id=1, source_target_pairs={{28,20},{24,8},{20,28},{16,0},{12,4},{8,24},{4,12},{0,16},{29,21},... | collective-permute-start | bytes 393224 | tf_op jit(solution)/shard_map/ppermute | solution.py:381
  32.0 5.3 %collective-permute-start.14 = (f32[2,128,128]{2,1,0:T(8,128)S(1)}, f32[2,128,128]{2,1,0:T(8,128)S(1)}, u32[]{:S(2)}, u32[]{:S(2)}) collective-permute-start(f32[2,128,128]{2,1,0:T(8,128)S(1)} %shard_map.94.refs_7_), channel_id=1, source_target_pairs={{28,20},{24,8},{20,28},{16,0},{12,4},{8,24},{4,12},{0,16},{29,21},... | collective-permute-start | bytes 393224 | tf_op jit(solution)/shard_map/ppermute | solution.py:381
  35.7 6.3 %collective-permute-start.16 = (f32[2,128,128]{2,1,0:T(8,128)S(1)}, f32[2,128,128]{2,1,0:T(8,128)S(1)}, u32[]{:S(2)}, u32[]{:S(2)}) collective-permute-start(f32[2,128,128]{2,1,0:T(8,128)S(1)} %shard_map.96.refs_4_.refs_7_), channel_id=1, source_target_pairs={{28,12},{24,16},{20,4},{16,24},{12,28},{8,0},{4,20},{0,8},{29,13},... | collective-permute-start | bytes 393224 | tf_op jit(solution)/shard_map/ppermute | solution.py:381
  37.3 5.3 %collective-permute-start.15 = (f32[2,128,128]{2,1,0:T(8,128)S(1)}, f32[2,128,128]{2,1,0:T(8,128)S(1)}, u32[]{:S(2)}, u32[]{:S(2)}) collective-permute-start(f32[2,128,128]{2,1,0:T(8,128)S(1)} %shard_map.97.refs_8_), channel_id=1, source_target_pairs={{28,12},{24,16},{20,4},{16,24},{12,28},{8,0},{4,20},{0,8},{29,13},... | collective-permute-start | bytes 393224 | tf_op jit(solution)/shard_map/ppermute | solution.py:381
  42.1 1.4 %collective-permute-start.18 = (f32[2,128,128]{2,1,0:T(8,128)S(1)}, f32[2,128,128]{2,1,0:T(8,128)S(1)}, u32[]{:S(2)}, u32[]{:S(2)}) collective-permute-start(f32[2,128,128]{2,1,0:T(8,128)S(1)} %get-tuple-element.122.refs_5_), channel_id=1, source_target_pairs={{28,24},{24,28},{20,16},{16,20},{12,8},{8,12},{4,0},{0,4},{29,25},... | collective-permute-start | bytes 393224 | tf_op jit(solution)/shard_map/ppermute | solution.py:381
  42.6 2.2 %collective-permute-start.17 = (f32[2,128,128]{2,1,0:T(8,128)S(1)}, f32[2,128,128]{2,1,0:T(8,128)S(1)}, u32[]{:S(2)}, u32[]{:S(2)}) collective-permute-start(f32[2,128,128]{2,1,0:T(8,128)S(1)} %get-tuple-element.126), channel_id=1, source_target_pairs={{28,24},{24,28},{20,16},{16,20},{12,8},{8,12},{4,0},{0,4},{29,25},... | collective-permute-start | bytes 393224 | tf_op jit(solution)/shard_map/ppermute | solution.py:381

commit v13 on v12

--- a/solution.py
+++ b/solution.py
@@ -385,6 +385,21 @@
     return move(value, [(r, r ^ 1) for r in range(lax.axis_size("seq"))], backward)
 
 
+def add_kernel(left_ref, right_ref, out_ref):
+    out_ref[...] = left_ref[...] + right_ref[...]
+
+
+def head_sums(sums):
+    peers = lax.axis_size("head")
+    distance, parts = 1, [sums]
+    while distance < peers:
+        if len(parts) == 2:
+            sums = run(add_kernel, sums.size, [VMEM] * 2, VMEM, shape(sums.shape, F32), parts)
+        parts = [sums, lax.ppermute(sums, "head", [(r, r ^ distance) for r in range(peers)])]
+        distance *= 2
+    return parts
+
+
 def shards(query, key_in, value, out_grad, gain):
     rows, width = query.shape
     half = width // 2
@@ -453,10 +468,7 @@
         attn, *sums = attn_of(number, inner, state, sums)
         attns.append(attn)
     sums = sums[0]
-    parts = [sums] + [
-        lax.ppermute(sums, "head", [(r, r ^ other) for r in range(peers)])
-        for other in range(1, peers)
-    ]
+    parts = head_sums(sums)
 
     posts = shape((chunks, PIECE, HEAD_DIM, HEAD_DIM), BF16)
     piece_out = [shape((rows, PIECE * HEAD_DIM), BF16), posts, states]

time: 46.5 us -> 46.7 us (level)
    ppermute x3 -> x2, waiting for transfers between devices: 3.94 us -> 4.38 us  [head_sums(): lax.ppermute(sums, 'head', [(r, r ^ distance) for r in range(peers)])]
    ppermute x3 -> x2, starting transfers between devices: 4.45 us -> 4.23 us  [head_sums(): lax.ppermute(sums, 'head', [(r, r ^ distance) for r in range(peers)])]
    pallas_call x28 -> x29, Pallas kernels: 21.8 us -> 21.8 us  [run(): pl.pallas_call(kernel, in_specs=in_specs, out_specs=out_specs, out_shape=...]
  transfers between devices with their start and end apart: 19 -> 18, of which waited for: 8 -> 8; matrix products, arithmetic and copies ran while one was open for 0% -> 0% of each run, Pallas kernels for 37% -> 37%
where the time goes in v13:
time: 46.7 us; the launch traced here: 46.5 us
  Pallas kernels  21.8 us (47%)
  starting transfers between devices  17.7 us (38%)
  waiting for transfers between devices  5.96 us (13%)
  between operations  1.05 us (2%)
    pallas_call x29, Pallas kernels, run(): pl.pallas_call(kernel, in_specs=in_specs, out_specs=out_specs, out_shape=...  21.8 us
    ppermute x16, starting transfers between devices, move(): return lax.ppermute(value, 'seq', pairs)  13.5 us
    ppermute x2, waiting for transfers between devices, head_sums(): lax.ppermute(sums, 'head', [(r, r ^ distance) for r in range(peers)])  4.38 us
    ppermute x2, starting transfers between devices, head_sums(): lax.ppermute(sums, 'head', [(r, r ^ distance) for r in range(peers)])  4.23 us
    ppermute x16, waiting for transfers between devices, move(): return lax.ppermute(value, 'seq', pairs)  1.58 us
  transfers between devices with their start and end apart: 18, of which 8 were waited for; matrix products, arithmetic and copies ran while one was open for 0% of the time, Pallas kernels for 37%

profile of v13, /device:TPU:0, one launch (start us, length us, event | category | flops | bytes accessed | tf_op | source)
XLA Modules:
  0.0 46.5 jit_solution(8642350757050415951)
XLA Ops:
  0.6 2.1 %shard_map.76 = (bf16[768,512]{1,0:T(8,128)(2,1)S(1)}, bf16[768,512]{1,0:T(8,128)(2,1)S(1)}, bf16[768,512]{1,0:T(8,128)(2,1)S(1)}, bf16[768,512]{1,0:T(8,128)(2,...) custom-call(bf16[768,1024]{1,0:T(8,128)(2,1)} %k_hbm.1, ...), custom_call_target="tpu_custom_call" | custom-call | flops 100663296 | bytes 3145728 | tf_op jit(solution)/shard_map/pallas_call | solution.py:55
  2.8 0.5 %collective-permute-start = (f32[2,128,128]{2,1,0:T(8,128)S(1)}, f32[2,128,128]{2,1,0:T(8,128)S(1)}, u32[]{:S(2)}, u32[]{:S(2)}) collective-permute-start(f32[2,128,128]{2,1,0:T(8,128)S(1)} %get-tuple-element.73), channel_id=1, source_target_pairs={{0,4},{4,0},{8,12},{12,8},{16,20},{20,16},{24,28},{28,24},{1,5},{5... | collective-permute-start | bytes 393224 | tf_op jit(solution)/shard_map/ppermute | solution.py:381
  4.3 2.9 %collective-permute-start.2 = (f32[2,128,128]{2,1,0:T(8,128)S(1)}, f32[2,128,128]{2,1,0:T(8,128)S(1)}, u32[]{:S(2)}, u32[]{:S(2)}) collective-permute-start(f32[2,128,128]{2,1,0:T(8,128)S(1)} %shard_map.78.refs_2_.refs_0_), channel_id=1, source_target_pairs={{0,8},{4,20},{8,0},{12,28},{16,24},{20,4},{24,16},{28,12},{1,9},{5... | collective-permute-start | bytes 393224 | tf_op jit(solution)/shard_map/ppermute | solution.py:381
  7.4 3.3 %shard_map.80 = (bf16[768,512]{1,0:T(8,128)(2,1)S(1)}, f32[768,512]{1,0:T(8,128)S(1)}, f32[768,512]{1,0:T(8,128)S(1)}, bf16[512,768]{1,0:T(8,128)(2,1)S(1)}, bf16[4,768,256]{2,1,0:T(8,128)(2,1)S(1)}) custom-call(bf16[768,1024]{1,0:T(8,128)(2,1)} %q_hbm.3, bf16[768,1024]{1,0:T(8,128)(2,1)} %og_hbm.3, ...), custom_call_target="tpu_custom_call" | custom-call | flops 603979776 | bytes 3145728 | tf_op jit(solution)/shard_map/pallas_call | solution.py:55
  10.8 2.0 %collective-permute-start.3 = (f32[2,128,128]{2,1,0:T(8,128)S(1)}, f32[2,128,128]{2,1,0:T(8,128)S(1)}, u32[]{:S(2)}, u32[]{:S(2)}) collective-permute-start(f32[2,128,128]{2,1,0:T(8,128)S(1)} %shard_map.81.refs_4_.refs_0_), channel_id=1, source_target_pairs={{0,16},{4,12},{8,24},{12,4},{16,0},{20,28},{24,8},{28,20},{1,17},{... | collective-permute-start | bytes 393224 | tf_op jit(solution)/shard_map/ppermute | solution.py:381
  12.9 1.0 %collective-permute-start.5 = (f32[2,128,128]{2,1,0:T(8,128)S(1)}, f32[2,128,128]{2,1,0:T(8,128)S(1)}, u32[]{:S(2)}, u32[]{:S(2)}) collective-permute-start(f32[2,128,128]{2,1,0:T(8,128)S(1)} %shard_map.82.refs_1_), channel_id=1, source_target_pairs={{0,16},{4,12},{8,24},{12,4},{16,0},{20,28},{24,8},{28,20},{1,17},{... | collective-permute-start | bytes 393224 | tf_op jit(solution)/shard_map/ppermute | solution.py:381
  13.9 3.3 %shard_map.83 = (bf16[768,512]{1,0:T(8,128)(2,1)S(1)}, f32[768,512]{1,0:T(8,128)S(1)}, f32[768,512]{1,0:T(8,128)S(1)}, bf16[512,768]{1,0:T(8,128)(2,1)S(1)}, bf16[4,768,256]{2,1,0:T(8,128)(2,1)S(1)}) custom-call(bf16[768,1024]{1,0:T(8,128)(2,1)} %q_hbm.3, bf16[768,1024]{1,0:T(8,128)(2,1)} %og_hbm.3, bf16[768,512]{1,0:T(8,128)(2,1)S(1)} %get-tuple-element.78.k_ref.refs_0_, ...), custom_call_target="tpu_custom_call" | custom-call | flops 603979776 | bytes 3145728 | tf_op jit(solution)/shard_map/pallas_call | solution.py:55
  19.4 0.5 %shard_map.89 = (f32[768,256]{1,0:T(8,128)S(1)}, f32[8,768]{1,0:T(8,128)S(1)}) custom-call(bf16[768,512]{1,0:T(8,128)(2,1)S(1)} %get-tuple-element.88.q_ref, f32[768,512]{1,0:T(8,128)S(1)} %get-tuple-element.89.inner_ref, f32[768,512]{1,0:T(8,128)S(1)} %get-tuple-element.90.scaled_ref.refs_2_, f32[2,128,128]{2,1,0:T(8,128)S(1)} %collective-permute-done.6.state_ref.refs_1_, ...), custom_call_target="tpu_custom_call" | custom-call | flops 50331648 | tf_op jit(solution)/shard_map/pallas_call | solution.py:55
  19.9 1.6 %collective-permute-start.8 = (f32[8,768]{1,0:T(8,128)S(1)}, f32[8,768]{1,0:T(8,128)S(1)}, u32[]{:S(2)}, u32[]{:S(2)}) collective-permute-start(f32[8,768]{1,0:T(8,128)S(1)} %get-tuple-element.97.left_ref), channel_id=1, source_target_pairs={{0,1},{1,0},{2,3},{3,2},{4,5},{5,4},{6,7},{7,6},{8,9},{9,8},{10,11... | collective-permute-start | bytes 73736 | tf_op jit(solution)/shard_map/ppermute | solution.py:398
  21.6 2.2 %collective-permute-done.8.right_ref = f32[8,768]{1,0:T(8,128)S(1)} collective-permute-done((f32[8,768]{1,0:T(8,128)S(1)}, f32[8,768]{1,0:T(8,128)S(1)}, u32[]{:S(2)}, u32[]{:S(2)}) %collective-permute-start.8) | collective-permute-done | bytes 24608 | tf_op jit(solution)/shard_map/ppermute | solution.py:398
  23.8 2.6 %collective-permute-start.9 = (f32[8,768]{1,0:T(8,128)S(1)}, f32[8,768]{1,0:T(8,128)S(1)}, u32[]{:S(2)}, u32[]{:S(2)}) collective-permute-start(f32[8,768]{1,0:T(8,128)S(1)} %shard_map.90.refs_0_), channel_id=1, source_target_pairs={{0,2},{1,3},{2,0},{3,1},{4,6},{5,7},{6,4},{7,5},{8,10},{9,11},{10,... | collective-permute-start | bytes 73736 | tf_op jit(solution)/shard_map/ppermute | solution.py:398
  26.4 2.1 %collective-permute-done.9.refs_1_ = f32[8,768]{1,0:T(8,128)S(1)} collective-permute-done((f32[8,768]{1,0:T(8,128)S(1)}, f32[8,768]{1,0:T(8,128)S(1)}, u32[]{:S(2)}, u32[]{:S(2)}) %collective-permute-start.9) | collective-permute-done | bytes 24608 | tf_op jit(solution)/shard_map/ppermute | solution.py:398
  28.5 0.7 %shard_map.91 = (bf16[768,256]{1,0:T(8,128)(2,1)S(1)}, bf16[3,2,128,128]{3,2,1,0:T(8,128)(2,1)S(1)}, f32[2,128,128]{2,1,0:T(8,128)S(1)}, f32[768,128]{1,0:T(8,128)S(1)}, f32[768,128]{1,0:T(8,128)S(1)}) custom-call(f32[8,768]{1,0:T(8,128)S(1)} %shard_map.90.refs_0_, f32[8,768]{1,0:T(8,128)S(1)} %collective-permute-done.9.refs_1_, ...), custom_call_target="tpu_custom_call" | custom-call | flops 50331648 | tf_op jit(solution)/shard_map/pallas_call | solution.py:55
  29.7 0.6 %collective-permute-start.11 = (f32[2,128,128]{2,1,0:T(8,128)S(1)}, f32[2,128,128]{2,1,0:T(8,128)S(1)}, u32[]{:S(2)}, u32[]{:S(2)}) collective-permute-start(f32[2,128,128]{2,1,0:T(8,128)S(1)} %get-tuple-element.117), channel_id=1, source_target_pairs={{28,24},{24,28},{20,16},{16,20},{12,8},{8,12},{4,0},{0,4},{29,25},... | collective-permute-start | bytes 393224 | tf_op jit(solution)/shard_map/ppermute | solution.py:381
  30.2 0.6 %shard_map.93 = (bf16[768,256]{1,0:T(8,128)(2,1)S(1)}, bf16[3,2,128,128]{3,2,1,0:T(8,128)(2,1)S(1)}, f32[2,128,128]{2,1,0:T(8,128)S(1)}, bf16[768,256]{1,0:T(8,1...) custom-call(f32[768,128]{1,0:T(8,128)S(1)} %get-tuple-element.101.refs_0_, ...), custom_call_target="tpu_custom_call" | custom-call | flops 100663296 | tf_op jit(solution)/shard_map/pallas_call | solution.py:55
  30.8 1.4 %collective-permute-start.12 = (f32[2,128,128]{2,1,0:T(8,128)S(1)}, f32[2,128,128]{2,1,0:T(8,128)S(1)}, u32[]{:S(2)}, u32[]{:S(2)}) collective-permute-start(f32[2,128,128]{2,1,0:T(8,128)S(1)} %shard_map.94.refs_2_.refs_6_), channel_id=1, source_target_pairs={{28,20},{24,8},{20,28},{16,0},{12,4},{8,24},{4,12},{0,16},{29,21},... | collective-permute-start | bytes 393224 | tf_op jit(solution)/shard_map/ppermute | solution.py:381
  32.2 0.8 %collective-permute-start.13 = (f32[2,128,128]{2,1,0:T(8,128)S(1)}, f32[2,128,128]{2,1,0:T(8,128)S(1)}, u32[]{:S(2)}, u32[]{:S(2)}) collective-permute-start(f32[2,128,128]{2,1,0:T(8,128)S(1)} %shard_map.95.refs_7_), channel_id=1, source_target_pairs={{28,20},{24,8},{20,28},{16,0},{12,4},{8,24},{4,12},{0,16},{29,21},... | collective-permute-start | bytes 393224 | tf_op jit(solution)/shard_map/ppermute | solution.py:381
  33.0 2.7 %shard_map.96 = (bf16[768,512]{1,0:T(8,128)(2,1)S(1)}, f32[768,512]{1,0:T(8,128)S(1)}, f32[768,512]{1,0:T(8,128)S(1)}) custom-call(bf16[768,512]{1,0:T(8,128)(2,1)S(1)} %get-tuple-element.88.q_ref, bf16[768,512]{1,0:T(8,128)(2,1)S(1)} %get-tuple-element.78.k_ref.refs_0_, bf16[768,512]{1,0:T(8,128)(2,1)S(1)} %get-tuple-element.79.v_ref.refs_1_, ...), custom_call_target="tpu_custom_call" | custom-call | flops 905969664 | tf_op jit(solution)/shard_map/pallas_call | solution.py:55
  35.9 1.6 %collective-permute-start.15 = (f32[2,128,128]{2,1,0:T(8,128)S(1)}, f32[2,128,128]{2,1,0:T(8,128)S(1)}, u32[]{:S(2)}, u32[]{:S(2)}) collective-permute-start(f32[2,128,128]{2,1,0:T(8,128)S(1)} %shard_map.97.refs_4_.refs_7_), channel_id=1, source_target_pairs={{28,12},{24,16},{20,4},{16,24},{12,28},{8,0},{4,20},{0,8},{29,13},... | collective-permute-start | bytes 393224 | tf_op jit(solution)/shard_map/ppermute | solution.py:381
  37.5 1.4 %collective-permute-start.14 = (f32[2,128,128]{2,1,0:T(8,128)S(1)}, f32[2,128,128]{2,1,0:T(8,128)S(1)}, u32[]{:S(2)}, u32[]{:S(2)}) collective-permute-start(f32[2,128,128]{2,1,0:T(8,128)S(1)} %shard_map.98.refs_8_), channel_id=1, source_target_pairs={{28,12},{24,16},{20,4},{16,24},{12,28},{8,0},{4,20},{0,8},{29,13},... | collective-permute-start | bytes 393224 | tf_op jit(solution)/shard_map/ppermute | solution.py:381
  38.9 3.3 %shard_map.99 = (bf16[768,1024]{1,0:T(8,128)(2,1)}, bf16[256,512]{1,0:T(8,128)(2,1)S(1)}, f32[768,512]{1,0:T(8,128)S(1)}, f32[768,512]{1,0:T(8,128)S(1)}) custom-call(bf16[768,512]{1,0:T(8,128)(2,1)S(1)} %get-tuple-element.76.q_ref, bf16[768,512]{1,0:T(8,128)(2,1)S(1)} %get-tuple-element.69.k_ref.refs_5_.refs_0_, ...), custom_call_target="tpu_custom_call" | custom-call | flops 905969664 | tf_op jit(solution)/shard_map/pallas_call | solution.py:55
  42.9 0.6 %collective-permute-start.16 = (f32[2,128,128]{2,1,0:T(8,128)S(1)}, f32[2,128,128]{2,1,0:T(8,128)S(1)}, u32[]{:S(2)}, u32[]{:S(2)}) collective-permute-start(f32[2,128,128]{2,1,0:T(8,128)S(1)} %get-tuple-element.126), channel_id=1, source_target_pairs={{28,24},{24,28},{20,16},{16,20},{12,8},{8,12},{4,0},{0,4},{29,25},... | collective-permute-start | bytes 393224 | tf_op jit(solution)/shard_map/ppermute | solution.py:381
  43.7 1.3 %shard_map.103 = (bf16[768,1024]{1,0:T(8,128)(2,1)}, bf16[768,1024]{1,0:T(8,128)(2,1)}, bf16[768,256]{1,0:T(8,128)(2,1)S(1)}, bf16[768,256]{1,0:T(8,128)(2,1)S(1)}) custom-call(bf16[768,512]{1,0:T(8,128)(2,1)S(1)} %get-tuple-element.78.k_ref.refs_0_, bf16[768,512]{1,0:T(8,128)(2,1)S(1)} %get-tuple-element.79.v_ref.refs_1_, ...), custom_call_target="tpu_custom_call" | custom-call | flops 201326592 | tf_op jit(solution)/shard_map/pallas_call | solution.py:55
  45.0 1.3 %shard_map.104 = (bf16[768,1024]{1,0:T(8,128)(2,1)}, bf16[768,1024]{1,0:T(8,128)(2,1)}, bf16[768,1024]{1,0:T(8,128)(2,1)}) custom-call(bf16[768,512]{1,0:T(8,128)(2,1)S(1)} %get-tuple-element.69.k_ref.refs_5_.refs_0_, bf16[768,512]{1,0:T(8,128)(2,1)S(1)} %get-tuple-element.70.v_ref.refs_6_.refs_1_, ...), custom_call_target="tpu_custom_call", output_to_operand_aliasing={{0}: (8, {}), {1}: (9, {}), {2}: (10, {})} | custom-call | flops 100663296 | bytes 4718592 | tf_op jit(solution)/shard_map/pallas_call | solution.py:55
  (43 shorter events, 5.0 us)
Async XLA Ops:
  2.8 4.6 %copy-start = (f32[1024]{0:T(1024)S(1)}, f32[1024]{0:T(1024)}, u32[]{:S(2)}) copy-start(f32[1024]{0:T(1024)} %param.9) | copy-start | bytes 12292
  2.8 1.5 %collective-permute-start = (f32[2,128,128]{2,1,0:T(8,128)S(1)}, f32[2,128,128]{2,1,0:T(8,128)S(1)}, u32[]{:S(2)}, u32[]{:S(2)}) collective-permute-start(f32[2,128,128]{2,1,0:T(8,128)S(1)} %get-tuple-element.73), channel_id=1, source_target_pairs={{0,4},{4,0},{8,12},{12,8},{16,20},{20,16},{24,28},{28,24},{1,5},{5... | collective-permute-start | bytes 393224 | tf_op jit(solution)/shard_map/ppermute | solution.py:381
  3.3 3.9 %collective-permute-start.1 = (f32[2,128,128]{2,1,0:T(8,128)S(1)}, f32[2,128,128]{2,1,0:T(8,128)S(1)}, u32[]{:S(2)}, u32[]{:S(2)}) collective-permute-start(f32[2,128,128]{2,1,0:T(8,128)S(1)} %get-tuple-element.75), channel_id=1, source_target_pairs={{0,4},{4,0},{8,12},{12,8},{16,20},{20,16},{24,28},{28,24},{1,5},{5... | collective-permute-start | bytes 393224 | tf_op jit(solution)/shard_map/ppermute | solution.py:381
  4.3 6.4 %collective-permute-start.2 = (f32[2,128,128]{2,1,0:T(8,128)S(1)}, f32[2,128,128]{2,1,0:T(8,128)S(1)}, u32[]{:S(2)}, u32[]{:S(2)}) collective-permute-start(f32[2,128,128]{2,1,0:T(8,128)S(1)} %shard_map.78.refs_2_.refs_0_), channel_id=1, source_target_pairs={{0,8},{4,20},{8,0},{12,28},{16,24},{20,4},{24,16},{28,12},{1,9},{5... | collective-permute-start | bytes 393224 | tf_op jit(solution)/shard_map/ppermute | solution.py:381
  7.3 5.6 %collective-permute-start.4 = (f32[2,128,128]{2,1,0:T(8,128)S(1)}, f32[2,128,128]{2,1,0:T(8,128)S(1)}, u32[]{:S(2)}, u32[]{:S(2)}) collective-permute-start(f32[2,128,128]{2,1,0:T(8,128)S(1)} %shard_map.79.refs_1_), channel_id=1, source_target_pairs={{0,8},{4,20},{8,0},{12,28},{16,24},{20,4},{24,16},{28,12},{1,9},{5... | collective-permute-start | bytes 393224 | tf_op jit(solution)/shard_map/ppermute | solution.py:381
  10.8 6.4 %collective-permute-start.3 = (f32[2,128,128]{2,1,0:T(8,128)S(1)}, f32[2,128,128]{2,1,0:T(8,128)S(1)}, u32[]{:S(2)}, u32[]{:S(2)}) collective-permute-start(f32[2,128,128]{2,1,0:T(8,128)S(1)} %shard_map.81.refs_4_.refs_0_), channel_id=1, source_target_pairs={{0,16},{4,12},{8,24},{12,4},{16,0},{20,28},{24,8},{28,20},{1,17},{... | collective-permute-start | bytes 393224 | tf_op jit(solution)/shard_map/ppermute | solution.py:381
  12.9 5.0 %collective-permute-start.5 = (f32[2,128,128]{2,1,0:T(8,128)S(1)}, f32[2,128,128]{2,1,0:T(8,128)S(1)}, u32[]{:S(2)}, u32[]{:S(2)}) collective-permute-start(f32[2,128,128]{2,1,0:T(8,128)S(1)} %shard_map.82.refs_1_), channel_id=1, source_target_pairs={{0,16},{4,12},{8,24},{12,4},{16,0},{20,28},{24,8},{28,20},{1,17},{... | collective-permute-start | bytes 393224 | tf_op jit(solution)/shard_map/ppermute | solution.py:381
  17.3 1.4 %collective-permute-start.7 = (f32[2,128,128]{2,1,0:T(8,128)S(1)}, f32[2,128,128]{2,1,0:T(8,128)S(1)}, u32[]{:S(2)}, u32[]{:S(2)}) collective-permute-start(f32[2,128,128]{2,1,0:T(8,128)S(1)} %get-tuple-element.83.refs_5_), channel_id=1, source_target_pairs={{0,4},{4,0},{8,12},{12,8},{16,20},{20,16},{24,28},{28,24},{1,5},{5... | collective-permute-start | bytes 393224 | tf_op jit(solution)/shard_map/ppermute | solution.py:381
  18.0 1.4 %collective-permute-start.6 = (f32[2,128,128]{2,1,0:T(8,128)S(1)}, f32[2,128,128]{2,1,0:T(8,128)S(1)}, u32[]{:S(2)}, u32[]{:S(2)}) collective-permute-start(f32[2,128,128]{2,1,0:T(8,128)S(1)} %get-tuple-element.91), channel_id=1, source_target_pairs={{0,4},{4,0},{8,12},{12,8},{16,20},{20,16},{24,28},{28,24},{1,5},{5... | collective-permute-start | bytes 393224 | tf_op jit(solution)/shard_map/ppermute | solution.py:381
  19.9 3.9 %collective-permute-start.8 = (f32[8,768]{1,0:T(8,128)S(1)}, f32[8,768]{1,0:T(8,128)S(1)}, u32[]{:S(2)}, u32[]{:S(2)}) collective-permute-start(f32[8,768]{1,0:T(8,128)S(1)} %get-tuple-element.97.left_ref), channel_id=1, source_target_pairs={{0,1},{1,0},{2,3},{3,2},{4,5},{5,4},{6,7},{7,6},{8,9},{9,8},{10,11... | collective-permute-start | bytes 73736 | tf_op jit(solution)/shard_map/ppermute | solution.py:398
  23.8 4.7 %collective-permute-start.9 = (f32[8,768]{1,0:T(8,128)S(1)}, f32[8,768]{1,0:T(8,128)S(1)}, u32[]{:S(2)}, u32[]{:S(2)}) collective-permute-start(f32[8,768]{1,0:T(8,128)S(1)} %shard_map.90.refs_0_), channel_id=1, source_target_pairs={{0,2},{1,3},{2,0},{3,1},{4,6},{5,7},{6,4},{7,5},{8,10},{9,11},{10,... | collective-permute-start | bytes 73736 | tf_op jit(solution)/shard_map/ppermute | solution.py:398
  29.2 1.6 %collective-permute-start.10 = (f32[2,128,128]{2,1,0:T(8,128)S(1)}, f32[2,128,128]{2,1,0:T(8,128)S(1)}, u32[]{:S(2)}, u32[]{:S(2)}) collective-permute-start(f32[2,128,128]{2,1,0:T(8,128)S(1)} %get-tuple-element.115), channel_id=1, source_target_pairs={{28,24},{24,28},{20,16},{16,20},{12,8},{8,12},{4,0},{0,4},{29,25},... | collective-permute-start | bytes 393224 | tf_op jit(solution)/shard_map/ppermute | solution.py:381
  29.7 2.5 %collective-permute-start.11 = (f32[2,128,128]{2,1,0:T(8,128)S(1)}, f32[2,128,128]{2,1,0:T(8,128)S(1)}, u32[]{:S(2)}, u32[]{:S(2)}) collective-permute-start(f32[2,128,128]{2,1,0:T(8,128)S(1)} %get-tuple-element.117), channel_id=1, source_target_pairs={{28,24},{24,28},{20,16},{16,20},{12,8},{8,12},{4,0},{0,4},{29,25},... | collective-permute-start | bytes 393224 | tf_op jit(solution)/shard_map/ppermute | solution.py:381
  30.8 5.0 %collective-permute-start.12 = (f32[2,128,128]{2,1,0:T(8,128)S(1)}, f32[2,128,128]{2,1,0:T(8,128)S(1)}, u32[]{:S(2)}, u32[]{:S(2)}) collective-permute-start(f32[2,128,128]{2,1,0:T(8,128)S(1)} %shard_map.94.refs_2_.refs_6_), channel_id=1, source_target_pairs={{28,20},{24,8},{20,28},{16,0},{12,4},{8,24},{4,12},{0,16},{29,21},... | collective-permute-start | bytes 393224 | tf_op jit(solution)/shard_map/ppermute | solution.py:381
  32.2 5.3 %collective-permute-start.13 = (f32[2,128,128]{2,1,0:T(8,128)S(1)}, f32[2,128,128]{2,1,0:T(8,128)S(1)}, u32[]{:S(2)}, u32[]{:S(2)}) collective-permute-start(f32[2,128,128]{2,1,0:T(8,128)S(1)} %shard_map.95.refs_7_), channel_id=1, source_target_pairs={{28,20},{24,8},{20,28},{16,0},{12,4},{8,24},{4,12},{0,16},{29,21},... | collective-permute-start | bytes 393224 | tf_op jit(solution)/shard_map/ppermute | solution.py:381
  35.9 6.3 %collective-permute-start.15 = (f32[2,128,128]{2,1,0:T(8,128)S(1)}, f32[2,128,128]{2,1,0:T(8,128)S(1)}, u32[]{:S(2)}, u32[]{:S(2)}) collective-permute-start(f32[2,128,128]{2,1,0:T(8,128)S(1)} %shard_map.97.refs_4_.refs_7_), channel_id=1, source_target_pairs={{28,12},{24,16},{20,4},{16,24},{12,28},{8,0},{4,20},{0,8},{29,13},... | collective-permute-start | bytes 393224 | tf_op jit(solution)/shard_map/ppermute | solution.py:381
  37.5 5.3 %collective-permute-start.14 = (f32[2,128,128]{2,1,0:T(8,128)S(1)}, f32[2,128,128]{2,1,0:T(8,128)S(1)}, u32[]{:S(2)}, u32[]{:S(2)}) collective-permute-start(f32[2,128,128]{2,1,0:T(8,128)S(1)} %shard_map.98.refs_8_), channel_id=1, source_target_pairs={{28,12},{24,16},{20,4},{16,24},{12,28},{8,0},{4,20},{0,8},{29,13},... | collective-permute-start | bytes 393224 | tf_op jit(solution)/shard_map/ppermute | solution.py:381
  42.3 1.4 %collective-permute-start.17 = (f32[2,128,128]{2,1,0:T(8,128)S(1)}, f32[2,128,128]{2,1,0:T(8,128)S(1)}, u32[]{:S(2)}, u32[]{:S(2)}) collective-permute-start(f32[2,128,128]{2,1,0:T(8,128)S(1)} %get-tuple-element.122.refs_5_), channel_id=1, source_target_pairs={{28,24},{24,28},{20,16},{16,20},{12,8},{8,12},{4,0},{0,4},{29,25},... | collective-permute-start | bytes 393224 | tf_op jit(solution)/shard_map/ppermute | solution.py:381
  42.9 2.2 %collective-permute-start.16 = (f32[2,128,128]{2,1,0:T(8,128)S(1)}, f32[2,128,128]{2,1,0:T(8,128)S(1)}, u32[]{:S(2)}, u32[]{:S(2)}) collective-permute-start(f32[2,128,128]{2,1,0:T(8,128)S(1)} %get-tuple-element.126), channel_id=1, source_target_pairs={{28,24},{24,28},{20,16},{16,20},{12,8},{8,12},{4,0},{0,4},{29,25},... | collective-permute-start | bytes 393224 | tf_op jit(solution)/shard_map/ppermute | solution.py:381

commit v14 on v12

--- a/solution.py
+++ b/solution.py
@@ -136,7 +136,10 @@
 
 def attn_kernel(piece, first, last, q_ref, inner_ref, scaled_ref, state_ref, *refs):
     attn_ref = refs[0] if first else refs[2]
-    for part in chunks_of(q_ref.shape[0]):
+    parts = chunks_of(q_ref.shape[0])
+    if last:
+        refs[-1][...] = jnp.zeros_like(refs[-1])
+    for i, part in enumerate(parts):
         square, cross = (None, None) if first else (refs[0][part], refs[1][part])
         for j in range(PIECE):
             lanes = lanes_of(piece * PIECE + j)
@@ -147,34 +150,32 @@
             square = more if square is None else square + more
             cross = crossed if cross is None else cross + crossed
         if last:
-            square = jnp.sum(square.T, axis=0, keepdims=True)
-            cross = jnp.sum(cross.T, axis=0, keepdims=True)
-            row = lax.broadcasted_iota(jnp.int32, (8, square.shape[1]), 0)
-            sums = jnp.where(row == 0, square, jnp.where(row == 1, cross, 0.0))
-            refs[-1][:, part] = sums
+            refs[-1][2 * i:2 * i + 1] = jnp.sum(square.T, axis=0, keepdims=True)
+            refs[-1][2 * i + 1:2 * i + 2] = jnp.sum(cross.T, axis=0, keepdims=True)
         else:
             refs[-2][part] = square
             refs[-1][part] = cross
 
 
-def factors_kernel(full, parts, refs):
+def factors_kernel(full, parts, inv_ref, slope_ref, refs):
     total = refs[0][...]
     for ref in refs[1:parts]:
         total = total + ref[...]
-    inv = lax.rsqrt(total[0:1] / full + 1e-6)
-    slope = inv * inv * inv * (total[1:2] / full)
-    row = lax.broadcasted_iota(jnp.int32, total.shape, 0)
-    both = jnp.where(row == 0, inv, slope).T
-    wide = (both.shape[0], HEAD_DIM)
-    return jnp.broadcast_to(both[:, 0:1], wide), jnp.broadcast_to(both[:, 1:2], wide)
+    rows = []
+    for i, _ in enumerate(chunks_of(inv_ref.shape[0])):
+        inv = lax.rsqrt(total[2 * i:2 * i + 1] / full + 1e-6)
+        rows += [inv, inv * inv * inv * (total[2 * i + 1:2 * i + 2] / full)]
+    both = jnp.concatenate(rows + [total[len(rows):]], axis=0).T
+    for i, part in enumerate(chunks_of(inv_ref.shape[0])):
+        wide = (both.shape[0], HEAD_DIM)
+        inv_ref[part] = jnp.broadcast_to(both[:, 2 * i:2 * i + 1], wide)
+        slope_ref[part] = jnp.broadcast_to(both[:, 2 * i + 1:2 * i + 2], wide)
 
 
 def grad_kernel(pieces, full, parts, *refs):
     if parts:
-        inv, slope = factors_kernel(full, parts, refs)
-        refs[-2][...] = inv
-        refs[-1][...] = slope
         inv_ref, slope_ref = refs[-2:]
+        factors_kernel(full, parts, inv_ref, slope_ref, refs)
         refs = refs[parts:-2]
     else:
         inv_ref, slope_ref = refs[:2]
@@ -435,7 +436,7 @@
         return run(
             partial(attn_kernel, number % count, number == 0, last), unit // count,
             [VMEM] * (4 + len(sums)), [VMEM] * (2 if last else 3),
-            [piece_wide] + ([shape((8, rows), F32)] if last else [lane_sums] * 2),
+            [piece_wide] + ([shape((-(-chunks // 4) * 8, rows // chunks), F32)] if last else [lane_sums] * 2),
             (*inner, state, *sums),
         )
 

time: 46.5 us -> 46.4 us (level)
  no operation moved by 1% of the time
where the time goes in v14:
time: 46.4 us; the launch traced here: 46.2 us
  Pallas kernels  21.9 us (47%)
  starting transfers between devices  17.9 us (39%)
  waiting for transfers between devices  5.35 us (12%)
  between operations  1.05 us (2%)
    pallas_call x28, Pallas kernels, run(): pl.pallas_call(kernel, in_specs=in_specs, out_specs=out_specs, out_shape=...  21.9 us
    ppermute x16, starting transfers between devices, move(): return lax.ppermute(value, 'seq', pairs)  13.5 us
    ppermute x3, starting transfers between devices, shards(): lax.ppermute(sums, 'head', [(r, r ^ other) for r in range(peers)])  4.45 us
    ppermute x3, waiting for transfers between devices, shards(): lax.ppermute(sums, 'head', [(r, r ^ other) for r in range(peers)])  3.77 us
    ppermute x16, waiting for transfers between devices, move(): return lax.ppermute(value, 'seq', pairs)  1.58 us
  transfers between devices with their start and end apart: 19, of which 8 were waited for; matrix products, arithmetic and copies ran while one was open for 0% of the time, Pallas kernels for 37%

profile of v14, /device:TPU:0, one launch (start us, length us, event | category | flops | bytes accessed | tf_op | source)
XLA Modules:
  0.0 46.2 jit_solution(3751927684831292350)
XLA Ops:
  0.6 2.1 %shard_map.76 = (bf16[768,512]{1,0:T(8,128)(2,1)S(1)}, bf16[768,512]{1,0:T(8,128)(2,1)S(1)}, bf16[768,512]{1,0:T(8,128)(2,1)S(1)}, bf16[768,512]{1,0:T(8,128)(2,...) custom-call(bf16[768,1024]{1,0:T(8,128)(2,1)} %k_hbm.1, ...), custom_call_target="tpu_custom_call" | custom-call | flops 100663296 | bytes 3145728 | tf_op jit(solution)/shard_map/pallas_call | solution.py:55
  2.8 0.5 %collective-permute-start = (f32[2,128,128]{2,1,0:T(8,128)S(1)}, f32[2,128,128]{2,1,0:T(8,128)S(1)}, u32[]{:S(2)}, u32[]{:S(2)}) collective-permute-start(f32[2,128,128]{2,1,0:T(8,128)S(1)} %get-tuple-element.73), channel_id=1, source_target_pairs={{0,4},{4,0},{8,12},{12,8},{16,20},{20,16},{24,28},{28,24},{1,5},{5... | collective-permute-start | bytes 393224 | tf_op jit(solution)/shard_map/ppermute | solution.py:382
  4.3 2.9 %collective-permute-start.2 = (f32[2,128,128]{2,1,0:T(8,128)S(1)}, f32[2,128,128]{2,1,0:T(8,128)S(1)}, u32[]{:S(2)}, u32[]{:S(2)}) collective-permute-start(f32[2,128,128]{2,1,0:T(8,128)S(1)} %shard_map.78.refs_2_.refs_0_), channel_id=1, source_target_pairs={{0,8},{4,20},{8,0},{12,28},{16,24},{20,4},{24,16},{28,12},{1,9},{5... | collective-permute-start | bytes 393224 | tf_op jit(solution)/shard_map/ppermute | solution.py:382
  7.4 3.3 %shard_map.80 = (bf16[768,512]{1,0:T(8,128)(2,1)S(1)}, f32[768,512]{1,0:T(8,128)S(1)}, f32[768,512]{1,0:T(8,128)S(1)}, bf16[512,768]{1,0:T(8,128)(2,1)S(1)}, bf16[4,768,256]{2,1,0:T(8,128)(2,1)S(1)}) custom-call(bf16[768,1024]{1,0:T(8,128)(2,1)} %q_hbm.3, bf16[768,1024]{1,0:T(8,128)(2,1)} %og_hbm.3, ...), custom_call_target="tpu_custom_call" | custom-call | flops 603979776 | bytes 3145728 | tf_op jit(solution)/shard_map/pallas_call | solution.py:55
  10.8 2.0 %collective-permute-start.3 = (f32[2,128,128]{2,1,0:T(8,128)S(1)}, f32[2,128,128]{2,1,0:T(8,128)S(1)}, u32[]{:S(2)}, u32[]{:S(2)}) collective-permute-start(f32[2,128,128]{2,1,0:T(8,128)S(1)} %shard_map.81.refs_4_.refs_0_), channel_id=1, source_target_pairs={{0,16},{4,12},{8,24},{12,4},{16,0},{20,28},{24,8},{28,20},{1,17},{... | collective-permute-start | bytes 393224 | tf_op jit(solution)/shard_map/ppermute | solution.py:382
  12.9 1.0 %collective-permute-start.5 = (f32[2,128,128]{2,1,0:T(8,128)S(1)}, f32[2,128,128]{2,1,0:T(8,128)S(1)}, u32[]{:S(2)}, u32[]{:S(2)}) collective-permute-start(f32[2,128,128]{2,1,0:T(8,128)S(1)} %shard_map.82.refs_1_), channel_id=1, source_target_pairs={{0,16},{4,12},{8,24},{12,4},{16,0},{20,28},{24,8},{28,20},{1,17},{... | collective-permute-start | bytes 393224 | tf_op jit(solution)/shard_map/ppermute | solution.py:382
  13.9 3.3 %shard_map.83 = (bf16[768,512]{1,0:T(8,128)(2,1)S(1)}, f32[768,512]{1,0:T(8,128)S(1)}, f32[768,512]{1,0:T(8,128)S(1)}, bf16[512,768]{1,0:T(8,128)(2,1)S(1)}, bf16[4,768,256]{2,1,0:T(8,128)(2,1)S(1)}) custom-call(bf16[768,1024]{1,0:T(8,128)(2,1)} %q_hbm.3, bf16[768,1024]{1,0:T(8,128)(2,1)} %og_hbm.3, bf16[768,512]{1,0:T(8,128)(2,1)S(1)} %get-tuple-element.78.k_ref.refs_0_, ...), custom_call_target="tpu_custom_call" | custom-call | flops 603979776 | bytes 3145728 | tf_op jit(solution)/shard_map/pallas_call | solution.py:55
  19.4 0.5 %shard_map.89 = (f32[768,256]{1,0:T(8,128)S(1)}, f32[8,256]{1,0:T(8,128)S(1)}) custom-call(bf16[768,512]{1,0:T(8,128)(2,1)S(1)} %get-tuple-element.88.q_ref, f32[768,512]{1,0:T(8,128)S(1)} %get-tuple-element.89.inner_ref, f32[768,512]{1,0:T(8,128)S(1)} %get-tuple-element.90.scaled_ref.refs_2_, f32[2,128,128]{2,1,0:T(8,128)S(1)} %collective-permute-done.6.state_ref.refs_1_, ...), custom_call_target="tpu_custom_call" | custom-call | flops 50331648 | tf_op jit(solution)/shard_map/pallas_call | solution.py:55
  19.9 3.7 %collective-permute-start.10 = (f32[8,256]{1,0:T(8,128)S(1)}, f32[8,256]{1,0:T(8,128)S(1)}, u32[]{:S(2)}, u32[]{:S(2)}) collective-permute-start(f32[8,256]{1,0:T(8,128)S(1)} %get-tuple-element.97.refs_0_), channel_id=1, source_target_pairs={{0,3},{1,2},{2,1},{3,0},{4,7},{5,6},{6,5},{7,4},{8,11},{9,10},{10,... | collective-permute-start | bytes 24584 | tf_op jit(solution)/shard_map/ppermute | solution.py:458
  23.6 0.8 %collective-permute-start.8 = (f32[8,256]{1,0:T(8,128)S(1)}, f32[8,256]{1,0:T(8,128)S(1)}, u32[]{:S(2)}, u32[]{:S(2)}) collective-permute-start(f32[8,256]{1,0:T(8,128)S(1)} %get-tuple-element.97.refs_0_), channel_id=1, source_target_pairs={{0,1},{1,0},{2,3},{3,2},{4,5},{5,4},{6,7},{7,6},{8,9},{9,8},{10,11... | collective-permute-start | bytes 24584 | tf_op jit(solution)/shard_map/ppermute | solution.py:458
  24.4 1.1 %collective-permute-done.10.refs_3_ = f32[8,256]{1,0:T(8,128)S(1)} collective-permute-done((f32[8,256]{1,0:T(8,128)S(1)}, f32[8,256]{1,0:T(8,128)S(1)}, u32[]{:S(2)}, u32[]{:S(2)}) %collective-permute-start.10) | collective-permute-done | bytes 8224 | tf_op jit(solution)/shard_map/ppermute | solution.py:458
  25.4 2.7 %collective-permute-done.9.refs_2_ = f32[8,256]{1,0:T(8,128)S(1)} collective-permute-done((f32[8,256]{1,0:T(8,128)S(1)}, f32[8,256]{1,0:T(8,128)S(1)}, u32[]{:S(2)}, u32[]{:S(2)}) %collective-permute-start.9) | collective-permute-done | bytes 8224 | tf_op jit(solution)/shard_map/ppermute | solution.py:458
  28.1 0.8 %shard_map.90 = (bf16[768,256]{1,0:T(8,128)(2,1)S(1)}, bf16[3,2,128,128]{3,2,1,0:T(8,128)(2,1)S(1)}, f32[2,128,128]{2,1,0:T(8,128)S(1)}, f32[768,128]{1,0:T(8,128)S(1)}, f32[768,128]{1,0:T(8,128)S(1)}) custom-call(f32[8,256]{1,0:T(8,128)S(1)} %get-tuple-element.97.refs_0_, f32[8,256]{1,0:T(8,128)S(1)} %collective-permute-done.8.refs_1_, ...), custom_call_target="tpu_custom_call" | custom-call | flops 50331648 | tf_op jit(solution)/shard_map/pallas_call | solution.py:55
  29.4 0.6 %collective-permute-start.12 = (f32[2,128,128]{2,1,0:T(8,128)S(1)}, f32[2,128,128]{2,1,0:T(8,128)S(1)}, u32[]{:S(2)}, u32[]{:S(2)}) collective-permute-start(f32[2,128,128]{2,1,0:T(8,128)S(1)} %get-tuple-element.117), channel_id=1, source_target_pairs={{28,24},{24,28},{20,16},{16,20},{12,8},{8,12},{4,0},{0,4},{29,25},... | collective-permute-start | bytes 393224 | tf_op jit(solution)/shard_map/ppermute | solution.py:382
  30.0 0.6 %shard_map.92 = (bf16[768,256]{1,0:T(8,128)(2,1)S(1)}, bf16[3,2,128,128]{3,2,1,0:T(8,128)(2,1)S(1)}, f32[2,128,128]{2,1,0:T(8,128)S(1)}, bf16[768,256]{1,0:T(8,1...) custom-call(f32[768,128]{1,0:T(8,128)S(1)} %get-tuple-element.101.refs_0_, ...), custom_call_target="tpu_custom_call" | custom-call | flops 100663296 | tf_op jit(solution)/shard_map/pallas_call | solution.py:55
  30.6 1.4 %collective-permute-start.13 = (f32[2,128,128]{2,1,0:T(8,128)S(1)}, f32[2,128,128]{2,1,0:T(8,128)S(1)}, u32[]{:S(2)}, u32[]{:S(2)}) collective-permute-start(f32[2,128,128]{2,1,0:T(8,128)S(1)} %shard_map.93.refs_2_.refs_6_), channel_id=1, source_target_pairs={{28,20},{24,8},{20,28},{16,0},{12,4},{8,24},{4,12},{0,16},{29,21},... | collective-permute-start | bytes 393224 | tf_op jit(solution)/shard_map/ppermute | solution.py:382
  31.9 0.8 %collective-permute-start.14 = (f32[2,128,128]{2,1,0:T(8,128)S(1)}, f32[2,128,128]{2,1,0:T(8,128)S(1)}, u32[]{:S(2)}, u32[]{:S(2)}) collective-permute-start(f32[2,128,128]{2,1,0:T(8,128)S(1)} %shard_map.94.refs_7_), channel_id=1, source_target_pairs={{28,20},{24,8},{20,28},{16,0},{12,4},{8,24},{4,12},{0,16},{29,21},... | collective-permute-start | bytes 393224 | tf_op jit(solution)/shard_map/ppermute | solution.py:382
  32.7 2.7 %shard_map.95 = (bf16[768,512]{1,0:T(8,128)(2,1)S(1)}, f32[768,512]{1,0:T(8,128)S(1)}, f32[768,512]{1,0:T(8,128)S(1)}) custom-call(bf16[768,512]{1,0:T(8,128)(2,1)S(1)} %get-tuple-element.88.q_ref, bf16[768,512]{1,0:T(8,128)(2,1)S(1)} %get-tuple-element.78.k_ref.refs_0_, bf16[768,512]{1,0:T(8,128)(2,1)S(1)} %get-tuple-element.79.v_ref.refs_1_, ...), custom_call_target="tpu_custom_call" | custom-call | flops 905969664 | tf_op jit(solution)/shard_map/pallas_call | solution.py:55
  35.6 1.6 %collective-permute-start.16 = (f32[2,128,128]{2,1,0:T(8,128)S(1)}, f32[2,128,128]{2,1,0:T(8,128)S(1)}, u32[]{:S(2)}, u32[]{:S(2)}) collective-permute-start(f32[2,128,128]{2,1,0:T(8,128)S(1)} %shard_map.96.refs_4_.refs_7_), channel_id=1, source_target_pairs={{28,12},{24,16},{20,4},{16,24},{12,28},{8,0},{4,20},{0,8},{29,13},... | collective-permute-start | bytes 393224 | tf_op jit(solution)/shard_map/ppermute | solution.py:382
  37.2 1.4 %collective-permute-start.15 = (f32[2,128,128]{2,1,0:T(8,128)S(1)}, f32[2,128,128]{2,1,0:T(8,128)S(1)}, u32[]{:S(2)}, u32[]{:S(2)}) collective-permute-start(f32[2,128,128]{2,1,0:T(8,128)S(1)} %shard_map.97.refs_8_), channel_id=1, source_target_pairs={{28,12},{24,16},{20,4},{16,24},{12,28},{8,0},{4,20},{0,8},{29,13},... | collective-permute-start | bytes 393224 | tf_op jit(solution)/shard_map/ppermute | solution.py:382
  38.6 3.3 %shard_map.98 = (bf16[768,1024]{1,0:T(8,128)(2,1)}, bf16[256,512]{1,0:T(8,128)(2,1)S(1)}, f32[768,512]{1,0:T(8,128)S(1)}, f32[768,512]{1,0:T(8,128)S(1)}) custom-call(bf16[768,512]{1,0:T(8,128)(2,1)S(1)} %get-tuple-element.76.q_ref, bf16[768,512]{1,0:T(8,128)(2,1)S(1)} %get-tuple-element.69.k_ref.refs_5_.refs_0_, ...), custom_call_target="tpu_custom_call" | custom-call | flops 905969664 | tf_op jit(solution)/shard_map/pallas_call | solution.py:55
  42.6 0.6 %collective-permute-start.17 = (f32[2,128,128]{2,1,0:T(8,128)S(1)}, f32[2,128,128]{2,1,0:T(8,128)S(1)}, u32[]{:S(2)}, u32[]{:S(2)}) collective-permute-start(f32[2,128,128]{2,1,0:T(8,128)S(1)} %get-tuple-element.126), channel_id=1, source_target_pairs={{28,24},{24,28},{20,16},{16,20},{12,8},{8,12},{4,0},{0,4},{29,25},... | collective-permute-start | bytes 393224 | tf_op jit(solution)/shard_map/ppermute | solution.py:382
  43.4 1.3 %shard_map.102 = (bf16[768,1024]{1,0:T(8,128)(2,1)}, bf16[768,1024]{1,0:T(8,128)(2,1)}, bf16[768,256]{1,0:T(8,128)(2,1)S(1)}, bf16[768,256]{1,0:T(8,128)(2,1)S(1)}) custom-call(bf16[768,512]{1,0:T(8,128)(2,1)S(1)} %get-tuple-element.78.k_ref.refs_0_, bf16[768,512]{1,0:T(8,128)(2,1)S(1)} %get-tuple-element.79.v_ref.refs_1_, ...), custom_call_target="tpu_custom_call" | custom-call | flops 201326592 | tf_op jit(solution)/shard_map/pallas_call | solution.py:55
  44.7 1.3 %shard_map.103 = (bf16[768,1024]{1,0:T(8,128)(2,1)}, bf16[768,1024]{1,0:T(8,128)(2,1)}, bf16[768,1024]{1,0:T(8,128)(2,1)}) custom-call(bf16[768,512]{1,0:T(8,128)(2,1)S(1)} %get-tuple-element.69.k_ref.refs_5_.refs_0_, bf16[768,512]{1,0:T(8,128)(2,1)S(1)} %get-tuple-element.70.v_ref.refs_6_.refs_1_, ...), custom_call_target="tpu_custom_call", output_to_operand_aliasing={{0}: (8, {}), {1}: (9, {}), {2}: (10, {})} | custom-call | flops 100663296 | bytes 4718592 | tf_op jit(solution)/shard_map/pallas_call | solution.py:55
  (44 shorter events, 5.0 us)
Async XLA Ops:
  2.8 4.6 %copy-start = (f32[1024]{0:T(1024)S(1)}, f32[1024]{0:T(1024)}, u32[]{:S(2)}) copy-start(f32[1024]{0:T(1024)} %param.9) | copy-start | bytes 12292
  2.8 1.5 %collective-permute-start = (f32[2,128,128]{2,1,0:T(8,128)S(1)}, f32[2,128,128]{2,1,0:T(8,128)S(1)}, u32[]{:S(2)}, u32[]{:S(2)}) collective-permute-start(f32[2,128,128]{2,1,0:T(8,128)S(1)} %get-tuple-element.73), channel_id=1, source_target_pairs={{0,4},{4,0},{8,12},{12,8},{16,20},{20,16},{24,28},{28,24},{1,5},{5... | collective-permute-start | bytes 393224 | tf_op jit(solution)/shard_map/ppermute | solution.py:382
  3.3 3.9 %collective-permute-start.1 = (f32[2,128,128]{2,1,0:T(8,128)S(1)}, f32[2,128,128]{2,1,0:T(8,128)S(1)}, u32[]{:S(2)}, u32[]{:S(2)}) collective-permute-start(f32[2,128,128]{2,1,0:T(8,128)S(1)} %get-tuple-element.75), channel_id=1, source_target_pairs={{0,4},{4,0},{8,12},{12,8},{16,20},{20,16},{24,28},{28,24},{1,5},{5... | collective-permute-start | bytes 393224 | tf_op jit(solution)/shard_map/ppermute | solution.py:382
  4.3 6.4 %collective-permute-start.2 = (f32[2,128,128]{2,1,0:T(8,128)S(1)}, f32[2,128,128]{2,1,0:T(8,128)S(1)}, u32[]{:S(2)}, u32[]{:S(2)}) collective-permute-start(f32[2,128,128]{2,1,0:T(8,128)S(1)} %shard_map.78.refs_2_.refs_0_), channel_id=1, source_target_pairs={{0,8},{4,20},{8,0},{12,28},{16,24},{20,4},{24,16},{28,12},{1,9},{5... | collective-permute-start | bytes 393224 | tf_op jit(solution)/shard_map/ppermute | solution.py:382
  7.3 5.6 %collective-permute-start.4 = (f32[2,128,128]{2,1,0:T(8,128)S(1)}, f32[2,128,128]{2,1,0:T(8,128)S(1)}, u32[]{:S(2)}, u32[]{:S(2)}) collective-permute-start(f32[2,128,128]{2,1,0:T(8,128)S(1)} %shard_map.79.refs_1_), channel_id=1, source_target_pairs={{0,8},{4,20},{8,0},{12,28},{16,24},{20,4},{24,16},{28,12},{1,9},{5... | collective-permute-start | bytes 393224 | tf_op jit(solution)/shard_map/ppermute | solution.py:382
  10.8 6.4 %collective-permute-start.3 = (f32[2,128,128]{2,1,0:T(8,128)S(1)}, f32[2,128,128]{2,1,0:T(8,128)S(1)}, u32[]{:S(2)}, u32[]{:S(2)}) collective-permute-start(f32[2,128,128]{2,1,0:T(8,128)S(1)} %shard_map.81.refs_4_.refs_0_), channel_id=1, source_target_pairs={{0,16},{4,12},{8,24},{12,4},{16,0},{20,28},{24,8},{28,20},{1,17},{... | collective-permute-start | bytes 393224 | tf_op jit(solution)/shard_map/ppermute | solution.py:382
  12.9 5.0 %collective-permute-start.5 = (f32[2,128,128]{2,1,0:T(8,128)S(1)}, f32[2,128,128]{2,1,0:T(8,128)S(1)}, u32[]{:S(2)}, u32[]{:S(2)}) collective-permute-start(f32[2,128,128]{2,1,0:T(8,128)S(1)} %shard_map.82.refs_1_), channel_id=1, source_target_pairs={{0,16},{4,12},{8,24},{12,4},{16,0},{20,28},{24,8},{28,20},{1,17},{... | collective-permute-start | bytes 393224 | tf_op jit(solution)/shard_map/ppermute | solution.py:382
  17.3 1.4 %collective-permute-start.7 = (f32[2,128,128]{2,1,0:T(8,128)S(1)}, f32[2,128,128]{2,1,0:T(8,128)S(1)}, u32[]{:S(2)}, u32[]{:S(2)}) collective-permute-start(f32[2,128,128]{2,1,0:T(8,128)S(1)} %get-tuple-element.83.refs_5_), channel_id=1, source_target_pairs={{0,4},{4,0},{8,12},{12,8},{16,20},{20,16},{24,28},{28,24},{1,5},{5... | collective-permute-start | bytes 393224 | tf_op jit(solution)/shard_map/ppermute | solution.py:382
  18.0 1.4 %collective-permute-start.6 = (f32[2,128,128]{2,1,0:T(8,128)S(1)}, f32[2,128,128]{2,1,0:T(8,128)S(1)}, u32[]{:S(2)}, u32[]{:S(2)}) collective-permute-start(f32[2,128,128]{2,1,0:T(8,128)S(1)} %get-tuple-element.91), channel_id=1, source_target_pairs={{0,4},{4,0},{8,12},{12,8},{16,20},{20,16},{24,28},{28,24},{1,5},{5... | collective-permute-start | bytes 393224 | tf_op jit(solution)/shard_map/ppermute | solution.py:382
  19.9 5.5 %collective-permute-start.10 = (f32[8,256]{1,0:T(8,128)S(1)}, f32[8,256]{1,0:T(8,128)S(1)}, u32[]{:S(2)}, u32[]{:S(2)}) collective-permute-start(f32[8,256]{1,0:T(8,128)S(1)} %get-tuple-element.97.refs_0_), channel_id=1, source_target_pairs={{0,3},{1,2},{2,1},{3,0},{4,7},{5,6},{6,5},{7,4},{8,11},{9,10},{10,... | collective-permute-start | bytes 24584 | tf_op jit(solution)/shard_map/ppermute | solution.py:458
  23.6 4.5 %collective-permute-start.9 = (f32[8,256]{1,0:T(8,128)S(1)}, f32[8,256]{1,0:T(8,128)S(1)}, u32[]{:S(2)}, u32[]{:S(2)}) collective-permute-start(f32[8,256]{1,0:T(8,128)S(1)} %get-tuple-element.97.refs_0_), channel_id=1, source_target_pairs={{0,2},{1,3},{2,0},{3,1},{4,6},{5,7},{6,4},{7,5},{8,10},{9,11},{10,... | collective-permute-start | bytes 24584 | tf_op jit(solution)/shard_map/ppermute | solution.py:458
  23.6 4.5 %collective-permute-start.8 = (f32[8,256]{1,0:T(8,128)S(1)}, f32[8,256]{1,0:T(8,128)S(1)}, u32[]{:S(2)}, u32[]{:S(2)}) collective-permute-start(f32[8,256]{1,0:T(8,128)S(1)} %get-tuple-element.97.refs_0_), channel_id=1, source_target_pairs={{0,1},{1,0},{2,3},{3,2},{4,5},{5,4},{6,7},{7,6},{8,9},{9,8},{10,11... | collective-permute-start | bytes 24584 | tf_op jit(solution)/shard_map/ppermute | solution.py:458
  29.0 1.6 %collective-permute-start.11 = (f32[2,128,128]{2,1,0:T(8,128)S(1)}, f32[2,128,128]{2,1,0:T(8,128)S(1)}, u32[]{:S(2)}, u32[]{:S(2)}) collective-permute-start(f32[2,128,128]{2,1,0:T(8,128)S(1)} %get-tuple-element.115), channel_id=1, source_target_pairs={{28,24},{24,28},{20,16},{16,20},{12,8},{8,12},{4,0},{0,4},{29,25},... | collective-permute-start | bytes 393224 | tf_op jit(solution)/shard_map/ppermute | solution.py:382
  29.4 2.5 %collective-permute-start.12 = (f32[2,128,128]{2,1,0:T(8,128)S(1)}, f32[2,128,128]{2,1,0:T(8,128)S(1)}, u32[]{:S(2)}, u32[]{:S(2)}) collective-permute-start(f32[2,128,128]{2,1,0:T(8,128)S(1)} %get-tuple-element.117), channel_id=1, source_target_pairs={{28,24},{24,28},{20,16},{16,20},{12,8},{8,12},{4,0},{0,4},{29,25},... | collective-permute-start | bytes 393224 | tf_op jit(solution)/shard_map/ppermute | solution.py:382
  30.6 5.0 %collective-permute-start.13 = (f32[2,128,128]{2,1,0:T(8,128)S(1)}, f32[2,128,128]{2,1,0:T(8,128)S(1)}, u32[]{:S(2)}, u32[]{:S(2)}) collective-permute-start(f32[2,128,128]{2,1,0:T(8,128)S(1)} %shard_map.93.refs_2_.refs_6_), channel_id=1, source_target_pairs={{28,20},{24,8},{20,28},{16,0},{12,4},{8,24},{4,12},{0,16},{29,21},... | collective-permute-start | bytes 393224 | tf_op jit(solution)/shard_map/ppermute | solution.py:382
  31.9 5.3 %collective-permute-start.14 = (f32[2,128,128]{2,1,0:T(8,128)S(1)}, f32[2,128,128]{2,1,0:T(8,128)S(1)}, u32[]{:S(2)}, u32[]{:S(2)}) collective-permute-start(f32[2,128,128]{2,1,0:T(8,128)S(1)} %shard_map.94.refs_7_), channel_id=1, source_target_pairs={{28,20},{24,8},{20,28},{16,0},{12,4},{8,24},{4,12},{0,16},{29,21},... | collective-permute-start | bytes 393224 | tf_op jit(solution)/shard_map/ppermute | solution.py:382
  35.6 6.3 %collective-permute-start.16 = (f32[2,128,128]{2,1,0:T(8,128)S(1)}, f32[2,128,128]{2,1,0:T(8,128)S(1)}, u32[]{:S(2)}, u32[]{:S(2)}) collective-permute-start(f32[2,128,128]{2,1,0:T(8,128)S(1)} %shard_map.96.refs_4_.refs_7_), channel_id=1, source_target_pairs={{28,12},{24,16},{20,4},{16,24},{12,28},{8,0},{4,20},{0,8},{29,13},... | collective-permute-start | bytes 393224 | tf_op jit(solution)/shard_map/ppermute | solution.py:382
  37.2 5.2 %collective-permute-start.15 = (f32[2,128,128]{2,1,0:T(8,128)S(1)}, f32[2,128,128]{2,1,0:T(8,128)S(1)}, u32[]{:S(2)}, u32[]{:S(2)}) collective-permute-start(f32[2,128,128]{2,1,0:T(8,128)S(1)} %shard_map.97.refs_8_), channel_id=1, source_target_pairs={{28,12},{24,16},{20,4},{16,24},{12,28},{8,0},{4,20},{0,8},{29,13},... | collective-permute-start | bytes 393224 | tf_op jit(solution)/shard_map/ppermute | solution.py:382
  42.0 1.4 %collective-permute-start.18 = (f32[2,128,128]{2,1,0:T(8,128)S(1)}, f32[2,128,128]{2,1,0:T(8,128)S(1)}, u32[]{:S(2)}, u32[]{:S(2)}) collective-permute-start(f32[2,128,128]{2,1,0:T(8,128)S(1)} %get-tuple-element.122.refs_5_), channel_id=1, source_target_pairs={{28,24},{24,28},{20,16},{16,20},{12,8},{8,12},{4,0},{0,4},{29,25},... | collective-permute-start | bytes 393224 | tf_op jit(solution)/shard_map/ppermute | solution.py:382
  42.6 2.2 %collective-permute-start.17 = (f32[2,128,128]{2,1,0:T(8,128)S(1)}, f32[2,128,128]{2,1,0:T(8,128)S(1)}, u32[]{:S(2)}, u32[]{:S(2)}) collective-permute-start(f32[2,128,128]{2,1,0:T(8,128)S(1)} %get-tuple-element.126), channel_id=1, source_target_pairs={{28,24},{24,28},{20,16},{16,20},{12,8},{8,12},{4,0},{0,4},{29,25},... | collective-permute-start | bytes 393224 | tf_op jit(solution)/shard_map/ppermute | solution.py:382

commit v15 on v14

--- a/solution.py
+++ b/solution.py
@@ -150,8 +150,9 @@
             square = more if square is None else square + more
             cross = crossed if cross is None else cross + crossed
         if last:
-            refs[-1][2 * i:2 * i + 1] = jnp.sum(square.T, axis=0, keepdims=True)
-            refs[-1][2 * i + 1:2 * i + 2] = jnp.sum(cross.T, axis=0, keepdims=True)
+            other = refs[-1].shape[0] // 2 + i
+            refs[-1][i:i + 1] = jnp.sum(square.T, axis=0, keepdims=True)
+            refs[-1][other:other + 1] = jnp.sum(cross.T, axis=0, keepdims=True)
         else:
             refs[-2][part] = square
             refs[-1][part] = cross
@@ -161,15 +162,14 @@
     total = refs[0][...]
     for ref in refs[1:parts]:
         total = total + ref[...]
-    rows = []
-    for i, _ in enumerate(chunks_of(inv_ref.shape[0])):
-        inv = lax.rsqrt(total[2 * i:2 * i + 1] / full + 1e-6)
-        rows += [inv, inv * inv * inv * (total[2 * i + 1:2 * i + 2] / full)]
-    both = jnp.concatenate(rows + [total[len(rows):]], axis=0).T
+    middle = total.shape[0] // 2
+    inv = lax.rsqrt(total[:middle] / full + 1e-6)
+    slope = (inv * inv * inv * (total[middle:] / full)).T
+    inv = inv.T
     for i, part in enumerate(chunks_of(inv_ref.shape[0])):
-        wide = (both.shape[0], HEAD_DIM)
-        inv_ref[part] = jnp.broadcast_to(both[:, 2 * i:2 * i + 1], wide)
-        slope_ref[part] = jnp.broadcast_to(both[:, 2 * i + 1:2 * i + 2], wide)
+        wide = (inv.shape[0], HEAD_DIM)
+        inv_ref[part] = jnp.broadcast_to(inv[:, i:i + 1], wide)
+        slope_ref[part] = jnp.broadcast_to(slope[:, i:i + 1], wide)
 
 
 def grad_kernel(pieces, full, parts, *refs):
@@ -436,7 +436,7 @@
         return run(
             partial(attn_kernel, number % count, number == 0, last), unit // count,
             [VMEM] * (4 + len(sums)), [VMEM] * (2 if last else 3),
-            [piece_wide] + ([shape((-(-chunks // 4) * 8, rows // chunks), F32)] if last else [lane_sums] * 2),
+            [piece_wide] + ([shape((-(-chunks // 8) * 16, rows // chunks), F32)] if last else [lane_sums] * 2),
             (*inner, state, *sums),
         )
 

time: 46.4 us -> 46.4 us (level)
  no operation moved by 1% of the time
where the time goes in v15:
time: 46.4 us; the launch traced here: 46.2 us
  Pallas kernels  21.7 us (47%)
  starting transfers between devices  17.9 us (39%)
  waiting for transfers between devices  5.43 us (12%)
  between operations  1.05 us (2%)
    pallas_call x28, Pallas kernels, run(): pl.pallas_call(kernel, in_specs=in_specs, out_specs=out_specs, out_shape=...  21.7 us
    ppermute x16, starting transfers between devices, move(): return lax.ppermute(value, 'seq', pairs)  13.5 us
    ppermute x3, starting transfers between devices, shards(): lax.ppermute(sums, 'head', [(r, r ^ other) for r in range(peers)])  4.45 us
    ppermute x3, waiting for transfers between devices, shards(): lax.ppermute(sums, 'head', [(r, r ^ other) for r in range(peers)])  3.86 us
    ppermute x16, waiting for transfers between devices, move(): return lax.ppermute(value, 'seq', pairs)  1.58 us
  transfers between devices with their start and end apart: 19, of which 8 were waited for; matrix products, arithmetic and copies ran while one was open for 0% of the time, Pallas kernels for 37%

profile of v15, /device:TPU:0, one launch (start us, length us, event | category | flops | bytes accessed | tf_op | source)
XLA Modules:
  0.0 46.2 jit_solution(4094320536589343231)
XLA Ops:
  0.6 2.1 %shard_map.76 = (bf16[768,512]{1,0:T(8,128)(2,1)S(1)}, bf16[768,512]{1,0:T(8,128)(2,1)S(1)}, bf16[768,512]{1,0:T(8,128)(2,1)S(1)}, bf16[768,512]{1,0:T(8,128)(2,...) custom-call(bf16[768,1024]{1,0:T(8,128)(2,1)} %k_hbm.1, ...), custom_call_target="tpu_custom_call" | custom-call | flops 100663296 | bytes 3145728 | tf_op jit(solution)/shard_map/pallas_call | solution.py:55
  2.8 0.5 %collective-permute-start = (f32[2,128,128]{2,1,0:T(8,128)S(1)}, f32[2,128,128]{2,1,0:T(8,128)S(1)}, u32[]{:S(2)}, u32[]{:S(2)}) collective-permute-start(f32[2,128,128]{2,1,0:T(8,128)S(1)} %get-tuple-element.73), channel_id=1, source_target_pairs={{0,4},{4,0},{8,12},{12,8},{16,20},{20,16},{24,28},{28,24},{1,5},{5... | collective-permute-start | bytes 393224 | tf_op jit(solution)/shard_map/ppermute | solution.py:382
  4.3 2.9 %collective-permute-start.2 = (f32[2,128,128]{2,1,0:T(8,128)S(1)}, f32[2,128,128]{2,1,0:T(8,128)S(1)}, u32[]{:S(2)}, u32[]{:S(2)}) collective-permute-start(f32[2,128,128]{2,1,0:T(8,128)S(1)} %shard_map.78.refs_2_.refs_0_), channel_id=1, source_target_pairs={{0,8},{4,20},{8,0},{12,28},{16,24},{20,4},{24,16},{28,12},{1,9},{5... | collective-permute-start | bytes 393224 | tf_op jit(solution)/shard_map/ppermute | solution.py:382
  7.4 3.3 %shard_map.80 = (bf16[768,512]{1,0:T(8,128)(2,1)S(1)}, f32[768,512]{1,0:T(8,128)S(1)}, f32[768,512]{1,0:T(8,128)S(1)}, bf16[512,768]{1,0:T(8,128)(2,1)S(1)}, bf16[4,768,256]{2,1,0:T(8,128)(2,1)S(1)}) custom-call(bf16[768,1024]{1,0:T(8,128)(2,1)} %q_hbm.3, bf16[768,1024]{1,0:T(8,128)(2,1)} %og_hbm.3, ...), custom_call_target="tpu_custom_call" | custom-call | flops 603979776 | bytes 3145728 | tf_op jit(solution)/shard_map/pallas_call | solution.py:55
  10.8 2.0 %collective-permute-start.3 = (f32[2,128,128]{2,1,0:T(8,128)S(1)}, f32[2,128,128]{2,1,0:T(8,128)S(1)}, u32[]{:S(2)}, u32[]{:S(2)}) collective-permute-start(f32[2,128,128]{2,1,0:T(8,128)S(1)} %shard_map.81.refs_4_.refs_0_), channel_id=1, source_target_pairs={{0,16},{4,12},{8,24},{12,4},{16,0},{20,28},{24,8},{28,20},{1,17},{... | collective-permute-start | bytes 393224 | tf_op jit(solution)/shard_map/ppermute | solution.py:382
  12.9 1.0 %collective-permute-start.5 = (f32[2,128,128]{2,1,0:T(8,128)S(1)}, f32[2,128,128]{2,1,0:T(8,128)S(1)}, u32[]{:S(2)}, u32[]{:S(2)}) collective-permute-start(f32[2,128,128]{2,1,0:T(8,128)S(1)} %shard_map.82.refs_1_), channel_id=1, source_target_pairs={{0,16},{4,12},{8,24},{12,4},{16,0},{20,28},{24,8},{28,20},{1,17},{... | collective-permute-start | bytes 393224 | tf_op jit(solution)/shard_map/ppermute | solution.py:382
  13.9 3.3 %shard_map.83 = (bf16[768,512]{1,0:T(8,128)(2,1)S(1)}, f32[768,512]{1,0:T(8,128)S(1)}, f32[768,512]{1,0:T(8,128)S(1)}, bf16[512,768]{1,0:T(8,128)(2,1)S(1)}, bf16[4,768,256]{2,1,0:T(8,128)(2,1)S(1)}) custom-call(bf16[768,1024]{1,0:T(8,128)(2,1)} %q_hbm.3, bf16[768,1024]{1,0:T(8,128)(2,1)} %og_hbm.3, bf16[768,512]{1,0:T(8,128)(2,1)S(1)} %get-tuple-element.78.k_ref.refs_0_, ...), custom_call_target="tpu_custom_call" | custom-call | flops 603979776 | bytes 3145728 | tf_op jit(solution)/shard_map/pallas_call | solution.py:55
  19.4 0.5 %shard_map.89 = (f32[768,256]{1,0:T(8,128)S(1)}, f32[16,256]{1,0:T(8,128)S(1)}) custom-call(bf16[768,512]{1,0:T(8,128)(2,1)S(1)} %get-tuple-element.88.q_ref, f32[768,512]{1,0:T(8,128)S(1)} %get-tuple-element.89.inner_ref, f32[768,512]{1,0:T(8,128)S(1)} %get-tuple-element.90.scaled_ref.refs_2_, f32[2,128,128]{2,1,0:T(8,128)S(1)} %collective-permute-done.6.state_ref.refs_1_, ...), custom_call_target="tpu_custom_call" | custom-call | flops 50331648 | tf_op jit(solution)/shard_map/pallas_call | solution.py:55
  19.9 3.7 %collective-permute-start.10 = (f32[16,256]{1,0:T(8,128)S(1)}, f32[16,256]{1,0:T(8,128)S(1)}, u32[]{:S(2)}, u32[]{:S(2)}) collective-permute-start(f32[16,256]{1,0:T(8,128)S(1)} %get-tuple-element.97.refs_0_), channel_id=1, source_target_pairs={{0,3},{1,2},{2,1},{3,0},{4,7},{5,6},{6,5},{7,4},{8,11},{9,10},{10,... | collective-permute-start | bytes 49160 | tf_op jit(solution)/shard_map/ppermute | solution.py:458
  23.6 0.8 %collective-permute-start.8 = (f32[16,256]{1,0:T(8,128)S(1)}, f32[16,256]{1,0:T(8,128)S(1)}, u32[]{:S(2)}, u32[]{:S(2)}) collective-permute-start(f32[16,256]{1,0:T(8,128)S(1)} %get-tuple-element.97.refs_0_), channel_id=1, source_target_pairs={{0,1},{1,0},{2,3},{3,2},{4,5},{5,4},{6,7},{7,6},{8,9},{9,8},{10,11... | collective-permute-start | bytes 49160 | tf_op jit(solution)/shard_map/ppermute | solution.py:458
  24.4 1.1 %collective-permute-done.10.refs_3_ = f32[16,256]{1,0:T(8,128)S(1)} collective-permute-done((f32[16,256]{1,0:T(8,128)S(1)}, f32[16,256]{1,0:T(8,128)S(1)}, u32[]{:S(2)}, u32[]{:S(2)}) %collective-permute-start.10) | collective-permute-done | bytes 16416 | tf_op jit(solution)/shard_map/ppermute | solution.py:458
  25.5 2.7 %collective-permute-done.9.refs_2_ = f32[16,256]{1,0:T(8,128)S(1)} collective-permute-done((f32[16,256]{1,0:T(8,128)S(1)}, f32[16,256]{1,0:T(8,128)S(1)}, u32[]{:S(2)}, u32[]{:S(2)}) %collective-permute-start.9) | collective-permute-done | bytes 16416 | tf_op jit(solution)/shard_map/ppermute | solution.py:458
  28.2 0.7 %shard_map.90 = (bf16[768,256]{1,0:T(8,128)(2,1)S(1)}, bf16[3,2,128,128]{3,2,1,0:T(8,128)(2,1)S(1)}, f32[2,128,128]{2,1,0:T(8,128)S(1)}, f32[768,128]{1,0:T(8,128)S(1)}, f32[768,128]{1,0:T(8,128)S(1)}) custom-call(f32[16,256]{1,0:T(8,128)S(1)} %get-tuple-element.97.refs_0_, f32[16,256]{1,0:T(8,128)S(1)} %collective-permute-done.8.refs_1_, ...), custom_call_target="tpu_custom_call" | custom-call | flops 50331648 | tf_op jit(solution)/shard_map/pallas_call | solution.py:55
  29.3 0.6 %collective-permute-start.12 = (f32[2,128,128]{2,1,0:T(8,128)S(1)}, f32[2,128,128]{2,1,0:T(8,128)S(1)}, u32[]{:S(2)}, u32[]{:S(2)}) collective-permute-start(f32[2,128,128]{2,1,0:T(8,128)S(1)} %get-tuple-element.117), channel_id=1, source_target_pairs={{28,24},{24,28},{20,16},{16,20},{12,8},{8,12},{4,0},{0,4},{29,25},... | collective-permute-start | bytes 393224 | tf_op jit(solution)/shard_map/ppermute | solution.py:382
  29.9 0.6 %shard_map.92 = (bf16[768,256]{1,0:T(8,128)(2,1)S(1)}, bf16[3,2,128,128]{3,2,1,0:T(8,128)(2,1)S(1)}, f32[2,128,128]{2,1,0:T(8,128)S(1)}, bf16[768,256]{1,0:T(8,1...) custom-call(f32[768,128]{1,0:T(8,128)S(1)} %get-tuple-element.101.refs_0_, ...), custom_call_target="tpu_custom_call" | custom-call | flops 100663296 | tf_op jit(solution)/shard_map/pallas_call | solution.py:55
  30.5 1.4 %collective-permute-start.13 = (f32[2,128,128]{2,1,0:T(8,128)S(1)}, f32[2,128,128]{2,1,0:T(8,128)S(1)}, u32[]{:S(2)}, u32[]{:S(2)}) collective-permute-start(f32[2,128,128]{2,1,0:T(8,128)S(1)} %shard_map.93.refs_2_.refs_6_), channel_id=1, source_target_pairs={{28,20},{24,8},{20,28},{16,0},{12,4},{8,24},{4,12},{0,16},{29,21},... | collective-permute-start | bytes 393224 | tf_op jit(solution)/shard_map/ppermute | solution.py:382
  31.9 0.8 %collective-permute-start.14 = (f32[2,128,128]{2,1,0:T(8,128)S(1)}, f32[2,128,128]{2,1,0:T(8,128)S(1)}, u32[]{:S(2)}, u32[]{:S(2)}) collective-permute-start(f32[2,128,128]{2,1,0:T(8,128)S(1)} %shard_map.94.refs_7_), channel_id=1, source_target_pairs={{28,20},{24,8},{20,28},{16,0},{12,4},{8,24},{4,12},{0,16},{29,21},... | collective-permute-start | bytes 393224 | tf_op jit(solution)/shard_map/ppermute | solution.py:382
  32.7 2.7 %shard_map.95 = (bf16[768,512]{1,0:T(8,128)(2,1)S(1)}, f32[768,512]{1,0:T(8,128)S(1)}, f32[768,512]{1,0:T(8,128)S(1)}) custom-call(bf16[768,512]{1,0:T(8,128)(2,1)S(1)} %get-tuple-element.88.q_ref, bf16[768,512]{1,0:T(8,128)(2,1)S(1)} %get-tuple-element.78.k_ref.refs_0_, bf16[768,512]{1,0:T(8,128)(2,1)S(1)} %get-tuple-element.79.v_ref.refs_1_, ...), custom_call_target="tpu_custom_call" | custom-call | flops 905969664 | tf_op jit(solution)/shard_map/pallas_call | solution.py:55
  35.6 1.6 %collective-permute-start.16 = (f32[2,128,128]{2,1,0:T(8,128)S(1)}, f32[2,128,128]{2,1,0:T(8,128)S(1)}, u32[]{:S(2)}, u32[]{:S(2)}) collective-permute-start(f32[2,128,128]{2,1,0:T(8,128)S(1)} %shard_map.96.refs_4_.refs_7_), channel_id=1, source_target_pairs={{28,12},{24,16},{20,4},{16,24},{12,28},{8,0},{4,20},{0,8},{29,13},... | collective-permute-start | bytes 393224 | tf_op jit(solution)/shard_map/ppermute | solution.py:382
  37.2 1.4 %collective-permute-start.15 = (f32[2,128,128]{2,1,0:T(8,128)S(1)}, f32[2,128,128]{2,1,0:T(8,128)S(1)}, u32[]{:S(2)}, u32[]{:S(2)}) collective-permute-start(f32[2,128,128]{2,1,0:T(8,128)S(1)} %shard_map.97.refs_8_), channel_id=1, source_target_pairs={{28,12},{24,16},{20,4},{16,24},{12,28},{8,0},{4,20},{0,8},{29,13},... | collective-permute-start | bytes 393224 | tf_op jit(solution)/shard_map/ppermute | solution.py:382
  38.5 3.3 %shard_map.98 = (bf16[768,1024]{1,0:T(8,128)(2,1)}, bf16[256,512]{1,0:T(8,128)(2,1)S(1)}, f32[768,512]{1,0:T(8,128)S(1)}, f32[768,512]{1,0:T(8,128)S(1)}) custom-call(bf16[768,512]{1,0:T(8,128)(2,1)S(1)} %get-tuple-element.76.q_ref, bf16[768,512]{1,0:T(8,128)(2,1)S(1)} %get-tuple-element.69.k_ref.refs_5_.refs_0_, ...), custom_call_target="tpu_custom_call" | custom-call | flops 905969664 | tf_op jit(solution)/shard_map/pallas_call | solution.py:55
  42.5 0.6 %collective-permute-start.17 = (f32[2,128,128]{2,1,0:T(8,128)S(1)}, f32[2,128,128]{2,1,0:T(8,128)S(1)}, u32[]{:S(2)}, u32[]{:S(2)}) collective-permute-start(f32[2,128,128]{2,1,0:T(8,128)S(1)} %get-tuple-element.126), channel_id=1, source_target_pairs={{28,24},{24,28},{20,16},{16,20},{12,8},{8,12},{4,0},{0,4},{29,25},... | collective-permute-start | bytes 393224 | tf_op jit(solution)/shard_map/ppermute | solution.py:382
  43.4 1.3 %shard_map.102 = (bf16[768,1024]{1,0:T(8,128)(2,1)}, bf16[768,1024]{1,0:T(8,128)(2,1)}, bf16[768,256]{1,0:T(8,128)(2,1)S(1)}, bf16[768,256]{1,0:T(8,128)(2,1)S(1)}) custom-call(bf16[768,512]{1,0:T(8,128)(2,1)S(1)} %get-tuple-element.78.k_ref.refs_0_, bf16[768,512]{1,0:T(8,128)(2,1)S(1)} %get-tuple-element.79.v_ref.refs_1_, ...), custom_call_target="tpu_custom_call" | custom-call | flops 201326592 | tf_op jit(solution)/shard_map/pallas_call | solution.py:55
  44.7 1.3 %shard_map.103 = (bf16[768,1024]{1,0:T(8,128)(2,1)}, bf16[768,1024]{1,0:T(8,128)(2,1)}, bf16[768,1024]{1,0:T(8,128)(2,1)}) custom-call(bf16[768,512]{1,0:T(8,128)(2,1)S(1)} %get-tuple-element.69.k_ref.refs_5_.refs_0_, bf16[768,512]{1,0:T(8,128)(2,1)S(1)} %get-tuple-element.70.v_ref.refs_6_.refs_1_, ...), custom_call_target="tpu_custom_call", output_to_operand_aliasing={{0}: (8, {}), {1}: (9, {}), {2}: (10, {})} | custom-call | flops 100663296 | bytes 4718592 | tf_op jit(solution)/shard_map/pallas_call | solution.py:55
  (44 shorter events, 5.0 us)
Async XLA Ops:
  2.8 4.6 %copy-start = (f32[1024]{0:T(1024)S(1)}, f32[1024]{0:T(1024)}, u32[]{:S(2)}) copy-start(f32[1024]{0:T(1024)} %param.9) | copy-start | bytes 12292
  2.8 1.5 %collective-permute-start = (f32[2,128,128]{2,1,0:T(8,128)S(1)}, f32[2,128,128]{2,1,0:T(8,128)S(1)}, u32[]{:S(2)}, u32[]{:S(2)}) collective-permute-start(f32[2,128,128]{2,1,0:T(8,128)S(1)} %get-tuple-element.73), channel_id=1, source_target_pairs={{0,4},{4,0},{8,12},{12,8},{16,20},{20,16},{24,28},{28,24},{1,5},{5... | collective-permute-start | bytes 393224 | tf_op jit(solution)/shard_map/ppermute | solution.py:382
  3.3 3.9 %collective-permute-start.1 = (f32[2,128,128]{2,1,0:T(8,128)S(1)}, f32[2,128,128]{2,1,0:T(8,128)S(1)}, u32[]{:S(2)}, u32[]{:S(2)}) collective-permute-start(f32[2,128,128]{2,1,0:T(8,128)S(1)} %get-tuple-element.75), channel_id=1, source_target_pairs={{0,4},{4,0},{8,12},{12,8},{16,20},{20,16},{24,28},{28,24},{1,5},{5... | collective-permute-start | bytes 393224 | tf_op jit(solution)/shard_map/ppermute | solution.py:382
  4.3 6.4 %collective-permute-start.2 = (f32[2,128,128]{2,1,0:T(8,128)S(1)}, f32[2,128,128]{2,1,0:T(8,128)S(1)}, u32[]{:S(2)}, u32[]{:S(2)}) collective-permute-start(f32[2,128,128]{2,1,0:T(8,128)S(1)} %shard_map.78.refs_2_.refs_0_), channel_id=1, source_target_pairs={{0,8},{4,20},{8,0},{12,28},{16,24},{20,4},{24,16},{28,12},{1,9},{5... | collective-permute-start | bytes 393224 | tf_op jit(solution)/shard_map/ppermute | solution.py:382
  7.3 5.6 %collective-permute-start.4 = (f32[2,128,128]{2,1,0:T(8,128)S(1)}, f32[2,128,128]{2,1,0:T(8,128)S(1)}, u32[]{:S(2)}, u32[]{:S(2)}) collective-permute-start(f32[2,128,128]{2,1,0:T(8,128)S(1)} %shard_map.79.refs_1_), channel_id=1, source_target_pairs={{0,8},{4,20},{8,0},{12,28},{16,24},{20,4},{24,16},{28,12},{1,9},{5... | collective-permute-start | bytes 393224 | tf_op jit(solution)/shard_map/ppermute | solution.py:382
  10.8 6.4 %collective-permute-start.3 = (f32[2,128,128]{2,1,0:T(8,128)S(1)}, f32[2,128,128]{2,1,0:T(8,128)S(1)}, u32[]{:S(2)}, u32[]{:S(2)}) collective-permute-start(f32[2,128,128]{2,1,0:T(8,128)S(1)} %shard_map.81.refs_4_.refs_0_), channel_id=1, source_target_pairs={{0,16},{4,12},{8,24},{12,4},{16,0},{20,28},{24,8},{28,20},{1,17},{... | collective-permute-start | bytes 393224 | tf_op jit(solution)/shard_map/ppermute | solution.py:382
  12.9 5.0 %collective-permute-start.5 = (f32[2,128,128]{2,1,0:T(8,128)S(1)}, f32[2,128,128]{2,1,0:T(8,128)S(1)}, u32[]{:S(2)}, u32[]{:S(2)}) collective-permute-start(f32[2,128,128]{2,1,0:T(8,128)S(1)} %shard_map.82.refs_1_), channel_id=1, source_target_pairs={{0,16},{4,12},{8,24},{12,4},{16,0},{20,28},{24,8},{28,20},{1,17},{... | collective-permute-start | bytes 393224 | tf_op jit(solution)/shard_map/ppermute | solution.py:382
  17.3 1.4 %collective-permute-start.7 = (f32[2,128,128]{2,1,0:T(8,128)S(1)}, f32[2,128,128]{2,1,0:T(8,128)S(1)}, u32[]{:S(2)}, u32[]{:S(2)}) collective-permute-start(f32[2,128,128]{2,1,0:T(8,128)S(1)} %get-tuple-element.83.refs_5_), channel_id=1, source_target_pairs={{0,4},{4,0},{8,12},{12,8},{16,20},{20,16},{24,28},{28,24},{1,5},{5... | collective-permute-start | bytes 393224 | tf_op jit(solution)/shard_map/ppermute | solution.py:382
  18.0 1.4 %collective-permute-start.6 = (f32[2,128,128]{2,1,0:T(8,128)S(1)}, f32[2,128,128]{2,1,0:T(8,128)S(1)}, u32[]{:S(2)}, u32[]{:S(2)}) collective-permute-start(f32[2,128,128]{2,1,0:T(8,128)S(1)} %get-tuple-element.91), channel_id=1, source_target_pairs={{0,4},{4,0},{8,12},{12,8},{16,20},{20,16},{24,28},{28,24},{1,5},{5... | collective-permute-start | bytes 393224 | tf_op jit(solution)/shard_map/ppermute | solution.py:382
  19.9 5.6 %collective-permute-start.10 = (f32[16,256]{1,0:T(8,128)S(1)}, f32[16,256]{1,0:T(8,128)S(1)}, u32[]{:S(2)}, u32[]{:S(2)}) collective-permute-start(f32[16,256]{1,0:T(8,128)S(1)} %get-tuple-element.97.refs_0_), channel_id=1, source_target_pairs={{0,3},{1,2},{2,1},{3,0},{4,7},{5,6},{6,5},{7,4},{8,11},{9,10},{10,... | collective-permute-start | bytes 49160 | tf_op jit(solution)/shard_map/ppermute | solution.py:458
  23.6 4.6 %collective-permute-start.9 = (f32[16,256]{1,0:T(8,128)S(1)}, f32[16,256]{1,0:T(8,128)S(1)}, u32[]{:S(2)}, u32[]{:S(2)}) collective-permute-start(f32[16,256]{1,0:T(8,128)S(1)} %get-tuple-element.97.refs_0_), channel_id=1, source_target_pairs={{0,2},{1,3},{2,0},{3,1},{4,6},{5,7},{6,4},{7,5},{8,10},{9,11},{10,... | collective-permute-start | bytes 49160 | tf_op jit(solution)/shard_map/ppermute | solution.py:458
  23.6 4.6 %collective-permute-start.8 = (f32[16,256]{1,0:T(8,128)S(1)}, f32[16,256]{1,0:T(8,128)S(1)}, u32[]{:S(2)}, u32[]{:S(2)}) collective-permute-start(f32[16,256]{1,0:T(8,128)S(1)} %get-tuple-element.97.refs_0_), channel_id=1, source_target_pairs={{0,1},{1,0},{2,3},{3,2},{4,5},{5,4},{6,7},{7,6},{8,9},{9,8},{10,11... | collective-permute-start | bytes 49160 | tf_op jit(solution)/shard_map/ppermute | solution.py:458
  28.9 1.6 %collective-permute-start.11 = (f32[2,128,128]{2,1,0:T(8,128)S(1)}, f32[2,128,128]{2,1,0:T(8,128)S(1)}, u32[]{:S(2)}, u32[]{:S(2)}) collective-permute-start(f32[2,128,128]{2,1,0:T(8,128)S(1)} %get-tuple-element.115), channel_id=1, source_target_pairs={{28,24},{24,28},{20,16},{16,20},{12,8},{8,12},{4,0},{0,4},{29,25},... | collective-permute-start | bytes 393224 | tf_op jit(solution)/shard_map/ppermute | solution.py:382
  29.3 2.5 %collective-permute-start.12 = (f32[2,128,128]{2,1,0:T(8,128)S(1)}, f32[2,128,128]{2,1,0:T(8,128)S(1)}, u32[]{:S(2)}, u32[]{:S(2)}) collective-permute-start(f32[2,128,128]{2,1,0:T(8,128)S(1)} %get-tuple-element.117), channel_id=1, source_target_pairs={{28,24},{24,28},{20,16},{16,20},{12,8},{8,12},{4,0},{0,4},{29,25},... | collective-permute-start | bytes 393224 | tf_op jit(solution)/shard_map/ppermute | solution.py:382
  30.5 5.0 %collective-permute-start.13 = (f32[2,128,128]{2,1,0:T(8,128)S(1)}, f32[2,128,128]{2,1,0:T(8,128)S(1)}, u32[]{:S(2)}, u32[]{:S(2)}) collective-permute-start(f32[2,128,128]{2,1,0:T(8,128)S(1)} %shard_map.93.refs_2_.refs_6_), channel_id=1, source_target_pairs={{28,20},{24,8},{20,28},{16,0},{12,4},{8,24},{4,12},{0,16},{29,21},... | collective-permute-start | bytes 393224 | tf_op jit(solution)/shard_map/ppermute | solution.py:382
  31.9 5.2 %collective-permute-start.14 = (f32[2,128,128]{2,1,0:T(8,128)S(1)}, f32[2,128,128]{2,1,0:T(8,128)S(1)}, u32[]{:S(2)}, u32[]{:S(2)}) collective-permute-start(f32[2,128,128]{2,1,0:T(8,128)S(1)} %shard_map.94.refs_7_), channel_id=1, source_target_pairs={{28,20},{24,8},{20,28},{16,0},{12,4},{8,24},{4,12},{0,16},{29,21},... | collective-permute-start | bytes 393224 | tf_op jit(solution)/shard_map/ppermute | solution.py:382
  35.6 6.3 %collective-permute-start.16 = (f32[2,128,128]{2,1,0:T(8,128)S(1)}, f32[2,128,128]{2,1,0:T(8,128)S(1)}, u32[]{:S(2)}, u32[]{:S(2)}) collective-permute-start(f32[2,128,128]{2,1,0:T(8,128)S(1)} %shard_map.96.refs_4_.refs_7_), channel_id=1, source_target_pairs={{28,12},{24,16},{20,4},{16,24},{12,28},{8,0},{4,20},{0,8},{29,13},... | collective-permute-start | bytes 393224 | tf_op jit(solution)/shard_map/ppermute | solution.py:382
  37.2 5.3 %collective-permute-start.15 = (f32[2,128,128]{2,1,0:T(8,128)S(1)}, f32[2,128,128]{2,1,0:T(8,128)S(1)}, u32[]{:S(2)}, u32[]{:S(2)}) collective-permute-start(f32[2,128,128]{2,1,0:T(8,128)S(1)} %shard_map.97.refs_8_), channel_id=1, source_target_pairs={{28,12},{24,16},{20,4},{16,24},{12,28},{8,0},{4,20},{0,8},{29,13},... | collective-permute-start | bytes 393224 | tf_op jit(solution)/shard_map/ppermute | solution.py:382
  42.0 1.4 %collective-permute-start.18 = (f32[2,128,128]{2,1,0:T(8,128)S(1)}, f32[2,128,128]{2,1,0:T(8,128)S(1)}, u32[]{:S(2)}, u32[]{:S(2)}) collective-permute-start(f32[2,128,128]{2,1,0:T(8,128)S(1)} %get-tuple-element.122.refs_5_), channel_id=1, source_target_pairs={{28,24},{24,28},{20,16},{16,20},{12,8},{8,12},{4,0},{0,4},{29,25},... | collective-permute-start | bytes 393224 | tf_op jit(solution)/shard_map/ppermute | solution.py:382
  42.5 2.2 %collective-permute-start.17 = (f32[2,128,128]{2,1,0:T(8,128)S(1)}, f32[2,128,128]{2,1,0:T(8,128)S(1)}, u32[]{:S(2)}, u32[]{:S(2)}) collective-permute-start(f32[2,128,128]{2,1,0:T(8,128)S(1)} %get-tuple-element.126), channel_id=1, source_target_pairs={{28,24},{24,28},{20,16},{16,20},{12,8},{8,12},{4,0},{0,4},{29,25},... | collective-permute-start | bytes 393224 | tf_op jit(solution)/shard_map/ppermute | solution.py:382

commit v16 on v14

--- a/solution.py
+++ b/solution.py
@@ -112,25 +112,24 @@
         copy.wait()
 
 
-def inner_kernel(same, q_hbm, og_hbm, k_ref, v_ref, gain_ref, pre_ref, *refs):
-    q_ref, inner_ref, scaled_ref, qturned_ref, turned_ref, og_ref, sems = refs[-7:]
+def inner_kernel(same, query_ref, og_ref, k_ref, v_ref, gain_ref, pre_ref, *refs):
+    q_ref, inner_ref, scaled_ref, qturned_ref, turned_ref = refs[-5:]
     rows, width = q_ref.shape
-    copies = fetches((q_hbm, og_hbm), (q_ref, og_ref), sems, same)
-    for copy in copies:
-        copy.start()
+    odd = lax.rem(lax.axis_index("seq"), 2)
+    first = (odd if same else 1 - odd) * width
     gain = gain_ref[:, columns(same, width)]
     for i, part in enumerate(chunks_of(rows)):
-        for copy in copies[2 * i:2 * i + 2]:
-            copy.wait()
         for j in range(width // HEAD_DIM):
             lanes = lanes_of(j)
-            q, k = q_ref[part, lanes], k_ref[part, lanes]
+            source = pl.ds(pl.multiple_of(first + j * HEAD_DIM, HEAD_DIM), HEAD_DIM)
+            q, k = query_ref[part, source], k_ref[part, lanes]
+            q_ref[part, lanes] = q
             size = q.shape[0]
             scores = jnp.where(lower(size), dot(q, k, 1, 1), 0.0).astype(BF16)
             turned_ref[j, part] = jnp.where(upper(size), dot(k, q, 1, 1), 0.0).astype(BF16)
             inner = dot(scores, v_ref[part, lanes])
             inner_ref[part, lanes] = inner + dot(q, pre_ref[i, j]) if i else inner
-            scaled_ref[part, lanes] = gain[:, lanes] * og_ref[part, lanes].astype(F32)
+            scaled_ref[part, lanes] = gain[:, lanes] * og_ref[part, source].astype(F32)
             qturned_ref[lanes, part] = q.T
 
 
@@ -395,7 +394,7 @@
     full = width * peers
     gain = gain.reshape(1, width)
     pin = lambda x: pltpu.with_memory_space_constraint(x, pltpu.HBM)
-    query, key_in, value, out_grad = (pin(x) for x in (query, key_in, value, out_grad))
+    key_in, value = pin(key_in), pin(value)
     unit = 2 * rows * half * HEAD_DIM
     partial = functools.partial
 
@@ -420,13 +419,12 @@
     def inner_of(same, k, v, pre):
         return lambda messages: run(
             partial(inner_kernel, same), 6 * unit,
-            [HBM, HBM, VMEM, VMEM, VMEM, VMEM] + [ANYWHERE] * len(messages), [VMEM] * 5,
+            [VMEM] * 6 + [ANYWHERE] * len(messages), [VMEM] * 5,
             [
                 thin, wide, wide,
                 shape((half, rows), BF16), shape((heads, rows, rows // chunks), BF16),
             ],
             (query, out_grad, k, v, gain, pre, *messages),
-            [pltpu.VMEM((rows, half), BF16), sems],
         )
 
     piece_wide = shape((rows, PIECE * HEAD_DIM), F32)

time: 46.4 us -> 46 us (level)
  Pallas kernels: 21.9 us -> 19.2 us
  waiting for transfers between devices: 5.35 us -> 7.34 us
    pallas_call x28, Pallas kernels: 21.9 us -> 19.2 us  [run(): pl.pallas_call(kernel, in_specs=in_specs, out_specs=out_specs, out_shape=...]
    ppermute x16, waiting for transfers between devices: 1.58 us -> 3.58 us  [move(): return lax.ppermute(value, 'seq', pairs)]
  transfers between devices with their start and end apart: 19 -> 19, of which waited for: 8 -> 8; matrix products, arithmetic and copies ran while one was open for 0% -> 0% of each run, Pallas kernels for 37% -> 31%
where the time goes in v16:
time: 46 us; the launch traced here: 45.9 us
  Pallas kernels  19.2 us (42%)
  starting transfers between devices  18.2 us (40%)
  waiting for transfers between devices  7.34 us (16%)
  between operations  1.07 us (2%)
    pallas_call x28, Pallas kernels, run(): pl.pallas_call(kernel, in_specs=in_specs, out_specs=out_specs, out_shape=...  19.2 us
    ppermute x16, starting transfers between devices, move(): return lax.ppermute(value, 'seq', pairs)  13.8 us
    ppermute x3, starting transfers between devices, shards(): lax.ppermute(sums, 'head', [(r, r ^ other) for r in range(peers)])  4.45 us
    ppermute x3, waiting for transfers between devices, shards(): lax.ppermute(sums, 'head', [(r, r ^ other) for r in range(peers)])  3.77 us
    ppermute x16, waiting for transfers between devices, move(): return lax.ppermute(value, 'seq', pairs)  3.58 us
  transfers between devices with their start and end apart: 19, of which 8 were waited for; matrix products, arithmetic and copies ran while one was open for 0% of the time, Pallas kernels for 31%

profile of v16, /device:TPU:0, one launch (start us, length us, event | category | flops | bytes accessed | tf_op | source)
XLA Modules:
  0.0 45.9 jit_solution(4157076168675952314)
XLA Ops:
  0.6 2.3 %shard_map.76 = (bf16[768,512]{1,0:T(8,128)(2,1)S(1)}, bf16[768,512]{1,0:T(8,128)(2,1)S(1)}, bf16[768,512]{1,0:T(8,128)(2,1)S(1)}, bf16[768,512]{1,0:T(8,128)(2,...) custom-call(bf16[768,1024]{1,0:T(8,128)(2,1)} %k_hbm.1, ...), custom_call_target="tpu_custom_call" | custom-call | flops 100663296 | bytes 3145728 | tf_op jit(solution)/shard_map/pallas_call | solution.py:55
  4.5 2.9 %collective-permute-start.2 = (f32[2,128,128]{2,1,0:T(8,128)S(1)}, f32[2,128,128]{2,1,0:T(8,128)S(1)}, u32[]{:S(2)}, u32[]{:S(2)}) collective-permute-start(f32[2,128,128]{2,1,0:T(8,128)S(1)} %shard_map.78.refs_2_.refs_0_), channel_id=1, source_target_pairs={{0,8},{4,20},{8,0},{12,28},{16,24},{20,4},{24,16},{28,12},{1,9},{5... | collective-permute-start | bytes 393224 | tf_op jit(solution)/shard_map/ppermute | solution.py:381
  7.6 1.9 %shard_map.80 = (bf16[768,512]{1,0:T(8,128)(2,1)S(1)}, f32[768,512]{1,0:T(8,128)S(1)}, f32[768,512]{1,0:T(8,128)S(1)}, bf16[512,768]{1,0:T(8,128)(2,1)S(1)}, bf16[4,768,256]{2,1,0:T(8,128)(2,1)S(1)}) custom-call(bf16[768,1024]{1,0:T(8,128)(2,1)S(1)} %copy-done, bf16[768,1024]{1,0:T(8,128)(2,1)S(1)} %copy-done.1, ...), custom_call_target="tpu_custom_call" | custom-call | flops 603979776 | tf_op jit(solution)/shard_map/pallas_call | solution.py:55
  9.5 0.8 %collective-permute-done.2.refs_2_ = f32[2,128,128]{2,1,0:T(8,128)S(1)} collective-permute-done((f32[2,128,128]{2,1,0:T(8,128)S(1)}, f32[2,128,128]{2,1,0:T(8,128)S(1)}, u32[]{:S(2)}, u32[]{:S(2)}) %collective-permute-start.2) | collective-permute-done | bytes 131104 | tf_op jit(solution)/shard_map/ppermute | solution.py:381
  10.4 2.1 %collective-permute-start.3 = (f32[2,128,128]{2,1,0:T(8,128)S(1)}, f32[2,128,128]{2,1,0:T(8,128)S(1)}, u32[]{:S(2)}, u32[]{:S(2)}) collective-permute-start(f32[2,128,128]{2,1,0:T(8,128)S(1)} %shard_map.81.refs_4_.refs_0_), channel_id=1, source_target_pairs={{0,16},{4,12},{8,24},{12,4},{16,0},{20,28},{24,8},{28,20},{1,17},{... | collective-permute-start | bytes 393224 | tf_op jit(solution)/shard_map/ppermute | solution.py:381
  12.5 1.5 %collective-permute-start.5 = (f32[2,128,128]{2,1,0:T(8,128)S(1)}, f32[2,128,128]{2,1,0:T(8,128)S(1)}, u32[]{:S(2)}, u32[]{:S(2)}) collective-permute-start(f32[2,128,128]{2,1,0:T(8,128)S(1)} %shard_map.82.refs_1_), channel_id=1, source_target_pairs={{0,16},{4,12},{8,24},{12,4},{16,0},{20,28},{24,8},{28,20},{1,17},{... | collective-permute-start | bytes 393224 | tf_op jit(solution)/shard_map/ppermute | solution.py:381
  14.1 1.9 %shard_map.83 = (bf16[768,512]{1,0:T(8,128)(2,1)S(1)}, f32[768,512]{1,0:T(8,128)S(1)}, f32[768,512]{1,0:T(8,128)S(1)}, bf16[512,768]{1,0:T(8,128)(2,1)S(1)}, bf16[4,768,256]{2,1,0:T(8,128)(2,1)S(1)}) custom-call(bf16[768,1024]{1,0:T(8,128)(2,1)S(1)} %copy-done, bf16[768,1024]{1,0:T(8,128)(2,1)S(1)} %copy-done.1, ...), custom_call_target="tpu_custom_call" | custom-call | flops 603979776 | tf_op jit(solution)/shard_map/pallas_call | solution.py:55
  16.5 1.1 %collective-permute-done.5.refs_3_ = f32[2,128,128]{2,1,0:T(8,128)S(1)} collective-permute-done((f32[2,128,128]{2,1,0:T(8,128)S(1)}, f32[2,128,128]{2,1,0:T(8,128)S(1)}, u32[]{:S(2)}, u32[]{:S(2)}) %collective-permute-start.5) | collective-permute-done | bytes 131104 | tf_op jit(solution)/shard_map/ppermute | solution.py:381
  18.4 0.7 %collective-permute-done.6.state_ref.refs_1_ = f32[2,128,128]{2,1,0:T(8,128)S(1)} collective-permute-done((f32[2,128,128]{2,1,0:T(8,128)S(1)}, f32[2,128,128]{2,1,0:T(8,128)S(1)}, u32[]{:S(2)}, u32[]{:S(2)}) %collective-permute-start.6) | collective-permute-done | bytes 131104 | tf_op jit(solution)/shard_map/ppermute | solution.py:381
  19.6 3.7 %collective-permute-start.10 = (f32[8,256]{1,0:T(8,128)S(1)}, f32[8,256]{1,0:T(8,128)S(1)}, u32[]{:S(2)}, u32[]{:S(2)}) collective-permute-start(f32[8,256]{1,0:T(8,128)S(1)} %get-tuple-element.97.refs_0_), channel_id=1, source_target_pairs={{0,3},{1,2},{2,1},{3,0},{4,7},{5,6},{6,5},{7,4},{8,11},{9,10},{10,... | collective-permute-start | bytes 24584 | tf_op jit(solution)/shard_map/ppermute | solution.py:456
  23.2 0.8 %collective-permute-start.8 = (f32[8,256]{1,0:T(8,128)S(1)}, f32[8,256]{1,0:T(8,128)S(1)}, u32[]{:S(2)}, u32[]{:S(2)}) collective-permute-start(f32[8,256]{1,0:T(8,128)S(1)} %get-tuple-element.97.refs_0_), channel_id=1, source_target_pairs={{0,1},{1,0},{2,3},{3,2},{4,5},{5,4},{6,7},{7,6},{8,9},{9,8},{10,11... | collective-permute-start | bytes 24584 | tf_op jit(solution)/shard_map/ppermute | solution.py:456
  24.0 1.1 %collective-permute-done.10.refs_3_ = f32[8,256]{1,0:T(8,128)S(1)} collective-permute-done((f32[8,256]{1,0:T(8,128)S(1)}, f32[8,256]{1,0:T(8,128)S(1)}, u32[]{:S(2)}, u32[]{:S(2)}) %collective-permute-start.10) | collective-permute-done | bytes 8224 | tf_op jit(solution)/shard_map/ppermute | solution.py:456
  25.1 2.7 %collective-permute-done.9.refs_2_ = f32[8,256]{1,0:T(8,128)S(1)} collective-permute-done((f32[8,256]{1,0:T(8,128)S(1)}, f32[8,256]{1,0:T(8,128)S(1)}, u32[]{:S(2)}, u32[]{:S(2)}) %collective-permute-start.9) | collective-permute-done | bytes 8224 | tf_op jit(solution)/shard_map/ppermute | solution.py:456
  27.8 0.8 %shard_map.90 = (bf16[768,256]{1,0:T(8,128)(2,1)S(1)}, bf16[3,2,128,128]{3,2,1,0:T(8,128)(2,1)S(1)}, f32[2,128,128]{2,1,0:T(8,128)S(1)}, f32[768,128]{1,0:T(8,128)S(1)}, f32[768,128]{1,0:T(8,128)S(1)}) custom-call(f32[8,256]{1,0:T(8,128)S(1)} %get-tuple-element.97.refs_0_, f32[8,256]{1,0:T(8,128)S(1)} %collective-permute-done.8.refs_1_, ...), custom_call_target="tpu_custom_call" | custom-call | flops 50331648 | tf_op jit(solution)/shard_map/pallas_call | solution.py:55
  29.0 0.6 %collective-permute-start.12 = (f32[2,128,128]{2,1,0:T(8,128)S(1)}, f32[2,128,128]{2,1,0:T(8,128)S(1)}, u32[]{:S(2)}, u32[]{:S(2)}) collective-permute-start(f32[2,128,128]{2,1,0:T(8,128)S(1)} %get-tuple-element.117), channel_id=1, source_target_pairs={{28,24},{24,28},{20,16},{16,20},{12,8},{8,12},{4,0},{0,4},{29,25},... | collective-permute-start | bytes 393224 | tf_op jit(solution)/shard_map/ppermute | solution.py:381
  30.2 1.5 %collective-permute-start.13 = (f32[2,128,128]{2,1,0:T(8,128)S(1)}, f32[2,128,128]{2,1,0:T(8,128)S(1)}, u32[]{:S(2)}, u32[]{:S(2)}) collective-permute-start(f32[2,128,128]{2,1,0:T(8,128)S(1)} %shard_map.93.refs_2_.refs_6_), channel_id=1, source_target_pairs={{28,20},{24,8},{20,28},{16,0},{12,4},{8,24},{4,12},{0,16},{29,21},... | collective-permute-start | bytes 393224 | tf_op jit(solution)/shard_map/ppermute | solution.py:381
  31.7 0.6 %collective-permute-start.14 = (f32[2,128,128]{2,1,0:T(8,128)S(1)}, f32[2,128,128]{2,1,0:T(8,128)S(1)}, u32[]{:S(2)}, u32[]{:S(2)}) collective-permute-start(f32[2,128,128]{2,1,0:T(8,128)S(1)} %shard_map.94.refs_7_), channel_id=1, source_target_pairs={{28,20},{24,8},{20,28},{16,0},{12,4},{8,24},{4,12},{0,16},{29,21},... | collective-permute-start | bytes 393224 | tf_op jit(solution)/shard_map/ppermute | solution.py:381
  32.4 2.7 %shard_map.95 = (bf16[768,512]{1,0:T(8,128)(2,1)S(1)}, f32[768,512]{1,0:T(8,128)S(1)}, f32[768,512]{1,0:T(8,128)S(1)}) custom-call(bf16[768,512]{1,0:T(8,128)(2,1)S(1)} %get-tuple-element.88.q_ref, bf16[768,512]{1,0:T(8,128)(2,1)S(1)} %get-tuple-element.78.k_ref.refs_0_, bf16[768,512]{1,0:T(8,128)(2,1)S(1)} %get-tuple-element.79.v_ref.refs_1_, ...), custom_call_target="tpu_custom_call" | custom-call | flops 905969664 | tf_op jit(solution)/shard_map/pallas_call | solution.py:55
  35.3 1.6 %collective-permute-start.16 = (f32[2,128,128]{2,1,0:T(8,128)S(1)}, f32[2,128,128]{2,1,0:T(8,128)S(1)}, u32[]{:S(2)}, u32[]{:S(2)}) collective-permute-start(f32[2,128,128]{2,1,0:T(8,128)S(1)} %shard_map.96.refs_4_.refs_7_), channel_id=1, source_target_pairs={{28,12},{24,16},{20,4},{16,24},{12,28},{8,0},{4,20},{0,8},{29,13},... | collective-permute-start | bytes 393224 | tf_op jit(solution)/shard_map/ppermute | solution.py:381
  36.9 1.4 %collective-permute-start.15 = (f32[2,128,128]{2,1,0:T(8,128)S(1)}, f32[2,128,128]{2,1,0:T(8,128)S(1)}, u32[]{:S(2)}, u32[]{:S(2)}) collective-permute-start(f32[2,128,128]{2,1,0:T(8,128)S(1)} %shard_map.97.refs_8_), channel_id=1, source_target_pairs={{28,12},{24,16},{20,4},{16,24},{12,28},{8,0},{4,20},{0,8},{29,13},... | collective-permute-start | bytes 393224 | tf_op jit(solution)/shard_map/ppermute | solution.py:381
  38.2 3.3 %shard_map.98 = (bf16[768,1024]{1,0:T(8,128)(2,1)}, bf16[256,512]{1,0:T(8,128)(2,1)S(1)}, f32[768,512]{1,0:T(8,128)S(1)}, f32[768,512]{1,0:T(8,128)S(1)}) custom-call(bf16[768,512]{1,0:T(8,128)(2,1)S(1)} %get-tuple-element.76.q_ref, bf16[768,512]{1,0:T(8,128)(2,1)S(1)} %get-tuple-element.69.k_ref.refs_5_.refs_0_, ...), custom_call_target="tpu_custom_call" | custom-call | flops 905969664 | tf_op jit(solution)/shard_map/pallas_call | solution.py:55
  42.2 0.6 %collective-permute-start.17 = (f32[2,128,128]{2,1,0:T(8,128)S(1)}, f32[2,128,128]{2,1,0:T(8,128)S(1)}, u32[]{:S(2)}, u32[]{:S(2)}) collective-permute-start(f32[2,128,128]{2,1,0:T(8,128)S(1)} %get-tuple-element.126), channel_id=1, source_target_pairs={{28,24},{24,28},{20,16},{16,20},{12,8},{8,12},{4,0},{0,4},{29,25},... | collective-permute-start | bytes 393224 | tf_op jit(solution)/shard_map/ppermute | solution.py:381
  43.1 1.3 %shard_map.102 = (bf16[768,1024]{1,0:T(8,128)(2,1)}, bf16[768,1024]{1,0:T(8,128)(2,1)}, bf16[768,256]{1,0:T(8,128)(2,1)S(1)}, bf16[768,256]{1,0:T(8,128)(2,1)S(1)}) custom-call(bf16[768,512]{1,0:T(8,128)(2,1)S(1)} %get-tuple-element.78.k_ref.refs_0_, bf16[768,512]{1,0:T(8,128)(2,1)S(1)} %get-tuple-element.79.v_ref.refs_1_, ...), custom_call_target="tpu_custom_call" | custom-call | flops 201326592 | tf_op jit(solution)/shard_map/pallas_call | solution.py:55
  44.4 1.3 %shard_map.103 = (bf16[768,1024]{1,0:T(8,128)(2,1)}, bf16[768,1024]{1,0:T(8,128)(2,1)}, bf16[768,1024]{1,0:T(8,128)(2,1)}) custom-call(bf16[768,512]{1,0:T(8,128)(2,1)S(1)} %get-tuple-element.69.k_ref.refs_5_.refs_0_, bf16[768,512]{1,0:T(8,128)(2,1)S(1)} %get-tuple-element.70.v_ref.refs_6_.refs_1_, ...), custom_call_target="tpu_custom_call", output_to_operand_aliasing={{0}: (8, {}), {1}: (9, {}), {2}: (10, {})} | custom-call | flops 100663296 | bytes 4718592 | tf_op jit(solution)/shard_map/pallas_call | solution.py:55
  (48 shorter events, 5.7 us)
Async XLA Ops:
  0.6 6.9 %copy-start.1 = (bf16[768,1024]{1,0:T(8,128)(2,1)S(1)}, bf16[768,1024]{1,0:T(8,128)(2,1)}, u32[]{:S(2)}) copy-start(bf16[768,1024]{1,0:T(8,128)(2,1)} %og_ref.3) | copy-start | bytes 4718596
  2.9 4.7 %copy-start = (bf16[768,1024]{1,0:T(8,128)(2,1)S(1)}, bf16[768,1024]{1,0:T(8,128)(2,1)}, u32[]{:S(2)}) copy-start(bf16[768,1024]{1,0:T(8,128)(2,1)} %query_ref.3) | copy-start | bytes 4718596
  2.9 4.7 %copy-start.2 = (f32[1024]{0:T(1024)S(1)}, f32[1024]{0:T(1024)}, u32[]{:S(2)}) copy-start(f32[1024]{0:T(1024)} %param.9) | copy-start | bytes 12292
  2.9 1.5 %collective-permute-start = (f32[2,128,128]{2,1,0:T(8,128)S(1)}, f32[2,128,128]{2,1,0:T(8,128)S(1)}, u32[]{:S(2)}, u32[]{:S(2)}) collective-permute-start(f32[2,128,128]{2,1,0:T(8,128)S(1)} %get-tuple-element.73), channel_id=1, source_target_pairs={{0,4},{4,0},{8,12},{12,8},{16,20},{20,16},{24,28},{28,24},{1,5},{5... | collective-permute-start | bytes 393224 | tf_op jit(solution)/shard_map/ppermute | solution.py:381
  3.5 3.9 %collective-permute-start.1 = (f32[2,128,128]{2,1,0:T(8,128)S(1)}, f32[2,128,128]{2,1,0:T(8,128)S(1)}, u32[]{:S(2)}, u32[]{:S(2)}) collective-permute-start(f32[2,128,128]{2,1,0:T(8,128)S(1)} %get-tuple-element.75), channel_id=1, source_target_pairs={{0,4},{4,0},{8,12},{12,8},{16,20},{20,16},{24,28},{28,24},{1,5},{5... | collective-permute-start | bytes 393224 | tf_op jit(solution)/shard_map/ppermute | solution.py:381
  4.5 5.9 %collective-permute-start.2 = (f32[2,128,128]{2,1,0:T(8,128)S(1)}, f32[2,128,128]{2,1,0:T(8,128)S(1)}, u32[]{:S(2)}, u32[]{:S(2)}) collective-permute-start(f32[2,128,128]{2,1,0:T(8,128)S(1)} %shard_map.78.refs_2_.refs_0_), channel_id=1, source_target_pairs={{0,8},{4,20},{8,0},{12,28},{16,24},{20,4},{24,16},{28,12},{1,9},{5... | collective-permute-start | bytes 393224 | tf_op jit(solution)/shard_map/ppermute | solution.py:381
  7.4 5.1 %collective-permute-start.4 = (f32[2,128,128]{2,1,0:T(8,128)S(1)}, f32[2,128,128]{2,1,0:T(8,128)S(1)}, u32[]{:S(2)}, u32[]{:S(2)}) collective-permute-start(f32[2,128,128]{2,1,0:T(8,128)S(1)} %shard_map.79.refs_1_), channel_id=1, source_target_pairs={{0,8},{4,20},{8,0},{12,28},{16,24},{20,4},{24,16},{28,12},{1,9},{5... | collective-permute-start | bytes 393224 | tf_op jit(solution)/shard_map/ppermute | solution.py:381
  10.4 5.6 %collective-permute-start.3 = (f32[2,128,128]{2,1,0:T(8,128)S(1)}, f32[2,128,128]{2,1,0:T(8,128)S(1)}, u32[]{:S(2)}, u32[]{:S(2)}) collective-permute-start(f32[2,128,128]{2,1,0:T(8,128)S(1)} %shard_map.81.refs_4_.refs_0_), channel_id=1, source_target_pairs={{0,16},{4,12},{8,24},{12,4},{16,0},{20,28},{24,8},{28,20},{1,17},{... | collective-permute-start | bytes 393224 | tf_op jit(solution)/shard_map/ppermute | solution.py:381
  12.5 5.0 %collective-permute-start.5 = (f32[2,128,128]{2,1,0:T(8,128)S(1)}, f32[2,128,128]{2,1,0:T(8,128)S(1)}, u32[]{:S(2)}, u32[]{:S(2)}) collective-permute-start(f32[2,128,128]{2,1,0:T(8,128)S(1)} %shard_map.82.refs_1_), channel_id=1, source_target_pairs={{0,16},{4,12},{8,24},{12,4},{16,0},{20,28},{24,8},{28,20},{1,17},{... | collective-permute-start | bytes 393224 | tf_op jit(solution)/shard_map/ppermute | solution.py:381
  16.1 2.0 %collective-permute-start.7 = (f32[2,128,128]{2,1,0:T(8,128)S(1)}, f32[2,128,128]{2,1,0:T(8,128)S(1)}, u32[]{:S(2)}, u32[]{:S(2)}) collective-permute-start(f32[2,128,128]{2,1,0:T(8,128)S(1)} %get-tuple-element.83.refs_5_), channel_id=1, source_target_pairs={{0,4},{4,0},{8,12},{12,8},{16,20},{20,16},{24,28},{28,24},{1,5},{5... | collective-permute-start | bytes 393224 | tf_op jit(solution)/shard_map/ppermute | solution.py:381
  17.6 1.4 %collective-permute-start.6 = (f32[2,128,128]{2,1,0:T(8,128)S(1)}, f32[2,128,128]{2,1,0:T(8,128)S(1)}, u32[]{:S(2)}, u32[]{:S(2)}) collective-permute-start(f32[2,128,128]{2,1,0:T(8,128)S(1)} %get-tuple-element.91), channel_id=1, source_target_pairs={{0,4},{4,0},{8,12},{12,8},{16,20},{20,16},{24,28},{28,24},{1,5},{5... | collective-permute-start | bytes 393224 | tf_op jit(solution)/shard_map/ppermute | solution.py:381
  19.6 5.5 %collective-permute-start.10 = (f32[8,256]{1,0:T(8,128)S(1)}, f32[8,256]{1,0:T(8,128)S(1)}, u32[]{:S(2)}, u32[]{:S(2)}) collective-permute-start(f32[8,256]{1,0:T(8,128)S(1)} %get-tuple-element.97.refs_0_), channel_id=1, source_target_pairs={{0,3},{1,2},{2,1},{3,0},{4,7},{5,6},{6,5},{7,4},{8,11},{9,10},{10,... | collective-permute-start | bytes 24584 | tf_op jit(solution)/shard_map/ppermute | solution.py:456
  23.2 4.5 %collective-permute-start.9 = (f32[8,256]{1,0:T(8,128)S(1)}, f32[8,256]{1,0:T(8,128)S(1)}, u32[]{:S(2)}, u32[]{:S(2)}) collective-permute-start(f32[8,256]{1,0:T(8,128)S(1)} %get-tuple-element.97.refs_0_), channel_id=1, source_target_pairs={{0,2},{1,3},{2,0},{3,1},{4,6},{5,7},{6,4},{7,5},{8,10},{9,11},{10,... | collective-permute-start | bytes 24584 | tf_op jit(solution)/shard_map/ppermute | solution.py:456
  23.2 4.5 %collective-permute-start.8 = (f32[8,256]{1,0:T(8,128)S(1)}, f32[8,256]{1,0:T(8,128)S(1)}, u32[]{:S(2)}, u32[]{:S(2)}) collective-permute-start(f32[8,256]{1,0:T(8,128)S(1)} %get-tuple-element.97.refs_0_), channel_id=1, source_target_pairs={{0,1},{1,0},{2,3},{3,2},{4,5},{5,4},{6,7},{7,6},{8,9},{9,8},{10,11... | collective-permute-start | bytes 24584 | tf_op jit(solution)/shard_map/ppermute | solution.py:456
  28.6 1.6 %collective-permute-start.11 = (f32[2,128,128]{2,1,0:T(8,128)S(1)}, f32[2,128,128]{2,1,0:T(8,128)S(1)}, u32[]{:S(2)}, u32[]{:S(2)}) collective-permute-start(f32[2,128,128]{2,1,0:T(8,128)S(1)} %get-tuple-element.115), channel_id=1, source_target_pairs={{28,24},{24,28},{20,16},{16,20},{12,8},{8,12},{4,0},{0,4},{29,25},... | collective-permute-start | bytes 393224 | tf_op jit(solution)/shard_map/ppermute | solution.py:381
  29.0 2.7 %collective-permute-start.12 = (f32[2,128,128]{2,1,0:T(8,128)S(1)}, f32[2,128,128]{2,1,0:T(8,128)S(1)}, u32[]{:S(2)}, u32[]{:S(2)}) collective-permute-start(f32[2,128,128]{2,1,0:T(8,128)S(1)} %get-tuple-element.117), channel_id=1, source_target_pairs={{28,24},{24,28},{20,16},{16,20},{12,8},{8,12},{4,0},{0,4},{29,25},... | collective-permute-start | bytes 393224 | tf_op jit(solution)/shard_map/ppermute | solution.py:381
  30.2 5.0 %collective-permute-start.13 = (f32[2,128,128]{2,1,0:T(8,128)S(1)}, f32[2,128,128]{2,1,0:T(8,128)S(1)}, u32[]{:S(2)}, u32[]{:S(2)}) collective-permute-start(f32[2,128,128]{2,1,0:T(8,128)S(1)} %shard_map.93.refs_2_.refs_6_), channel_id=1, source_target_pairs={{28,20},{24,8},{20,28},{16,0},{12,4},{8,24},{4,12},{0,16},{29,21},... | collective-permute-start | bytes 393224 | tf_op jit(solution)/shard_map/ppermute | solution.py:381
  31.7 5.1 %collective-permute-start.14 = (f32[2,128,128]{2,1,0:T(8,128)S(1)}, f32[2,128,128]{2,1,0:T(8,128)S(1)}, u32[]{:S(2)}, u32[]{:S(2)}) collective-permute-start(f32[2,128,128]{2,1,0:T(8,128)S(1)} %shard_map.94.refs_7_), channel_id=1, source_target_pairs={{28,20},{24,8},{20,28},{16,0},{12,4},{8,24},{4,12},{0,16},{29,21},... | collective-permute-start | bytes 393224 | tf_op jit(solution)/shard_map/ppermute | solution.py:381
  35.3 6.3 %collective-permute-start.16 = (f32[2,128,128]{2,1,0:T(8,128)S(1)}, f32[2,128,128]{2,1,0:T(8,128)S(1)}, u32[]{:S(2)}, u32[]{:S(2)}) collective-permute-start(f32[2,128,128]{2,1,0:T(8,128)S(1)} %shard_map.96.refs_4_.refs_7_), channel_id=1, source_target_pairs={{28,12},{24,16},{20,4},{16,24},{12,28},{8,0},{4,20},{0,8},{29,13},... | collective-permute-start | bytes 393224 | tf_op jit(solution)/shard_map/ppermute | solution.py:381
  36.9 5.3 %collective-permute-start.15 = (f32[2,128,128]{2,1,0:T(8,128)S(1)}, f32[2,128,128]{2,1,0:T(8,128)S(1)}, u32[]{:S(2)}, u32[]{:S(2)}) collective-permute-start(f32[2,128,128]{2,1,0:T(8,128)S(1)} %shard_map.97.refs_8_), channel_id=1, source_target_pairs={{28,12},{24,16},{20,4},{16,24},{12,28},{8,0},{4,20},{0,8},{29,13},... | collective-permute-start | bytes 393224 | tf_op jit(solution)/shard_map/ppermute | solution.py:381
  41.6 1.4 %collective-permute-start.18 = (f32[2,128,128]{2,1,0:T(8,128)S(1)}, f32[2,128,128]{2,1,0:T(8,128)S(1)}, u32[]{:S(2)}, u32[]{:S(2)}) collective-permute-start(f32[2,128,128]{2,1,0:T(8,128)S(1)} %get-tuple-element.122.refs_5_), channel_id=1, source_target_pairs={{28,24},{24,28},{20,16},{16,20},{12,8},{8,12},{4,0},{0,4},{29,25},... | collective-permute-start | bytes 393224 | tf_op jit(solution)/shard_map/ppermute | solution.py:381
  42.2 2.2 %collective-permute-start.17 = (f32[2,128,128]{2,1,0:T(8,128)S(1)}, f32[2,128,128]{2,1,0:T(8,128)S(1)}, u32[]{:S(2)}, u32[]{:S(2)}) collective-permute-start(f32[2,128,128]{2,1,0:T(8,128)S(1)} %get-tuple-element.126), channel_id=1, source_target_pairs={{28,24},{24,28},{20,16},{16,20},{12,8},{8,12},{4,0},{0,4},{29,25},... | collective-permute-start | bytes 393224 | tf_op jit(solution)/shard_map/ppermute | solution.py:381

commit v17 on v16

--- a/solution.py
+++ b/solution.py
@@ -101,15 +101,23 @@
         sum_refs[j // PIECE][j % PIECE] = totals[j]
 
 
-def first_kernel(k_hbm, v_hbm, k1, v1, k2, v2, pre_ref, *refs):
-    *sum_refs, sems1, sems2 = refs
-    now = fetches((k_hbm, v_hbm), (k1, v1), sems1, False)
-    later = fetches((k_hbm, v_hbm), (k2, v2), sems2, True)
-    for copy in now + later:
+def first_kernel(k_hbm, v_hbm, k1, v1, pre_ref, *refs):
+    *sum_refs, sems = refs
+    copies = fetches((k_hbm, v_hbm), (k1, v1), sems, False)
+    for copy in copies:
         copy.start()
-    sum_states(k1, v1, pre_ref, *sum_refs, copies=now)
-    for copy in later:
-        copy.wait()
+    sum_states(k1, v1, pre_ref, *sum_refs, copies=copies)
+
+
+def second_kernel(key_ref, value_ref, k2, v2, pre_ref, *sum_refs):
+    rows, width = k2.shape
+    first = lax.rem(lax.axis_index("seq"), 2) * width
+    for part in chunks_of(rows):
+        for j in range(width // HEAD_DIM):
+            source = pl.ds(pl.multiple_of(first + j * HEAD_DIM, HEAD_DIM), HEAD_DIM)
+            k2[part, lanes_of(j)] = key_ref[part, source]
+            v2[part, lanes_of(j)] = value_ref[part, source]
+    sum_states(k2, v2, pre_ref, *sum_refs)
 
 
 def inner_kernel(same, query_ref, og_ref, k_ref, v_ref, gain_ref, pre_ref, *refs):
@@ -394,7 +402,6 @@
     full = width * peers
     gain = gain.reshape(1, width)
     pin = lambda x: pltpu.with_memory_space_constraint(x, pltpu.HBM)
-    key_in, value = pin(key_in), pin(value)
     unit = 2 * rows * half * HEAD_DIM
     partial = functools.partial
 
@@ -407,13 +414,14 @@
     whole = shape((rows, width), BF16)
     sems = pltpu.SemaphoreType.DMA((2 * chunks,))
 
-    k1, v1, k2, v2, pre1, *sends = run(
-        first_kernel, unit, [HBM, HBM], [VMEM] * (5 + count), [thin] * 4 + [inside] + [states] * count,
-        (key_in, value), [sems, sems],
+    shapes = [thin, thin, inside] + [states] * count
+    k1, v1, pre1, *sends = run(
+        first_kernel, unit, [HBM, HBM], [VMEM] * len(shapes), shapes,
+        (pin(key_in), pin(value)), [sems],
     )
     extras = [nearby(send, False) for send in sends]
-    pre2, *keeps = run(
-        sum_states, unit, [VMEM, VMEM], [VMEM] * (1 + count), [inside] + [states] * count, (k2, v2)
+    k2, v2, pre2, *keeps = run(
+        second_kernel, unit, [VMEM, VMEM], [VMEM] * len(shapes), shapes, (key_in, value)
     )
 
     def inner_of(same, k, v, pre):

time: 46 us -> 46 us (level)
  Pallas kernels: 19.2 us -> 19.7 us
  waiting for transfers between devices: 7.34 us -> 6.84 us
    ppermute x16, waiting for transfers between devices: 3.58 us -> 3.07 us  [move(): return lax.ppermute(value, 'seq', pairs)]
    pallas_call x28, Pallas kernels: 19.2 us -> 19.7 us  [run(): pl.pallas_call(kernel, in_specs=in_specs, out_specs=out_specs, out_shape=...]
  transfers between devices with their start and end apart: 19 -> 19, of which waited for: 8 -> 7; matrix products, arithmetic and copies ran while one was open for 0% -> 0% of each run, Pallas kernels for 31% -> 33%
where the time goes in v17:
time: 46 us; the launch traced here: 45.9 us
  Pallas kernels  19.7 us (43%)
  starting transfers between devices  18.3 us (40%)
  waiting for transfers between devices  6.84 us (15%)
  between operations  1.08 us (2%)
    pallas_call x28, Pallas kernels, run(): pl.pallas_call(kernel, in_specs=in_specs, out_specs=out_specs, out_shape=...  19.7 us
    ppermute x16, starting transfers between devices, move(): return lax.ppermute(value, 'seq', pairs)  13.8 us
    ppermute x3, starting transfers between devices, shards(): lax.ppermute(sums, 'head', [(r, r ^ other) for r in range(peers)])  4.45 us
    ppermute x3, waiting for transfers between devices, shards(): lax.ppermute(sums, 'head', [(r, r ^ other) for r in range(peers)])  3.77 us
    ppermute x16, waiting for transfers between devices, move(): return lax.ppermute(value, 'seq', pairs)  3.07 us
  transfers between devices with their start and end apart: 19, of which 7 were waited for; matrix products, arithmetic and copies ran while one was open for 0% of the time, Pallas kernels for 33%

profile of v17, /device:TPU:0, one launch (start us, length us, event | category | flops | bytes accessed | tf_op | source)
XLA Modules:
  0.0 45.9 jit_solution(13290319523936331182)
XLA Ops:
  0.7 2.1 %shard_map.77 = (bf16[768,512]{1,0:T(8,128)(2,1)S(1)}, bf16[768,512]{1,0:T(8,128)(2,1)S(1)}, bf16[3,4,128,128]{3,2,1,0:T(8,128)(2,1)S(1)}, f32[2,128,128]{2,1,0:T(8,128)S(1)}, f32[2,128,128]{2,1,0:T(8,128)S(1)}) custom-call(bf16[768,1024]{1,0:T(8,128)(2,1)} %k_hbm.1, bf16[768,1024]{1,0:T(8,128)(2,1)} %v_hbm.1), custom_call_target="tpu_custom_call" | custom-call | flops 100663296 | bytes 3145728 | tf_op jit(solution)/shard_map/pallas_call | solution.py:55
  3.4 0.9 %shard_map.76 = (bf16[768,512]{1,0:T(8,128)(2,1)S(1)}, bf16[768,512]{1,0:T(8,128)(2,1)S(1)}, bf16[3,4,128,128]{3,2,1,0:T(8,128)(2,1)S(1)}, f32[2,128,128]{2,1,0:T(8,128)S(1)}, f32[2,128,128]{2,1,0:T(8,128)S(1)}) custom-call(bf16[768,1024]{1,0:T(8,128)(2,1)S(1)} %copy-done, bf16[768,1024]{1,0:T(8,128)(2,1)S(1)} %copy-done.1), custom_call_target="tpu_custom_call" | custom-call | flops 100663296 | tf_op jit(solution)/shard_map/pallas_call | solution.py:55
  4.3 2.9 %collective-permute-start.2 = (f32[2,128,128]{2,1,0:T(8,128)S(1)}, f32[2,128,128]{2,1,0:T(8,128)S(1)}, u32[]{:S(2)}, u32[]{:S(2)}) collective-permute-start(f32[2,128,128]{2,1,0:T(8,128)S(1)} %shard_map.78.refs_2_.refs_0_), channel_id=1, source_target_pairs={{0,8},{4,20},{8,0},{12,28},{16,24},{20,4},{24,16},{28,12},{1,9},{5... | collective-permute-start | bytes 393224 | tf_op jit(solution)/shard_map/ppermute | solution.py:389
  7.4 1.9 %shard_map.80 = (bf16[768,512]{1,0:T(8,128)(2,1)S(1)}, f32[768,512]{1,0:T(8,128)S(1)}, f32[768,512]{1,0:T(8,128)S(1)}, bf16[512,768]{1,0:T(8,128)(2,1)S(1)}, bf16[4,768,256]{2,1,0:T(8,128)(2,1)S(1)}) custom-call(bf16[768,1024]{1,0:T(8,128)(2,1)S(1)} %copy-done.2, bf16[768,1024]{1,0:T(8,128)(2,1)S(1)} %copy-done.3, ...), custom_call_target="tpu_custom_call" | custom-call | flops 603979776 | tf_op jit(solution)/shard_map/pallas_call | solution.py:55
  9.3 0.9 %collective-permute-done.2.refs_2_ = f32[2,128,128]{2,1,0:T(8,128)S(1)} collective-permute-done((f32[2,128,128]{2,1,0:T(8,128)S(1)}, f32[2,128,128]{2,1,0:T(8,128)S(1)}, u32[]{:S(2)}, u32[]{:S(2)}) %collective-permute-start.2) | collective-permute-done | bytes 131104 | tf_op jit(solution)/shard_map/ppermute | solution.py:389
  10.2 2.1 %collective-permute-start.3 = (f32[2,128,128]{2,1,0:T(8,128)S(1)}, f32[2,128,128]{2,1,0:T(8,128)S(1)}, u32[]{:S(2)}, u32[]{:S(2)}) collective-permute-start(f32[2,128,128]{2,1,0:T(8,128)S(1)} %shard_map.81.refs_4_.refs_0_), channel_id=1, source_target_pairs={{0,16},{4,12},{8,24},{12,4},{16,0},{20,28},{24,8},{28,20},{1,17},{... | collective-permute-start | bytes 393224 | tf_op jit(solution)/shard_map/ppermute | solution.py:389
  12.4 1.5 %collective-permute-start.5 = (f32[2,128,128]{2,1,0:T(8,128)S(1)}, f32[2,128,128]{2,1,0:T(8,128)S(1)}, u32[]{:S(2)}, u32[]{:S(2)}) collective-permute-start(f32[2,128,128]{2,1,0:T(8,128)S(1)} %shard_map.82.refs_1_), channel_id=1, source_target_pairs={{0,16},{4,12},{8,24},{12,4},{16,0},{20,28},{24,8},{28,20},{1,17},{... | collective-permute-start | bytes 393224 | tf_op jit(solution)/shard_map/ppermute | solution.py:389
  13.9 1.9 %shard_map.83 = (bf16[768,512]{1,0:T(8,128)(2,1)S(1)}, f32[768,512]{1,0:T(8,128)S(1)}, f32[768,512]{1,0:T(8,128)S(1)}, bf16[512,768]{1,0:T(8,128)(2,1)S(1)}, bf16[4,768,256]{2,1,0:T(8,128)(2,1)S(1)}) custom-call(bf16[768,1024]{1,0:T(8,128)(2,1)S(1)} %copy-done.2, bf16[768,1024]{1,0:T(8,128)(2,1)S(1)} %copy-done.3, ...), custom_call_target="tpu_custom_call" | custom-call | flops 603979776 | tf_op jit(solution)/shard_map/pallas_call | solution.py:55
  16.3 1.1 %collective-permute-done.5.refs_3_ = f32[2,128,128]{2,1,0:T(8,128)S(1)} collective-permute-done((f32[2,128,128]{2,1,0:T(8,128)S(1)}, f32[2,128,128]{2,1,0:T(8,128)S(1)}, u32[]{:S(2)}, u32[]{:S(2)}) %collective-permute-start.5) | collective-permute-done | bytes 131104 | tf_op jit(solution)/shard_map/ppermute | solution.py:389
  18.2 0.7 %collective-permute-done.6.state_ref.refs_1_ = f32[2,128,128]{2,1,0:T(8,128)S(1)} collective-permute-done((f32[2,128,128]{2,1,0:T(8,128)S(1)}, f32[2,128,128]{2,1,0:T(8,128)S(1)}, u32[]{:S(2)}, u32[]{:S(2)}) %collective-permute-start.6) | collective-permute-done | bytes 131104 | tf_op jit(solution)/shard_map/ppermute | solution.py:389
  19.4 3.7 %collective-permute-start.10 = (f32[8,256]{1,0:T(8,128)S(1)}, f32[8,256]{1,0:T(8,128)S(1)}, u32[]{:S(2)}, u32[]{:S(2)}) collective-permute-start(f32[8,256]{1,0:T(8,128)S(1)} %get-tuple-element.97.refs_0_), channel_id=1, source_target_pairs={{0,3},{1,2},{2,1},{3,0},{4,7},{5,6},{6,5},{7,4},{8,11},{9,10},{10,... | collective-permute-start | bytes 24584 | tf_op jit(solution)/shard_map/ppermute | solution.py:464
  23.1 0.8 %collective-permute-start.8 = (f32[8,256]{1,0:T(8,128)S(1)}, f32[8,256]{1,0:T(8,128)S(1)}, u32[]{:S(2)}, u32[]{:S(2)}) collective-permute-start(f32[8,256]{1,0:T(8,128)S(1)} %get-tuple-element.97.refs_0_), channel_id=1, source_target_pairs={{0,1},{1,0},{2,3},{3,2},{4,5},{5,4},{6,7},{7,6},{8,9},{9,8},{10,11... | collective-permute-start | bytes 24584 | tf_op jit(solution)/shard_map/ppermute | solution.py:464
  23.9 1.1 %collective-permute-done.10.refs_3_ = f32[8,256]{1,0:T(8,128)S(1)} collective-permute-done((f32[8,256]{1,0:T(8,128)S(1)}, f32[8,256]{1,0:T(8,128)S(1)}, u32[]{:S(2)}, u32[]{:S(2)}) %collective-permute-start.10) | collective-permute-done | bytes 8224 | tf_op jit(solution)/shard_map/ppermute | solution.py:464
  24.9 2.7 %collective-permute-done.9.refs_2_ = f32[8,256]{1,0:T(8,128)S(1)} collective-permute-done((f32[8,256]{1,0:T(8,128)S(1)}, f32[8,256]{1,0:T(8,128)S(1)}, u32[]{:S(2)}, u32[]{:S(2)}) %collective-permute-start.9) | collective-permute-done | bytes 8224 | tf_op jit(solution)/shard_map/ppermute | solution.py:464
  27.6 0.8 %shard_map.90 = (bf16[768,256]{1,0:T(8,128)(2,1)S(1)}, bf16[3,2,128,128]{3,2,1,0:T(8,128)(2,1)S(1)}, f32[2,128,128]{2,1,0:T(8,128)S(1)}, f32[768,128]{1,0:T(8,128)S(1)}, f32[768,128]{1,0:T(8,128)S(1)}) custom-call(f32[8,256]{1,0:T(8,128)S(1)} %get-tuple-element.97.refs_0_, f32[8,256]{1,0:T(8,128)S(1)} %collective-permute-done.8.refs_1_, ...), custom_call_target="tpu_custom_call" | custom-call | flops 50331648 | tf_op jit(solution)/shard_map/pallas_call | solution.py:55
  28.9 0.6 %collective-permute-start.12 = (f32[2,128,128]{2,1,0:T(8,128)S(1)}, f32[2,128,128]{2,1,0:T(8,128)S(1)}, u32[]{:S(2)}, u32[]{:S(2)}) collective-permute-start(f32[2,128,128]{2,1,0:T(8,128)S(1)} %get-tuple-element.117), channel_id=1, source_target_pairs={{28,24},{24,28},{20,16},{16,20},{12,8},{8,12},{4,0},{0,4},{29,25},... | collective-permute-start | bytes 393224 | tf_op jit(solution)/shard_map/ppermute | solution.py:389
  30.1 1.5 %collective-permute-start.13 = (f32[2,128,128]{2,1,0:T(8,128)S(1)}, f32[2,128,128]{2,1,0:T(8,128)S(1)}, u32[]{:S(2)}, u32[]{:S(2)}) collective-permute-start(f32[2,128,128]{2,1,0:T(8,128)S(1)} %shard_map.93.refs_2_.refs_6_), channel_id=1, source_target_pairs={{28,20},{24,8},{20,28},{16,0},{12,4},{8,24},{4,12},{0,16},{29,21},... | collective-permute-start | bytes 393224 | tf_op jit(solution)/shard_map/ppermute | solution.py:389
  31.6 0.6 %collective-permute-start.14 = (f32[2,128,128]{2,1,0:T(8,128)S(1)}, f32[2,128,128]{2,1,0:T(8,128)S(1)}, u32[]{:S(2)}, u32[]{:S(2)}) collective-permute-start(f32[2,128,128]{2,1,0:T(8,128)S(1)} %shard_map.94.refs_7_), channel_id=1, source_target_pairs={{28,20},{24,8},{20,28},{16,0},{12,4},{8,24},{4,12},{0,16},{29,21},... | collective-permute-start | bytes 393224 | tf_op jit(solution)/shard_map/ppermute | solution.py:389
  32.2 2.8 %shard_map.95 = (bf16[768,512]{1,0:T(8,128)(2,1)S(1)}, f32[768,512]{1,0:T(8,128)S(1)}, f32[768,512]{1,0:T(8,128)S(1)}) custom-call(bf16[768,512]{1,0:T(8,128)(2,1)S(1)} %get-tuple-element.88.q_ref, bf16[768,512]{1,0:T(8,128)(2,1)S(1)} %get-tuple-element.78.k_ref.refs_0_, bf16[768,512]{1,0:T(8,128)(2,1)S(1)} %get-tuple-element.79.v_ref.refs_1_, ...), custom_call_target="tpu_custom_call" | custom-call | flops 905969664 | tf_op jit(solution)/shard_map/pallas_call | solution.py:55
  35.1 1.6 %collective-permute-start.16 = (f32[2,128,128]{2,1,0:T(8,128)S(1)}, f32[2,128,128]{2,1,0:T(8,128)S(1)}, u32[]{:S(2)}, u32[]{:S(2)}) collective-permute-start(f32[2,128,128]{2,1,0:T(8,128)S(1)} %shard_map.96.refs_4_.refs_7_), channel_id=1, source_target_pairs={{28,12},{24,16},{20,4},{16,24},{12,28},{8,0},{4,20},{0,8},{29,13},... | collective-permute-start | bytes 393224 | tf_op jit(solution)/shard_map/ppermute | solution.py:389
  36.7 1.4 %collective-permute-start.15 = (f32[2,128,128]{2,1,0:T(8,128)S(1)}, f32[2,128,128]{2,1,0:T(8,128)S(1)}, u32[]{:S(2)}, u32[]{:S(2)}) collective-permute-start(f32[2,128,128]{2,1,0:T(8,128)S(1)} %shard_map.97.refs_8_), channel_id=1, source_target_pairs={{28,12},{24,16},{20,4},{16,24},{12,28},{8,0},{4,20},{0,8},{29,13},... | collective-permute-start | bytes 393224 | tf_op jit(solution)/shard_map/ppermute | solution.py:389
  38.1 3.4 %shard_map.98 = (bf16[768,1024]{1,0:T(8,128)(2,1)}, bf16[256,512]{1,0:T(8,128)(2,1)S(1)}, f32[768,512]{1,0:T(8,128)S(1)}, f32[768,512]{1,0:T(8,128)S(1)}) custom-call(bf16[768,512]{1,0:T(8,128)(2,1)S(1)} %get-tuple-element.76.q_ref, bf16[768,512]{1,0:T(8,128)(2,1)S(1)} %get-tuple-element.69.k_ref.refs_5_.refs_0_, ...), custom_call_target="tpu_custom_call" | custom-call | flops 905969664 | tf_op jit(solution)/shard_map/pallas_call | solution.py:55
  43.0 1.3 %shard_map.102 = (bf16[768,1024]{1,0:T(8,128)(2,1)}, bf16[768,1024]{1,0:T(8,128)(2,1)}, bf16[768,256]{1,0:T(8,128)(2,1)S(1)}, bf16[768,256]{1,0:T(8,128)(2,1)S(1)}) custom-call(bf16[768,512]{1,0:T(8,128)(2,1)S(1)} %get-tuple-element.78.k_ref.refs_0_, bf16[768,512]{1,0:T(8,128)(2,1)S(1)} %get-tuple-element.79.v_ref.refs_1_, ...), custom_call_target="tpu_custom_call" | custom-call | flops 201326592 | tf_op jit(solution)/shard_map/pallas_call | solution.py:55
  44.4 1.3 %shard_map.103 = (bf16[768,1024]{1,0:T(8,128)(2,1)}, bf16[768,1024]{1,0:T(8,128)(2,1)}, bf16[768,1024]{1,0:T(8,128)(2,1)}) custom-call(bf16[768,512]{1,0:T(8,128)(2,1)S(1)} %get-tuple-element.69.k_ref.refs_5_.refs_0_, bf16[768,512]{1,0:T(8,128)(2,1)S(1)} %get-tuple-element.70.v_ref.refs_6_.refs_1_, ...), custom_call_target="tpu_custom_call", output_to_operand_aliasing={{0}: (8, {}), {1}: (9, {}), {2}: (10, {})} | custom-call | flops 100663296 | bytes 4718592 | tf_op jit(solution)/shard_map/pallas_call | solution.py:55
  (52 shorter events, 5.3 us)
Async XLA Ops:
  0.6 2.7 %copy-start.1 = (bf16[768,1024]{1,0:T(8,128)(2,1)S(1)}, bf16[768,1024]{1,0:T(8,128)(2,1)}, u32[]{:S(2)}) copy-start(bf16[768,1024]{1,0:T(8,128)(2,1)} %v_hbm.1) | copy-start | bytes 4718596
  0.6 2.7 %copy-start = (bf16[768,1024]{1,0:T(8,128)(2,1)S(1)}, bf16[768,1024]{1,0:T(8,128)(2,1)}, u32[]{:S(2)}) copy-start(bf16[768,1024]{1,0:T(8,128)(2,1)} %k_hbm.1) | copy-start | bytes 4718596
  2.7 1.5 %collective-permute-start = (f32[2,128,128]{2,1,0:T(8,128)S(1)}, f32[2,128,128]{2,1,0:T(8,128)S(1)}, u32[]{:S(2)}, u32[]{:S(2)}) collective-permute-start(f32[2,128,128]{2,1,0:T(8,128)S(1)} %get-tuple-element.73), channel_id=1, source_target_pairs={{0,4},{4,0},{8,12},{12,8},{16,20},{20,16},{24,28},{28,24},{1,5},{5... | collective-permute-start | bytes 393224 | tf_op jit(solution)/shard_map/ppermute | solution.py:389
  3.3 4.1 %copy-start.2 = (bf16[768,1024]{1,0:T(8,128)(2,1)S(1)}, bf16[768,1024]{1,0:T(8,128)(2,1)}, u32[]{:S(2)}) copy-start(bf16[768,1024]{1,0:T(8,128)(2,1)} %query_ref.3) | copy-start | bytes 4718596
  3.3 4.1 %copy-start.3 = (bf16[768,1024]{1,0:T(8,128)(2,1)S(1)}, bf16[768,1024]{1,0:T(8,128)(2,1)}, u32[]{:S(2)}) copy-start(bf16[768,1024]{1,0:T(8,128)(2,1)} %og_ref.3) | copy-start | bytes 4718596
  3.3 4.1 %copy-start.4 = (f32[1024]{0:T(1024)S(1)}, f32[1024]{0:T(1024)}, u32[]{:S(2)}) copy-start(f32[1024]{0:T(1024)} %param.9) | copy-start | bytes 12292
  3.3 4.0 %collective-permute-start.1 = (f32[2,128,128]{2,1,0:T(8,128)S(1)}, f32[2,128,128]{2,1,0:T(8,128)S(1)}, u32[]{:S(2)}, u32[]{:S(2)}) collective-permute-start(f32[2,128,128]{2,1,0:T(8,128)S(1)} %get-tuple-element.75), channel_id=1, source_target_pairs={{0,4},{4,0},{8,12},{12,8},{16,20},{20,16},{24,28},{28,24},{1,5},{5... | collective-permute-start | bytes 393224 | tf_op jit(solution)/shard_map/ppermute | solution.py:389
  4.3 5.9 %collective-permute-start.2 = (f32[2,128,128]{2,1,0:T(8,128)S(1)}, f32[2,128,128]{2,1,0:T(8,128)S(1)}, u32[]{:S(2)}, u32[]{:S(2)}) collective-permute-start(f32[2,128,128]{2,1,0:T(8,128)S(1)} %shard_map.78.refs_2_.refs_0_), channel_id=1, source_target_pairs={{0,8},{4,20},{8,0},{12,28},{16,24},{20,4},{24,16},{28,12},{1,9},{5... | collective-permute-start | bytes 393224 | tf_op jit(solution)/shard_map/ppermute | solution.py:389
  7.3 5.1 %collective-permute-start.4 = (f32[2,128,128]{2,1,0:T(8,128)S(1)}, f32[2,128,128]{2,1,0:T(8,128)S(1)}, u32[]{:S(2)}, u32[]{:S(2)}) collective-permute-start(f32[2,128,128]{2,1,0:T(8,128)S(1)} %shard_map.79.refs_1_), channel_id=1, source_target_pairs={{0,8},{4,20},{8,0},{12,28},{16,24},{20,4},{24,16},{28,12},{1,9},{5... | collective-permute-start | bytes 393224 | tf_op jit(solution)/shard_map/ppermute | solution.py:389
  10.2 5.6 %collective-permute-start.3 = (f32[2,128,128]{2,1,0:T(8,128)S(1)}, f32[2,128,128]{2,1,0:T(8,128)S(1)}, u32[]{:S(2)}, u32[]{:S(2)}) collective-permute-start(f32[2,128,128]{2,1,0:T(8,128)S(1)} %shard_map.81.refs_4_.refs_0_), channel_id=1, source_target_pairs={{0,16},{4,12},{8,24},{12,4},{16,0},{20,28},{24,8},{28,20},{1,17},{... | collective-permute-start | bytes 393224 | tf_op jit(solution)/shard_map/ppermute | solution.py:389
  12.4 5.0 %collective-permute-start.5 = (f32[2,128,128]{2,1,0:T(8,128)S(1)}, f32[2,128,128]{2,1,0:T(8,128)S(1)}, u32[]{:S(2)}, u32[]{:S(2)}) collective-permute-start(f32[2,128,128]{2,1,0:T(8,128)S(1)} %shard_map.82.refs_1_), channel_id=1, source_target_pairs={{0,16},{4,12},{8,24},{12,4},{16,0},{20,28},{24,8},{28,20},{1,17},{... | collective-permute-start | bytes 393224 | tf_op jit(solution)/shard_map/ppermute | solution.py:389
  15.9 2.0 %collective-permute-start.7 = (f32[2,128,128]{2,1,0:T(8,128)S(1)}, f32[2,128,128]{2,1,0:T(8,128)S(1)}, u32[]{:S(2)}, u32[]{:S(2)}) collective-permute-start(f32[2,128,128]{2,1,0:T(8,128)S(1)} %get-tuple-element.83.refs_5_), channel_id=1, source_target_pairs={{0,4},{4,0},{8,12},{12,8},{16,20},{20,16},{24,28},{28,24},{1,5},{5... | collective-permute-start | bytes 393224 | tf_op jit(solution)/shard_map/ppermute | solution.py:389
  17.5 1.4 %collective-permute-start.6 = (f32[2,128,128]{2,1,0:T(8,128)S(1)}, f32[2,128,128]{2,1,0:T(8,128)S(1)}, u32[]{:S(2)}, u32[]{:S(2)}) collective-permute-start(f32[2,128,128]{2,1,0:T(8,128)S(1)} %get-tuple-element.91), channel_id=1, source_target_pairs={{0,4},{4,0},{8,12},{12,8},{16,20},{20,16},{24,28},{28,24},{1,5},{5... | collective-permute-start | bytes 393224 | tf_op jit(solution)/shard_map/ppermute | solution.py:389
  19.4 5.5 %collective-permute-start.10 = (f32[8,256]{1,0:T(8,128)S(1)}, f32[8,256]{1,0:T(8,128)S(1)}, u32[]{:S(2)}, u32[]{:S(2)}) collective-permute-start(f32[8,256]{1,0:T(8,128)S(1)} %get-tuple-element.97.refs_0_), channel_id=1, source_target_pairs={{0,3},{1,2},{2,1},{3,0},{4,7},{5,6},{6,5},{7,4},{8,11},{9,10},{10,... | collective-permute-start | bytes 24584 | tf_op jit(solution)/shard_map/ppermute | solution.py:464
  23.1 4.5 %collective-permute-start.9 = (f32[8,256]{1,0:T(8,128)S(1)}, f32[8,256]{1,0:T(8,128)S(1)}, u32[]{:S(2)}, u32[]{:S(2)}) collective-permute-start(f32[8,256]{1,0:T(8,128)S(1)} %get-tuple-element.97.refs_0_), channel_id=1, source_target_pairs={{0,2},{1,3},{2,0},{3,1},{4,6},{5,7},{6,4},{7,5},{8,10},{9,11},{10,... | collective-permute-start | bytes 24584 | tf_op jit(solution)/shard_map/ppermute | solution.py:464
  23.1 4.5 %collective-permute-start.8 = (f32[8,256]{1,0:T(8,128)S(1)}, f32[8,256]{1,0:T(8,128)S(1)}, u32[]{:S(2)}, u32[]{:S(2)}) collective-permute-start(f32[8,256]{1,0:T(8,128)S(1)} %get-tuple-element.97.refs_0_), channel_id=1, source_target_pairs={{0,1},{1,0},{2,3},{3,2},{4,5},{5,4},{6,7},{7,6},{8,9},{9,8},{10,11... | collective-permute-start | bytes 24584 | tf_op jit(solution)/shard_map/ppermute | solution.py:464
  28.4 1.6 %collective-permute-start.11 = (f32[2,128,128]{2,1,0:T(8,128)S(1)}, f32[2,128,128]{2,1,0:T(8,128)S(1)}, u32[]{:S(2)}, u32[]{:S(2)}) collective-permute-start(f32[2,128,128]{2,1,0:T(8,128)S(1)} %get-tuple-element.115), channel_id=1, source_target_pairs={{28,24},{24,28},{20,16},{16,20},{12,8},{8,12},{4,0},{0,4},{29,25},... | collective-permute-start | bytes 393224 | tf_op jit(solution)/shard_map/ppermute | solution.py:389
  28.9 2.7 %collective-permute-start.12 = (f32[2,128,128]{2,1,0:T(8,128)S(1)}, f32[2,128,128]{2,1,0:T(8,128)S(1)}, u32[]{:S(2)}, u32[]{:S(2)}) collective-permute-start(f32[2,128,128]{2,1,0:T(8,128)S(1)} %get-tuple-element.117), channel_id=1, source_target_pairs={{28,24},{24,28},{20,16},{16,20},{12,8},{8,12},{4,0},{0,4},{29,25},... | collective-permute-start | bytes 393224 | tf_op jit(solution)/shard_map/ppermute | solution.py:389
  30.1 5.0 %collective-permute-start.13 = (f32[2,128,128]{2,1,0:T(8,128)S(1)}, f32[2,128,128]{2,1,0:T(8,128)S(1)}, u32[]{:S(2)}, u32[]{:S(2)}) collective-permute-start(f32[2,128,128]{2,1,0:T(8,128)S(1)} %shard_map.93.refs_2_.refs_6_), channel_id=1, source_target_pairs={{28,20},{24,8},{20,28},{16,0},{12,4},{8,24},{4,12},{0,16},{29,21},... | collective-permute-start | bytes 393224 | tf_op jit(solution)/shard_map/ppermute | solution.py:389
  31.6 5.1 %collective-permute-start.14 = (f32[2,128,128]{2,1,0:T(8,128)S(1)}, f32[2,128,128]{2,1,0:T(8,128)S(1)}, u32[]{:S(2)}, u32[]{:S(2)}) collective-permute-start(f32[2,128,128]{2,1,0:T(8,128)S(1)} %shard_map.94.refs_7_), channel_id=1, source_target_pairs={{28,20},{24,8},{20,28},{16,0},{12,4},{8,24},{4,12},{0,16},{29,21},... | collective-permute-start | bytes 393224 | tf_op jit(solution)/shard_map/ppermute | solution.py:389
  35.1 6.4 %collective-permute-start.16 = (f32[2,128,128]{2,1,0:T(8,128)S(1)}, f32[2,128,128]{2,1,0:T(8,128)S(1)}, u32[]{:S(2)}, u32[]{:S(2)}) collective-permute-start(f32[2,128,128]{2,1,0:T(8,128)S(1)} %shard_map.96.refs_4_.refs_7_), channel_id=1, source_target_pairs={{28,12},{24,16},{20,4},{16,24},{12,28},{8,0},{4,20},{0,8},{29,13},... | collective-permute-start | bytes 393224 | tf_op jit(solution)/shard_map/ppermute | solution.py:389
  36.7 5.3 %collective-permute-start.15 = (f32[2,128,128]{2,1,0:T(8,128)S(1)}, f32[2,128,128]{2,1,0:T(8,128)S(1)}, u32[]{:S(2)}, u32[]{:S(2)}) collective-permute-start(f32[2,128,128]{2,1,0:T(8,128)S(1)} %shard_map.97.refs_8_), channel_id=1, source_target_pairs={{28,12},{24,16},{20,4},{16,24},{12,28},{8,0},{4,20},{0,8},{29,13},... | collective-permute-start | bytes 393224 | tf_op jit(solution)/shard_map/ppermute | solution.py:389
  41.6 1.4 %collective-permute-start.18 = (f32[2,128,128]{2,1,0:T(8,128)S(1)}, f32[2,128,128]{2,1,0:T(8,128)S(1)}, u32[]{:S(2)}, u32[]{:S(2)}) collective-permute-start(f32[2,128,128]{2,1,0:T(8,128)S(1)} %get-tuple-element.122.refs_5_), channel_id=1, source_target_pairs={{28,24},{24,28},{20,16},{16,20},{12,8},{8,12},{4,0},{0,4},{29,25},... | collective-permute-start | bytes 393224 | tf_op jit(solution)/shard_map/ppermute | solution.py:389
  42.2 2.2 %collective-permute-start.17 = (f32[2,128,128]{2,1,0:T(8,128)S(1)}, f32[2,128,128]{2,1,0:T(8,128)S(1)}, u32[]{:S(2)}, u32[]{:S(2)}) collective-permute-start(f32[2,128,128]{2,1,0:T(8,128)S(1)} %get-tuple-element.126), channel_id=1, source_target_pairs={{28,24},{24,28},{20,16},{16,20},{12,8},{8,12},{4,0},{0,4},{29,25},... | collective-permute-start | bytes 393224 | tf_op jit(solution)/shard_map/ppermute | solution.py:389
